TPU v7x, 32 devices: a whole 2x2x4 slice. The times are simulated.
32 devices in a mesh: seq: 8 (over y, x, core), wt: 4 (over z).
Axes of the slice: x: 2, y: 2, z: 4, core: 2. Of those that a mesh axis runs over, the one named last changes fastest.
Arguments:
- tokens: bfloat16 [4, 2048, 2048], P('wt', 'seq'), may hold values from -6 to 6
- cotangent: bfloat16 [4, 2048, 2048], P('wt', 'seq'), may hold values from -6 to 6
- w_in: bfloat16 [2048, 8192], P(None, 'wt'), may hold values from -0.125 to 0.125
- w_out: bfloat16 [2048, 2048], P(None, 'wt'), may hold values from -0.125 to 0.125
- w_ffn: bfloat16 [2048, 11264], P(None, 'wt'), may hold values from -0.125 to 0.125
- w_down: bfloat16 [5632, 2048], P(None, 'wt'), may hold values from -0.078125 to 0.078125
- gain_mix: float32 [2048], replicated, may hold values from 0.1 to 1.9
- gain_gate: float32 [2048], replicated, may hold values from 0.1 to 1.9
- gain_ffn: float32 [2048], replicated, may hold values from 0.1 to 1.9
- forget_gap: float32 [2048], replicated, may hold values from 0.003 to 0.3
- in_a: bfloat16 [2048, 512], replicated, may hold values from -0.125 to 0.125
- in_b: bfloat16 [8192, 128], replicated, may hold values from -1 to 1
- out_a: bfloat16 [2048, 128], replicated, may hold values from -0.125 to 0.125
- out_b: bfloat16 [2048, 128], replicated, may hold values from -1 to 1
- ffn_a: bfloat16 [2048, 256], replicated, may hold values from -0.125 to 0.125
- ffn_b: bfloat16 [11264, 128], replicated, may hold values from -1 to 1
- down_a: bfloat16 [5632, 128], replicated, may hold values from -0.078125 to 0.078125
- down_b: bfloat16 [2048, 128], replicated, may hold values from -1 to 1
- order: int32 [4, 2048], P('wt'), may hold values from 0 to 2047, each once within a row
- lengths: int32 [4, 4], P('wt'), may hold values from 1 to 1024, 2048 in all within a row
- adapter_ids: int32 [4, 4], P('wt'), may hold values from 0 to 7
Outputs:
- block_out: bfloat16 [4, 2048, 2048], P('wt', 'seq')
- tokens_grad: bfloat16 [4, 2048, 2048], P('wt', 'seq')
- in_a_grad: float32 [2048, 512], P(('seq', 'wt'))
- in_b_grad: float32 [8192, 128], P(('seq', 'wt'))
- out_a_grad: float32 [2048, 128], P(('seq', 'wt'))
- out_b_grad: float32 [2048, 128], P(('seq', 'wt'))
- ffn_a_grad: float32 [2048, 256], P(('seq', 'wt'))
- ffn_b_grad: float32 [11264, 128], P(('seq', 'wt'))
- down_a_grad: float32 [5632, 128], P(('seq', 'wt'))
- down_b_grad: float32 [2048, 128], P(('seq', 'wt'))
Inputs may be any that keep to these rules, and one draw needn't show every extreme that they name: `order`: each row is a permutation of the group's positions. `lengths`: each row sums to 2048; its largest entry is exactly 1024.
All inputs are finite; a program needn't handle non-finite values.
Results may differ from a plain program's by a relative error of at most 0.015.
Values may be sent and summed in bfloat16 or wider, within the bound.
No kernel may reach another device: no remote copies, remote signals or barrier semaphores. Data moves between devices by JAX's collectives and lax.ppermute only.
A program may use at most 384 MiB of HBM per device.

v0:
```python
import jax
import jax.numpy as jnp
from jax import lax
from jax.sharding import PartitionSpec as P

HEAD = 128
RANK = 16
ADAPTERS = 8
SPAN = 64
BLOCK = 512


highest = lax.Precision.HIGHEST
eps_norm = 1e-06


def sequence_of(positions, seq_lengths):
    bounds = jnp.cumsum(seq_lengths)[:-1]
    return jnp.sum((positions[:, None] >= bounds[None, :]).astype(jnp.int32), axis=1)


def adapter_of(seq_numbers, seq_ids):
    numbers = jnp.arange(seq_ids.shape[0], dtype=jnp.int32)
    return jnp.sum(
        (seq_numbers[:, None] == numbers[None, :]).astype(jnp.int32) * seq_ids[None, :], axis=1
    )


def adapter_mask(adapter):
    columns = jnp.arange(ADAPTERS * RANK, dtype=jnp.int32) // RANK
    return (columns[None, :] == adapter[:, None]).astype(jnp.float32)


def block_terms(inputs):
    query_block, key_block, logf_block, value_block, seg_block = inputs
    width = query_block.shape[1]
    cumulative = jnp.cumsum(logf_block, axis=1)
    places = jnp.arange(width, dtype=jnp.int32)
    causal = places[:, None] >= places[None, :]
    allowed = causal[None] & (seg_block[:, :, None] == seg_block[:, None, :])
    log_gap = cumulative[:, :, None] - cumulative[:, None, :]
    decays = jnp.exp(jnp.where(allowed[:, :, :, None, None], log_gap, -1e30))
    scores = jnp.sum(query_block[:, :, None] * key_block[:, None, :] * decays, axis=-1)
    intra = jnp.einsum("btsh,bshv->bthv", scores, value_block, precision=highest)
    final_log = cumulative[:, -1]
    tail_ok = (seg_block == seg_block[:, -1:]).astype(jnp.float32)
    tail_keys = jnp.exp(final_log[:, None] - cumulative) * key_block * tail_ok[:, :, None, None]
    update = jnp.einsum("bshk,bshv->bhkv", tail_keys, value_block, precision=highest)
    return (intra, update, jnp.exp(final_log), query_block * jnp.exp(cumulative))


def mixer(queries, keys, logf, values, seg_nat):
    total, heads, width = queries.shape
    nchunk = total // SPAN
    per_block = BLOCK // SPAN

    def shape_blocks(array):
        return array.reshape((total // BLOCK, per_block, SPAN) + array.shape[1:])

    parts = lax.map(
        jax.checkpoint(block_terms),
        (
            shape_blocks(queries),
            shape_blocks(keys),
            shape_blocks(logf),
            shape_blocks(values),
            shape_blocks(seg_nat),
        ),
    )
    intra, update, decay, query_decayed = [
        piece.reshape((nchunk,) + piece.shape[2:]) for piece in parts
    ]
    seg_spans = seg_nat.reshape(nchunk, SPAN)
    before = jnp.concatenate([jnp.full((1,), -1, jnp.int32), seg_spans[:-1, -1]])
    carry_keep = (seg_spans[:, -1] == before).astype(jnp.float32)
    factor = decay * carry_keep[:, None, None]

    def combine(first, second):
        return (first[0] * second[0], second[0][..., None] * first[1] + second[1])

    scanned = lax.associative_scan(combine, (factor, update))
    end_states = scanned[1]
    start_states = jnp.concatenate([jnp.zeros_like(end_states[:1]), end_states[:-1]])
    carry_ok = (seg_spans == before[:, None]).astype(jnp.float32)
    inter = (
        jnp.einsum("cthk,chkv->cthv", query_decayed, start_states, precision=highest)
        * carry_ok[:, :, None, None]
    )
    return (intra + inter).reshape(total, heads, width)


def norm_factor(values):
    return lax.rsqrt(jnp.mean(values * values, axis=-1, keepdims=True) + eps_norm)


def norm_back(values, factor, gain, grad):
    scaled = grad * gain
    return factor * scaled - values * factor**3 * jnp.mean(values * scaled, axis=-1, keepdims=True)


def silu_slope(values, sigma):
    return sigma * (1.0 + values * (1.0 - sigma))


def branch_fwd(inputs, a_mat, b_mat, mask, count):
    row_count = inputs.shape[0]
    rank_all = a_mat.shape[1] // count
    lowered = jnp.dot(inputs, a_mat, preferred_element_type=jnp.float32) * jnp.tile(
        mask, (1, count)
    )
    hidden = lowered.astype(jnp.bfloat16)
    result = jnp.einsum(
        "tpr,pdr->tpd",
        hidden.reshape(row_count, count, rank_all),
        b_mat.reshape(count, -1, rank_all),
        preferred_element_type=jnp.float32,
    )
    return (hidden, result.reshape(row_count, -1))


def branch_back(inputs, grad, hidden, a_mat, b_mat, mask, count, pick):
    row_count = inputs.shape[0]
    rank_all = a_mat.shape[1] // count
    grad_parts = grad.reshape(row_count, count, -1)
    b_parts = b_mat.reshape(count, -1, rank_all)
    through = jnp.einsum(
        "tpd,pdr->tpr", grad_parts, b_parts, preferred_element_type=jnp.float32
    ).reshape(row_count, -1)
    d_hidden = (through * jnp.tile(mask, (1, count))).astype(jnp.bfloat16)
    d_slots = pick(d_hidden, count)
    hid_slots = pick(hidden, count)
    slot_width = d_slots.shape[1] // count
    grad_a = lax.dot_general(
        inputs, d_slots, (((0,), (0,)), ((), ())), preferred_element_type=jnp.float32
    )
    grad_b = jnp.einsum(
        "tpd,tpr->pdr",
        grad_parts,
        hid_slots.reshape(row_count, count, slot_width),
        preferred_element_type=jnp.float32,
    ).reshape(-1, slot_width)
    d_inputs = lax.dot_general(
        d_hidden, a_mat, (((1,), (1,)), ((), ())), preferred_element_type=jnp.float32
    )
    return (d_inputs, grad_a, grad_b)


def times_piece(left, piece):
    return jnp.dot(left, piece, preferred_element_type=jnp.float32)


def fold_back(grad, piece):
    return lax.dot_general(
        grad, piece, (((1,), (1,)), ((), ())), preferred_element_type=jnp.float32
    )


def local(
    tokens,
    cotangent,
    w_in,
    w_out,
    w_ffn,
    w_down,
    gain_mix,
    gain_gate,
    gain_ffn,
    forget_gap,
    in_a,
    in_b,
    out_a,
    out_b,
    ffn_a,
    ffn_b,
    down_a,
    down_b,
    order,
    lengths,
    adapter_ids,
):
    inputs = tokens[0].astype(jnp.float32)
    cot_rows = cotangent[0]
    order_g = order[0]
    lengths_g = lengths[0]
    ids_g = adapter_ids[0]
    row_count = inputs.shape[0]
    seq_count = lax.axis_size("seq")
    seq_index = lax.axis_index("seq")
    group = row_count * seq_count
    natural_mine = lax.dynamic_slice_in_dim(order_g, seq_index * row_count, row_count)
    seq_mine = sequence_of(natural_mine, lengths_g)
    mask = adapter_mask(adapter_of(seq_mine, ids_g))

    def pick(values, count):
        return values

    factor_one = norm_factor(inputs)
    normed = (inputs * factor_one * gain_mix).astype(jnp.bfloat16)
    proj_main = times_piece(normed, lax.all_gather(w_in, "wt", axis=1, tiled=True))
    hid_in, delta_in = branch_fwd(normed, in_a, in_b, mask, 4)
    zq, zf, zv, zg = jnp.split(proj_main + delta_in, 4, axis=1)
    sigma_q = jax.nn.sigmoid(zq)
    sent = (
        lax.all_to_all(
            (zq * sigma_q).astype(jnp.bfloat16), "seq", split_axis=1, concat_axis=0, tiled=True
        ),
        lax.all_to_all(zf.astype(jnp.bfloat16), "seq", split_axis=1, concat_axis=0, tiled=True),
        lax.all_to_all(zv.astype(jnp.bfloat16), "seq", split_axis=1, concat_axis=0, tiled=True),
    )
    inverse = jnp.zeros((group,), jnp.int32).at[order_g].set(jnp.arange(group, dtype=jnp.int32))
    seg_nat = sequence_of(jnp.arange(group, dtype=jnp.int32), lengths_g)
    width = sent[0].shape[1]
    local_heads = width // HEAD
    gap_mine = lax.dynamic_slice_in_dim(forget_gap, seq_index * width, width).reshape(
        local_heads, HEAD
    )

    def head_side(query_nat, forget_nat, value_nat):
        keys = gap_mine * (1.0 - jax.nn.sigmoid(forget_nat.reshape(group, local_heads, HEAD)))
        logf = jnp.log1p(-keys)
        result = mixer(
            query_nat.reshape(group, local_heads, HEAD),
            keys,
            logf,
            value_nat.reshape(group, local_heads, HEAD),
            seg_nat,
        )
        return result.reshape(group, width)

    natural_inputs = tuple((piece[inverse].astype(jnp.float32) for piece in sent))
    mixed_nat, head_pull = jax.vjp(head_side, *natural_inputs)
    returned = lax.all_to_all(
        mixed_nat[order_g].astype(jnp.bfloat16), "seq", split_axis=0, concat_axis=1, tiled=True
    )
    mixed = returned.astype(jnp.float32)
    factor_two = norm_factor(mixed)
    sigma_g = jax.nn.sigmoid(zg)
    silu_g = zg * sigma_g
    normed_mixed = mixed * factor_two * gain_gate
    gated = (normed_mixed * silu_g).astype(jnp.bfloat16)
    attn_main = times_piece(gated, lax.all_gather(w_out, "wt", axis=1, tiled=True))
    hid_out, delta_out = branch_fwd(gated, out_a, out_b, mask, 1)
    resid = inputs + attn_main + delta_out
    factor_three = norm_factor(resid)
    normed2 = (resid * factor_three * gain_ffn).astype(jnp.bfloat16)
    both_main = times_piece(normed2, lax.all_gather(w_ffn, "wt", axis=1, tiled=True))
    hid_ffn, delta_ffn = branch_fwd(normed2, ffn_a, ffn_b, mask, 2)
    gate, upper = jnp.split(both_main + delta_ffn, 2, axis=1)
    sigma_u = jax.nn.sigmoid(gate)
    silu_gate = gate * sigma_u
    hidden = (silu_gate * upper).astype(jnp.bfloat16)
    down_main = times_piece(hidden, lax.all_gather(w_down, "wt", axis=1, tiled=True))
    hid_down, delta_down = branch_fwd(hidden, down_a, down_b, mask, 1)
    block_out = (resid + down_main + delta_down).astype(jnp.bfloat16)
    d_hidden = fold_back(cot_rows, lax.all_gather(w_down, "wt", axis=1, tiled=True))
    extra_down, grad_a_down, grad_b_down = branch_back(
        hidden, cot_rows, hid_down, down_a, down_b, mask, 1, pick
    )
    d_hidden = d_hidden + extra_down
    d_gate = d_hidden * upper * silu_slope(gate, sigma_u)
    d_upper = d_hidden * silu_gate
    g_both = jnp.concatenate([d_gate, d_upper], axis=1).astype(jnp.bfloat16)
    d_normed2 = fold_back(g_both, lax.all_gather(w_ffn, "wt", axis=1, tiled=True))
    extra_ffn, grad_a_ffn, grad_b_ffn = branch_back(
        normed2, g_both, hid_ffn, ffn_a, ffn_b, mask, 2, pick
    )
    d_resid = cot_rows.astype(jnp.float32) + norm_back(
        resid, factor_three, gain_ffn, d_normed2 + extra_ffn
    )
    g_attn = d_resid.astype(jnp.bfloat16)
    d_gated = fold_back(g_attn, lax.all_gather(w_out, "wt", axis=1, tiled=True))
    extra_out, grad_a_out, grad_b_out = branch_back(
        gated, g_attn, hid_out, out_a, out_b, mask, 1, pick
    )
    d_gated = d_gated + extra_out
    d_zg = d_gated * normed_mixed * silu_slope(zg, sigma_g)
    d_mixed = norm_back(mixed, factor_two, gain_gate * silu_g, d_gated).astype(jnp.bfloat16)
    grad_heads = lax.all_to_all(d_mixed, "seq", split_axis=1, concat_axis=0, tiled=True)
    grad_query, grad_forget, grad_value = head_pull(grad_heads[inverse].astype(jnp.float32))
    sent_back = (
        lax.all_to_all(
            grad_query[order_g].astype(jnp.bfloat16), "seq", split_axis=0, concat_axis=1, tiled=True
        ),
        lax.all_to_all(
            grad_forget[order_g].astype(jnp.bfloat16),
            "seq",
            split_axis=0,
            concat_axis=1,
            tiled=True,
        ),
        lax.all_to_all(
            grad_value[order_g].astype(jnp.bfloat16), "seq", split_axis=0, concat_axis=1, tiled=True
        ),
    )
    d_zq = sent_back[0].astype(jnp.float32) * silu_slope(zq, sigma_q)
    g_proj = jnp.concatenate(
        [d_zq, sent_back[1].astype(jnp.float32), sent_back[2].astype(jnp.float32), d_zg], axis=1
    ).astype(jnp.bfloat16)
    d_normed = fold_back(g_proj, lax.all_gather(w_in, "wt", axis=1, tiled=True))
    extra_in, grad_a_in, grad_b_in = branch_back(normed, g_proj, hid_in, in_a, in_b, mask, 4, pick)
    tokens_grad = (d_resid + norm_back(inputs, factor_one, gain_mix, d_normed + extra_in)).astype(
        jnp.bfloat16
    )
    terms = (
        grad_a_in,
        grad_b_in,
        grad_a_out,
        grad_b_out,
        grad_a_ffn,
        grad_b_ffn,
        grad_a_down,
        grad_b_down,
    )
    summed = (
        lax.psum_scatter(terms[0], ("seq", "wt"), scatter_dimension=0, tiled=True),
        lax.psum_scatter(terms[1], ("seq", "wt"), scatter_dimension=0, tiled=True),
        lax.psum_scatter(terms[2], ("seq", "wt"), scatter_dimension=0, tiled=True),
        lax.psum_scatter(terms[3], ("seq", "wt"), scatter_dimension=0, tiled=True),
        lax.psum_scatter(terms[4], ("seq", "wt"), scatter_dimension=0, tiled=True),
        lax.psum_scatter(terms[5], ("seq", "wt"), scatter_dimension=0, tiled=True),
        lax.psum_scatter(terms[6], ("seq", "wt"), scatter_dimension=0, tiled=True),
        lax.psum_scatter(terms[7], ("seq", "wt"), scatter_dimension=0, tiled=True),
    )
    return (
        block_out[None],
        tokens_grad[None],
        summed[0],
        summed[1],
        summed[2],
        summed[3],
        summed[4],
        summed[5],
        summed[6],
        summed[7],
    )


def solution(mesh):
    placed = (
        P("wt", "seq", None),
        P("wt", "seq", None),
        P(None, "wt"),
        P(None, "wt"),
        P(None, "wt"),
        P(None, "wt"),
        P(),
        P(),
        P(),
        P(),
        P(),
        P(),
        P(),
        P(),
        P(),
        P(),
        P(),
        P(),
        P("wt", None),
        P("wt", None),
        P("wt", None),
    )
    return jax.shard_map(
        local,
        mesh=mesh,
        in_specs=placed,
        out_specs=(
            P("wt", "seq", None),
            P("wt", "seq", None),
            P(("seq", "wt"), None),
            P(("seq", "wt"), None),
            P(("seq", "wt"), None),
            P(("seq", "wt"), None),
            P(("seq", "wt"), None),
            P(("seq", "wt"), None),
            P(("seq", "wt"), None),
            P(("seq", "wt"), None),
        ),
        check_vma=False,
    )
```

profile of v0, /device:TPU:4, one launch (start us, length us, event | category | flops | bytes accessed | tf_op | source)
XLA Modules:
  0.0 3095.1 jit_solution(4179345891362536540)
XLA Ops:
  19.2 6.2 copy.474
  25.6 546.7 %all-gather.5.cloned.1.call-done = bf16[2048,8192]{1,0:T(8,128)(2,1)} async-done(((bf16[2048,2048]{1,0:T(8,128)(2,1)}), bf16[2048,8192]{1,0:T(8,128)(2,1)}) %all-gather.5.cloned.1.call-update) | async-done | bytes 33554448 | tf_op jit(solution)/shard_map/all_gather | solution.py:199
  572.3 26.3 fusion.148
  610.6 10.8 all-to-all-done.2
  621.4 5.6 all-to-all-start.1
  627.2 8.0 scatter_custom_fusion
  641.0 6.2 all-to-all-start
  651.2 9.8 gather_fusion.2
  667.3 9.9 gather_fusion.1
  680.3 9.9 gather_fusion
  700.4 135.9 %while.39 = (s32[]{:T(128)}, f32[4,8,64,2,128]{4,2,3,1,0:T(8,128)}, f32[4,8,2,128,128]{4,3,2,1,0:T(8,128)}, f32[4,8,2,128]{3,1,0,2:T(8,128)S(1)}, f32[4,8,64,2,1...) while((s32[]{:T(128)}, f32[4,8,64,2,128]{4,2,3,1,0:T(8,128)}, ...), condition=%wide.region_9.10_spmd.clone, body=%wide.region_6.9_spmd.clone.sunk | while | flops 352719872 | bytes 30281012 | solution.py:60
  711.7 17.5 multiply_reduce_fusion.16
  745.7 17.5 multiply_reduce_fusion.16
  779.6 17.5 multiply_reduce_fusion.16
  813.5 17.5 multiply_reduce_fusion.16
  854.9 5.7 pad.196
  870.9 10.1 pad.197
  881.0 10.1 pad.198
  895.0 18.5 pad.392
  918.1 18.5 pad.279
  940.9 6.7 bitcast_add_fusion
  949.9 9.8 gather_fusion.3
  964.0 14.1 fusion.99
  986.5 126.2 %all-gather.7.cloned.1.call-done = bf16[2048,2048]{1,0:T(8,128)(2,1)} async-done(((bf16[2048,512]{1,0:T(8,128)(2,1)}), bf16[2048,2048]{1,0:T(8,128)(2,1)}) %all-gather.7.cloned.1.call-update) | async-done | bytes 8388624 | tf_op jit(solution)/shard_map/all_gather | solution.py:241
  1112.7 6.3 fusion.60
  1123.1 9.2 convolution_bitcast_fusion.3
  1132.3 11.6 copy.476
  1143.9 736.2 %all-gather.9.cloned.1.call-done = bf16[2048,11264]{1,0:T(8,128)(2,1)} async-done(((bf16[2048,2816]{1,0:T(8,128)(2,1)}), bf16[2048,11264]{1,0:T(8,128)(2,1)}) %all-gather.9.cloned.1.call-update) | async-done | bytes 46137360 | tf_op jit(solution)/shard_map/all_gather | solution.py:246
  1880.1 27.2 convolution_add_fusion.1
  1907.3 9.3 multiply_convert_fusion.1
  1919.2 21.5 fusion.39
  1960.4 5.9 fusion.133
  1982.5 10.0 all-to-all-done.4
  1992.5 9.2 gather_fusion.4
  2003.8 11.1 fusion.52
  2014.9 8.4 fusion.82
  2055.8 10.2 pad.229
  2066.0 6.4 pad.230
  2072.3 5.7 pad.208
  2084.2 12.0 pad.231
  2097.4 18.5 pad.232
  2116.0 11.3 pad.202
  2127.4 8.4 add_add_fusion
  2140.4 308.0 %while.38 = (s32[]{:T(128)}, bf16[4,8,64,2,128]{4,3,2,1,0:T(2,128)(2,1)}, f32[4,8,64,2,128]{4,3,2,1,0:T(2,128)}, f32[4,8,64,2,128]{4,3,2,1,0:T(2,128)}, bf16[4,8...) while((s32[]{:T(128)}, ...), condition=%wide.region_32.33_spmd, body=%wide.region_23.32_spmd.sunk | while | flops 749214720 | bytes 54745584 | solution.py:60
  2153.5 13.0 fusion.245
  2172.3 36.7 %fusion.248 = (f32[8,64,2,128]{3,1,2,0:T(8,128)}, f32[8,64,2,128]{3,2,1,0:T(2,128)}, f32[8,64,64,2]{2,3,1,0:T(2,128)}, f32[8,64,2,128]{3,2,1,0:T(2,128)}, f32[8,64,2,128]{3,1,2,0:T(8,128)}) fusion(f32[8,64,2,128]{3,2,1,0:T(2,128)} %copy.602, f32[8,64,2,128]{3,1,2,0:T(8,128)S(1)} %bitcast.432, f32[8,64,2,128]{3,1,2,0:T(8,128)} %get-tuple-element.907, ...), kind=kLoop, calls=%fused_computation.20.clone.1 | loop fusion | flops 125239296 | bytes 4751360 | tf_op jit(solution)/shard_map/transpose(jvp())/while/body/eval_jaxpr/checkpoint/reduce_sum | solution.py:41
  2230.4 13.0 fusion.245
  2249.2 36.7 %fusion.248 = (f32[8,64,2,128]{3,1,2,0:T(8,128)}, f32[8,64,2,128]{3,2,1,0:T(2,128)}, f32[8,64,64,2]{2,3,1,0:T(2,128)}, f32[8,64,2,128]{3,2,1,0:T(2,128)}, f32[8,64,2,128]{3,1,2,0:T(8,128)}) fusion(f32[8,64,2,128]{3,2,1,0:T(2,128)} %copy.602, f32[8,64,2,128]{3,1,2,0:T(8,128)S(1)} %bitcast.432, f32[8,64,2,128]{3,1,2,0:T(8,128)} %get-tuple-element.907, ...), kind=kLoop, calls=%fused_computation.20.clone.1 | loop fusion | flops 125239296 | bytes 4751360 | tf_op jit(solution)/shard_map/transpose(jvp())/while/body/eval_jaxpr/checkpoint/reduce_sum | solution.py:41
  2307.3 13.0 fusion.245
  2326.2 36.7 %fusion.248 = (f32[8,64,2,128]{3,1,2,0:T(8,128)}, f32[8,64,2,128]{3,2,1,0:T(2,128)}, f32[8,64,64,2]{2,3,1,0:T(2,128)}, f32[8,64,2,128]{3,2,1,0:T(2,128)}, f32[8,64,2,128]{3,1,2,0:T(8,128)}) fusion(f32[8,64,2,128]{3,2,1,0:T(2,128)} %copy.602, f32[8,64,2,128]{3,1,2,0:T(8,128)S(1)} %bitcast.432, f32[8,64,2,128]{3,1,2,0:T(8,128)} %get-tuple-element.907, ...), kind=kLoop, calls=%fused_computation.20.clone.1 | loop fusion | flops 125239296 | bytes 4751360 | tf_op jit(solution)/shard_map/transpose(jvp())/while/body/eval_jaxpr/checkpoint/reduce_sum | solution.py:41
  2384.2 13.0 fusion.245
  2403.0 36.7 %fusion.248 = (f32[8,64,2,128]{3,1,2,0:T(8,128)}, f32[8,64,2,128]{3,2,1,0:T(2,128)}, f32[8,64,64,2]{2,3,1,0:T(2,128)}, f32[8,64,2,128]{3,2,1,0:T(2,128)}, f32[8,64,2,128]{3,1,2,0:T(8,128)}) fusion(f32[8,64,2,128]{3,2,1,0:T(2,128)} %copy.602, f32[8,64,2,128]{3,1,2,0:T(8,128)S(1)} %bitcast.432, f32[8,64,2,128]{3,1,2,0:T(8,128)} %get-tuple-element.907, ...), kind=kLoop, calls=%fused_computation.20.clone.1 | loop fusion | flops 125239296 | bytes 4751360 | tf_op jit(solution)/shard_map/transpose(jvp())/while/body/eval_jaxpr/checkpoint/reduce_sum | solution.py:41
  2449.8 9.1 gather_fusion.5
  2458.9 5.8 all-to-all-start.5
  2469.0 9.1 gather_fusion.6
  2486.0 9.1 gather_fusion.7
  2510.7 8.0 all-to-all-done.7
  2536.9 6.6 fusion.54
  2545.1 11.9 convolution_add_fusion.9
  2560.8 17.6 fusion.44
  2583.3 47.9 %reduce-scatter.23.cloned.1.call-done = f32[176,128]{1,0:T(8,128)} async-done(((f32[5632,128]{1,0:T(8,128)}), f32[176,128]{1,0:T(8,128)}) %reduce-scatter.23.cloned.1.call-update) | async-done | bytes 90128 | tf_op jit(solution)/shard_map/reduce_scatter | solution.py:321
  2631.1 149.7 %reduce-scatter.13.cloned.1.call-done = f32[256,128]{1,0:T(8,128)} async-done(((f32[8192,128]{1,0:T(8,128)}), f32[256,128]{1,0:T(8,128)}) %reduce-scatter.13.cloned.1.call-update) | async-done | bytes 131088 | tf_op jit(solution)/shard_map/reduce_scatter | solution.py:316
  2780.8 149.5 %reduce-scatter.11.cloned.1.call-done = f32[64,512]{1,0:T(8,128)} async-done(((f32[2048,512]{1,0:T(8,128)}), f32[64,512]{1,0:T(8,128)}) %reduce-scatter.11.cloned.1.call-update) | async-done | bytes 131088 | tf_op jit(solution)/shard_map/reduce_scatter | solution.py:315
  2930.4 157.4 %reduce-scatter.21.cloned.1.call-done = f32[352,128]{1,0:T(8,128)} async-done(((f32[11264,128]{1,0:T(8,128)}), f32[352,128]{1,0:T(8,128)}) %reduce-scatter.21.cloned.1.call-update) | async-done | bytes 180240 | tf_op jit(solution)/shard_map/reduce_scatter | solution.py:320
  (804 shorter events, 429.2 us)
Async XLA Ops:
  7.2 1115.3 %copy-start = (bf16[11264,128]{1,0:T(8,128)(2,1)S(1)}, bf16[11264,128]{1,0:T(8,128)(2,1)}, u32[]{:S(2)}) copy-start(bf16[11264,128]{1,0:T(8,128)(2,1)} %param.40) | copy-start | bytes 8650756
  7.2 565.1 %all-gather.5.cloned.1.call-start = ((), (), s32[]{:S(2)}) async-start(), calls=%async_computation.16 | async-start | bytes 41943040 | tf_op jit(solution)/shard_map/all_gather | solution.py:199
  7.9 956.0 %all-gather.11.cloned.1.call-start = ((), (), s32[]{:S(2)}) async-start(), calls=%async_computation.19 | async-start | bytes 28835840 | tf_op jit(solution)/shard_map/all_gather | solution.py:252
  8.7 1104.0 %all-gather.7.cloned.1.call-start = ((), (), s32[]{:S(2)}) async-start(), calls=%async_computation.17 | async-start | bytes 10485760 | tf_op jit(solution)/shard_map/all_gather | solution.py:241
  9.4 1870.6 %all-gather.9.cloned.1.call-start = ((), (), s32[]{:S(2)}) async-start(), calls=%async_computation.18 | async-start | bytes 57671680 | tf_op jit(solution)/shard_map/all_gather | solution.py:246
  10.3 638.6 %copy-start.130 = (s32[128]{0:T(128)}, s32[128]{0:T(128)S(1)}, u32[]{:S(2)}) copy-start(s32[128]{0:T(128)S(1)} %and_select_fusion) | copy-start | bytes 1540
  10.5 638.4 %copy-start.112 = (s32[256]{0:T(256)}, s32[256]{0:T(256)S(1)}, u32[]{:S(2)}) copy-start(s32[256]{0:T(256)S(1)} %select_reduce_fusion) | copy-start | bytes 3076
  15.1 557.2 %copy-start.133 = (f32[256]{0:T(256)}, f32[256]{0:T(256)S(1)}, u32[]{:S(2)}) copy-start(f32[256]{0:T(256)S(1)} %get-tuple-element.721) | copy-start | bytes 3076
  602.3 19.1 all-to-all-start.2
  621.4 19.7 all-to-all-start.1
  636.1 44.2 %copy-start.100 = (s32[2048]{0:T(1024)}, s32[2048]{0:T(1024)S(1)}, u32[]{:S(2)}) copy-start(s32[2048]{0:T(1024)S(1)} %fusion.119) | copy-start | bytes 24580
  636.2 12.7 copy-start.64
  641.0 39.2 %all-to-all-start = ((bf16[256,8,256]{2,0,1:T(8,128)(2,1)}), bf16[256,8,256]{2,0,1:T(8,128)(2,1)}, u32[]{:S(2)}, u32[]{:S(2)}) async-start(bf16[256,8,256]{2,0,1:T(8,128)(2,1)} %bitcast.466), calls=%async_computation | async-start | bytes 2097152 | tf_op jit(solution)/shard_map/all_to_all | solution.py:208
  647.3 189.1 %copy-start.144 = (f32[32]{0:T(128)}, f32[32]{0:T(128)S(1)}, u32[]{:S(2)}) copy-start(f32[32]{0:T(128)S(1)} %compare_convert_fusion.4) | copy-start | bytes 388
  711.7 17.5 copy-start.10
  711.7 18.9 copy-start.7
  745.6 17.5 copy-start.10
  745.7 18.9 copy-start.7
  779.6 17.5 copy-start.10
  779.6 18.9 copy-start.7
  813.5 17.5 copy-start.10
  813.5 18.9 copy-start.7
  847.4 13.2 copy-start.51
  895.0 18.5 copy-start.106
  959.7 18.4 all-to-all-start.3
  963.9 1619.4 %reduce-scatter.15.cloned.1.call-start = ((), (), s32[]{:S(2)}) async-start(), calls=%async_computation.22 | async-start | bytes 1081344 | tf_op jit(solution)/shard_map/reduce_scatter | solution.py:317
  986.5 132.5 %copy-start.88 = (bf16[256,128]{1,0:T(8,128)(2,1)}, bf16[256,128]{1,0:T(8,128)(2,1)S(1)}, u32[]{:S(2)}) copy-start(bf16[256,128]{1,0:T(8,128)(2,1)S(1)} %fusion.90) | copy-start | bytes 196612
  986.5 132.5 %copy-start.77 = (bf16[2048,128]{1,0:T(8,128)(2,1)S(1)}, bf16[2048,128]{1,0:T(8,128)(2,1)}, u32[]{:S(2)}) copy-start(bf16[2048,128]{1,0:T(8,128)(2,1)} %param.38) | copy-start | bytes 1572868
  1919.1 21.5 copy-start.12
  1919.2 21.5 copy-start.124
  1948.1 635.2 %reduce-scatter.17.cloned.1.call-start = ((), (), s32[]{:S(2)}) async-start(), calls=%async_computation.23 | async-start | bytes 1081344 | tf_op jit(solution)/shard_map/reduce_scatter | solution.py:318
  1950.0 633.3 %reduce-scatter.25.cloned.1.call-start = ((), (), s32[]{:S(2)}) async-start(), calls=%async_computation.27 | async-start | bytes 1081344
  1957.2 626.1 %reduce-scatter.19.cloned.1.call-start = ((), (), s32[]{:S(2)}) async-start(), calls=%async_computation.24 | async-start | bytes 2162688 | tf_op jit(solution)/shard_map/reduce_scatter | solution.py:319
  1973.7 18.8 all-to-all-start.4
  1978.0 653.1 %reduce-scatter.23.cloned.1.call-start = ((), (), s32[]{:S(2)}) async-start(), calls=%async_computation.26 | async-start | bytes 2973696 | tf_op jit(solution)/shard_map/reduce_scatter | solution.py:321
  2023.5 12.0 copy-start.48
  2040.4 11.8 copy-start.24
  2040.4 11.8 slice-start.4
  2084.2 12.1 copy-start.120
  2084.2 12.1 copy-start.111
  2084.2 12.3 copy-start.103
  2084.2 12.6 copy-start.94
  2097.4 18.5 copy-start.50
  2116.0 11.3 copy-start.145
  2116.0 11.4 slice-start.2
  2153.5 15.1 copy-start.4
  2153.5 14.1 copy-start.6
  2230.3 15.1 copy-start.4
  2230.3 14.1 copy-start.6
  2307.3 15.1 copy-start.4
  2307.3 14.1 copy-start.6
  2384.2 15.1 copy-start.4
  2384.2 14.1 copy-start.6
  2458.9 20.7 all-to-all-start.5
  2479.5 19.4 all-to-all-start.6
  2498.9 19.8 all-to-all-start.7
  2503.8 277.0 %reduce-scatter.13.cloned.1.call-start = ((), (), s32[]{:S(2)}) async-start(), calls=%async_computation.21 | async-start | bytes 4325376 | tf_op jit(solution)/shard_map/reduce_scatter | solution.py:316
  2527.2 403.2 %reduce-scatter.11.cloned.1.call-start = ((), (), s32[]{:S(2)}) async-start(), calls=%async_computation.20 | async-start | bytes 4325376 | tf_op jit(solution)/shard_map/reduce_scatter | solution.py:315
  2535.1 552.7 %reduce-scatter.21.cloned.1.call-start = ((), (), s32[]{:S(2)}) async-start(), calls=%async_computation.25 | async-start | bytes 5947392 | tf_op jit(solution)/shard_map/reduce_scatter | solution.py:320
  2545.1 11.9 copy-start.65
  2545.1 11.9 copy-start.87
  2560.8 17.6 copy-start.20
  2560.8 17.6 copy-start.67
  2581.7 506.1 %copy-start.1 = (bf16[11264,128]{1,0:T(8,128)(2,1)S(1)}, bf16[11264,128]{1,0:T(8,128)(2,1)}, u32[]{:S(2)}) copy-start(bf16[11264,128]{1,0:T(8,128)(2,1)} %param.40) | copy-start | bytes 8650756
  (143 other events, 398.9 us)
Sparse Core Ops, SparseCore 0:
  9.6 562.5 all-gather.4
  573.8 389.2 all-gather.10
  964.7 147.9 all-gather.6
  1114.1 765.9 all-gather.8
  1948.2 133.2 reduce-scatter.14
  2084.2 131.9 reduce-scatter.16
  2219.0 131.9 reduce-scatter.24
  2353.9 135.6 reduce-scatter.18
  2492.5 138.5 reduce-scatter.22
  2633.8 146.9 reduce-scatter.12
  2783.7 146.6 reduce-scatter.10
  2933.1 154.6 reduce-scatter.20
where the time goes:
time: 3110 us; the launch traced here: 3100 us
  waiting for transfers between devices  1950 us (63%)
  local copies, waits for them, and re-layouts  426 us (14%)
  other arithmetic  393 us (13%)
  matrix products  263 us (8%)
  starting transfers between devices  41.8 us (1%)
    all_gather x1, waiting for transfers between devices, local(): lax.all_gather(w_ffn, 'wt', axis=1, tiled=True)  736 us
    all_gather x1, waiting for transfers between devices, local(): lax.all_gather(w_in, 'wt', axis=1, tiled=True)  547 us
    reduce_scatter x1, waiting for transfers between devices, local(): lax.psum_scatter(terms[5], ('seq', 'wt'), scatter_dimension=0, tiled=True)  157 us
    reduce_scatter x1, waiting for transfers between devices, local(): lax.psum_scatter(terms[1], ('seq', 'wt'), scatter_dimension=0, tiled=True)  150 us
    reduce_scatter x1, waiting for transfers between devices, local(): lax.psum_scatter(terms[0], ('seq', 'wt'), scatter_dimension=0, tiled=True)  150 us
    reduce_sum x4, other arithmetic, block_terms(): log_gap = cumulative[:, :, None] - cumulative[:, None, :]  147 us
    all_gather x1, waiting for transfers between devices, local(): lax.all_gather(w_out, 'wt', axis=1, tiled=True)  126 us
    pad x32, local copies, waits for them, and re-layouts, mixer(): scanned = lax.associative_scan(combine, (factor, update))  114 us
  transfers between devices with their start and end apart: 20, of which 13 were waited for; matrix products, arithmetic and copies ran while one was open for 32% of the time, Pallas kernels for 0%

commit v1 on v0

v1 whole, which is shorter than its diff:
```python
import jax
import jax.numpy as jnp
from jax import lax
from jax.sharding import PartitionSpec as P
from jax.experimental import pallas as pl
from jax.experimental.pallas import tpu as pltpu

HEAD = 128
CHUNK = 128
TILE = 512
NN = (((1,), (0,)), ((), ()))
NT = (((1,), (1,)), ((), ()))
TN = (((0,), (0,)), ((), ()))


def mm(left, right, dims=NN):
    return lax.dot_general(left, right, dims, preferred_element_type=jnp.float32)


def halves(values):
    high = values.astype(jnp.bfloat16)
    return high, (values - high.astype(jnp.float32)).astype(jnp.bfloat16)


def mm3(left, right, dims=NN):
    return mm(left[0], right[0], dims) + (mm(left[0], right[1], dims) + mm(left[1], right[0], dims))


def mm2(left, right, dims=NN):
    return mm(left[0], right, dims) + mm(left[1], right, dims)


def mm2r(left, right, dims=NN):
    return mm(left, right[0], dims) + mm(left, right[1], dims)


def sum_with(ones, values):
    high, rest = halves(values)
    mid = (values - high.astype(jnp.float32) - rest.astype(jnp.float32)).astype(jnp.bfloat16)
    return mm(ones, high) + (mm(ones, rest) + mm(ones, mid))


def move_rows(picks, pairs):
    total = pairs[0][0].shape[0]

    @pl.loop(0, total // TILE)
    def _(tile):
        start = pl.multiple_of(tile * TILE, TILE)
        chosen = picks(start, total)
        for source, target in pairs:
            target[pl.ds(start, TILE), :] = mm(chosen, source[...]).astype(jnp.bfloat16)


def picks_natural(order_row_ref):
    def picks(start, total):
        places = lax.broadcasted_iota(jnp.int32, (TILE, total), 0) + start
        return jnp.where(order_row_ref[...] == places, 1.0, 0.0).astype(jnp.bfloat16)

    return picks


def picks_packed(order_column_ref):
    def picks(start, total):
        places = lax.broadcasted_iota(jnp.int32, (TILE, total), 1)
        return jnp.where(order_column_ref[pl.ds(start, TILE), :] == places, 1.0, 0.0).astype(jnp.bfloat16)

    return picks


def segment_terms(ends_ref, start):
    count = ends_ref.shape[0] - 1

    def seg_of(positions):
        return sum((positions >= ends_ref[j]).astype(jnp.int32) for j in range(count))

    rows = lax.broadcasted_iota(jnp.int32, (CHUNK, CHUNK), 0)
    cols = lax.broadcasted_iota(jnp.int32, (CHUNK, CHUNK), 1)
    same = seg_of(rows + start) == seg_of(cols + start)
    wide = seg_of(lax.broadcasted_iota(jnp.int32, (CHUNK, HEAD), 0) + start)
    before = jnp.where(start == 0, -1, seg_of(start - 1))
    last = seg_of(start + CHUNK - 1)
    carry_ok = (wide == before).astype(jnp.float32)
    tail_ok = (wide == last).astype(jnp.float32)
    keep = (last == before).astype(jnp.float32)
    return (rows >= cols) & same, (rows <= cols) & same, carry_ok, tail_ok, keep


def chunk_decays(forget, gap, lower):
    sigma = jax.nn.sigmoid(forget)
    keys = gap * (1.0 - sigma)
    cumulative = sum_with(lower, jnp.log1p(-keys))
    middle = cumulative[CHUNK // 2 - 1 : CHUNK // 2]
    total = cumulative[CHUNK - 1 : CHUNK]
    return sigma, keys, cumulative, middle, total


def lower_ones():
    rows = lax.broadcasted_iota(jnp.int32, (CHUNK, CHUNK), 0)
    cols = lax.broadcasted_iota(jnp.int32, (CHUNK, CHUNK), 1)
    return jnp.where(rows >= cols, 1.0, 0.0).astype(jnp.bfloat16)


def forward_kernel(
    ends_ref, order_row_ref, order_column_ref, query_ref, forget_ref, value_ref, gap_ref,
    mixed_ref, query_nat, forget_nat, value_nat, states_ref, out_nat, state_now,
):
    total, width = query_ref.shape
    heads = width // HEAD
    move_rows(
        picks_natural(order_row_ref),
        ((query_ref, query_nat), (forget_ref, forget_nat), (value_ref, value_nat)),
    )
    state_now[...] = jnp.zeros_like(state_now)
    lower = lower_ones()

    @pl.loop(0, total // CHUNK)
    def _(chunk):
        start = pl.multiple_of(chunk * CHUNK, CHUNK)
        rows = pl.ds(start, CHUNK)
        allowed, _, carry_ok, tail_ok, keep = segment_terms(ends_ref, start)
        for head in range(heads):
            lanes = slice(head * HEAD, (head + 1) * HEAD)
            query = query_nat[rows, lanes].astype(jnp.float32)
            value = value_nat[rows, lanes]
            _, keys, cumulative, middle, final = chunk_decays(
                forget_nat[rows, lanes].astype(jnp.float32), gap_ref[:, lanes], lower
            )
            grown = jnp.exp(cumulative - middle)
            shrunk = jnp.exp(middle - cumulative)
            scores = mm3(halves(query * grown), halves(keys * shrunk), NT)
            scores = jnp.where(allowed, scores, 0.0)
            state = state_now[head]
            states_ref[chunk, head] = state
            inter = mm3(halves(query * jnp.exp(cumulative) * carry_ok), halves(state), NT)
            out_nat[rows, lanes] = (mm2(halves(scores), value) + inter).astype(jnp.bfloat16)
            tail = keys * jnp.exp(final - cumulative) * tail_ok
            state_now[head] = state * (jnp.exp(final) * keep) + mm2r(value, halves(tail), TN)

    states_ref[total // CHUNK] = state_now[...]
    move_rows(picks_packed(order_column_ref), ((out_nat, mixed_ref),))


def backward_kernel(
    ends_ref, order_row_ref, order_column_ref, grad_ref, query_nat, forget_nat, value_nat, states_ref, gap_ref,
    d_query_ref, d_forget_ref, d_value_ref, grad_nat, d_query_nat, d_forget_nat, d_value_nat, slope_now,
):
    total, width = grad_ref.shape
    heads = width // HEAD
    move_rows(picks_natural(order_row_ref), ((grad_ref, grad_nat),))
    slope_now[...] = jnp.zeros_like(slope_now)
    lower = lower_ones()

    @pl.loop(0, total // CHUNK)
    def _(step):
        chunk = total // CHUNK - 1 - step
        start = pl.multiple_of(chunk * CHUNK, CHUNK)
        rows = pl.ds(start, CHUNK)
        allowed, later, carry_ok, tail_ok, keep = segment_terms(ends_ref, start)
        later = jnp.where(later, 1.0, 0.0).astype(jnp.bfloat16)
        for head in range(heads):
            lanes = slice(head * HEAD, (head + 1) * HEAD)
            query = query_nat[rows, lanes].astype(jnp.float32)
            value = value_nat[rows, lanes]
            grad = grad_nat[rows, lanes]
            sigma, keys, cumulative, middle, final = chunk_decays(
                forget_nat[rows, lanes].astype(jnp.float32), gap_ref[:, lanes], lower
            )
            grown = jnp.exp(cumulative - middle)
            shrunk = jnp.exp(middle - cumulative)
            query_grown = halves(query * grown)
            keys_shrunk = halves(keys * shrunk)
            scores = halves(jnp.where(allowed, mm3(query_grown, keys_shrunk, NT), 0.0))
            d_scores = halves(jnp.where(allowed, mm(grad, value, NT), 0.0))
            state = halves(states_ref[chunk, head])
            slope = slope_now[head]
            slope_parts = halves(slope)
            from_start = jnp.exp(cumulative) * carry_ok
            to_end = jnp.exp(final - cumulative) * tail_ok
            d_query = mm3(d_scores, keys_shrunk) * grown + mm2r(grad, state) * from_start
            d_keys = mm3(d_scores, query_grown, TN) * shrunk + mm2r(value, slope_parts) * to_end
            d_value = mm2(scores, grad, TN) + mm3(halves(keys * to_end), slope_parts, NT)
            past = jnp.sum(states_ref[chunk + 1, head] * slope, axis=0, keepdims=True)
            d_logf = sum_with(later, query * d_query - keys * d_keys) + tail_ok * past
            d_keys = d_keys - d_logf / (1.0 - keys)
            slope_now[head] = slope * (jnp.exp(final) * keep) + mm2r(grad, halves(query * from_start), TN)
            d_query_nat[rows, lanes] = d_query.astype(jnp.bfloat16)
            d_forget_nat[rows, lanes] = (-d_keys * keys * sigma).astype(jnp.bfloat16)
            d_value_nat[rows, lanes] = d_value.astype(jnp.bfloat16)

    move_rows(
        picks_packed(order_column_ref),
        ((d_query_nat, d_query_ref), (d_forget_nat, d_forget_ref), (d_value_nat, d_value_ref)),
    )


def mixer_cost(total, width, matmuls):
    flops = 2 * total * width * (CHUNK * matmuls + total * 4)
    return pl.CostEstimate(flops=flops, bytes_accessed=20 * total * width, transcendentals=6 * total * width)


VMEM = pl.BlockSpec(memory_space=pltpu.VMEM)
SMEM = pl.BlockSpec(memory_space=pltpu.SMEM)


def mixer_forward(ends, order, queries, forgets, values, gap):
    total, width = queries.shape
    heads = width // HEAD
    rows = jax.ShapeDtypeStruct((total, width), jnp.bfloat16)
    states = jax.ShapeDtypeStruct((total // CHUNK + 1, heads, HEAD, HEAD), jnp.float32)
    return pl.pallas_call(
        forward_kernel,
        out_shape=(rows, rows, rows, rows, states),
        in_specs=[SMEM] + [VMEM] * 6,
        out_specs=(VMEM,) * 5,
        scratch_shapes=[
            pltpu.VMEM((total, width), jnp.bfloat16),
            pltpu.VMEM((heads, HEAD, HEAD), jnp.float32),
        ],
        compiler_params=pltpu.CompilerParams(vmem_limit_bytes=40 * 2**20),
        cost_estimate=mixer_cost(total, width, 12),
    )(ends, order.reshape(1, total), order.reshape(total, 1), queries, forgets, values, gap.reshape(1, width))


def mixer_backward(ends, order, grads, kept, gap):
    total, width = grads.shape
    heads = width // HEAD
    rows = jax.ShapeDtypeStruct((total, width), jnp.bfloat16)
    return pl.pallas_call(
        backward_kernel,
        out_shape=(rows, rows, rows),
        in_specs=[SMEM] + [VMEM] * 8,
        out_specs=(VMEM,) * 3,
        scratch_shapes=[pltpu.VMEM((total, width), jnp.bfloat16)] * 4
        + [pltpu.VMEM((heads, HEAD, HEAD), jnp.float32)],
        compiler_params=pltpu.CompilerParams(vmem_limit_bytes=40 * 2**20),
        cost_estimate=mixer_cost(total, width, 40),
    )(ends, order.reshape(1, total), order.reshape(total, 1), grads, *kept, gap.reshape(1, width))


ADAPTERS = 8
RANK = 16
RANKS = ADAPTERS * RANK
PROJECTIONS = 4
eps_norm = 1e-06
f32 = jnp.float32
bf16 = jnp.bfloat16


def sequence_of(positions, seq_lengths):
    bounds = jnp.cumsum(seq_lengths)[:-1]
    return jnp.sum((positions[:, None] >= bounds[None, :]).astype(jnp.int32), axis=1)


def adapter_of(seq_numbers, seq_ids):
    numbers = jnp.arange(seq_ids.shape[0], dtype=jnp.int32)
    return jnp.sum(
        (seq_numbers[:, None] == numbers[None, :]).astype(jnp.int32) * seq_ids[None, :], axis=1
    )


def adapter_mask(adapter):
    columns = jnp.arange(RANKS, dtype=jnp.int32) // RANK
    return (columns[None, :] == adapter[:, None]).astype(f32)


def norm_factor(values):
    return lax.rsqrt(jnp.mean(values * values, axis=-1, keepdims=True) + eps_norm)


def norm_back(values, factor, gain, grad):
    scaled = grad * gain
    return factor * scaled - values * factor**3 * jnp.mean(values * scaled, axis=-1, keepdims=True)


def silu_slope(values, sigma):
    return sigma * (1.0 + values * (1.0 - sigma))


def relative(blocks, index):
    count, rest = blocks.shape[0], blocks.shape[1:]
    bit = 1
    while bit < count:
        pairs = blocks.reshape((count // (2 * bit), 2, bit) + rest)
        blocks = jnp.where((index & bit) != 0, pairs[:, ::-1], pairs).reshape((count,) + rest)
        bit *= 2
    return blocks


def across(values, bits, axis="seq"):
    size = lax.axis_size(axis)
    return lax.ppermute(values, axis, [(i, i ^ bits) for i in range(size)])


def gather_direct(block):
    return [block] + [across(block, k) for k in range(1, lax.axis_size("seq"))]


def scatter_direct(parts, axis="seq"):
    total = parts[0].astype(f32)
    for k in range(1, lax.axis_size(axis)):
        total = total + across(parts[k], k, axis).astype(f32)
    return total


def gather_blocks(block):
    if lax.axis_size("seq") != 8:
        return gather_direct(block)
    half = block.shape[0] // 2
    by_x, by_y = across(block, 2), across(block, 4)
    far = jnp.concatenate([across(by_x[:half], 4), across(by_y[half:], 2)])
    near = [block, by_x, by_y, far]
    return [piece for own in near for piece in (own, across(own, 1))]


def scatter_blocks(parts):
    if lax.axis_size("seq") != 8:
        return scatter_direct(parts)
    half = parts[0].shape[0] // 2
    far, by_y, by_x, own = [
        parts[k].astype(f32) + across(parts[k + 1], 1).astype(f32) for k in (6, 4, 2, 0)
    ]
    by_x_more = by_x[half:] + across(far[half:].astype(bf16), 4).astype(f32)
    by_y_more = by_y[:half] + across(far[:half].astype(bf16), 2).astype(f32)
    from_x = [across(by_x[:half].astype(bf16), 2), across(by_x_more.astype(bf16), 2)]
    from_y = [across(by_y_more.astype(bf16), 4), across(by_y[half:].astype(bf16), 4)]
    return (
        own
        + jnp.concatenate(from_x).astype(f32)
        + jnp.concatenate(from_y).astype(f32)
    )


def exchange(parts):
    return [parts[0]] + [across(parts[k], k) for k in range(1, len(parts))]


def line_gather(block):
    count, place = lax.axis_size("wt"), lax.axis_index("wt")
    rising, falling = [block], [block]
    for step in range(1, count):
        rising.append(
            lax.ppermute(rising[-1], "wt", [(i, i + 1) for i in range(step - 1, count - 1)])
        )
        falling.append(
            lax.ppermute(falling[-1], "wt", [(i, i - 1) for i in range(1, count - step + 1)])
        )
    result = jnp.zeros((count,) + block.shape, block.dtype)
    result = lax.dynamic_update_index_in_dim(result, block, place, 0)
    for step in range(1, count):
        piece = jnp.where(place + step < count, falling[step], rising[count - step])
        result = lax.dynamic_update_index_in_dim(result, piece, (place + step) % count, 0)
    return result


def line_reduce(values):
    count, place = lax.axis_size("wt"), lax.axis_index("wt")
    parts = [lax.dynamic_index_in_dim(values, place ^ k, 0, False) for k in range(count)]
    return scatter_direct(parts, "wt")


def to_rows(pieces):
    count = pieces.shape[0]
    size, place = lax.axis_size("seq"), lax.axis_index("seq")
    span = size // count
    result = jnp.zeros_like(pieces)
    for k in range(count):
        piece = lax.dynamic_index_in_dim(pieces, (place % count + k) % count, 0, False)
        moves = [(i, ((i % count + k) % count) * span + i // count) for i in range(size)]
        got = lax.ppermute(piece, "seq", moves)
        result = lax.dynamic_update_index_in_dim(result, got, (place // span + count - k) % count, 0)
    return result.reshape((-1,) + pieces.shape[2:])


def with_scalars(block, scalars):
    rows, columns = block.shape
    lines = []
    for values in scalars:
        high, rest = halves(values)
        last = (values - high.astype(f32) - rest.astype(f32)).astype(bf16)
        lines += [high, rest, last]
    lines = jnp.concatenate(lines).reshape(-1, columns)
    return jnp.concatenate([block, jnp.pad(lines, ((0, -lines.shape[0] % 16), (0, 0)))])


def split_scalars(packed, rows, count):
    columns = packed.shape[1]
    lines = packed[rows : rows + 3 * count * rows // columns].astype(f32).reshape(count, 3, rows)
    return packed[:rows], [lines[i, 0] + lines[i, 1] + lines[i, 2] for i in range(count)]


def fold_columns(count):
    source = jnp.arange(count * RANKS)
    target = jnp.arange(RANKS)
    wanted = (source // RANKS) * RANK + source % RANK
    return (wanted[:, None] == target[None, :]).astype(bf16)


def local(
    tokens,
    cotangent,
    w_in,
    w_out,
    w_ffn,
    w_down,
    gain_mix,
    gain_gate,
    gain_ffn,
    forget_gap,
    in_a,
    in_b,
    out_a,
    out_b,
    ffn_a,
    ffn_b,
    down_a,
    down_b,
    order,
    lengths,
    adapter_ids,
):
    n, wt = lax.axis_size("seq"), lax.axis_size("wt")
    mine = lax.axis_index("seq")
    inputs = tokens[0].astype(f32)
    cot_rows = cotangent[0]
    rows, model = inputs.shape
    total = n * rows
    wide = model // n
    pair = 2 * rows
    pairs = n // 2

    def my_columns(values, extent, axis):
        return lax.dynamic_slice_in_dim(values, mine * extent, extent, axis)

    def my_piece(values, axis):
        return lax.dynamic_index_in_dim(values, mine, axis, False)

    def in_pairs(blocks):
        return [jnp.concatenate(blocks[2 * i : 2 * i + 2]) for i in range(pairs)]

    def of_pair(values, i):
        return values[i * pair : (i + 1) * pair]

    def blocks_of(values):
        return [values[k * rows : (k + 1) * rows] for k in range(n)]

    order_mine = relative(order[0].reshape(n, rows), mine).reshape(total)
    ends = jnp.cumsum(lengths[0])
    mask = adapter_mask(adapter_of(sequence_of(order_mine, lengths[0]), adapter_ids[0]))
    mask_own = mask[:rows]
    gap_mine = my_columns(forget_gap, wide, 0)
    gain_mine = my_columns(gain_gate, wide, 0)

    if wt == PROJECTIONS:
        win = line_gather(my_columns(w_in, wide, 1).T)
    else:
        whole = lax.all_gather(w_in, "wt", axis=1, tiled=True)
        win = jnp.transpose(my_piece(whole.reshape(model, PROJECTIONS, n, wide), 2), (1, 2, 0))
    win = win.reshape(PROJECTIONS * wide, model)
    in_b_mine = my_piece(in_b.reshape(PROJECTIONS, n, wide, RANKS), 1)

    factor_one = norm_factor(inputs)
    normed = (inputs * factor_one * gain_mix).astype(bf16)
    normed_pairs = in_pairs(gather_blocks(normed))

    wout = line_gather(my_columns(w_out, wide, 0))
    wout = jnp.transpose(wout, (1, 0, 2)).reshape(wide, model)
    wout = jnp.concatenate(gather_blocks(wout))
    out_a_mine = relative(out_a.reshape(n, wide, RANKS), mine).reshape(model, RANKS)

    units = w_ffn.shape[1] // n
    wffn = line_gather(my_columns(w_ffn, units, 1).T)
    w_gate = wffn[: wt // 2].reshape(-1, model)
    w_up = wffn[wt // 2 :].reshape(-1, model)
    wdown = my_piece(w_down.reshape(wt // 2, n, units, -1), 1).reshape(wt // 2 * units, -1)
    wdown = jnp.transpose(line_gather(wdown), (1, 0, 2)).reshape(wt // 2 * units, model)
    ffn_b_mine = my_piece(ffn_b.reshape(wt, n, units, RANKS), 1)
    b_gate = ffn_b_mine[: wt // 2].reshape(-1, RANKS)
    b_up = ffn_b_mine[wt // 2 :].reshape(-1, RANKS)
    down_a_mine = my_piece(down_a.reshape(wt // 2, n, units, RANKS), 1).reshape(-1, RANKS)

    masks = [of_pair(mask, i) for i in range(pairs)]
    hid_in, projected = [], []
    for i in range(pairs):
        hid = (mm(normed_pairs[i], in_a) * jnp.tile(masks[i], (1, PROJECTIONS))).astype(bf16)
        main = mm(normed_pairs[i], win, NT)
        projected.append(
            [
                main[:, j * wide : (j + 1) * wide] + mm(hid[:, j * RANKS : (j + 1) * RANKS], in_b_mine[j], NT)
                for j in range(PROJECTIONS)
            ]
        )
        hid_in.append(hid)
    zq, zf, zv, zg = [jnp.concatenate(pieces) for pieces in zip(*projected)]
    sigma_q = jax.nn.sigmoid(zq)
    mixed_bf, *kept = mixer_forward(
        ends, order_mine, (zq * sigma_q).astype(bf16), zf.astype(bf16), zv.astype(bf16), gap_mine
    )
    mixed = mixed_bf.astype(f32)
    sigma_g = jax.nn.sigmoid(zg)
    silu_g = zg * sigma_g
    raw = (mixed * gain_mine * silu_g).astype(bf16)
    squares = jnp.sum(mixed * mixed, axis=-1)
    sent = [with_scalars(part, [sq]) for part, sq in zip(blocks_of(raw), blocks_of(squares))]
    came = [split_scalars(packed, rows, 1) for packed in exchange(sent)]
    factor_two = lax.rsqrt(sum(sq[0] for _, sq in came) / model + eps_norm)[:, None]
    raw_own = jnp.concatenate([part for part, _ in came], axis=1).astype(f32)

    gated = (raw_own * factor_two).astype(bf16)
    hid_out = (mm(gated, out_a_mine) * mask_own).astype(bf16)
    resid = inputs + mm(gated, wout) + mm(hid_out, out_b, NT)
    factor_three = norm_factor(resid)
    normed2 = (resid * factor_three * gain_ffn).astype(bf16)

    cot_pairs = in_pairs(gather_blocks(cot_rows))
    normed2_pairs = in_pairs(gather_blocks(normed2))
    hid_ffn, d_hid_down, hidden, d_gates, d_uppers, back_parts, small_parts, down_parts = [[] for _ in range(8)]
    fold_ffn = fold_columns(3)
    for i in range(pairs):
        mask_two = jnp.tile(masks[i], (1, 2))
        hid = (mm(normed2_pairs[i], ffn_a) * mask_two).astype(bf16)
        gate = mm(normed2_pairs[i], w_gate, NT) + mm(hid[:, :RANKS], b_gate, NT)
        upper = mm(normed2_pairs[i], w_up, NT) + mm(hid[:, RANKS:], b_up, NT)
        d_hid = (mm(cot_pairs[i], down_b) * masks[i]).astype(bf16)
        d_hidden = mm(cot_pairs[i], wdown, NT) + mm(d_hid, down_a_mine, NT)
        sigma = jax.nn.sigmoid(gate)
        silu_gate = gate * sigma
        hidden.append((silu_gate * upper).astype(bf16))
        d_gates.append((d_hidden * upper * silu_slope(gate, sigma)).astype(bf16))
        d_uppers.append((d_hidden * silu_gate).astype(bf16))
        through = jnp.concatenate([mm(d_gates[i], b_gate), mm(d_uppers[i], b_up)], axis=1)
        through = (through * mask_two).astype(bf16)
        back = mm(d_gates[i], w_gate) + mm(d_uppers[i], w_up) + mm(through, ffn_a, NT)
        lowered = (mm(hidden[i], down_a_mine) * masks[i]).astype(bf16)
        down = mm(hidden[i], wdown) + mm(lowered, down_b, NT)
        small = mm(jnp.concatenate([lowered, through], axis=1), fold_ffn).astype(bf16)
        hid_ffn.append(hid)
        d_hid_down.append(d_hid)
        back_parts += [back[:rows].astype(bf16), back[rows:].astype(bf16)]
        down_parts += [down[:rows].astype(bf16), down[rows:].astype(bf16)]
        small_parts += [small[:rows], small[rows:]]
    d_normed2 = scatter_blocks(back_parts)
    d_resid = cot_rows.astype(f32) + norm_back(resid, factor_three, gain_ffn, d_normed2)

    g_attn = d_resid.astype(bf16)
    d_hid_out = (mm(g_attn, out_b) * mask_own).astype(bf16)
    d_gated = mm(g_attn, wout, NT) + mm(d_hid_out, out_a_mine, NT)
    mean_two = jnp.mean(raw_own * d_gated, axis=-1)
    sent = [
        with_scalars(d_gated[:, k * wide : (k + 1) * wide].astype(bf16), [factor_two[:, 0], mean_two])
        for k in range(n)
    ]
    came = [split_scalars(packed, rows, 2) for packed in exchange(sent)]
    d_gated_heads = jnp.concatenate([part for part, _ in came]).astype(f32)
    factor_heads = jnp.concatenate([pieces[0] for _, pieces in came])[:, None]
    mean_heads = jnp.concatenate([pieces[1] for _, pieces in came])[:, None]
    d_zg = d_gated_heads * (mixed * factor_heads * gain_mine) * silu_slope(zg, sigma_g)
    d_mixed = factor_heads * (d_gated_heads * gain_mine * silu_g) - mixed * factor_heads**3 * mean_heads

    d_query, d_forget, d_value = mixer_backward(ends, order_mine, d_mixed.astype(bf16), kept, gap_mine)
    d_zq = d_query.astype(f32) * silu_slope(zq, sigma_q)
    g_proj = [d_zq.astype(bf16), d_forget, d_value, d_zg.astype(bf16)]
    mask_four = jnp.tile(mask, (1, PROJECTIONS))
    through = jnp.concatenate([mm(g_proj[j], in_b_mine[j]) for j in range(PROJECTIONS)], axis=1)
    fold_in = fold_columns(PROJECTIONS)
    small_in = mm((through * mask_four).astype(bf16), fold_in).astype(bf16)
    small_in = jnp.concatenate(gather_direct(scatter_direct(blocks_of(small_in)).astype(bf16)))
    d_hid_in = (mm(small_in, fold_in, NT) * mask_four).astype(bf16)
    g_proj_all = jnp.concatenate(g_proj, axis=1)
    in_parts = []
    for i in range(pairs):
        back = mm(of_pair(g_proj_all, i), win)
        in_parts += [back[:rows].astype(bf16), back[rows:].astype(bf16)]
    d_normed = scatter_blocks(in_parts) + mm(d_hid_in[:rows], in_a, NT)
    tokens_grad = (d_resid + norm_back(inputs, factor_one, gain_mix, d_normed)).astype(bf16)

    block_out = (resid + scatter_blocks(down_parts)).astype(bf16)

    small_ffn = jnp.concatenate(gather_direct(scatter_direct(small_parts).astype(bf16)))
    spread = (mm(small_ffn, fold_ffn, NT) * jnp.tile(mask, (1, 3))).astype(bf16)
    hid_down, d_hid_ffn = spread[:, :RANKS], spread[:, RANKS:]

    def over_pairs(lefts, rights):
        return sum(mm(left, right, TN) for left, right in zip(lefts, rights))

    def my_features(values):
        return [my_columns(piece, wide, 1) for piece in values]

    split_pairs = lambda values: [of_pair(values, i) for i in range(pairs)]
    down_b_rows = over_pairs(my_features(cot_pairs), split_pairs(hid_down))
    ffn_a_rows = over_pairs(my_features(normed2_pairs), split_pairs(d_hid_ffn))
    down_a_rows = over_pairs(hidden, d_hid_down).reshape(wt // 2, units, RANKS)
    ffn_b_rows = jnp.concatenate(
        [
            over_pairs(d_gates, [hid[:, :RANKS] for hid in hid_ffn]),
            over_pairs(d_uppers, [hid[:, RANKS:] for hid in hid_ffn]),
        ]
    ).reshape(wt, units, RANKS)
    d_hid_out_all = jnp.concatenate(gather_direct(d_hid_out))
    gated_heads = (raw.astype(f32) * factor_heads).astype(bf16)
    out_a_rows = mm(gated_heads, d_hid_out_all, TN)
    out_b_parts = relative(mm(g_attn, hid_out, TN).reshape(n, wide, RANKS), mine)
    out_b_rows = scatter_direct([out_b_parts[k] for k in range(n)])
    in_a_rows = over_pairs(my_features(normed_pairs), split_pairs(d_hid_in))
    in_b_rows = jnp.stack(
        [
            over_pairs(split_pairs(g_proj[j]), [hid[:, j * RANKS : (j + 1) * RANKS] for hid in hid_in])
            for j in range(PROJECTIONS)
        ]
    )

    def reduced(arrays):
        packed = [
            jnp.concatenate(
                [
                    array[:, c * RANKS : (c + 1) * RANKS].reshape(wt, -1, RANKS)
                    for c in range(array.shape[1] // RANKS)
                ],
                axis=1,
            )
            for array in arrays
        ]
        summed = line_reduce(jnp.concatenate(packed, axis=1))
        results, start = [], 0
        for array in arrays:
            height = array.shape[0] // wt
            count = array.shape[1] // RANKS
            results.append(
                jnp.concatenate(
                    [summed[start + c * height : start + (c + 1) * height] for c in range(count)], axis=1
                )
            )
            start += count * height
        return results

    ffn_b_grad, down_a_grad, down_b_grad, ffn_a_grad = reduced(
        [to_rows(ffn_b_rows), to_rows(down_a_rows), down_b_rows, ffn_a_rows]
    )
    out_a_grad, out_b_grad = reduced([out_a_rows, out_b_rows])
    in_a_grad, in_b_grad = reduced([in_a_rows, to_rows(in_b_rows)])
    return (
        block_out[None],
        tokens_grad[None],
        in_a_grad,
        in_b_grad,
        out_a_grad,
        out_b_grad,
        ffn_a_grad,
        ffn_b_grad,
        down_a_grad,
        down_b_grad,
    )


def solution(mesh):
    placed = (
        P("wt", "seq", None),
        P("wt", "seq", None),
        P(None, "wt"),
        P(None, "wt"),
        P(None, "wt"),
        P(None, "wt"),
        P(),
        P(),
        P(),
        P(),
        P(),
        P(),
        P(),
        P(),
        P(),
        P(),
        P(),
        P(),
        P("wt", None),
        P("wt", None),
        P("wt", None),
    )
    return jax.shard_map(
        local,
        mesh=mesh,
        in_specs=placed,
        out_specs=(
            P("wt", "seq", None),
            P("wt", "seq", None),
            P(("seq", "wt"), None),
            P(("seq", "wt"), None),
            P(("seq", "wt"), None),
            P(("seq", "wt"), None),
            P(("seq", "wt"), None),
            P(("seq", "wt"), None),
            P(("seq", "wt"), None),
            P(("seq", "wt"), None),
        ),
        check_vma=False,
    )
```

time: 3110 us -> 1130 us (0.36)
  waiting for transfers between devices: 1950 us -> 364 us
  other arithmetic: 393 us -> 71.8 us
  local copies, waits for them, and re-layouts: 426 us -> 246 us
  starting transfers between devices: 41.8 us -> 205 us
  matrix products: 263 us -> 159 us
  Pallas kernels: 0 us -> 59.6 us
    all_gather x4 -> x0, waiting for transfers between devices: 1410 us -> none  [the longest x1 736 us: local(): lax.all_gather(w_ffn, 'wt', axis=1, tiled=True)]
    reduce_scatter x7 -> x0, waiting for transfers between devices: 505 us -> none  [the longest x1 157 us: local(): lax.psum_scatter(terms[5], ('seq', 'wt'), scatter_dimension=0, tiled=True)]
    ppermute x0 -> x161, waiting for transfers between devices: none -> 364 us  [the longest x127 220 us: across(): return lax.ppermute(values, axis, [(i, i ^ bits) for i in range(size)])]
    reduce_sum x21 -> x3, other arithmetic: 233 us -> 2.57 us  [the longest x2 1.78 us: norm_back(): jnp.mean(values * scaled, axis=-1, keepdims=True)]
    ppermute x0 -> x161, starting transfers between devices: none -> 205 us  [the longest x127 117 us: across(): return lax.ppermute(values, axis, [(i, i ^ bits) for i in range(size)])]
    pad x32 -> x0, local copies, waits for them, and re-layouts: 114 us -> none  [mixer(): scanned = lax.associative_scan(combine, (factor, update))]
    dot_general x58 -> x152, matrix products: 255 us -> 159 us  [mm(): lax.dot_general(left, right, dims, preferred_element_type=jnp.float32)]
    dynamic_update_slice x16 -> x17, local copies, waits for them, and re-layouts: 16.4 us -> 108 us  [the longest x3 78.5 us: line_gather(): lax.dynamic_update_index_in_dim(result, piece, (place + step) % count, 0)]
  transfers between devices with their start and end apart: 20 -> 161, of which waited for: 13 -> 59; matrix products, arithmetic and copies ran while one was open for 32% -> 36% of each run, Pallas kernels for 0% -> 2%
where the time goes in v1:
time: 1130 us; the launch traced here: 1110 us
  waiting for transfers between devices  364 us (32%)
  local copies, waits for them, and re-layouts  246 us (22%)
  starting transfers between devices  205 us (18%)
  matrix products  159 us (14%)
  other arithmetic  71.8 us (6%)
  Pallas kernels  59.6 us (5%)
    ppermute x127, waiting for transfers between devices, across(): return lax.ppermute(values, axis, [(i, i ^ bits) for i in range(size)])  220 us
    dot_general x152, matrix products, mm(): lax.dot_general(left, right, dims, preferred_element_type=jnp.float32)  159 us
    ppermute x127, starting transfers between devices, across(): return lax.ppermute(values, axis, [(i, i ^ bits) for i in range(size)])  117 us
    ppermute x12, waiting for transfers between devices, line_gather(): lax.ppermute(falling[-1], 'wt', [(i, i - 1) for i in range(1, count - ste...  111 us
    dynamic_update_slice x3, local copies, waits for them, and re-layouts, line_gather(): lax.dynamic_update_index_in_dim(result, piece, (place + step) % count, 0)  78.5 us
    unnamed x501, local copies, waits for them, and re-layouts  66.4 us
    ppermute x12, starting transfers between devices, line_gather(): lax.ppermute(rising[-1], 'wt', [(i, i + 1) for i in range(step - 1, count...  44.5 us
    pallas_call x1, Pallas kernels, mixer_backward(): pl.pallas_call(backward_kernel, out_shape=(rows, rows, rows), in_specs=[S...  33.3 us
  transfers between devices with their start and end apart: 161, of which 59 were waited for; matrix products, arithmetic and copies ran while one was open for 36% of the time, Pallas kernels for 2%

profile of v1, /device:TPU:4, one launch (start us, length us, event | category | flops | bytes accessed | tf_op | source)
XLA Modules:
  0.0 1111.6 jit_solution(3391657849432893340)
XLA Ops:
  4.3 4.2 collective-permute-start.22
  23.0 3.5 constant_dynamic-slice_fusion.4
  57.6 3.6 copy.138
  63.5 26.2 %dynamic_update_slice.97 = bf16[4,704,512]{2,0,1:T(4,128)(2,1)} dynamic-update-slice(bf16[4,704,512]{2,0,1:T(4,128)(2,1)} %broadcast_in_dim.150, bf16[1,704,512]{2,0,1:T(2,128)(2,1)} %copy.118, s32[]{:T(128)S(6)} %select_n.486, s32[]{:T(128)} %constant.407.clone.1, s32[]{:T(128)} %constant.407.clone.1) | dynamic-update-slice | bytes 1441796 | tf_op jit(solution)/shard_map/jit(dynamic_update_index_in_dim)/dynamic_update_slice | solution.py:348
  97.4 10.4 collective-permute-done.26
  122.5 5.5 collective-permute-done.43
  127.9 5.8 collective-permute-start.2
  146.8 9.7 collective-permute-done.46
  160.8 4.1 collective-permute-done.71
  167.5 3.9 collective-permute-done.12
  173.1 9.5 collective-permute-done.73
  186.3 16.1 %collective-permute-done.28 = bf16[256,2048]{0,1:T(8,128)(2,1)S(1)} collective-permute-done((bf16[256,2048]{0,1:T(8,128)(2,1)}, bf16[256,2048]{0,1:T(8,128)(2,1)S(1)}, u32[]{:S(2)}, u32[]{:S(2)}) %collective-permute-start.28) | collective-permute-done | bytes 1048608 | tf_op jit(solution)/shard_map/ppermute | solution.py:291
  204.8 21.8 %collective-permute-start.37 = (bf16[352,2048]{1,0:T(8,128)(2,1)}, bf16[352,2048]{1,0:T(8,128)(2,1)}, u32[]{:S(2)}, u32[]{:S(2)}) collective-permute-start(bf16[352,2048]{1,0:T(8,128)(2,1)} %bitcast.45), channel_id=1, source_target_pairs={{0,1},{1,2},{2,3},{4,5},{5,6},{6,7},{8,9},{9,10},{10,11},{12,13},{... | collective-permute-start | bytes 4325384 | tf_op jit(solution)/shard_map/ppermute | solution.py:342
  238.1 8.6 collective-permute-done.1
  250.0 12.2 %collective-permute-done.47 = bf16[704,512]{1,0:T(8,128)(2,1)S(1)} collective-permute-done((bf16[704,512]{1,0:T(8,128)(2,1)S(1)}, bf16[704,512]{1,0:T(8,128)(2,1)S(1)}, u32[]{:S(2)}, u32[]{:S(2)}) %collective-permute-start.47) | collective-permute-done | bytes 720928 | tf_op jit(solution)/shard_map/ppermute | solution.py:345
  271.0 26.2 %dynamic_update_slice.98 = bf16[4,704,512]{2,0,1:T(4,128)(2,1)} dynamic-update-slice(bf16[4,704,512]{2,0,1:T(4,128)(2,1)} %dynamic_update_slice.97, bf16[1,704,512]{2,0,1:T(2,128)(2,1)} %copy.119, s32[]{:T(128)S(6)} %select_n.490, s32[]{:T(128)} %constant.407.clone.1, s32[]{:T(128)} %constant.407.clone.1) | dynamic-update-slice | bytes 1441796 | tf_op jit(solution)/shard_map/jit(dynamic_update_index_in_dim)/dynamic_update_slice | solution.py:351
  297.2 26.2 %dynamic_update_slice.99 = bf16[4,704,512]{2,0,1:T(4,128)(2,1)} dynamic-update-slice(bf16[4,704,512]{2,0,1:T(4,128)(2,1)} %dynamic_update_slice.98, bf16[1,704,512]{2,0,1:T(2,128)(2,1)} %copy.120, s32[]{:T(128)S(6)} %select_n.494, s32[]{:T(128)} %constant.407.clone.1, s32[]{:T(128)} %constant.407.clone.1) | dynamic-update-slice | bytes 1441796 | tf_op jit(solution)/shard_map/jit(dynamic_update_index_in_dim)/dynamic_update_slice | solution.py:351
  323.3 26.2 %dynamic_update_slice.100 = bf16[4,704,512]{2,0,1:T(4,128)(2,1)} dynamic-update-slice(bf16[4,704,512]{2,0,1:T(4,128)(2,1)} %dynamic_update_slice.99, bf16[1,704,512]{2,0,1:T(2,128)(2,1)} %copy.121, s32[]{:T(128)S(6)} %select_n.498, s32[]{:T(128)} %constant.407.clone.1, s32[]{:T(128)} %constant.407.clone.1) | dynamic-update-slice | bytes 1441796 | tf_op jit(solution)/shard_map/jit(dynamic_update_index_in_dim)/dynamic_update_slice | solution.py:351
  349.5 4.6 copy.161
  371.3 36.1 %collective-permute-done.5 = bf16[256,2048]{1,0:T(8,128)(2,1)S(1)} collective-permute-done((bf16[256,2048]{1,0:T(8,128)(2,1)S(1)}, bf16[256,2048]{1,0:T(8,128)(2,1)S(1)}, u32[]{:S(2)}, u32[]{:S(2)}) %collective-permute-start.5) | collective-permute-done | bytes 1048608 | tf_op jit(solution)/shard_map/ppermute | solution.py:345
  411.7 26.8 %collective-permute-done.40 = bf16[352,2048]{1,0:T(8,128)(2,1)} collective-permute-done((bf16[352,2048]{1,0:T(8,128)(2,1)}, bf16[352,2048]{1,0:T(8,128)(2,1)}, u32[]{:S(2)}, u32[]{:S(2)}) %collective-permute-start.40) | collective-permute-done | bytes 1441824 | tf_op jit(solution)/shard_map/ppermute | solution.py:345
  440.2 10.1 collective-permute-start.41
  455.0 5.8 collective-permute-done.6
  470.7 3.8 fusion.30
  478.1 26.2 %shard_map.276 = (bf16[2048,256]{1,0:T(8,128)(2,1)S(1)}, bf16[2048,256]{1,0:T(8,128)(2,1)S(1)}, bf16[2048,256]{1,0:T(8,128)(2,1)S(1)}, bf16[2048,256]{1,0:T(8,128)(2,1)S(1)}, f32[17,2,128,128]{3,2,1,0:T(8,128)S(1)}) custom-call(s32[4]{0:T(128)S(1)} %bitcast.527, s32[1,2048]{1,0:T(1,128)S(1)} %reshape_reshape_reshape.8.order_row_ref, ...), custom_call_target="tpu_custom_call" | custom-call | flops 10200547328 | bytes 10485760 | tf_op jit(solution)/shard_map/pallas_call | solution.py:210
  554.4 6.1 multiply_reduce_fusion.1
  576.8 3.9 multiply_convert_fusion.11
  600.6 6.3 collective-permute-done.55
  620.3 3.8 fusion.436
  669.0 3.8 multiply_convert_fusion.7
  690.9 3.6 collective-permute-done.151
  695.4 3.5 collective-permute-done.152
  698.9 4.1 collective-permute-done.153
  703.8 3.5 collective-permute-done.154
  707.3 3.7 collective-permute-done.155
  712.5 3.6 collective-permute-done.156
  716.2 4.6 collective-permute-done.157
  735.1 6.1 collective-permute-done.138
  743.2 4.8 collective-permute-done.139
  748.0 5.5 collective-permute-done.140
  755.4 5.8 collective-permute-done.141
  761.3 5.7 collective-permute-done.143
  774.1 7.7 collective-permute-done.158
  781.9 15.8 %collective-permute-done.159 = f32[720,128]{1,0:T(8,128)S(1)} collective-permute-done((f32[720,128]{1,0:T(8,128)S(1)}, f32[720,128]{1,0:T(8,128)S(1)}, u32[]{:S(2)}, u32[]{:S(2)}) %collective-permute-start.159) | collective-permute-done | bytes 368672 | tf_op jit(solution)/shard_map/ppermute | solution.py:291
  805.5 16.0 %collective-permute-done.76 = bf16[128,2048]{1,0:T(8,128)(2,1)S(1)} collective-permute-done((bf16[128,2048]{1,0:T(8,128)(2,1)S(1)}, bf16[128,2048]{1,0:T(8,128)(2,1)S(1)}, u32[]{:S(2)}, u32[]{:S(2)}) %collective-permute-start.76) | collective-permute-done | bytes 524320 | tf_op jit(solution)/shard_map/ppermute | solution.py:291
  824.2 9.4 collective-permute-done.58
  840.6 7.5 collective-permute-done.77
  852.4 7.0 collective-permute-done.52
  859.3 8.0 collective-permute-done.59
  867.4 5.9 subtract_add_fusion
  880.8 3.5 fusion.4
  904.5 6.1 collective-permute-done.132
  918.2 6.8 collective-permute-done.86
  939.6 4.2 fusion.8
  943.9 33.3 %shard_map.277 = (bf16[2048,256]{1,0:T(8,128)(2,1)S(1)}, bf16[2048,256]{1,0:T(8,128)(2,1)S(1)}, bf16[2048,256]{1,0:T(8,128)(2,1)S(1)}) custom-call(s32[4]{0:T(128)S(1)} %bitcast.528, s32[1,2048]{1,0:T(1,128)S(1)} %reshape_reshape_reshape.8.order_row_ref, s32[2048,1]{1,0:T(8,128)S(1)} %copy-done.4, bf16[2048,256]{1,0:T(8,128)(2,1)S(1)} %get-tuple-element.58.grad_ref, ...), custom_call_target="tpu_custom_call" | custom-call | flops 13958643712 | bytes 10485760 | tf_op jit(solution)/shard_map/pallas_call | solution.py:228
  1006.4 8.4 collective-permute-start.135
  1019.8 3.9 collective-permute-start.115
  1033.3 3.5 collective-permute-done.109
  1041.2 4.1 collective-permute-done.111
  1047.0 3.4 collective-permute-done.112
  1050.4 4.7 collective-permute-done.113
  1069.8 10.7 collective-permute-done.94
  1092.4 6.1 collective-permute-done.92
  1099.9 7.7 collective-permute-done.95
  (1186 shorter events, 506.9 us)
Async XLA Ops:
  4.3 36.4 %collective-permute-start.22 = (bf16[256,512]{0,1:T(8,128)(2,1)}, bf16[256,512]{0,1:T(8,128)(2,1)}, u32[]{:S(2)}, u32[]{:S(2)}) collective-permute-start(bf16[256,512]{0,1:T(8,128)(2,1)} %copy.153), channel_id=1, source_target_pairs={{0,1},{1,2},{2,3},{4,5},{5,6},{6,7},{8,9},{9,10},{10,11},{12,13},{... | collective-permute-start | bytes 786440 | tf_op jit(solution)/shard_map/ppermute | solution.py:342
  8.5 35.5 %collective-permute-start.21 = (bf16[256,512]{0,1:T(8,128)(2,1)}, bf16[256,512]{0,1:T(8,128)(2,1)}, u32[]{:S(2)}, u32[]{:S(2)}) collective-permute-start(bf16[256,512]{0,1:T(8,128)(2,1)} %copy.153), channel_id=1, source_target_pairs={{1,0},{2,1},{3,2},{5,4},{6,5},{7,6},{9,8},{10,9},{11,10},{13,12},{... | collective-permute-start | bytes 786440 | tf_op jit(solution)/shard_map/ppermute | solution.py:345
  13.2 102.0 %collective-permute-start.9 = (bf16[256,2048]{1,0:T(8,128)(2,1)}, bf16[256,2048]{1,0:T(8,128)(2,1)}, u32[]{:S(2)}, u32[]{:S(2)}) collective-permute-start(bf16[256,2048]{1,0:T(8,128)(2,1)} %fusion.18), channel_id=1, source_target_pairs={{0,16},{4,20},{8,24},{12,28},{16,0},{20,4},{24,8},{28,12},{1,17},{... | collective-permute-start | bytes 3145736 | tf_op jit(solution)/shard_map/ppermute | solution.py:291
  13.7 104.2 %collective-permute-start.7 = (bf16[256,2048]{1,0:T(8,128)(2,1)}, bf16[256,2048]{1,0:T(8,128)(2,1)}, u32[]{:S(2)}, u32[]{:S(2)}) collective-permute-start(bf16[256,2048]{1,0:T(8,128)(2,1)} %fusion.18), channel_id=1, source_target_pairs={{0,8},{4,12},{8,0},{12,4},{16,24},{20,28},{24,16},{28,20},{1,9},{5... | collective-permute-start | bytes 3145736 | tf_op jit(solution)/shard_map/ppermute | solution.py:291
  15.2 95.2 %collective-permute-start.65 = (bf16[256,2048]{1,0:T(8,128)(2,1)}, bf16[256,2048]{1,0:T(8,128)(2,1)}, u32[]{:S(2)}, u32[]{:S(2)}) collective-permute-start(bf16[256,2048]{1,0:T(8,128)(2,1)} %bitcast.65), channel_id=1, source_target_pairs={{0,4},{4,0},{8,12},{12,8},{16,20},{20,16},{24,28},{28,24},{1,5},{5... | collective-permute-start | bytes 3145736 | tf_op jit(solution)/shard_map/ppermute | solution.py:291
  44.0 47.9 %collective-permute-start.25 = (bf16[256,512]{0,1:T(8,128)(2,1)}, bf16[256,512]{0,1:T(8,128)(2,1)}, u32[]{:S(2)}, u32[]{:S(2)}) collective-permute-start(bf16[256,512]{0,1:T(8,128)(2,1)} %collective-permute-done.21), channel_id=1, source_target_pairs={{1,0},{2,1},{5,4},{6,5},{9,8},{10,9},{13,12},{14,13},{17,16},{18,1... | collective-permute-start | bytes 786440 | tf_op jit(solution)/shard_map/ppermute | solution.py:345
  45.3 47.2 %collective-permute-start.24 = (bf16[256,512]{0,1:T(8,128)(2,1)}, bf16[256,512]{0,1:T(8,128)(2,1)}, u32[]{:S(2)}, u32[]{:S(2)}) collective-permute-start(bf16[256,512]{0,1:T(8,128)(2,1)} %collective-permute-done.23), channel_id=1, source_target_pairs={{2,3},{6,7},{10,11},{14,15},{18,19},{22,23},{26,27},{30,31}} | collective-permute-start | bytes 786440 | tf_op jit(solution)/shard_map/ppermute | solution.py:342
  91.9 47.1 %collective-permute-start = (bf16[256,2048]{1,0:T(8,128)(2,1)}, bf16[256,2048]{1,0:T(8,128)(2,1)S(1)}, u32[]{:S(2)}, u32[]{:S(2)}) collective-permute-start(bf16[256,2048]{1,0:T(8,128)(2,1)} %fusion.18), channel_id=1, source_target_pairs={{0,4},{4,0},{8,12},{12,8},{16,20},{20,16},{24,28},{28,24},{1,5},{5... | collective-permute-start | bytes 3145736 | tf_op jit(solution)/shard_map/ppermute | solution.py:291
  107.8 28.2 %collective-permute-start.67 = (bf16[256,2048]{1,0:T(8,128)(2,1)}, bf16[256,2048]{1,0:T(8,128)(2,1)S(1)}, u32[]{:S(2)}, u32[]{:S(2)}) collective-permute-start(bf16[256,2048]{1,0:T(8,128)(2,1)} %bitcast.65), channel_id=1, source_target_pairs={{0,8},{4,12},{8,0},{12,4},{16,24},{20,28},{24,16},{28,20},{1,9},{5... | collective-permute-start | bytes 3145736 | tf_op jit(solution)/shard_map/ppermute | solution.py:291
  117.9 26.5 %collective-permute-start.72 = (bf16[256,2048]{1,0:T(8,128)(2,1)}, bf16[256,2048]{1,0:T(8,128)(2,1)S(1)}, u32[]{:S(2)}, u32[]{:S(2)}) collective-permute-start(bf16[256,2048]{1,0:T(8,128)(2,1)} %bitcast.65), channel_id=1, source_target_pairs={{0,16},{4,20},{8,24},{12,28},{16,0},{20,4},{24,8},{28,12},{1,17},{... | collective-permute-start | bytes 3145736 | tf_op jit(solution)/shard_map/ppermute | solution.py:291
  127.9 108.9 %collective-permute-start.2 = (bf16[256,2048]{1,0:T(8,128)(2,1)S(1)}, bf16[256,2048]{1,0:T(8,128)(2,1)}, u32[]{:S(2)}, u32[]{:S(2)}) collective-permute-start(bf16[256,2048]{1,0:T(8,128)(2,1)S(1)} %bitcast.586), channel_id=1, source_target_pairs={{0,1},{1,2},{2,3},{4,5},{5,6},{6,7},{8,9},{9,10},{10,11},{12,13},{... | collective-permute-start | bytes 3145736 | tf_op jit(solution)/shard_map/ppermute | solution.py:342
  139.1 21.3 %collective-permute-start.11 = (bf16[128,2048]{1,0:T(8,128)(2,1)S(1)}, bf16[128,2048]{1,0:T(8,128)(2,1)S(1)}, u32[]{:S(2)}, u32[]{:S(2)}) collective-permute-start(bf16[128,2048]{1,0:T(8,128)(2,1)S(1)} %slice.1324), channel_id=1, source_target_pairs={{0,16},{4,20},{8,24},{12,28},{16,0},{20,4},{24,8},{28,12},{1,17},{... | collective-permute-start | bytes 1572872 | tf_op jit(solution)/shard_map/ppermute | solution.py:291
  146.7 38.9 %collective-permute-start.27 = (bf16[256,2048]{0,1:T(8,128)(2,1)}, bf16[256,2048]{0,1:T(8,128)(2,1)S(1)}, u32[]{:S(2)}, u32[]{:S(2)}) collective-permute-start(bf16[256,2048]{0,1:T(8,128)(2,1)} %bitcast.39), channel_id=1, source_target_pairs={{0,4},{4,0},{8,12},{12,8},{16,20},{20,16},{24,28},{28,24},{1,5},{5... | collective-permute-start | bytes 3145736 | tf_op jit(solution)/shard_map/ppermute | solution.py:291
  160.4 22.1 %collective-permute-start.73 = (bf16[128,2048]{1,0:T(8,128)(2,1)S(1)}, bf16[128,2048]{1,0:T(8,128)(2,1)S(1)}, u32[]{:S(2)}, u32[]{:S(2)}) collective-permute-start(bf16[128,2048]{1,0:T(8,128)(2,1)S(1)} %slice.1443), channel_id=1, source_target_pairs={{0,8},{4,12},{8,0},{12,4},{16,24},{20,28},{24,16},{28,20},{1,9},{5... | collective-permute-start | bytes 1572872 | tf_op jit(solution)/shard_map/ppermute | solution.py:291
  164.9 37.4 %collective-permute-start.28 = (bf16[256,2048]{0,1:T(8,128)(2,1)}, bf16[256,2048]{0,1:T(8,128)(2,1)S(1)}, u32[]{:S(2)}, u32[]{:S(2)}) collective-permute-start(bf16[256,2048]{0,1:T(8,128)(2,1)} %bitcast.39), channel_id=1, source_target_pairs={{0,8},{4,12},{8,0},{12,4},{16,24},{20,28},{24,16},{28,20},{1,9},{5... | collective-permute-start | bytes 3145736 | tf_op jit(solution)/shard_map/ppermute | solution.py:291
  171.3 31.2 %collective-permute-start.30 = (bf16[256,2048]{0,1:T(8,128)(2,1)}, bf16[256,2048]{0,1:T(8,128)(2,1)S(1)}, u32[]{:S(2)}, u32[]{:S(2)}) collective-permute-start(bf16[256,2048]{0,1:T(8,128)(2,1)} %bitcast.39), channel_id=1, source_target_pairs={{0,16},{4,20},{8,24},{12,28},{16,0},{20,4},{24,8},{28,12},{1,17},{... | collective-permute-start | bytes 3145736 | tf_op jit(solution)/shard_map/ppermute | solution.py:291
  182.6 22.2 %collective-permute-start.10 = (bf16[256,2048]{1,0:T(8,128)(2,1)}, bf16[256,2048]{1,0:T(8,128)(2,1)S(1)}, u32[]{:S(2)}, u32[]{:S(2)}) collective-permute-start(bf16[256,2048]{1,0:T(8,128)(2,1)} %collective-permute-done.9), channel_id=1, source_target_pairs={{0,4},{4,0},{8,12},{12,8},{16,20},{20,16},{24,28},{28,24},{1,5},{5... | collective-permute-start | bytes 3145736 | tf_op jit(solution)/shard_map/ppermute | solution.py:291
  185.6 43.4 %collective-permute-start.8 = (bf16[256,2048]{1,0:T(8,128)(2,1)}, bf16[256,2048]{1,0:T(8,128)(2,1)S(1)}, u32[]{:S(2)}, u32[]{:S(2)}) collective-permute-start(bf16[256,2048]{1,0:T(8,128)(2,1)} %collective-permute-done.7), channel_id=1, source_target_pairs={{0,4},{4,0},{8,12},{12,8},{16,20},{20,16},{24,28},{28,24},{1,5},{5... | collective-permute-start | bytes 3145736 | tf_op jit(solution)/shard_map/ppermute | solution.py:291
  202.3 27.1 %collective-permute-start.68 = (bf16[256,2048]{1,0:T(8,128)(2,1)S(1)}, bf16[256,2048]{1,0:T(8,128)(2,1)S(1)}, u32[]{:S(2)}, u32[]{:S(2)}) collective-permute-start(bf16[256,2048]{1,0:T(8,128)(2,1)S(1)} %collective-permute-done.67), channel_id=1, source_target_pairs={{0,4},{4,0},{8,12},{12,8},{16,20},{20,16},{24,28},{28,24},{1,5},{5... | collective-permute-start | bytes 3145736 | tf_op jit(solution)/shard_map/ppermute | solution.py:291
  202.6 44.2 %collective-permute-start.1 = (bf16[256,2048]{1,0:T(8,128)(2,1)S(1)}, bf16[256,2048]{1,0:T(8,128)(2,1)S(1)}, u32[]{:S(2)}, u32[]{:S(2)}) collective-permute-start(bf16[256,2048]{1,0:T(8,128)(2,1)S(1)} %bitcast.587), channel_id=1, source_target_pairs={{1,0},{2,1},{3,2},{5,4},{6,5},{7,6},{9,8},{10,9},{11,10},{13,12},{... | collective-permute-start | bytes 3145736 | tf_op jit(solution)/shard_map/ppermute | solution.py:345
  204.8 155.2 %collective-permute-start.37 = (bf16[352,2048]{1,0:T(8,128)(2,1)}, bf16[352,2048]{1,0:T(8,128)(2,1)}, u32[]{:S(2)}, u32[]{:S(2)}) collective-permute-start(bf16[352,2048]{1,0:T(8,128)(2,1)} %bitcast.45), channel_id=1, source_target_pairs={{0,1},{1,2},{2,3},{4,5},{5,6},{6,7},{8,9},{9,10},{10,11},{12,13},{... | collective-permute-start | bytes 4325384 | tf_op jit(solution)/shard_map/ppermute | solution.py:342
  233.2 29.0 %collective-permute-start.47 = (bf16[704,512]{1,0:T(8,128)(2,1)S(1)}, bf16[704,512]{1,0:T(8,128)(2,1)S(1)}, u32[]{:S(2)}, u32[]{:S(2)}) collective-permute-start(bf16[704,512]{1,0:T(8,128)(2,1)S(1)} %collective-permute-done.46), channel_id=1, source_target_pairs={{1,0},{5,4},{9,8},{13,12},{17,16},{21,20},{25,24},{29,28}} | collective-permute-start | bytes 2162696 | tf_op jit(solution)/shard_map/ppermute | solution.py:345
  236.8 126.2 %collective-permute-start.36 = (bf16[352,2048]{1,0:T(8,128)(2,1)}, bf16[352,2048]{1,0:T(8,128)(2,1)}, u32[]{:S(2)}, u32[]{:S(2)}) collective-permute-start(bf16[352,2048]{1,0:T(8,128)(2,1)} %bitcast.45), channel_id=1, source_target_pairs={{1,0},{2,1},{3,2},{5,4},{6,5},{7,6},{9,8},{10,9},{11,10},{13,12},{... | collective-permute-start | bytes 4325384 | tf_op jit(solution)/shard_map/ppermute | solution.py:345
  246.8 109.6 %collective-permute-start.74 = (bf16[256,2048]{1,0:T(8,128)(2,1)}, bf16[256,2048]{1,0:T(8,128)(2,1)}, u32[]{:S(2)}, u32[]{:S(2)}) collective-permute-start(bf16[256,2048]{1,0:T(8,128)(2,1)} %pad_maximum_fusion.21), channel_id=1, source_target_pairs={{0,4},{4,0},{8,12},{12,8},{16,20},{20,16},{24,28},{28,24},{1,5},{5... | collective-permute-start | bytes 3145736 | tf_op jit(solution)/shard_map/ppermute | solution.py:291
  262.2 91.8 %collective-permute-start.33 = (bf16[128,2048]{0,1:T(8,128)(2,1)}, bf16[128,2048]{0,1:T(8,128)(2,1)}, u32[]{:S(2)}, u32[]{:S(2)}) collective-permute-start(bf16[128,2048]{0,1:T(8,128)(2,1)} %slice.1408), channel_id=1, source_target_pairs={{0,8},{4,12},{8,0},{12,4},{16,24},{20,28},{24,16},{28,20},{1,9},{5... | collective-permute-start | bytes 1572872 | tf_op jit(solution)/shard_map/ppermute | solution.py:291
  267.0 97.9 %collective-permute-start.3 = (bf16[256,2048]{1,0:T(8,128)(2,1)}, bf16[256,2048]{1,0:T(8,128)(2,1)}, u32[]{:S(2)}, u32[]{:S(2)}) collective-permute-start(bf16[256,2048]{1,0:T(8,128)(2,1)} %collective-permute-done.2), channel_id=1, source_target_pairs={{1,2},{2,3},{5,6},{6,7},{9,10},{10,11},{13,14},{14,15},{17,18},{18... | collective-permute-start | bytes 3145736 | tf_op jit(solution)/shard_map/ppermute | solution.py:342
  356.4 51.1 %collective-permute-start.5 = (bf16[256,2048]{1,0:T(8,128)(2,1)S(1)}, bf16[256,2048]{1,0:T(8,128)(2,1)S(1)}, u32[]{:S(2)}, u32[]{:S(2)}) collective-permute-start(bf16[256,2048]{1,0:T(8,128)(2,1)S(1)} %copy-done.142), channel_id=1, source_target_pairs={{1,0},{2,1},{5,4},{6,5},{9,8},{10,9},{13,12},{14,13},{17,16},{18,1... | collective-permute-start | bytes 3145736 | tf_op jit(solution)/shard_map/ppermute | solution.py:345
  360.0 48.1 %collective-permute-start.29 = (bf16[256,2048]{0,1:T(8,128)(2,1)S(1)}, bf16[256,2048]{0,1:T(8,128)(2,1)S(1)}, u32[]{:S(2)}, u32[]{:S(2)}) collective-permute-start(bf16[256,2048]{0,1:T(8,128)(2,1)S(1)} %copy-done.86), channel_id=1, source_target_pairs={{0,4},{4,0},{8,12},{12,8},{16,20},{20,16},{24,28},{28,24},{1,5},{5... | collective-permute-start | bytes 3145736 | tf_op jit(solution)/shard_map/ppermute | solution.py:291
  363.0 48.6 %collective-permute-start.38 = (bf16[352,2048]{1,0:T(8,128)(2,1)}, bf16[352,2048]{1,0:T(8,128)(2,1)}, u32[]{:S(2)}, u32[]{:S(2)}) collective-permute-start(bf16[352,2048]{1,0:T(8,128)(2,1)} %collective-permute-done.37), channel_id=1, source_target_pairs={{1,2},{2,3},{5,6},{6,7},{9,10},{10,11},{13,14},{14,15},{17,18},{18... | collective-permute-start | bytes 4325384 | tf_op jit(solution)/shard_map/ppermute | solution.py:342
  364.9 73.5 %collective-permute-start.40 = (bf16[352,2048]{1,0:T(8,128)(2,1)}, bf16[352,2048]{1,0:T(8,128)(2,1)}, u32[]{:S(2)}, u32[]{:S(2)}) collective-permute-start(bf16[352,2048]{1,0:T(8,128)(2,1)} %collective-permute-done.36), channel_id=1, source_target_pairs={{1,0},{2,1},{5,4},{6,5},{9,8},{10,9},{13,12},{14,13},{17,16},{18,1... | collective-permute-start | bytes 4325384 | tf_op jit(solution)/shard_map/ppermute | solution.py:345
  367.7 72.5 %collective-permute-start.31 = (bf16[256,2048]{0,1:T(8,128)(2,1)S(1)}, bf16[256,2048]{0,1:T(8,128)(2,1)S(1)}, u32[]{:S(2)}, u32[]{:S(2)}) collective-permute-start(bf16[256,2048]{0,1:T(8,128)(2,1)S(1)} %copy-done.84), channel_id=1, source_target_pairs={{0,4},{4,0},{8,12},{12,8},{16,20},{20,16},{24,28},{28,24},{1,5},{5... | collective-permute-start | bytes 3145736 | tf_op jit(solution)/shard_map/ppermute | solution.py:291
  407.4 46.8 %collective-permute-start.4 = (bf16[256,2048]{1,0:T(8,128)(2,1)}, bf16[256,2048]{1,0:T(8,128)(2,1)S(1)}, u32[]{:S(2)}, u32[]{:S(2)}) collective-permute-start(bf16[256,2048]{1,0:T(8,128)(2,1)} %collective-permute-done.3), channel_id=1, source_target_pairs={{2,3},{6,7},{10,11},{14,15},{18,19},{22,23},{26,27},{30,31}} | collective-permute-start | bytes 3145736 | tf_op jit(solution)/shard_map/ppermute | solution.py:342
  408.2 52.6 %collective-permute-start.6 = (bf16[256,2048]{1,0:T(8,128)(2,1)S(1)}, bf16[256,2048]{1,0:T(8,128)(2,1)S(1)}, u32[]{:S(2)}, u32[]{:S(2)}) collective-permute-start(bf16[256,2048]{1,0:T(8,128)(2,1)S(1)} %collective-permute-done.5), channel_id=1, source_target_pairs={{1,0},{5,4},{9,8},{13,12},{17,16},{21,20},{25,24},{29,28}} | collective-permute-start | bytes 3145736 | tf_op jit(solution)/shard_map/ppermute | solution.py:345
  411.7 140.3 %collective-permute-start.34 = (bf16[256,2048]{0,1:T(8,128)(2,1)}, bf16[256,2048]{0,1:T(8,128)(2,1)}, u32[]{:S(2)}, u32[]{:S(2)}) collective-permute-start(bf16[256,2048]{0,1:T(8,128)(2,1)} %pad_maximum_fusion.19), channel_id=1, source_target_pairs={{0,4},{4,0},{8,12},{12,8},{16,20},{20,16},{24,28},{28,24},{1,5},{5... | collective-permute-start | bytes 3145736 | tf_op jit(solution)/shard_map/ppermute | solution.py:291
  438.4 125.4 %collective-permute-start.39 = (bf16[352,2048]{1,0:T(8,128)(2,1)}, bf16[352,2048]{1,0:T(8,128)(2,1)}, u32[]{:S(2)}, u32[]{:S(2)}) collective-permute-start(bf16[352,2048]{1,0:T(8,128)(2,1)} %collective-permute-done.38), channel_id=1, source_target_pairs={{2,3},{6,7},{10,11},{14,15},{18,19},{22,23},{26,27},{30,31}} | collective-permute-start | bytes 4325384 | tf_op jit(solution)/shard_map/ppermute | solution.py:342
  440.2 127.6 %collective-permute-start.41 = (bf16[352,2048]{1,0:T(8,128)(2,1)}, bf16[352,2048]{1,0:T(8,128)(2,1)}, u32[]{:S(2)}, u32[]{:S(2)}) collective-permute-start(bf16[352,2048]{1,0:T(8,128)(2,1)} %collective-permute-done.40), channel_id=1, source_target_pairs={{1,0},{5,4},{9,8},{13,12},{17,16},{21,20},{25,24},{29,28}} | collective-permute-start | bytes 4325384 | tf_op jit(solution)/shard_map/ppermute | solution.py:345
  561.5 25.6 %collective-permute-start.49 = (bf16[256,2048]{1,0:T(8,128)(2,1)S(1)}, bf16[256,2048]{1,0:T(8,128)(2,1)S(1)}, u32[]{:S(2)}, u32[]{:S(2)}) collective-permute-start(bf16[256,2048]{1,0:T(8,128)(2,1)S(1)} %multiply_convert_fusion.3), channel_id=1, source_target_pairs={{0,8},{4,12},{8,0},{12,4},{16,24},{20,28},{24,16},{28,20},{1,9},{5... | collective-permute-start | bytes 3145736 | tf_op jit(solution)/shard_map/ppermute | solution.py:291
  563.0 29.7 %collective-permute-start.54 = (bf16[256,2048]{1,0:T(8,128)(2,1)S(1)}, bf16[256,2048]{1,0:T(8,128)(2,1)S(1)}, u32[]{:S(2)}, u32[]{:S(2)}) collective-permute-start(bf16[256,2048]{1,0:T(8,128)(2,1)S(1)} %multiply_convert_fusion.3), channel_id=1, source_target_pairs={{0,16},{4,20},{8,24},{12,28},{16,0},{20,4},{24,8},{28,12},{1,17},{... | collective-permute-start | bytes 3145736 | tf_op jit(solution)/shard_map/ppermute | solution.py:291
  583.1 100.0 %collective-permute-start.144 = (bf16[256,128]{1,0:T(8,128)(2,1)}, bf16[256,128]{1,0:T(8,128)(2,1)S(1)}, u32[]{:S(2)}, u32[]{:S(2)}) collective-permute-start(bf16[256,128]{1,0:T(8,128)(2,1)} %slice.1581), channel_id=1, source_target_pairs={{0,4},{4,0},{8,12},{12,8},{16,20},{20,16},{24,28},{28,24},{1,5},{5... | collective-permute-start | bytes 196616 | tf_op jit(solution)/shard_map/ppermute | solution.py:291
  608.0 53.0 %collective-permute-start.56 = (bf16[256,2048]{1,0:T(8,128)(2,1)}, bf16[256,2048]{1,0:T(8,128)(2,1)}, u32[]{:S(2)}, u32[]{:S(2)}) collective-permute-start(bf16[256,2048]{1,0:T(8,128)(2,1)} %pad_maximum_fusion.20), channel_id=1, source_target_pairs={{0,4},{4,0},{8,12},{12,8},{16,20},{20,16},{24,28},{28,24},{1,5},{5... | collective-permute-start | bytes 3145736 | tf_op jit(solution)/shard_map/ppermute | solution.py:291
  643.0 41.6 %collective-permute-start.145 = (bf16[256,128]{1,0:T(8,128)(2,1)}, bf16[256,128]{1,0:T(8,128)(2,1)}, u32[]{:S(2)}, u32[]{:S(2)}) collective-permute-start(bf16[256,128]{1,0:T(8,128)(2,1)} %get-tuple-element.152), channel_id=1, source_target_pairs={{0,8},{4,12},{8,0},{12,4},{16,24},{20,28},{24,16},{28,20},{1,9},{5... | collective-permute-start | bytes 196616 | tf_op jit(solution)/shard_map/ppermute | solution.py:291
  643.8 41.7 %collective-permute-start.146 = (bf16[256,128]{1,0:T(8,128)(2,1)}, bf16[256,128]{1,0:T(8,128)(2,1)}, u32[]{:S(2)}, u32[]{:S(2)}) collective-permute-start(bf16[256,128]{1,0:T(8,128)(2,1)} %get-tuple-element.153), channel_id=1, source_target_pairs={{0,12},{4,8},{8,4},{12,0},{16,28},{20,24},{24,20},{28,16},{1,13},{... | collective-permute-start | bytes 196616 | tf_op jit(solution)/shard_map/ppermute | solution.py:291
  645.3 42.3 %collective-permute-start.147 = (bf16[256,128]{1,0:T(8,128)(2,1)}, bf16[256,128]{1,0:T(8,128)(2,1)}, u32[]{:S(2)}, u32[]{:S(2)}) collective-permute-start(bf16[256,128]{1,0:T(8,128)(2,1)} %get-tuple-element.154), channel_id=1, source_target_pairs={{0,16},{4,20},{8,24},{12,28},{16,0},{20,4},{24,8},{28,12},{1,17},{... | collective-permute-start | bytes 196616 | tf_op jit(solution)/shard_map/ppermute | solution.py:291
  661.0 26.8 %collective-permute-start.148 = (bf16[256,128]{1,0:T(8,128)(2,1)S(1)}, bf16[256,128]{1,0:T(8,128)(2,1)S(1)}, u32[]{:S(2)}, u32[]{:S(2)}) collective-permute-start(bf16[256,128]{1,0:T(8,128)(2,1)S(1)} %copy-done.178), channel_id=1, source_target_pairs={{0,20},{4,16},{8,28},{12,24},{16,4},{20,0},{24,12},{28,8},{1,21},{... | collective-permute-start | bytes 196616 | tf_op jit(solution)/shard_map/ppermute | solution.py:291
  686.6 137.3 %collective-permute-start.66 = (bf16[256,2048]{1,0:T(8,128)(2,1)S(1)}, bf16[256,2048]{1,0:T(8,128)(2,1)S(1)}, u32[]{:S(2)}, u32[]{:S(2)}) collective-permute-start(bf16[256,2048]{1,0:T(8,128)(2,1)S(1)} %copy-done.135), channel_id=1, source_target_pairs={{0,4},{4,0},{8,12},{12,8},{16,20},{20,16},{24,28},{28,24},{1,5},{5... | collective-permute-start | bytes 3145736 | tf_op jit(solution)/shard_map/ppermute | solution.py:291
  687.6 79.6 %collective-permute-start.51 = (bf16[256,2048]{1,0:T(8,128)(2,1)S(1)}, bf16[256,2048]{1,0:T(8,128)(2,1)S(1)}, u32[]{:S(2)}, u32[]{:S(2)}) collective-permute-start(bf16[256,2048]{1,0:T(8,128)(2,1)S(1)} %copy-done.140), channel_id=1, source_target_pairs={{0,4},{4,0},{8,12},{12,8},{16,20},{20,16},{24,28},{28,24},{1,5},{5... | collective-permute-start | bytes 3145736 | tf_op jit(solution)/shard_map/ppermute | solution.py:291
  687.8 80.4 %collective-permute-start.61 = (bf16[256,2048]{1,0:T(8,128)(2,1)S(1)}, bf16[256,2048]{1,0:T(8,128)(2,1)S(1)}, u32[]{:S(2)}, u32[]{:S(2)}) collective-permute-start(bf16[256,2048]{1,0:T(8,128)(2,1)S(1)} %copy-done.139), channel_id=1, source_target_pairs={{0,4},{4,0},{8,12},{12,8},{16,20},{20,16},{24,28},{28,24},{1,5},{5... | collective-permute-start | bytes 3145736 | tf_op jit(solution)/shard_map/ppermute | solution.py:291
  688.4 81.0 %collective-permute-start.69 = (bf16[256,2048]{1,0:T(8,128)(2,1)S(1)}, bf16[256,2048]{1,0:T(8,128)(2,1)S(1)}, u32[]{:S(2)}, u32[]{:S(2)}) collective-permute-start(bf16[256,2048]{1,0:T(8,128)(2,1)S(1)} %copy-done.138), channel_id=1, source_target_pairs={{0,4},{4,0},{8,12},{12,8},{16,20},{20,16},{24,28},{28,24},{1,5},{5... | collective-permute-start | bytes 3145736 | tf_op jit(solution)/shard_map/ppermute | solution.py:291
  767.2 33.2 %collective-permute-start.75 = (bf16[256,2048]{1,0:T(8,128)(2,1)S(1)}, bf16[256,2048]{1,0:T(8,128)(2,1)S(1)}, u32[]{:S(2)}, u32[]{:S(2)}) collective-permute-start(bf16[256,2048]{1,0:T(8,128)(2,1)S(1)} %slice.1445), channel_id=1, source_target_pairs={{0,4},{4,0},{8,12},{12,8},{16,20},{20,16},{24,28},{28,24},{1,5},{5... | collective-permute-start | bytes 3145736 | tf_op jit(solution)/shard_map/ppermute | solution.py:291
  769.5 28.2 %collective-permute-start.159 = (f32[720,128]{1,0:T(8,128)S(1)}, f32[720,128]{1,0:T(8,128)S(1)}, u32[]{:S(2)}, u32[]{:S(2)}) collective-permute-start(f32[720,128]{1,0:T(8,128)S(1)} %get-tuple-element.80), channel_id=1, source_target_pairs={{0,2},{1,3},{2,0},{3,1},{4,6},{5,7},{6,4},{7,5},{8,10},{9,11},{10,... | collective-permute-start | bytes 1105928 | tf_op jit(solution)/shard_map/ppermute | solution.py:291
  770.4 27.3 %collective-permute-start.160 = (f32[720,128]{1,0:T(8,128)S(1)}, f32[720,128]{1,0:T(8,128)S(1)}, u32[]{:S(2)}, u32[]{:S(2)}) collective-permute-start(f32[720,128]{1,0:T(8,128)S(1)} %get-tuple-element.79), channel_id=1, source_target_pairs={{0,3},{1,2},{2,1},{3,0},{4,7},{5,6},{6,5},{7,4},{8,11},{9,10},{10,... | collective-permute-start | bytes 1105928 | tf_op jit(solution)/shard_map/ppermute | solution.py:291
  781.9 21.1 %collective-permute-start.57 = (bf16[256,2048]{1,0:T(8,128)(2,1)S(1)}, bf16[256,2048]{1,0:T(8,128)(2,1)S(1)}, u32[]{:S(2)}, u32[]{:S(2)}) collective-permute-start(bf16[256,2048]{1,0:T(8,128)(2,1)S(1)} %slice.1427), channel_id=1, source_target_pairs={{0,4},{4,0},{8,12},{12,8},{16,20},{20,16},{24,28},{28,24},{1,5},{5... | collective-permute-start | bytes 3145736 | tf_op jit(solution)/shard_map/ppermute | solution.py:291
  797.7 39.3 %collective-permute-start.70 = (bf16[128,2048]{1,0:T(8,128)(2,1)S(1)}, bf16[128,2048]{1,0:T(8,128)(2,1)S(1)}, u32[]{:S(2)}, u32[]{:S(2)}) collective-permute-start(bf16[128,2048]{1,0:T(8,128)(2,1)S(1)} %slice.2195), channel_id=1, source_target_pairs={{0,8},{4,12},{8,0},{12,4},{16,24},{20,28},{24,16},{28,20},{1,9},{5... | collective-permute-start | bytes 1572872 | tf_op jit(solution)/shard_map/ppermute | solution.py:291
  797.7 41.1 %collective-permute-start.82 = (bf16[128,2048]{1,0:T(8,128)(2,1)S(1)}, bf16[128,2048]{1,0:T(8,128)(2,1)S(1)}, u32[]{:S(2)}, u32[]{:S(2)}) collective-permute-start(bf16[128,2048]{1,0:T(8,128)(2,1)S(1)} %slice.2194), channel_id=1, source_target_pairs={{0,16},{4,20},{8,24},{12,28},{16,0},{20,4},{24,8},{28,12},{1,17},{... | collective-permute-start | bytes 1572872 | tf_op jit(solution)/shard_map/ppermute | solution.py:291
  800.9 20.6 %collective-permute-start.76 = (bf16[128,2048]{1,0:T(8,128)(2,1)S(1)}, bf16[128,2048]{1,0:T(8,128)(2,1)S(1)}, u32[]{:S(2)}, u32[]{:S(2)}) collective-permute-start(bf16[128,2048]{1,0:T(8,128)(2,1)S(1)} %get-tuple-element.101), channel_id=1, source_target_pairs={{0,16},{4,20},{8,24},{12,28},{16,0},{20,4},{24,8},{28,12},{1,17},{... | collective-permute-start | bytes 1572872 | tf_op jit(solution)/shard_map/ppermute | solution.py:291
  823.9 24.2 %collective-permute-start.77 = (bf16[128,2048]{1,0:T(8,128)(2,1)S(1)}, bf16[128,2048]{1,0:T(8,128)(2,1)S(1)}, u32[]{:S(2)}, u32[]{:S(2)}) collective-permute-start(bf16[128,2048]{1,0:T(8,128)(2,1)S(1)} %fusion.67), channel_id=1, source_target_pairs={{0,8},{4,12},{8,0},{12,4},{16,24},{20,28},{24,16},{28,20},{1,9},{5... | collective-permute-start | bytes 1572872 | tf_op jit(solution)/shard_map/ppermute | solution.py:291
  837.0 22.3 %collective-permute-start.52 = (bf16[128,2048]{1,0:T(8,128)(2,1)S(1)}, bf16[128,2048]{1,0:T(8,128)(2,1)S(1)}, u32[]{:S(2)}, u32[]{:S(2)}) collective-permute-start(bf16[128,2048]{1,0:T(8,128)(2,1)S(1)} %slice.2197), channel_id=1, source_target_pairs={{0,8},{4,12},{8,0},{12,4},{16,24},{20,28},{24,16},{28,20},{1,9},{5... | collective-permute-start | bytes 1572872 | tf_op jit(solution)/shard_map/ppermute | solution.py:291
  1017.3 43.9 %collective-permute-start.114 = (f32[256,128]{1,0:T(8,128)S(1)}, f32[256,128]{1,0:T(8,128)S(1)}, u32[]{:S(2)}, u32[]{:S(2)}) collective-permute-start(f32[256,128]{1,0:T(8,128)S(1)} %get-tuple-element.126), channel_id=1, source_target_pairs={{0,0},{4,8},{8,16},{12,24},{16,4},{20,12},{24,20},{28,28},{1,1},{5... | collective-permute-start | bytes 393224 | tf_op jit(solution)/shard_map/ppermute | solution.py:369
  1019.8 42.0 %collective-permute-start.115 = (f32[256,128]{1,0:T(8,128)S(1)}, f32[256,128]{1,0:T(8,128)S(1)}, u32[]{:S(2)}, u32[]{:S(2)}) collective-permute-start(f32[256,128]{1,0:T(8,128)S(1)} %get-tuple-element.125), channel_id=1, source_target_pairs={{0,8},{4,16},{8,24},{12,0},{16,12},{20,20},{24,28},{28,4},{1,9},{5... | collective-permute-start | bytes 393224 | tf_op jit(solution)/shard_map/ppermute | solution.py:369
  1023.8 38.2 %collective-permute-start.116 = (f32[256,128]{1,0:T(8,128)S(1)}, f32[256,128]{1,0:T(8,128)S(1)}, u32[]{:S(2)}, u32[]{:S(2)}) collective-permute-start(f32[256,128]{1,0:T(8,128)S(1)} %get-tuple-element.124), channel_id=1, source_target_pairs={{0,16},{4,24},{8,0},{12,8},{16,20},{20,28},{24,4},{28,12},{1,17},{... | collective-permute-start | bytes 393224 | tf_op jit(solution)/shard_map/ppermute | solution.py:369
  1023.9 38.7 %collective-permute-start.117 = (f32[256,128]{1,0:T(8,128)S(1)}, f32[256,128]{1,0:T(8,128)S(1)}, u32[]{:S(2)}, u32[]{:S(2)}) collective-permute-start(f32[256,128]{1,0:T(8,128)S(1)} %get-tuple-element.123), channel_id=1, source_target_pairs={{0,24},{4,0},{8,8},{12,16},{16,28},{20,4},{24,12},{28,20},{1,25},{... | collective-permute-start | bytes 393224 | tf_op jit(solution)/shard_map/ppermute | solution.py:369
  1055.1 37.3 %collective-permute-start.90 = (bf16[256,2048]{1,0:T(8,128)(2,1)S(1)}, bf16[256,2048]{1,0:T(8,128)(2,1)S(1)}, u32[]{:S(2)}, u32[]{:S(2)}) collective-permute-start(bf16[256,2048]{1,0:T(8,128)(2,1)S(1)} %slice.1524), channel_id=1, source_target_pairs={{0,4},{4,0},{8,12},{12,8},{16,20},{20,16},{24,28},{28,24},{1,5},{5... | collective-permute-start | bytes 3145736 | tf_op jit(solution)/shard_map/ppermute | solution.py:291
  1063.6 21.4 %collective-permute-start.118 = (f32[512,128]{1,0:T(8,128)S(1)}, f32[512,128]{1,0:T(8,128)S(1)}, u32[]{:S(2)}, u32[]{:S(2)}) collective-permute-start(f32[512,128]{1,0:T(8,128)S(1)} %get-tuple-element.88), channel_id=1, source_target_pairs={{0,1},{1,0},{2,3},{3,2},{4,5},{5,4},{6,7},{7,6},{8,9},{9,8},{10,11... | collective-permute-start | bytes 786440 | tf_op jit(solution)/shard_map/ppermute | solution.py:291
  1086.0 21.6 %collective-permute-start.95 = (bf16[128,2048]{1,0:T(8,128)(2,1)S(1)}, bf16[128,2048]{1,0:T(8,128)(2,1)S(1)}, u32[]{:S(2)}, u32[]{:S(2)}) collective-permute-start(bf16[128,2048]{1,0:T(8,128)(2,1)S(1)} %fusion.63), channel_id=1, source_target_pairs={{0,8},{4,12},{8,0},{12,4},{16,24},{20,28},{24,16},{28,20},{1,9},{5... | collective-permute-start | bytes 1572872 | tf_op jit(solution)/shard_map/ppermute | solution.py:291
  (306 other events, 4228.3 us)

commit v2 on v1

v2 whole, which is shorter than its diff:
```python
import jax
import jax.numpy as jnp
from jax import lax
from jax.sharding import PartitionSpec as P
from jax.experimental import pallas as pl
from jax.experimental.pallas import tpu as pltpu

HEAD = 128
CHUNK = 128
TILE = 512
NN = (((1,), (0,)), ((), ()))
NT = (((1,), (1,)), ((), ()))
TN = (((0,), (0,)), ((), ()))


def mm(left, right, dims=NN):
    return lax.dot_general(left, right, dims, preferred_element_type=jnp.float32)


def halves(values):
    high = values.astype(jnp.bfloat16)
    return high, (values - high.astype(jnp.float32)).astype(jnp.bfloat16)


def mm3(left, right, dims=NN):
    return mm(left[0], right[0], dims) + (mm(left[0], right[1], dims) + mm(left[1], right[0], dims))


def mm2(left, right, dims=NN):
    return mm(left[0], right, dims) + mm(left[1], right, dims)


def mm2r(left, right, dims=NN):
    return mm(left, right[0], dims) + mm(left, right[1], dims)


def sum_with(ones, values):
    high, rest = halves(values)
    mid = (values - high.astype(jnp.float32) - rest.astype(jnp.float32)).astype(jnp.bfloat16)
    return mm(ones, high) + (mm(ones, rest) + mm(ones, mid))


def move_rows(picks, pairs):
    total = pairs[0][0].shape[0]

    @pl.loop(0, total // TILE)
    def _(tile):
        start = pl.multiple_of(tile * TILE, TILE)
        chosen = picks(start, total)
        for source, target in pairs:
            target[pl.ds(start, TILE), :] = mm(chosen, source[...]).astype(jnp.bfloat16)


def picks_natural(order_row_ref):
    def picks(start, total):
        places = lax.broadcasted_iota(jnp.int32, (TILE, total), 0) + start
        return jnp.where(order_row_ref[...] == places, 1.0, 0.0).astype(jnp.bfloat16)

    return picks


def picks_packed(order_column_ref):
    def picks(start, total):
        places = lax.broadcasted_iota(jnp.int32, (TILE, total), 1)
        return jnp.where(order_column_ref[pl.ds(start, TILE), :] == places, 1.0, 0.0).astype(jnp.bfloat16)

    return picks


def segment_terms(ends_ref, start):
    count = ends_ref.shape[0] - 1

    def seg_of(positions):
        return sum((positions >= ends_ref[j]).astype(jnp.int32) for j in range(count))

    rows = lax.broadcasted_iota(jnp.int32, (CHUNK, CHUNK), 0)
    cols = lax.broadcasted_iota(jnp.int32, (CHUNK, CHUNK), 1)
    same = seg_of(rows + start) == seg_of(cols + start)
    wide = seg_of(lax.broadcasted_iota(jnp.int32, (CHUNK, HEAD), 0) + start)
    before = jnp.where(start == 0, -1, seg_of(start - 1))
    last = seg_of(start + CHUNK - 1)
    carry_ok = (wide == before).astype(jnp.float32)
    tail_ok = (wide == last).astype(jnp.float32)
    keep = (last == before).astype(jnp.float32)
    return (rows >= cols) & same, (rows <= cols) & same, carry_ok, tail_ok, keep


def chunk_decays(forget, gap, lower):
    sigma = jax.nn.sigmoid(forget)
    keys = gap * (1.0 - sigma)
    cumulative = sum_with(lower, jnp.log1p(-keys))
    middle = cumulative[CHUNK // 2 - 1 : CHUNK // 2]
    total = cumulative[CHUNK - 1 : CHUNK]
    return sigma, keys, cumulative, middle, total


def lower_ones():
    rows = lax.broadcasted_iota(jnp.int32, (CHUNK, CHUNK), 0)
    cols = lax.broadcasted_iota(jnp.int32, (CHUNK, CHUNK), 1)
    return jnp.where(rows >= cols, 1.0, 0.0).astype(jnp.bfloat16)


VMEM = pl.BlockSpec(memory_space=pltpu.VMEM)
SMEM = pl.BlockSpec(memory_space=pltpu.SMEM)
ANY = pl.BlockSpec(memory_space=pl.ANY)


def params(mebibytes):
    return pltpu.CompilerParams(vmem_limit_bytes=mebibytes * 2**20)


def cost(flops, read):
    return pl.CostEstimate(flops=int(flops), bytes_accessed=int(read), transcendentals=0)


def block_order(count):
    return list(range(0, count, 2)) + list(range(1, count, 2))


def tile_spec(rows, columns):
    return pl.BlockSpec((rows, columns), lambda i: (i, 0))


def row_to_column(row):
    size = row.shape[1]
    eye = lax.broadcasted_iota(jnp.int32, (size, size), 0) == lax.broadcasted_iota(jnp.int32, (size, size), 1)
    return jnp.sum(jnp.where(eye, row, 0.0), axis=1, keepdims=True)


def column_to_row(column):
    size = column.shape[0]
    eye = lax.broadcasted_iota(jnp.int32, (size, size), 0) == lax.broadcasted_iota(jnp.int32, (size, size), 1)
    return jnp.sum(jnp.where(eye, column, 0.0), axis=0, keepdims=True)


def packed_lines(rows_of, width):
    lines = []
    for row in rows_of:
        high, rest = halves(row)
        last = row - high.astype(jnp.float32) - rest.astype(jnp.float32)
        for part in (high.astype(jnp.float32), rest.astype(jnp.float32), last):
            lines += [part[:, i : i + width] for i in range(0, row.shape[1], width)]
    lines.append(jnp.zeros((16 - len(lines), width), jnp.float32))
    return jnp.concatenate(lines, axis=0).astype(jnp.bfloat16)


def unpacked_row(lines, which, each):
    first = 3 * each * which
    return [
        lines[first + i : first + i + 1]
        + lines[first + each + i : first + each + i + 1]
        + lines[first + 2 * each + i : first + 2 * each + i + 1]
        for i in range(each)
    ]


def line_copies(refs, place, target, sem):
    if len(refs) == 1:
        return [(None, pltpu.make_async_copy(refs[0], target(None), sem))]
    count = (len(refs) + 1) // 2
    rising, falling = refs[1:count], refs[count:]
    copies = []
    for step in range(count):
        where = lax.rem(place + step, count)
        if step == 0:
            copies.append((None, pltpu.make_async_copy(refs[0], target(where), sem)))
        else:
            up = place + step < count
            copies.append((up, pltpu.make_async_copy(falling[step - 1], target(where), sem)))
            copies.append((jnp.logical_not(up), pltpu.make_async_copy(rising[count - step - 1], target(where), sem)))
    return copies


def go(copies, what):
    for condition, copy in copies:
        if condition is None:
            getattr(copy, what)()
        else:
            pl.when(condition)(getattr(copy, what))


class Stream:
    def __init__(self, blocks):
        self.pieces = [piece for block in blocks for piece in block]
        self.shapes = [[piece.shape[0] for piece in block] for block in blocks]

    def bind(self, refs, slots, sems):
        self.refs, self.slots, self.sems = refs, slots, sems

    def copies(self, block, slot):
        first = sum(len(shape) for shape in self.shapes[:block])
        result, start = [], 0
        for i, size in enumerate(self.shapes[block]):
            result.append(
                pltpu.make_async_copy(
                    self.refs[first + i], self.slots.at[slot, pl.ds(start, size)], self.sems.at[slot, i]
                )
            )
            start += size
        return result

    def fetch(self, step):
        count = len(self.shapes)

        @pl.when(step == 0)
        def _():
            for copy in self.copies(0, 0):
                copy.start()

        for block in range(count):

            @pl.when(step == block)
            def _(block=block):
                if block + 1 < count:
                    for copy in self.copies(block + 1, (block + 1) % 2):
                        copy.start()
                for copy in self.copies(block, block % 2):
                    copy.wait()

        return self.slots[lax.rem(step, 2)]


def stream_scratch(rows, columns):
    return [pltpu.VMEM((2, rows, columns), jnp.bfloat16), pltpu.SemaphoreType.DMA((2, 2))]


def lower_kernel(stream, wide, *refs):
    mine_ref, refs = refs[0], refs[1:]
    pieces, refs = refs[: len(stream.pieces)], refs[len(stream.pieces) :]
    a_ref, mask_ref, hid_ref, mine_out_ref, slots, sems = refs
    stream.bind(pieces, slots, sems)
    step = pl.program_id(0)
    block = stream.fetch(step)
    lowered = mm(block, a_ref[...])
    mask = mask_ref[...].astype(jnp.float32)
    ranks = mask.shape[1]
    for j in range(lowered.shape[1] // ranks):
        lanes = slice(j * ranks, (j + 1) * ranks)
        hid_ref[:, lanes] = (lowered[:, lanes] * mask).astype(jnp.bfloat16)
    columns = pl.ds(pl.multiple_of(mine_ref[0] * wide, 128), wide)
    mine_out_ref[...] = slots[lax.rem(step, 2), :, columns]


def lower(mine, blocks, a_mat, mask, wide):
    stream = Stream(blocks)
    rows, columns = blocks[0][0].shape
    total = rows * len(blocks)
    ranks = a_mat.shape[1]
    return pl.pallas_call(
        lambda *refs: lower_kernel(stream, wide, *refs),
        grid=(len(blocks),),
        out_shape=(
            jax.ShapeDtypeStruct((total, ranks), jnp.bfloat16),
            jax.ShapeDtypeStruct((total, wide), jnp.bfloat16),
        ),
        in_specs=[SMEM] + [ANY] * len(stream.pieces)
        + [pl.BlockSpec(a_mat.shape, lambda i: (0, 0)), tile_spec(rows, mask.shape[1])],
        out_specs=(tile_spec(rows, ranks), tile_spec(rows, wide)),
        scratch_shapes=stream_scratch(rows, columns),
        compiler_params=params(32),
        cost_estimate=cost(2 * total * columns * ranks, 2 * total * columns),
    )(mine, *stream.pieces, a_mat, mask)


def forward_kernel(stream, win_count, *refs):
    ends_ref, mine_ref, place_ref, refs = refs[0], refs[1], refs[2], refs[3:]
    pieces, refs = refs[: len(stream.pieces)], refs[len(stream.pieces) :]
    win_pieces, refs = refs[:win_count], refs[win_count:]
    (
        order_row_ref, order_column_ref, hid_ref, b_ref, gap_ref, gain_ref,
        sent_ref, win_ref, zq_ref, zg_ref, mixed_ref, query_nat, forget_nat, value_nat, states_ref,
        query_ref, forget_ref, value_ref, out_nat, state_now, slots, sems, win_sem,
    ) = refs
    total, width = mixed_ref.shape
    heads = width // HEAD
    devices = sent_ref.shape[0]
    rows_each = total // devices
    stream.bind(pieces, slots, sems)
    win_copies = line_copies(
        win_pieces,
        place_ref[0],
        lambda w: win_ref if w is None else win_ref.at[pl.ds(pl.multiple_of(w * width, 128), width)],
        win_sem,
    )
    go(win_copies, "start")
    go(win_copies, "wait")

    @pl.loop(0, devices)
    def _(step):
        block = stream.fetch(step)
        rows = pl.ds(pl.multiple_of(step * rows_each, rows_each), rows_each)
        main = mm(block, win_ref[...], NT) + mm(hid_ref[rows, :], b_ref[...], NT)
        zq = main[:, 0:width]
        zq_ref[rows, :] = zq
        query_ref[rows, :] = (zq * jax.nn.sigmoid(zq)).astype(jnp.bfloat16)
        forget_ref[rows, :] = main[:, width : 2 * width].astype(jnp.bfloat16)
        value_ref[rows, :] = main[:, 2 * width : 3 * width].astype(jnp.bfloat16)
        zg_ref[rows, :] = main[:, 3 * width : 4 * width]

    move_rows(
        picks_natural(order_row_ref),
        ((query_ref, query_nat), (forget_ref, forget_nat), (value_ref, value_nat)),
    )
    state_now[...] = jnp.zeros_like(state_now)
    lower = lower_ones()

    @pl.loop(0, total // CHUNK)
    def _(chunk):
        start = pl.multiple_of(chunk * CHUNK, CHUNK)
        rows = pl.ds(start, CHUNK)
        allowed, _, carry_ok, tail_ok, keep = segment_terms(ends_ref, start)
        for head in range(heads):
            lanes = slice(head * HEAD, (head + 1) * HEAD)
            query = query_nat[rows, lanes].astype(jnp.float32)
            value = value_nat[rows, lanes]
            _, keys, cumulative, middle, final = chunk_decays(
                forget_nat[rows, lanes].astype(jnp.float32), gap_ref[:, lanes], lower
            )
            grown = jnp.exp(cumulative - middle)
            shrunk = jnp.exp(middle - cumulative)
            scores = mm3(halves(query * grown), halves(keys * shrunk), NT)
            scores = jnp.where(allowed, scores, 0.0)
            state = state_now[head]
            states_ref[chunk, head] = state
            inter = mm3(halves(query * jnp.exp(cumulative) * carry_ok), halves(state), NT)
            out_nat[rows, lanes] = (mm2(halves(scores), value) + inter).astype(jnp.bfloat16)
            tail = keys * jnp.exp(final - cumulative) * tail_ok
            state_now[head] = state * (jnp.exp(final) * keep) + mm2r(value, halves(tail), TN)

    states_ref[total // CHUNK] = state_now[...]
    move_rows(picks_packed(order_column_ref), ((out_nat, mixed_ref),))

    for place, bits in enumerate(block_order(devices)):
        rows = slice(place * rows_each, (place + 1) * rows_each)
        target = mine_ref[0] ^ bits
        mixed = mixed_ref[rows, :].astype(jnp.float32)
        zg = zg_ref[rows, :]
        raw = mixed * gain_ref[...] * (zg * jax.nn.sigmoid(zg))
        sent_ref[target, 0:rows_each, :] = raw.astype(jnp.bfloat16)
        squares = halves(mixed * mixed)
        ones = jnp.ones((8, width), jnp.bfloat16)
        squares = (mm(ones, squares[0], NT) + mm(ones, squares[1], NT))[0:1]
        sent_ref[target, rows_each : rows_each + 16, :] = packed_lines([squares], width)


def mixer_forward(ends, mine, place, order, blocks, win_pieces, hid_in, in_b_wide, gap, gain):
    stream = Stream(blocks)
    devices = len(blocks)
    rows_each, model = blocks[0][0].shape
    total, width = rows_each * devices, gap.shape[0]
    heads = width // HEAD
    rows = jax.ShapeDtypeStruct((total, width), jnp.bfloat16)
    wide_rows = jax.ShapeDtypeStruct((total, width), jnp.float32)
    states = jax.ShapeDtypeStruct((total // CHUNK + 1, heads, HEAD, HEAD), jnp.float32)
    sent = jax.ShapeDtypeStruct((devices, rows_each + 16, width), jnp.bfloat16)
    win = jax.ShapeDtypeStruct((4 * width, model), jnp.bfloat16)
    return pl.pallas_call(
        lambda *refs: forward_kernel(stream, len(win_pieces), *refs),
        out_shape=(sent, win, wide_rows, wide_rows, rows, rows, rows, rows, states),
        in_specs=[SMEM] * 3 + [ANY] * (len(stream.pieces) + len(win_pieces)) + [VMEM] * 6,
        out_specs=(VMEM,) * 9,
        scratch_shapes=[pltpu.VMEM((total, width), jnp.bfloat16)] * 4
        + [pltpu.VMEM((heads, HEAD, HEAD), jnp.float32)]
        + stream_scratch(rows_each, model)
        + [pltpu.SemaphoreType.DMA(())],
        compiler_params=params(56),
        cost_estimate=cost(2 * total * width * (4 * model + CHUNK * 12 + total * 4), 24 * total * width),
    )(
        ends, mine, place, *stream.pieces, *win_pieces, order.reshape(1, total), order.reshape(total, 1),
        hid_in, in_b_wide, gap.reshape(1, width), gain.reshape(1, width),
    )


def backward_kernel(
    ends_ref, mine_ref, order_row_ref, order_column_ref, came_ref, zq_ref, zg_ref, mixed_ref,
    query_nat, forget_nat, value_nat, states_ref, gap_ref, gain_ref, hid_ref, b_ref, mask_ref, fold_ref,
    g_proj_ref, gated_ref, small_ref, b_rows_ref,
    grad_ref, grad_nat, d_query_nat, d_forget_nat, d_value_nat, slope_now,
):
    total, width = mixed_ref.shape
    heads = width // HEAD
    devices = came_ref.shape[0]
    rows_each = total // devices

    for place, bits in enumerate(block_order(devices)):
        rows = slice(place * rows_each, (place + 1) * rows_each)
        source = mine_ref[0] ^ bits
        d_gated = came_ref[source, 0:rows_each, :].astype(jnp.float32)
        scalars = came_ref[source, rows_each : rows_each + 16, :].astype(jnp.float32)
        factor, mean = [
            jnp.concatenate([row_to_column(row) for row in unpacked_row(scalars, i, rows_each // width)])
            for i in range(2)
        ]
        mixed = mixed_ref[rows, :].astype(jnp.float32)
        zg = zg_ref[rows, :]
        sigma = jax.nn.sigmoid(zg)
        silu = zg * sigma
        gained = mixed * gain_ref[...]
        gated_ref[rows, :] = ((gained * silu).astype(jnp.bfloat16).astype(jnp.float32) * factor).astype(jnp.bfloat16)
        d_zg = d_gated * (gained * factor) * (sigma * (1.0 + zg * (1.0 - sigma)))
        g_proj_ref[rows, 3 * width : 4 * width] = d_zg.astype(jnp.bfloat16)
        scaled = d_gated * gain_ref[...] * silu
        cube = factor * factor * factor
        grad_ref[rows, :] = (factor * scaled - mixed * (cube * mean)).astype(jnp.bfloat16)

    move_rows(picks_natural(order_row_ref), ((grad_ref, grad_nat),))
    slope_now[...] = jnp.zeros_like(slope_now)
    lower = lower_ones()

    @pl.loop(0, total // CHUNK)
    def _(step):
        chunk = total // CHUNK - 1 - step
        start = pl.multiple_of(chunk * CHUNK, CHUNK)
        rows = pl.ds(start, CHUNK)
        allowed, later, carry_ok, tail_ok, keep = segment_terms(ends_ref, start)
        later = jnp.where(later, 1.0, 0.0).astype(jnp.bfloat16)
        for head in range(heads):
            lanes = slice(head * HEAD, (head + 1) * HEAD)
            query = query_nat[rows, lanes].astype(jnp.float32)
            value = value_nat[rows, lanes]
            grad = grad_nat[rows, lanes]
            sigma, keys, cumulative, middle, final = chunk_decays(
                forget_nat[rows, lanes].astype(jnp.float32), gap_ref[:, lanes], lower
            )
            grown = jnp.exp(cumulative - middle)
            shrunk = jnp.exp(middle - cumulative)
            query_grown = halves(query * grown)
            keys_shrunk = halves(keys * shrunk)
            scores = halves(jnp.where(allowed, mm3(query_grown, keys_shrunk, NT), 0.0))
            d_scores = halves(jnp.where(allowed, mm(grad, value, NT), 0.0))
            state = halves(states_ref[chunk, head])
            slope = slope_now[head]
            slope_parts = halves(slope)
            from_start = jnp.exp(cumulative) * carry_ok
            to_end = jnp.exp(final - cumulative) * tail_ok
            d_query = mm3(d_scores, keys_shrunk) * grown + mm2r(grad, state) * from_start
            d_keys = mm3(d_scores, query_grown, TN) * shrunk + mm2r(value, slope_parts) * to_end
            d_value = mm2(scores, grad, TN) + mm3(halves(keys * to_end), slope_parts, NT)
            past = jnp.sum(states_ref[chunk + 1, head] * slope, axis=0, keepdims=True)
            d_logf = sum_with(later, query * d_query - keys * d_keys) + tail_ok * past
            d_keys = d_keys - d_logf / (1.0 - keys)
            slope_now[head] = slope * (jnp.exp(final) * keep) + mm2r(grad, halves(query * from_start), TN)
            d_query_nat[rows, lanes] = d_query.astype(jnp.bfloat16)
            d_forget_nat[rows, lanes] = (-d_keys * keys * sigma).astype(jnp.bfloat16)
            d_value_nat[rows, lanes] = d_value.astype(jnp.bfloat16)

    picks = picks_packed(order_column_ref)

    @pl.loop(0, total // TILE)
    def _(tile):
        start = pl.multiple_of(tile * TILE, TILE)
        rows = pl.ds(start, TILE)
        chosen = picks(start, total)
        zq = zq_ref[rows, :]
        sigma = jax.nn.sigmoid(zq)
        d_query = mm(chosen, d_query_nat[...])
        g_proj_ref[rows, 0:width] = (d_query * (sigma * (1.0 + zq * (1.0 - sigma)))).astype(jnp.bfloat16)
        g_proj_ref[rows, width : 2 * width] = mm(chosen, d_forget_nat[...]).astype(jnp.bfloat16)
        g_proj_ref[rows, 2 * width : 3 * width] = mm(chosen, d_value_nat[...]).astype(jnp.bfloat16)
        mask = mask_ref[rows, :].astype(jnp.float32)
        through = mm(g_proj_ref[rows, :], b_ref[...])
        ranks = mask.shape[1]
        parts = [(through[:, j * ranks : (j + 1) * ranks] * mask).astype(jnp.bfloat16) for j in range(4)]
        small_ref[rows, :] = mm(jnp.concatenate(parts, axis=1), fold_ref[...]).astype(jnp.bfloat16)

    ranks = mask_ref.shape[1]
    for j in range(4):
        b_rows_ref[j * width : (j + 1) * width, :] = mm(
            g_proj_ref[:, j * width : (j + 1) * width], hid_ref[:, j * ranks : (j + 1) * ranks], TN
        )


def mixer_backward(ends, mine, order, came, kept, gap, gain, hid_in, in_b_wide, mask, fold):
    total, width = kept[0].shape
    ranks = mask.shape[1]
    heads = width // HEAD
    rows = jax.ShapeDtypeStruct((total, width), jnp.bfloat16)
    return pl.pallas_call(
        backward_kernel,
        out_shape=(
            jax.ShapeDtypeStruct((total, 4 * width), jnp.bfloat16),
            rows,
            jax.ShapeDtypeStruct((total, ranks), jnp.bfloat16),
            jax.ShapeDtypeStruct((4 * width, ranks), jnp.float32),
        ),
        in_specs=[SMEM] * 2 + [VMEM] * 16,
        out_specs=(VMEM,) * 4,
        scratch_shapes=[pltpu.VMEM((total, width), jnp.bfloat16)] * 5
        + [pltpu.VMEM((heads, HEAD, HEAD), jnp.float32)],
        compiler_params=params(56),
        cost_estimate=cost(2 * total * width * (CHUNK * 60 + total * 4), 30 * total * width),
    )(
        ends, mine, order.reshape(1, total), order.reshape(total, 1), came, *kept,
        gap.reshape(1, width), gain.reshape(1, width), hid_in, in_b_wide, mask, fold,
    )


def spans(blocks):
    result = []
    for index, block in enumerate(blocks):
        start = 0
        for piece in block:
            result.append((index, start, piece.shape[0]))
            start += piece.shape[0]
    return result


def token_forward_kernel(where, count, *refs):
    mine_ref, came_ref, x_ref, a_ref, b_ref, mask_ref, gain_ref = refs[:7]
    weights, refs = refs[7 : 7 + count], refs[7 + count :]
    resid_ref, normed_ref, hid_ref, all_ref, gated_ref, a_mine, sems = refs
    devices = came_ref.shape[0]
    rows, model = x_ref.shape
    width = came_ref.shape[2]
    bits = block_order(devices)
    copies = [
        pltpu.make_async_copy(weights[i], all_ref.at[pl.ds(block * width + start, size)], sems.at[i])
        for i, (block, start, size) in enumerate(where)
    ]
    for copy in copies:
        copy.start()
    squares = jnp.zeros((1, rows), jnp.float32)
    for d in range(devices):
        lines = came_ref[d, rows : rows + 16, :].astype(jnp.float32)
        squares = squares + jnp.concatenate(unpacked_row(lines, 0, rows // width), axis=1)
    factor = lax.rsqrt(row_to_column(squares) / model + eps_norm)
    for place, bit in enumerate(bits):
        source = mine_ref[0] ^ bit
        lanes = slice(place * width, (place + 1) * width)
        raw = came_ref[source, 0:rows, :].astype(jnp.float32)
        gated_ref[:, lanes] = (raw * factor).astype(jnp.bfloat16)
        a_mine[lanes, :] = a_ref[pl.ds(pl.multiple_of(source * width, 128), width), :]
    gated = gated_ref[...]
    hid = (mm(gated, a_mine[...]) * mask_ref[...].astype(jnp.float32)).astype(jnp.bfloat16)
    hid_ref[...] = hid
    extra = mm(hid, b_ref[...], NT)
    for copy in copies:
        copy.wait()
    resid = x_ref[...].astype(jnp.float32) + mm(gated, all_ref[...]) + extra
    resid_ref[...] = resid
    factor = lax.rsqrt(jnp.mean(resid * resid, axis=-1, keepdims=True) + eps_norm)
    normed_ref[...] = (resid * factor * gain_ref[...]).astype(jnp.bfloat16)


def token_forward(mine, came, x, out_a, out_b, mask_own, gain, weights):
    rows, model = x.shape
    where = spans(weights)
    pieces = [piece for block in weights for piece in block]
    ranks = out_a.shape[1]
    return pl.pallas_call(
        lambda *refs: token_forward_kernel(where, len(pieces), *refs),
        out_shape=(
            jax.ShapeDtypeStruct((rows, model), jnp.float32),
            jax.ShapeDtypeStruct((rows, model), jnp.bfloat16),
            jax.ShapeDtypeStruct((rows, ranks), jnp.bfloat16),
        ),
        in_specs=[SMEM] + [VMEM] * 6 + [ANY] * len(pieces),
        out_specs=(VMEM,) * 3,
        scratch_shapes=[
            pltpu.VMEM((model, model), jnp.bfloat16),
            pltpu.VMEM((rows, model), jnp.bfloat16),
            pltpu.VMEM((model, ranks), jnp.bfloat16),
            pltpu.SemaphoreType.DMA((len(pieces),)),
        ],
        compiler_params=params(40),
        cost_estimate=cost(2 * rows * model * model, 2 * model * model),
    )(mine, came, x, out_a, out_b, mask_own, gain.reshape(1, model), *pieces)


def summed(refs):
    own, other, from_x, from_y = refs
    total = own[...].astype(jnp.float32) + other[...].astype(jnp.float32)
    for pieces in (from_x, from_y):
        if pieces:
            total = total + jnp.concatenate([piece[...] for piece in pieces]).astype(jnp.float32)
    return total


def first_block(rows, columns):
    return pl.BlockSpec((rows, columns), lambda i: (0, 0))


def whole(array):
    return pl.BlockSpec(array.shape, lambda i: (0,) * array.ndim)


def token_backward_kernel(where, count, near, nears, *refs):
    mine_ref, came_ref, cot_ref, resid_ref, a_ref, b_ref, mask_ref, gain_ref, hid_ref, own, other = refs[:11]
    refs = refs[11:]
    from_x, from_y, refs = refs[:near], refs[near:nears], refs[nears:]
    weights, refs = refs[:count], refs[count:]
    sent_ref, d_resid_ref, d_hid_ref, b_rows_ref, all_ref, sems = refs
    devices = came_ref.shape[0]
    rows, model = resid_ref.shape
    width = came_ref.shape[2]
    copies = [
        pltpu.make_async_copy(weights[i], all_ref.at[pl.ds(block * width + start, size)], sems.at[i])
        for i, (block, start, size) in enumerate(where)
    ]
    for copy in copies:
        copy.start()
    squares = jnp.zeros((1, rows), jnp.float32)
    for d in range(devices):
        lines = came_ref[d, rows : rows + 16, :].astype(jnp.float32)
        squares = squares + jnp.concatenate(unpacked_row(lines, 0, rows // width), axis=1)
    factor_two = lax.rsqrt(squares / model + eps_norm)

    resid = resid_ref[...]
    factor = lax.rsqrt(jnp.mean(resid * resid, axis=-1, keepdims=True) + eps_norm)
    scaled = summed((own, other, from_x, from_y)) * gain_ref[...]
    mean = jnp.mean(resid * scaled, axis=-1, keepdims=True)
    d_resid = cot_ref[...].astype(jnp.float32) + factor * scaled - resid * (factor * factor * factor * mean)
    d_resid_ref[...] = d_resid
    g_attn = d_resid.astype(jnp.bfloat16)
    d_hid = (mm(g_attn, b_ref[...]) * mask_ref[...].astype(jnp.float32)).astype(jnp.bfloat16)
    d_hid_ref[...] = d_hid
    b_rows_ref[...] = mm(g_attn, hid_ref[...], TN)
    for copy in copies:
        copy.wait()
    total = jnp.zeros((rows, 1), jnp.float32)
    for place, bit in enumerate(block_order(devices)):
        target = mine_ref[0] ^ bit
        block = slice(place * width, (place + 1) * width)
        a_block = a_ref[pl.ds(pl.multiple_of(target * width, 128), width), :]
        d_gated = mm(g_attn, all_ref[block, :], NT) + mm(d_hid, a_block, NT)
        raw = came_ref[target, 0:rows, :].astype(jnp.float32)
        total = total + jnp.sum(raw * d_gated, axis=-1, keepdims=True)
        sent_ref[target, 0:rows, :] = d_gated.astype(jnp.bfloat16)
    lines = packed_lines([factor_two, column_to_row(total / model)], width)
    for d in range(devices):
        sent_ref[d, rows : rows + 16, :] = lines


def token_backward(mine, came, cot, resid, out_a, out_b, mask_own, gain, hid, parts, weights):
    rows, model = resid.shape
    own, other, from_x, from_y = parts
    where = spans(weights)
    pieces = [piece for block in weights for piece in block]
    ranks = out_a.shape[1]
    fixed = [came, cot, resid, out_a, out_b, mask_own, gain.reshape(1, model), hid]
    return pl.pallas_call(
        lambda *refs: token_backward_kernel(where, len(pieces), len(from_x), len(from_x + from_y), *refs),
        grid=(1,),
        out_shape=(
            jax.ShapeDtypeStruct(came.shape, jnp.bfloat16),
            jax.ShapeDtypeStruct((rows, model), jnp.float32),
            jax.ShapeDtypeStruct((rows, ranks), jnp.bfloat16),
            jax.ShapeDtypeStruct((model, ranks), jnp.float32),
        ),
        in_specs=[SMEM] + [whole(array) for array in fixed] + [first_block(rows, model)] * 2
        + [whole(piece) for piece in from_x + from_y] + [ANY] * len(pieces),
        out_specs=(
            pl.BlockSpec(came.shape, lambda i: (0, 0, 0)),
            first_block(rows, model),
            first_block(rows, ranks),
            first_block(model, ranks),
        ),
        scratch_shapes=[
            pltpu.VMEM((model, model), jnp.bfloat16),
            pltpu.SemaphoreType.DMA((len(pieces),)),
        ],
        compiler_params=params(56),
        cost_estimate=cost(2 * rows * model * model, 2 * model * model),
    )(mine, *fixed, own, other, *from_x, *from_y, *pieces)


def token_end_kernel(near, nears, *refs):
    x_ref, d_resid_ref, d_hid_ref, a_ref, gain_ref, own, other = refs[:7]
    refs = refs[7:]
    from_x, from_y, out_ref = refs[:near], refs[near:nears], refs[nears]
    x = x_ref[...].astype(jnp.float32)
    factor = lax.rsqrt(jnp.mean(x * x, axis=-1, keepdims=True) + eps_norm)
    d_normed = summed((own, other, from_x, from_y)) + mm(d_hid_ref[...], a_ref[...], NT)
    scaled = d_normed * gain_ref[...]
    mean = jnp.mean(x * scaled, axis=-1, keepdims=True)
    out = d_resid_ref[...] + factor * scaled - x * (factor * factor * factor * mean)
    out_ref[...] = out.astype(jnp.bfloat16)


def token_end(x, d_resid, d_hid, in_a, gain, parts):
    rows, model = x.shape
    own, other, from_x, from_y = parts
    fixed = [x, d_resid]
    return pl.pallas_call(
        lambda *refs: token_end_kernel(len(from_x), len(from_x + from_y), *refs),
        grid=(1,),
        out_shape=jax.ShapeDtypeStruct((rows, model), jnp.bfloat16),
        in_specs=[whole(x), whole(d_resid), first_block(rows, d_hid.shape[1]), whole(in_a), first_block(1, model)]
        + [first_block(rows, model)] * 2 + [whole(piece) for piece in from_x + from_y],
        out_specs=first_block(rows, model),
        compiler_params=params(40),
        cost_estimate=cost(2 * rows * model * in_a.shape[1], 16 * rows * model),
    )(x, d_resid, d_hid, in_a, gain.reshape(1, model), own, other, *from_x, *from_y)


def ffn_kernel(streams, counts, wt, *refs):
    mine_ref, place_ref, refs = refs[0], refs[1], refs[2:]
    normed_pieces, refs = refs[: len(streams[0].pieces)], refs[len(streams[0].pieces) :]
    cot_pieces, refs = refs[: len(streams[1].pieces)], refs[len(streams[1].pieces) :]
    ffn_pieces, refs = refs[: counts[0]], refs[counts[0] :]
    down_pieces, refs = refs[: counts[1]], refs[counts[1] :]
    (
        mask_ref, ffn_a_ref, b_gate_ref, b_up_ref, down_a_ref, down_b_ref, fold_ref,
        back_ref, down_ref, small_ref, normed_mine_ref, cot_mine_ref, down_a_rows, gate_rows, up_rows,
        w_both, w_down, normed_slots, normed_sems, cot_slots, cot_sems, ffn_sem, down_sem,
    ) = refs
    step = pl.program_id(0)
    streams[0].bind(normed_pieces, normed_slots, normed_sems)
    streams[1].bind(cot_pieces, cot_slots, cot_sems)
    hidden_units, model = w_down.shape
    wide = normed_mine_ref.shape[1]
    ranks = mask_ref.shape[1]
    each, narrow = 2 * hidden_units // wt, model // wt

    @pl.when(step == 0)
    def _():
        ffn = line_copies(
            ffn_pieces,
            place_ref[0],
            lambda w: w_both if w is None else w_both.at[pl.ds(pl.multiple_of(w * each, 16), each)],
            ffn_sem,
        )
        down = line_copies(
            down_pieces,
            place_ref[0],
            lambda w: w_down if w is None else w_down.at[:, pl.ds(pl.multiple_of(w * narrow, 128), narrow)],
            down_sem,
        )
        go(ffn, "start")
        go(down, "start")
        go(ffn, "wait")
        go(down, "wait")
        down_a_rows[...] = jnp.zeros_like(down_a_rows)
        gate_rows[...] = jnp.zeros_like(gate_rows)
        up_rows[...] = jnp.zeros_like(up_rows)

    normed = streams[0].fetch(step)
    cot = streams[1].fetch(step)
    slot = lax.rem(step, 2)
    columns = pl.ds(pl.multiple_of(mine_ref[0] * wide, 128), wide)
    normed_mine_ref[...] = normed_slots[slot, :, columns]
    cot_mine_ref[...] = cot_slots[slot, :, columns]
    mask = mask_ref[...].astype(jnp.float32)
    lowered = mm(normed, ffn_a_ref[...])
    hid_gate = (lowered[:, :ranks] * mask).astype(jnp.bfloat16)
    hid_up = (lowered[:, ranks:] * mask).astype(jnp.bfloat16)
    gate = mm(normed, w_both[0:hidden_units, :], NT) + mm(hid_gate, b_gate_ref[...], NT)
    upper = mm(normed, w_both[hidden_units:, :], NT) + mm(hid_up, b_up_ref[...], NT)
    sigma = jax.nn.sigmoid(gate)
    silu = gate * sigma
    hidden = (silu * upper).astype(jnp.bfloat16)
    d_hid = (mm(cot, down_b_ref[...]) * mask).astype(jnp.bfloat16)
    d_hidden = mm(cot, w_down[...], NT) + mm(d_hid, down_a_ref[...], NT)
    d_gate = (d_hidden * upper * (sigma * (1.0 + gate * (1.0 - sigma)))).astype(jnp.bfloat16)
    d_upper = (d_hidden * silu).astype(jnp.bfloat16)
    through_gate = (mm(d_gate, b_gate_ref[...]) * mask).astype(jnp.bfloat16)
    through_up = (mm(d_upper, b_up_ref[...]) * mask).astype(jnp.bfloat16)
    through = jnp.concatenate([through_gate, through_up], axis=1)
    back = mm(d_gate, w_both[0:hidden_units, :]) + mm(d_upper, w_both[hidden_units:, :])
    back_ref[...] = (back + mm(through, ffn_a_ref[...], NT)).astype(jnp.bfloat16)
    low = (mm(hidden, down_a_ref[...]) * mask).astype(jnp.bfloat16)
    down_ref[...] = (mm(hidden, w_down[...]) + mm(low, down_b_ref[...], NT)).astype(jnp.bfloat16)
    small_ref[...] = mm(jnp.concatenate([low, through], axis=1), fold_ref[...]).astype(jnp.bfloat16)
    down_a_rows[...] += mm(hidden, d_hid, TN)
    gate_rows[...] += mm(d_gate, hid_gate, TN)
    up_rows[...] += mm(d_upper, hid_up, TN)


def feed_forward(mine, place, normed, cot, ffn_pieces, down_pieces, mask, ffn_a, b_gate, b_up, down_a, down_b, fold, wide, wt):
    streams = [Stream(normed), Stream(cot)]
    rows, model = normed[0][0].shape
    blocks = len(normed)
    total = rows * blocks
    hidden_units, ranks = down_a.shape
    fixed = [ffn_a, b_gate, b_up, down_a, down_b, fold]
    grown = jax.ShapeDtypeStruct((total, model), jnp.bfloat16)
    mine_columns = jax.ShapeDtypeStruct((total, wide), jnp.bfloat16)
    term = jax.ShapeDtypeStruct((hidden_units, ranks), jnp.float32)
    return pl.pallas_call(
        lambda *refs: ffn_kernel(streams, (len(ffn_pieces), len(down_pieces)), wt, *refs),
        grid=(blocks,),
        out_shape=(
            grown, grown, jax.ShapeDtypeStruct((total, ranks), jnp.bfloat16), mine_columns, mine_columns,
            term, term, term,
        ),
        in_specs=[SMEM] * 2
        + [ANY] * (len(streams[0].pieces) + len(streams[1].pieces) + len(ffn_pieces) + len(down_pieces))
        + [tile_spec(rows, ranks)]
        + [whole(array) for array in fixed],
        out_specs=(
            tile_spec(rows, model), tile_spec(rows, model), tile_spec(rows, ranks),
            tile_spec(rows, wide), tile_spec(rows, wide),
        ) + (first_block(hidden_units, ranks),) * 3,
        scratch_shapes=[
            pltpu.VMEM((2 * hidden_units, model), jnp.bfloat16),
            pltpu.VMEM((hidden_units, model), jnp.bfloat16),
        ]
        + stream_scratch(rows, model) * 2
        + [pltpu.SemaphoreType.DMA(()), pltpu.SemaphoreType.DMA(())],
        compiler_params=params(58),
        cost_estimate=cost(14 * total * model * hidden_units, 6 * hidden_units * model + 8 * total * model),
    )(
        mine, place, *streams[0].pieces, *streams[1].pieces, *ffn_pieces, *down_pieces, mask, *fixed,
    )


def assemble_kernel(count, *refs):
    place_ref, pieces, out, sem = refs[0], refs[1 : 1 + count], refs[1 + count], refs[2 + count]
    width = pieces[0].shape[1]
    copies = line_copies(
        pieces,
        place_ref[0],
        lambda w: out if w is None else out.at[:, pl.ds(pl.multiple_of(w * width, 128), width)],
        sem,
    )
    go(copies, "start")
    go(copies, "wait")


def assemble(place, pieces, rows, columns):
    return pl.pallas_call(
        lambda *refs: assemble_kernel(len(pieces), *refs),
        out_shape=jax.ShapeDtypeStruct((rows, columns), pieces[0].dtype),
        in_specs=[SMEM] + [ANY] * len(pieces),
        out_specs=VMEM,
        scratch_shapes=[pltpu.SemaphoreType.DMA(())],
        cost_estimate=cost(0, 4 * rows * columns),
    )(place, *pieces)


ADAPTERS = 8
RANK = 16
RANKS = ADAPTERS * RANK
PROJECTIONS = 4
eps_norm = 1e-06
f32 = jnp.float32
bf16 = jnp.bfloat16


def sequence_of(positions, seq_lengths):
    bounds = jnp.cumsum(seq_lengths)[:-1]
    return jnp.sum((positions[:, None] >= bounds[None, :]).astype(jnp.int32), axis=1)


def adapter_of(seq_numbers, seq_ids):
    numbers = jnp.arange(seq_ids.shape[0], dtype=jnp.int32)
    return jnp.sum(
        (seq_numbers[:, None] == numbers[None, :]).astype(jnp.int32) * seq_ids[None, :], axis=1
    )


def adapter_mask(adapter):
    columns = jnp.arange(RANKS, dtype=jnp.int32) // RANK
    return (columns[None, :] == adapter[:, None]).astype(f32)


def norm_factor(values):
    return lax.rsqrt(jnp.mean(values * values, axis=-1, keepdims=True) + eps_norm)


def norm_back(values, factor, gain, grad):
    scaled = grad * gain
    return factor * scaled - values * factor**3 * jnp.mean(values * scaled, axis=-1, keepdims=True)


def silu_slope(values, sigma):
    return sigma * (1.0 + values * (1.0 - sigma))


def relative(blocks, index):
    count, rest = blocks.shape[0], blocks.shape[1:]
    bit = 1
    while bit < count:
        pairs = blocks.reshape((count // (2 * bit), 2, bit) + rest)
        blocks = jnp.where((index & bit) != 0, pairs[:, ::-1], pairs).reshape((count,) + rest)
        bit *= 2
    return blocks


def to_order(blocks, index):
    count = blocks.shape[0]
    blocks = relative(blocks, index)
    pairs = blocks.reshape((count // 2, 2) + blocks.shape[1:])
    return jnp.concatenate([pairs[:, 0], pairs[:, 1]])


def from_order(blocks, index):
    count = blocks.shape[0]
    pairs = jnp.stack([blocks[: count // 2], blocks[count // 2 :]], axis=1)
    return relative(pairs.reshape(blocks.shape), index)


def across(values, bits, axis="seq"):
    size = lax.axis_size(axis)
    return lax.ppermute(values, axis, [(i, i ^ bits) for i in range(size)])


def gather_near(block):
    size = lax.axis_size("seq")
    if size != 8:
        return [[block]] + [[across(block, k)] for k in range(2, size, 2)]
    half = block.shape[0] // 2
    by_x, by_y = across(block, 2), across(block, 4)
    return [[block], [by_x], [by_y], [across(by_x[:half], 4), across(by_y[half:], 2)]]


def other_core(blocks):
    return [[across(piece, 1) for piece in block] for block in blocks]


def scatter_near(near, other):
    size = lax.axis_size("seq")
    rows = near.shape[0] // (size // 2)

    def part(block, start, stop):
        at = slice(block * rows + start, block * rows + stop)
        return near[at].astype(f32) + other[at].astype(f32)

    if size != 8:
        rest = sum([across(part(i, 0, rows).astype(bf16), 2 * i).astype(f32) for i in range(1, size // 2)])
        return near, other, [rest.astype(bf16)], []
    half = rows // 2
    far_x, far_y = [part(3, i * half, (i + 1) * half).astype(bf16) for i in range(2)]
    far_x, far_y = across(far_x, 2), across(far_y, 4)
    by_x, by_y = part(1, 0, half).astype(bf16), part(2, half, rows).astype(bf16)
    by_x, by_y = across(by_x, 2), across(by_y, 4)
    by_x_more = across((part(1, half, rows) + far_y.astype(f32)).astype(bf16), 2)
    by_y_more = across((part(2, 0, half) + far_x.astype(f32)).astype(bf16), 4)
    return near, other, [by_x, by_x_more], [by_y_more, by_y]


def swap(values, axis="seq"):
    return lax.all_to_all(values, axis, split_axis=0, concat_axis=0, tiled=False)


def line_pieces(block):
    count = lax.axis_size("wt")
    rising, falling = [block], [block]
    for step in range(1, count):
        rising.append(
            lax.ppermute(rising[-1], "wt", [(i, i + 1) for i in range(step - 1, count - 1)])
        )
        falling.append(
            lax.ppermute(falling[-1], "wt", [(i, i - 1) for i in range(1, count - step + 1)])
        )
    return [block] + rising[1:] + falling[1:]


def after(values, *others):
    return lax.optimization_barrier((values,) + others)[0]


def to_owner(piece, count):
    size, lines = lax.axis_size("seq"), lax.axis_size("wt")
    each = lines // count
    moves = []
    for s in range(size):
        for q in range(lines):
            whole = (q // each) * size * each + s * each + q % each
            moves.append((s * lines + q, whole))
    return lax.ppermute(piece, ("seq", "wt"), moves)


def fold_columns(count):
    source = jnp.arange(count * RANKS)
    target = jnp.arange(RANKS)
    wanted = (source // RANKS) * RANK + source % RANK
    return (wanted[:, None] == target[None, :]).astype(bf16)


def local(
    tokens,
    cotangent,
    w_in,
    w_out,
    w_ffn,
    w_down,
    gain_mix,
    gain_gate,
    gain_ffn,
    forget_gap,
    in_a,
    in_b,
    out_a,
    out_b,
    ffn_a,
    ffn_b,
    down_a,
    down_b,
    order,
    lengths,
    adapter_ids,
):
    n, wt = lax.axis_size("seq"), lax.axis_size("wt")
    mine = lax.axis_index("seq")
    mine_ref = mine.astype(jnp.int32).reshape(1)
    place_ref = lax.axis_index("wt").astype(jnp.int32).reshape(1)
    x_rows = tokens[0]
    cot_rows = cotangent[0]
    rows, model = x_rows.shape
    total = n * rows
    wide = model // n
    half = total // 2
    units = w_ffn.shape[1] // n
    hidden_units = wt // 2 * units
    on_line = wt == PROJECTIONS and n == 8

    def my_columns(values, extent, axis):
        return lax.dynamic_slice_in_dim(values, mine * extent, extent, axis)

    def my_piece(values, axis):
        return lax.dynamic_index_in_dim(values, mine, axis, False)

    if on_line:
        win_pieces = line_pieces(my_columns(w_in, wide, 1).T)
        w_out = after(w_out, win_pieces[2])
    else:
        spread_in = lax.all_gather(w_in, "wt", axis=1, tiled=True)
        spread_in = my_piece(spread_in.reshape(model, PROJECTIONS, n, wide), 2)
        win_pieces = [jnp.transpose(spread_in, (1, 2, 0)).reshape(PROJECTIONS * wide, model)]

    order_mine = to_order(order[0].reshape(n, rows), mine).reshape(total)
    ends = jnp.cumsum(lengths[0])
    mask = adapter_mask(adapter_of(sequence_of(order_mine, lengths[0]), adapter_ids[0])).astype(bf16)
    mask_own = mask[:rows]
    gap_mine = my_columns(forget_gap, wide, 0)
    gain_mine = my_columns(gain_gate, wide, 0)
    in_b_mine = my_piece(in_b.reshape(PROJECTIONS, n, wide, RANKS), 1)
    in_b_wide = jnp.concatenate(
        [jnp.pad(in_b_mine[j], ((0, 0), (j * RANKS, (PROJECTIONS - 1 - j) * RANKS))) for j in range(PROJECTIONS)]
    )
    fold_in, fold_ffn = fold_columns(PROJECTIONS), fold_columns(3)

    inputs = x_rows.astype(f32)
    normed = (inputs * norm_factor(inputs) * gain_mix).astype(bf16)
    normed_near = gather_near(normed)
    normed_blocks = normed_near + other_core(normed_near)
    hid_in, normed_mine = lower(mine_ref, normed_blocks, in_a, mask, wide)

    cot_near = gather_near(after(cot_rows, normed_near[1][0]))
    cot_other = other_core(cot_near)

    sent, win, *kept = mixer_forward(
        ends, mine_ref, place_ref, order_mine, normed_blocks, win_pieces, hid_in, in_b_wide, gap_mine, gain_mine
    )

    if on_line:
        wout_pieces = line_pieces(my_columns(w_out, wide, 0))
        w_ffn, w_down = after((w_ffn, w_down), wout_pieces[2])
        ffn_pieces = line_pieces(my_columns(w_ffn, units, 1).T)
        w_down = after(w_down, ffn_pieces[2])
        down_pieces = my_piece(w_down.reshape(wt // 2, n, units, -1), 1).reshape(hidden_units, -1)
        down_pieces = line_pieces(down_pieces)
    else:
        wout_pieces = [lax.all_gather(my_columns(w_out, wide, 0), "wt", axis=1, tiled=True)]
        ffn_pieces = [lax.all_gather(my_columns(w_ffn, units, 1).T, "wt", axis=0, tiled=True)]
        down_pieces = my_piece(w_down.reshape(wt // 2, n, units, -1), 1).reshape(hidden_units, -1)
        down_pieces = [lax.all_gather(down_pieces, "wt", axis=1, tiled=True)]
    wout_near = gather_near(assemble(place_ref, wout_pieces, wide, model))
    wout_blocks = wout_near + other_core(wout_near)
    ffn_b_mine = my_piece(ffn_b.reshape(wt, n, units, RANKS), 1)
    b_gate = ffn_b_mine[: wt // 2].reshape(-1, RANKS)
    b_up = ffn_b_mine[wt // 2 :].reshape(-1, RANKS)
    down_a_mine = my_piece(down_a.reshape(wt // 2, n, units, RANKS), 1).reshape(-1, RANKS)

    came = swap(sent)
    resid, normed2, hid_out = token_forward(
        mine_ref, came, x_rows, out_a, out_b, mask_own, gain_ffn, wout_blocks
    )

    normed2_near = gather_near(normed2)
    ffn_args = (ffn_pieces, down_pieces)
    ffn_rest = (ffn_a, b_gate, b_up, down_a_mine, down_b, fold_ffn, wide, wt)
    sides = []
    for blocks, cots, masks in (
        (other_core(normed2_near), cot_other, mask[half:]),
        (normed2_near, cot_near, mask[:half]),
    ):
        sides.append(feed_forward(mine_ref, place_ref, blocks, cots, *ffn_args, masks, *ffn_rest))
    back_far, down_far, small_far, *rest_far = sides[0]
    back, down, small, *rest = sides[1]
    parts = scatter_near(back, across(back_far, 1))
    d_sent, d_resid, d_hid_out, out_b_part = token_backward(
        mine_ref, came, cot_rows, resid, out_a, out_b, mask_own, gain_ffn, hid_out, parts, wout_blocks
    )

    g_proj, gated_heads, small_in, in_b_rows = mixer_backward(
        ends, mine_ref, order_mine, swap(d_sent), kept, gap_mine, gain_mine, hid_in, in_b_wide, mask, fold_in
    )
    back_in_far = across(mm(g_proj[half:], win).astype(bf16), 1)
    back_in = mm(g_proj[:half], win).astype(bf16)
    parts_in = scatter_near(back_in, back_in_far)
    small_in = jnp.sum(swap(from_order(small_in.reshape(n, rows, RANKS), mine)).astype(f32), axis=0).astype(bf16)
    small_in = swap(jnp.broadcast_to(small_in, (n, rows, RANKS)))
    small_in = to_order(small_in, mine).reshape(total, RANKS)
    d_hid_in = (mm(small_in, fold_in, NT) * jnp.tile(mask, (1, PROJECTIONS))).astype(bf16)
    tokens_grad = token_end(x_rows, d_resid, d_hid_in, in_a, gain_mix, parts_in)

    near, other, from_x, from_y = scatter_near(down, across(down_far, 1))
    block_out = resid + near[:rows].astype(f32) + other[:rows].astype(f32)
    for pieces in (from_x, from_y):
        if pieces:
            block_out = block_out + jnp.concatenate(pieces).astype(f32)
    block_out = block_out.astype(bf16)

    small_ffn = jnp.concatenate([small, small_far]).reshape(n, rows, RANKS)
    small_ffn = jnp.sum(swap(from_order(small_ffn, mine)).astype(f32), axis=0).astype(bf16)
    small_ffn = to_order(lax.all_gather(small_ffn, "seq", axis=0), mine).reshape(total, RANKS)
    spread = (mm(small_ffn, fold_ffn, NT) * jnp.tile(mask, (1, 3))).astype(bf16)
    hid_down, d_hid_ffn = spread[:, :RANKS], spread[:, RANKS:]
    normed2_mine, cot_mine = [jnp.concatenate([rest[i], rest_far[i]]) for i in range(2)]
    down_a_rows, gate_rows, up_rows = [rest[i] + rest_far[i] for i in range(2, 5)]
    down_b_rows = mm(cot_mine, hid_down, TN)
    ffn_a_rows = mm(normed2_mine, d_hid_ffn, TN)
    ffn_b_rows = jnp.concatenate([gate_rows, up_rows])
    d_hid_out_all = to_order(lax.all_gather(d_hid_out, "seq", axis=0), mine).reshape(total, RANKS)
    out_a_rows = mm(gated_heads, d_hid_out_all, TN)
    out_b_rows = lax.psum_scatter(out_b_part, "seq", scatter_dimension=0, tiled=True)
    in_a_rows = mm(normed_mine, d_hid_in, TN)

    def reduced(arrays, how):
        packed = [
            jnp.concatenate(
                [
                    array[:, c * RANKS : (c + 1) * RANKS].reshape(wt, -1, RANKS)
                    for c in range(array.shape[1] // RANKS)
                ],
                axis=1,
            )
            for array in arrays
        ]
        summed = how(jnp.concatenate(packed, axis=1))
        results, start = [], 0
        for array in arrays:
            height = array.shape[0] // wt
            count = array.shape[1] // RANKS
            results.append(
                jnp.concatenate(
                    [summed[start + c * height : start + (c + 1) * height] for c in range(count)], axis=1
                )
            )
            start += count * height
        return results

    def by_offload(values):
        return lax.psum_scatter(values, "wt", scatter_dimension=0, tiled=False)

    def by_swap(values):
        return jnp.sum(swap(values, "wt"), axis=0)

    ffn_b_grad, down_a_grad, down_b_grad, ffn_a_grad = reduced(
        [ffn_b_rows, down_a_rows, down_b_rows, ffn_a_rows], by_offload
    )
    out_a_grad, out_b_grad, in_a_grad, in_b_grad = reduced(
        [out_a_rows, out_b_rows, in_a_rows, in_b_rows], by_swap
    )
    return (
        block_out[None],
        tokens_grad[None],
        in_a_grad,
        to_owner(in_b_grad, PROJECTIONS),
        out_a_grad,
        out_b_grad,
        ffn_a_grad,
        to_owner(ffn_b_grad, wt),
        to_owner(down_a_grad, wt // 2),
        down_b_grad,
    )


def solution(mesh):
    placed = (
        P("wt", "seq", None),
        P("wt", "seq", None),
        P(None, "wt"),
        P(None, "wt"),
        P(None, "wt"),
        P(None, "wt"),
        P(),
        P(),
        P(),
        P(),
        P(),
        P(),
        P(),
        P(),
        P(),
        P(),
        P(),
        P(),
        P("wt", None),
        P("wt", None),
        P("wt", None),
    )
    return jax.shard_map(
        local,
        mesh=mesh,
        in_specs=placed,
        out_specs=(
            P("wt", "seq", None),
            P("wt", "seq", None),
            P(("seq", "wt"), None),
            P(("seq", "wt"), None),
            P(("seq", "wt"), None),
            P(("seq", "wt"), None),
            P(("seq", "wt"), None),
            P(("seq", "wt"), None),
            P(("seq", "wt"), None),
            P(("seq", "wt"), None),
        ),
        check_vma=False,
    )
```

time: 1130 us -> 838 us (0.74)
  Pallas kernels: 59.6 us -> 216 us
  local copies, waits for them, and re-layouts: 246 us -> 103 us
  matrix products: 159 us -> 24 us
  waiting for transfers between devices: 364 us -> 265 us
  starting transfers between devices: 205 us -> 123 us
  blocking collectives: 0 us -> 30.7 us
  other arithmetic: 71.8 us -> 44.3 us
    pallas_call x2 -> x9, Pallas kernels: 59.6 us -> 216 us  [the longest x2 86.7 us: feed_forward(): pl.pallas_call(lambda *refs: ffn_kernel(streams, (len(ffn_pieces), len(do...]
    ppermute x127 -> x57, waiting for transfers between devices: 220 us -> 75.1 us  [across(): return lax.ppermute(values, axis, [(i, i ^ bits) for i in range(size)])]
    dot_general x152 -> x8, matrix products: 159 us -> 24 us  [mm(): lax.dot_general(left, right, dims, preferred_element_type=jnp.float32)]
    dynamic_update_slice x17 -> x0, local copies, waits for them, and re-layouts: 108 us -> none  [the longest x3 78.5 us: line_gather(): lax.dynamic_update_index_in_dim(result, piece, (place + step) % count, 0)]
    ppermute x127 -> x57, starting transfers between devices: 117 us -> 37.9 us  [across(): return lax.ppermute(values, axis, [(i, i ^ bits) for i in range(size)])]
    ppermute x34 -> x27, starting transfers between devices: 88.2 us -> 54.9 us  [the longest x12 28.2 us: line_pieces(): lax.ppermute(rising[-1], 'wt', [(i, i + 1) for i in range(step - 1, count...]
    all_gather x0 -> x2, blocking collectives: none -> 30.7 us  [the longest x1 20.7 us: local(): lax.all_gather(d_hid_out, 'seq', axis=0)]
    ppermute x34 -> x27, waiting for transfers between devices: 145 us -> 175 us  [the longest x12 133 us: line_pieces(): lax.ppermute(falling[-1], 'wt', [(i, i - 1) for i in range(1, count - ste...]
  transfers between devices with their start and end apart: 161 -> 92, of which waited for: 59 -> 26; matrix products, arithmetic and copies ran while one was open for 36% -> 16% of each run, Pallas kernels for 2% -> 21%
where the time goes in v2:
time: 838 us; the launch traced here: 823 us
  waiting for transfers between devices  265 us (32%)
  Pallas kernels  216 us (26%)
  starting transfers between devices  123 us (15%)
  local copies, waits for them, and re-layouts  103 us (12%)
  other arithmetic  44.3 us (5%)
  blocking collectives  30.7 us (4%)
  matrix products  24 us (3%)
  between operations  16.2 us (2%)
    ppermute x12, waiting for transfers between devices, line_pieces(): lax.ppermute(falling[-1], 'wt', [(i, i - 1) for i in range(1, count - ste...  133 us
    pallas_call x2, Pallas kernels, feed_forward(): pl.pallas_call(lambda *refs: ffn_kernel(streams, (len(ffn_pieces), len(do...  86.7 us
    ppermute x57, waiting for transfers between devices, across(): return lax.ppermute(values, axis, [(i, i ^ bits) for i in range(size)])  75.1 us
    pallas_call x1, Pallas kernels, mixer_forward(): pl.pallas_call(lambda *refs: forward_kernel(stream, len(win_pieces), *ref...  49.6 us
    unnamed x217, local copies, waits for them, and re-layouts  48.8 us
    pallas_call x1, Pallas kernels, mixer_backward(): pl.pallas_call(backward_kernel, out_shape=(jax.ShapeDtypeStruct((total, 4...  47.9 us
    ppermute x57, starting transfers between devices, across(): return lax.ppermute(values, axis, [(i, i ^ bits) for i in range(size)])  37.9 us
    all_to_all x6, starting transfers between devices, swap(): lax.all_to_all(values, axis, split_axis=0, concat_axis=0, tiled=False)  30 us
  transfers between devices with their start and end apart: 92, of which 26 were waited for; matrix products, arithmetic and copies ran while one was open for 16% of the time, Pallas kernels for 21%

profile of v2, /device:TPU:4, one launch (start us, length us, event | category | flops | bytes accessed | tf_op | source)
XLA Modules:
  0.0 823.1 jit_solution(18313193705701681895)
XLA Ops:
  7.2 2.4 constant_dynamic-slice_fusion.5
  9.6 2.3 copy.78
  11.9 3.7 collective-permute-start.9
  19.3 19.0 %collective-permute-done.9.refs_14_ = bf16[256,2048]{1,0:T(8,128)(2,1)S(1)} collective-permute-done((bf16[256,2048]{1,0:T(8,128)(2,1)}, bf16[256,2048]{1,0:T(8,128)(2,1)S(1)}, u32[]{:S(2)}, u32[]{:S(2)}) %collective-permute-start.9) | collective-permute-done | bytes 1048608 | tf_op jit(solution)/shard_map/ppermute | solution.py:941
  45.0 23.2 %collective-permute-done.12.refs_17_ = bf16[256,2048]{1,0:T(8,128)(2,1)S(1)} collective-permute-done((bf16[256,2048]{1,0:T(8,128)(2,1)S(1)}, bf16[256,2048]{1,0:T(8,128)(2,1)S(1)}, u32[]{:S(2)}, u32[]{:S(2)}) %collective-permute-start.12) | collective-permute-done | bytes 1048608 | tf_op jit(solution)/shard_map/ppermute | solution.py:944
  68.2 3.6 collective-permute-start.15
  73.3 2.5 collective-permute-done.15.refs_2_
  76.4 3.7 collective-permute-done.18.refs_5_
  88.0 2.9 collective-permute-done.19.refs_6_
  92.8 29.2 %collective-permute-done.20.refs_7_ = bf16[256,512]{1,0:T(8,128)(2,1)} collective-permute-done((bf16[256,512]{1,0:T(8,128)(2,1)S(1)}, bf16[256,512]{1,0:T(8,128)(2,1)}, u32[]{:S(2)}, u32[]{:S(2)}) %collective-permute-start.20) | collective-permute-done | bytes 262176 | tf_op jit(solution)/shard_map/ppermute | solution.py:944
  122.8 2.2 shard_map.278.refs_7_.refs_15_
  129.9 15.1 %copy.64 = bf16[2048,2816]{0,1:T(8,128)(2,1)} copy(bf16[2048,2816]{1,0:T(8,128)(2,1)} %param.25) | data formatting | bytes 23068672 | tf_op jit(solution)/shard_map/optimization_barrier | solution.py:950
  146.7 2.6 dynamic-slice_bitcast_fusion.refs_12_
  149.3 2.5 collective-permute-start.38
  154.0 26.3 %collective-permute-done.36.refs_10_ = bf16[128,2048]{1,0:T(8,128)(2,1)} collective-permute-done((bf16[128,2048]{1,0:T(8,128)(2,1)S(1)}, bf16[128,2048]{1,0:T(8,128)(2,1)}, u32[]{:S(2)}, u32[]{:S(2)}) %collective-permute-start.36) | collective-permute-done | bytes 524320 | tf_op jit(solution)/shard_map/ppermute | solution.py:895
  184.6 2.0 slice.390
  186.7 1.9 slice.391
  188.6 3.8 collective-permute-done.37.refs_11_
  208.3 7.2 shard_map.276
  220.2 49.6 %shard_map.277 = (bf16[8,272,256]{2,1,0:T(8,128)(2,1)}, bf16[1024,2048]{1,0:T(8,128)(2,1)}, f32[2048,256]{1,0:T(8,128)}, f32[2048,256]{1,0:T(8,128)}, bf16[2048,...) custom-call(s32[4]{0:T(128)} %bitcast.226, ...), custom_call_target="tpu_custom_call" | custom-call | flops 18790481920 | bytes 12582912 | tf_op jit(solution)/shard_map/pallas_call | solution.py:357
  269.8 5.4 all-to-all-start
  278.5 11.3 %all-to-all-done.refs_1_ = bf16[8,272,256]{2,1,0:T(8,128)(2,1)S(1)} async-done(((bf16[8,272,256]{2,1,0:T(8,128)(2,1)}), bf16[8,272,256]{2,1,0:T(8,128)(2,1)S(1)}, u32[]{:S(2)}, u32[]{:S(2)}) %all-to-all-start) | async-done | bytes 1114144 | tf_op jit(solution)/shard_map/all_to_all | solution.py:933
  291.2 7.8 shard_map.279
  304.4 10.1 %collective-permute-start.44 = (bf16[704,512]{1,0:T(8,128)(2,1)S(1)}, bf16[704,512]{1,0:T(8,128)(2,1)S(1)}, u32[]{:S(2)}, u32[]{:S(2)}) collective-permute-start(bf16[704,512]{1,0:T(8,128)(2,1)S(1)} %bitcast.186), channel_id=1, source_target_pairs={{0,1},{1,2},{2,3},{4,5},{5,6},{6,7},{8,9},{9,10},{10,11},{12,13},{... | collective-permute-start | bytes 2162696 | tf_op jit(solution)/shard_map/ppermute | solution.py:941
  314.5 8.3 %collective-permute-done.30.refs_3_ = bf16[256,2048]{1,0:T(8,128)(2,1)S(1)} collective-permute-done((bf16[256,2048]{1,0:T(8,128)(2,1)S(1)}, bf16[256,2048]{1,0:T(8,128)(2,1)S(1)}, u32[]{:S(2)}, u32[]{:S(2)}) %collective-permute-start.30) | collective-permute-done | bytes 1048608 | tf_op jit(solution)/shard_map/ppermute | solution.py:895
  323.6 2.1 collective-permute-done.31.refs_4_
  327.0 9.9 %collective-permute-done.42.refs_17_ = bf16[352,2048]{1,0:T(8,128)(2,1)S(1)} collective-permute-done((bf16[352,2048]{1,0:T(8,128)(2,1)}, bf16[352,2048]{1,0:T(8,128)(2,1)S(1)}, u32[]{:S(2)}, u32[]{:S(2)}) %collective-permute-start.42) | collective-permute-done | bytes 1441824 | tf_op jit(solution)/shard_map/ppermute | solution.py:944
  341.2 11.2 %collective-permute-done.47.refs_23_ = bf16[704,512]{1,0:T(8,128)(2,1)S(1)} collective-permute-done((bf16[704,512]{1,0:T(8,128)(2,1)S(1)}, bf16[704,512]{1,0:T(8,128)(2,1)S(1)}, u32[]{:S(2)}, u32[]{:S(2)}) %collective-permute-start.47) | collective-permute-done | bytes 720928 | tf_op jit(solution)/shard_map/ppermute | solution.py:944
  355.7 41.8 %collective-permute-done.48.refs_24_ = bf16[704,512]{1,0:T(8,128)(2,1)S(1)} collective-permute-done((bf16[704,512]{1,0:T(8,128)(2,1)S(1)}, bf16[704,512]{1,0:T(8,128)(2,1)S(1)}, u32[]{:S(2)}, u32[]{:S(2)}) %collective-permute-start.48) | collective-permute-done | bytes 720928 | tf_op jit(solution)/shard_map/ppermute | solution.py:944
  404.9 11.4 %collective-permute-done.49.refs_25_ = bf16[704,512]{1,0:T(8,128)(2,1)S(1)} collective-permute-done((bf16[704,512]{1,0:T(8,128)(2,1)S(1)}, bf16[704,512]{1,0:T(8,128)(2,1)S(1)}, u32[]{:S(2)}, u32[]{:S(2)}) %collective-permute-start.49) | collective-permute-done | bytes 720928 | tf_op jit(solution)/shard_map/ppermute | solution.py:944
  417.1 43.2 %shard_map.281 = (bf16[1024,2048]{1,0:T(8,128)(2,1)}, bf16[1024,2048]{1,0:T(8,128)(2,1)}, bf16[1024,128]{1,0:T(8,128)(2,1)}, bf16[1024,256]{1,0:T(8,128)(2,1)}, ...) custom-call(s32[1]{0:T(128)} %bitcast.refs_0_.refs_1_.mine_ref, ...), custom_call_target="tpu_custom_call" | custom-call | flops 20669530112 | bytes 25427968 | tf_op jit(solution)/shard_map/pallas_call | solution.py:779
  461.3 2.1 tile.5
  463.4 3.5 copy.76
  467.7 43.5 %shard_map.280 = (bf16[1024,2048]{1,0:T(8,128)(2,1)}, bf16[1024,2048]{1,0:T(8,128)(2,1)}, bf16[1024,128]{1,0:T(8,128)(2,1)}, bf16[1024,256]{1,0:T(8,128)(2,1)}, ...) custom-call(s32[1]{0:T(128)} %bitcast.refs_0_.refs_1_.mine_ref, ...), custom_call_target="tpu_custom_call" | custom-call | flops 20669530112 | bytes 25427968 | tf_op jit(solution)/shard_map/pallas_call | solution.py:779
  513.5 6.2 all-to-all-start.5
  523.6 4.4 all-to-all-done.5
  529.1 10.0 %all-gather.1 = bf16[2048,128]{1,0:T(8,128)(2,1)S(1)} all-gather(bf16[256,128]{1,0:T(8,128)(2,1)S(1)} %reduce_sum.65), channel_id=3, replica_groups=mesh['seq'=8,'wt'=4] {'seq'}, dimensions={0}, use_global_device_ids=true | all-gather | bytes 589824 | tf_op jit(solution)/shard_map/all_gather | solution.py:1108
  541.1 3.2 add_convert_fusion.7
  548.4 6.9 collective-permute-done.64
  555.3 3.3 add_convert_fusion.14
  559.1 18.1 %collective-permute-done.71 = bf16[128,2048]{1,0:T(8,128)(2,1)S(1)} collective-permute-done((bf16[128,2048]{1,0:T(8,128)(2,1)S(1)}, bf16[128,2048]{1,0:T(8,128)(2,1)S(1)}, u32[]{:S(2)}, u32[]{:S(2)}) %collective-permute-start.71) | collective-permute-done | bytes 524320 | tf_op jit(solution)/shard_map/ppermute | solution.py:895
  577.2 2.1 add_convert_fusion.8
  584.1 2.1 add_convert_fusion.16
  588.2 6.0 collective-permute-done.70.refs_12_
  595.5 11.1 %shard_map.282 = (bf16[8,272,256]{2,1,0:T(8,128)(2,1)}, f32[256,2048]{1,0:T(8,128)}, bf16[256,128]{1,0:T(8,128)(2,1)}, f32[2048,128]{1,0:T(8,128)}) custom-call(s32[1]{0:T(128)} %bitcast.refs_0_.refs_1_.mine_ref, bf16[8,272,256]{2,1,0:T(8,128)(2,1)} %copy-done.4, bf16[256,2048]{1,0:T(8,128)(2,1)} %bitcast.18.refs_7_.refs_2_, ...), custom_call_target="tpu_custom_call" | custom-call | flops 2147483648 | bytes 8388608 | tf_op jit(solution)/shard_map/pallas_call | solution.py:641
  606.7 5.8 all-to-all-start.1
  612.4 20.7 %all-gather = bf16[2048,128]{1,0:T(8,128)(2,1)S(1)} all-gather(bf16[256,128]{1,0:T(8,128)(2,1)S(1)} %copy-done.67), channel_id=2, replica_groups=mesh['seq'=8,'wt'=4] {'seq'}, dimensions={0}, use_global_device_ids=true | all-gather | bytes 589824 | tf_op jit(solution)/shard_map/all_gather | solution.py:1116
  642.3 47.9 %shard_map.283 = (bf16[2048,1024]{1,0:T(8,128)(2,1)}, bf16[2048,256]{1,0:T(8,128)(2,1)}, bf16[2048,128]{1,0:T(8,128)(2,1)}, f32[1024,128]{1,0:T(8,128)}) custom-call(s32[4]{0:T(128)} %bitcast.227, s32[1]{0:T(128)} %bitcast.refs_0_.refs_1_.mine_ref, s32[1,2048]{1,0:T(1,128)} %bitcast.212, s32[2048,1]{1,0:T(8,128)} %bitcast.179, ...), custom_call_target="tpu_custom_call" | custom-call | flops 16642998272 | bytes 15728640 | tf_op jit(solution)/shard_map/pallas_call | solution.py:478
  692.5 4.0 all-to-all-start.2
  696.7 9.4 %convolution_convert_fusion = bf16[1024,2048]{1,0:T(8,128)(2,1)} fusion(bf16[1024,2048]{1,0:T(8,128)(2,1)} %get-tuple-element.78, bf16[2048,1024]{1,0:T(8,128)(2,1)} %get-tuple-element.77), kind=kOutput, calls=%fused_computation.2 | convolution fusion | flops 4297064448 | bytes 10485760 | tf_op jit(solution)/shard_map/dot_general | solution.py:17
  708.8 4.4 all-to-all-start.3
  713.2 9.3 %convolution_convert_fusion.1.refs_5_ = bf16[1024,2048]{1,0:T(8,128)(2,1)} fusion(bf16[1024,2048]{1,0:T(8,128)(2,1)} %get-tuple-element.78, bf16[2048,1024]{1,0:T(8,128)(2,1)} %get-tuple-element.77), kind=kOutput, calls=%fused_computation.3 | convolution fusion | flops 4297064448 | bytes 10485760 | tf_op jit(solution)/shard_map/dot_general | solution.py:17
  724.0 2.1 convolution_dynamic-update-slice_fusion
  735.9 4.3 all-to-all-start.4
  740.2 4.2 add_convert_fusion.1
  746.5 4.1 fusion.15
  751.5 2.6 collective-permute-start.82
  755.0 6.7 collective-permute-start.83
  763.0 3.4 add_convert_fusion.2
  767.3 14.4 %collective-permute-done.83 = f32[176,128]{1,0:T(8,128)S(1)} collective-permute-done((f32[176,128]{1,0:T(8,128)S(1)}, f32[176,128]{1,0:T(8,128)S(1)}, u32[]{:S(2)}, u32[]{:S(2)}) %collective-permute-start.83) | collective-permute-done | bytes 90144 | tf_op jit(solution)/shard_map/ppermute | solution.py:961
  785.8 1.9 collective-permute-start.81
  789.0 5.5 collective-permute-done.81
  797.8 2.2 copy-done.3
  808.9 3.9 shard_map.284
  (459 shorter events, 159.6 us)
Async XLA Ops:
  11.9 26.3 %collective-permute-start.9 = (bf16[256,2048]{1,0:T(8,128)(2,1)}, bf16[256,2048]{1,0:T(8,128)(2,1)S(1)}, u32[]{:S(2)}, u32[]{:S(2)}) collective-permute-start(bf16[256,2048]{1,0:T(8,128)(2,1)} %bitcast.180), channel_id=1, source_target_pairs={{0,1},{1,2},{2,3},{4,5},{5,6},{6,7},{8,9},{9,10},{10,11},{12,13},{... | collective-permute-start | bytes 3145736 | tf_op jit(solution)/shard_map/ppermute | solution.py:941
  16.3 24.7 %collective-permute-start = (bf16[256,2048]{1,0:T(8,128)(2,1)S(1)}, bf16[256,2048]{1,0:T(8,128)(2,1)S(1)}, u32[]{:S(2)}, u32[]{:S(2)}) collective-permute-start(bf16[256,2048]{1,0:T(8,128)(2,1)S(1)} %fusion.3.refs_1_.refs_3_), channel_id=1, source_target_pairs={{0,8},{4,12},{8,0},{12,4},{16,24},{20,28},{24,16},{28,20},{1,9},{5... | collective-permute-start | bytes 3145736 | tf_op jit(solution)/shard_map/ppermute | solution.py:895
  17.8 24.4 %collective-permute-start.1 = (bf16[256,2048]{1,0:T(8,128)(2,1)S(1)}, bf16[256,2048]{1,0:T(8,128)(2,1)}, u32[]{:S(2)}, u32[]{:S(2)}) collective-permute-start(bf16[256,2048]{1,0:T(8,128)(2,1)S(1)} %fusion.3.refs_1_.refs_3_), channel_id=1, source_target_pairs={{0,16},{4,20},{8,24},{12,28},{16,0},{20,4},{24,8},{28,12},{1,17},{... | collective-permute-start | bytes 3145736 | tf_op jit(solution)/shard_map/ppermute | solution.py:895
  18.3 24.4 %collective-permute-start.4 = (bf16[256,2048]{1,0:T(8,128)(2,1)S(1)}, bf16[256,2048]{1,0:T(8,128)(2,1)S(1)}, u32[]{:S(2)}, u32[]{:S(2)}) collective-permute-start(bf16[256,2048]{1,0:T(8,128)(2,1)S(1)} %fusion.3.refs_1_.refs_3_), channel_id=1, source_target_pairs={{0,4},{4,0},{8,12},{12,8},{16,20},{20,16},{24,28},{28,24},{1,5},{5... | collective-permute-start | bytes 3145736 | tf_op jit(solution)/shard_map/ppermute | solution.py:895
  39.0 29.2 %collective-permute-start.12 = (bf16[256,2048]{1,0:T(8,128)(2,1)S(1)}, bf16[256,2048]{1,0:T(8,128)(2,1)S(1)}, u32[]{:S(2)}, u32[]{:S(2)}) collective-permute-start(bf16[256,2048]{1,0:T(8,128)(2,1)S(1)} %bitcast.182), channel_id=1, source_target_pairs={{1,0},{2,1},{3,2},{5,4},{6,5},{7,6},{9,8},{10,9},{11,10},{13,12},{... | collective-permute-start | bytes 3145736 | tf_op jit(solution)/shard_map/ppermute | solution.py:944
  40.9 40.5 %collective-permute-start.5 = (bf16[256,2048]{1,0:T(8,128)(2,1)S(1)}, bf16[256,2048]{1,0:T(8,128)(2,1)S(1)}, u32[]{:S(2)}, u32[]{:S(2)}) collective-permute-start(bf16[256,2048]{1,0:T(8,128)(2,1)S(1)} %collective-permute-done.refs_2_.refs_4_), channel_id=1, source_target_pairs={{0,4},{4,0},{8,12},{12,8},{16,20},{20,16},{24,28},{28,24},{1,5},{5... | collective-permute-start | bytes 3145736 | tf_op jit(solution)/shard_map/ppermute | solution.py:895
  42.3 29.6 %collective-permute-start.2 = (bf16[128,2048]{1,0:T(8,128)(2,1)S(1)}, bf16[128,2048]{1,0:T(8,128)(2,1)}, u32[]{:S(2)}, u32[]{:S(2)}) collective-permute-start(bf16[128,2048]{1,0:T(8,128)(2,1)S(1)} %slice.385), channel_id=1, source_target_pairs={{0,16},{4,20},{8,24},{12,28},{16,0},{20,4},{24,8},{28,12},{1,17},{... | collective-permute-start | bytes 1572872 | tf_op jit(solution)/shard_map/ppermute | solution.py:895
  42.8 43.9 %collective-permute-start.6 = (bf16[256,2048]{1,0:T(8,128)(2,1)}, bf16[256,2048]{1,0:T(8,128)(2,1)}, u32[]{:S(2)}, u32[]{:S(2)}) collective-permute-start(bf16[256,2048]{1,0:T(8,128)(2,1)} %collective-permute-done.1.refs_3_.refs_5_), channel_id=1, source_target_pairs={{0,4},{4,0},{8,12},{12,8},{16,20},{20,16},{24,28},{28,24},{1,5},{5... | collective-permute-start | bytes 3145736 | tf_op jit(solution)/shard_map/ppermute | solution.py:895
  44.3 28.9 %collective-permute-start.3 = (bf16[128,2048]{1,0:T(8,128)(2,1)S(1)}, bf16[128,2048]{1,0:T(8,128)(2,1)}, u32[]{:S(2)}, u32[]{:S(2)}) collective-permute-start(bf16[128,2048]{1,0:T(8,128)(2,1)S(1)} %slice.386), channel_id=1, source_target_pairs={{0,8},{4,12},{8,0},{12,4},{16,24},{20,28},{24,16},{28,20},{1,9},{5... | collective-permute-start | bytes 1572872 | tf_op jit(solution)/shard_map/ppermute | solution.py:895
  82.4 44.2 %collective-permute-start.34 = (bf16[256,2048]{1,0:T(8,128)(2,1)}, bf16[256,2048]{1,0:T(8,128)(2,1)}, u32[]{:S(2)}, u32[]{:S(2)}) collective-permute-start(bf16[256,2048]{1,0:T(8,128)(2,1)} %bitcast.18.refs_7_.refs_2_), channel_id=1, source_target_pairs={{0,8},{4,12},{8,0},{12,4},{16,24},{20,28},{24,16},{28,20},{1,9},{5... | collective-permute-start | bytes 3145736 | tf_op jit(solution)/shard_map/ppermute | solution.py:895
  86.7 42.6 %collective-permute-start.13 = (bf16[256,2048]{1,0:T(8,128)(2,1)}, bf16[256,2048]{1,0:T(8,128)(2,1)}, u32[]{:S(2)}, u32[]{:S(2)}) collective-permute-start(bf16[256,2048]{1,0:T(8,128)(2,1)} %copy-done.76), channel_id=1, source_target_pairs={{1,0},{2,1},{5,4},{6,5},{9,8},{10,9},{13,12},{14,13},{17,16},{18,1... | collective-permute-start | bytes 3145736 | tf_op jit(solution)/shard_map/ppermute | solution.py:944
  90.9 31.2 %collective-permute-start.20 = (bf16[256,512]{1,0:T(8,128)(2,1)S(1)}, bf16[256,512]{1,0:T(8,128)(2,1)}, u32[]{:S(2)}, u32[]{:S(2)}) collective-permute-start(bf16[256,512]{1,0:T(8,128)(2,1)S(1)} %collective-permute-done.19.refs_6_), channel_id=1, source_target_pairs={{1,0},{5,4},{9,8},{13,12},{17,16},{21,20},{25,24},{29,28}} | collective-permute-start | bytes 786440 | tf_op jit(solution)/shard_map/ppermute | solution.py:944
  92.2 52.8 %collective-permute-start.55 = (bf16[256,2048]{1,0:T(8,128)(2,1)}, bf16[256,2048]{1,0:T(8,128)(2,1)}, u32[]{:S(2)}, u32[]{:S(2)}) collective-permute-start(bf16[256,2048]{1,0:T(8,128)(2,1)} %bitcast.18.refs_7_.refs_2_), channel_id=1, source_target_pairs={{0,4},{4,0},{8,12},{12,8},{16,20},{20,16},{24,28},{28,24},{1,5},{5... | collective-permute-start | bytes 3145736 | tf_op jit(solution)/shard_map/ppermute | solution.py:895
  92.3 32.8 %collective-permute-start.8 = (bf16[128,2048]{1,0:T(8,128)(2,1)}, bf16[128,2048]{1,0:T(8,128)(2,1)S(1)}, u32[]{:S(2)}, u32[]{:S(2)}) collective-permute-start(bf16[128,2048]{1,0:T(8,128)(2,1)} %collective-permute-done.3.refs_5_.refs_7_), channel_id=1, source_target_pairs={{0,4},{4,0},{8,12},{12,8},{16,20},{20,16},{24,28},{28,24},{1,5},{5... | collective-permute-start | bytes 1572872 | tf_op jit(solution)/shard_map/ppermute | solution.py:895
  122.0 27.3 %collective-permute-start.35 = (bf16[256,2048]{1,0:T(8,128)(2,1)}, bf16[256,2048]{1,0:T(8,128)(2,1)}, u32[]{:S(2)}, u32[]{:S(2)}) collective-permute-start(bf16[256,2048]{1,0:T(8,128)(2,1)} %bitcast.18.refs_7_.refs_2_), channel_id=1, source_target_pairs={{0,16},{4,20},{8,24},{12,28},{16,0},{20,4},{24,8},{28,12},{1,17},{... | collective-permute-start | bytes 3145736 | tf_op jit(solution)/shard_map/ppermute | solution.py:895
  125.1 56.7 %collective-permute-start.21 = (bf16[256,2048]{1,0:T(8,128)(2,1)}, bf16[256,2048]{1,0:T(8,128)(2,1)}, u32[]{:S(2)}, u32[]{:S(2)}) collective-permute-start(bf16[256,2048]{1,0:T(8,128)(2,1)} %shard_map.278.refs_7_.refs_15_), channel_id=1, source_target_pairs={{0,8},{4,12},{8,0},{12,4},{16,24},{20,28},{24,16},{28,20},{1,9},{5... | collective-permute-start | bytes 3145736 | tf_op jit(solution)/shard_map/ppermute | solution.py:895
  126.6 56.4 %collective-permute-start.22 = (bf16[256,2048]{1,0:T(8,128)(2,1)}, bf16[256,2048]{1,0:T(8,128)(2,1)}, u32[]{:S(2)}, u32[]{:S(2)}) collective-permute-start(bf16[256,2048]{1,0:T(8,128)(2,1)} %shard_map.278.refs_7_.refs_15_), channel_id=1, source_target_pairs={{0,16},{4,20},{8,24},{12,28},{16,0},{20,4},{24,8},{28,12},{1,17},{... | collective-permute-start | bytes 3145736 | tf_op jit(solution)/shard_map/ppermute | solution.py:895
  129.3 51.0 %collective-permute-start.36 = (bf16[128,2048]{1,0:T(8,128)(2,1)S(1)}, bf16[128,2048]{1,0:T(8,128)(2,1)}, u32[]{:S(2)}, u32[]{:S(2)}) collective-permute-start(bf16[128,2048]{1,0:T(8,128)(2,1)S(1)} %slice.394), channel_id=1, source_target_pairs={{0,16},{4,20},{8,24},{12,28},{16,0},{20,4},{24,8},{28,12},{1,17},{... | collective-permute-start | bytes 1572872 | tf_op jit(solution)/shard_map/ppermute | solution.py:895
  145.0 48.6 %collective-permute-start.11 = (bf16[256,2048]{1,0:T(8,128)(2,1)}, bf16[256,2048]{1,0:T(8,128)(2,1)}, u32[]{:S(2)}, u32[]{:S(2)}) collective-permute-start(bf16[256,2048]{1,0:T(8,128)(2,1)} %copy-done.75), channel_id=1, source_target_pairs={{2,3},{6,7},{10,11},{14,15},{18,19},{22,23},{26,27},{30,31}} | collective-permute-start | bytes 3145736 | tf_op jit(solution)/shard_map/ppermute | solution.py:941
  149.3 69.8 %collective-permute-start.38 = (bf16[352,2048]{1,0:T(8,128)(2,1)}, bf16[352,2048]{1,0:T(8,128)(2,1)}, u32[]{:S(2)}, u32[]{:S(2)}) collective-permute-start(bf16[352,2048]{1,0:T(8,128)(2,1)} %dynamic-slice_bitcast_fusion.refs_12_), channel_id=1, source_target_pairs={{0,1},{1,2},{2,3},{4,5},{5,6},{6,7},{8,9},{9,10},{10,11},{12,13},{... | collective-permute-start | bytes 4325384 | tf_op jit(solution)/shard_map/ppermute | solution.py:941
  181.8 36.0 %collective-permute-start.14 = (bf16[256,2048]{1,0:T(8,128)(2,1)}, bf16[256,2048]{1,0:T(8,128)(2,1)}, u32[]{:S(2)}, u32[]{:S(2)}) collective-permute-start(bf16[256,2048]{1,0:T(8,128)(2,1)} %collective-permute-done.13.refs_18_), channel_id=1, source_target_pairs={{1,0},{5,4},{9,8},{13,12},{17,16},{21,20},{25,24},{29,28}} | collective-permute-start | bytes 3145736 | tf_op jit(solution)/shard_map/ppermute | solution.py:944
  183.1 36.0 %collective-permute-start.25 = (bf16[256,2048]{1,0:T(8,128)(2,1)}, bf16[256,2048]{1,0:T(8,128)(2,1)}, u32[]{:S(2)}, u32[]{:S(2)}) collective-permute-start(bf16[256,2048]{1,0:T(8,128)(2,1)} %shard_map.278.refs_7_.refs_15_), channel_id=1, source_target_pairs={{0,4},{4,0},{8,12},{12,8},{16,20},{20,16},{24,28},{28,24},{1,5},{5... | collective-permute-start | bytes 3145736 | tf_op jit(solution)/shard_map/ppermute | solution.py:895
  193.1 26.5 %collective-permute-start.23 = (bf16[128,2048]{1,0:T(8,128)(2,1)}, bf16[128,2048]{1,0:T(8,128)(2,1)}, u32[]{:S(2)}, u32[]{:S(2)}) collective-permute-start(bf16[128,2048]{1,0:T(8,128)(2,1)} %slice.390), channel_id=1, source_target_pairs={{0,16},{4,20},{8,24},{12,28},{16,0},{20,4},{24,8},{28,12},{1,17},{... | collective-permute-start | bytes 1572872 | tf_op jit(solution)/shard_map/ppermute | solution.py:895
  193.6 26.1 %collective-permute-start.24 = (bf16[128,2048]{1,0:T(8,128)(2,1)}, bf16[128,2048]{1,0:T(8,128)(2,1)}, u32[]{:S(2)}, u32[]{:S(2)}) collective-permute-start(bf16[128,2048]{1,0:T(8,128)(2,1)} %slice.391), channel_id=1, source_target_pairs={{0,8},{4,12},{8,0},{12,4},{16,24},{20,28},{24,16},{28,20},{1,9},{5... | collective-permute-start | bytes 1572872 | tf_op jit(solution)/shard_map/ppermute | solution.py:895
  217.8 82.0 %collective-permute-start.41 = (bf16[352,2048]{1,0:T(8,128)(2,1)}, bf16[352,2048]{1,0:T(8,128)(2,1)}, u32[]{:S(2)}, u32[]{:S(2)}) collective-permute-start(bf16[352,2048]{1,0:T(8,128)(2,1)} %dynamic-slice_bitcast_fusion.refs_12_), channel_id=1, source_target_pairs={{1,0},{2,1},{3,2},{5,4},{6,5},{7,6},{9,8},{10,9},{11,10},{13,12},{... | collective-permute-start | bytes 4325384 | tf_op jit(solution)/shard_map/ppermute | solution.py:944
  219.1 58.1 %collective-permute-start.26 = (bf16[256,2048]{1,0:T(8,128)(2,1)}, bf16[256,2048]{1,0:T(8,128)(2,1)}, u32[]{:S(2)}, u32[]{:S(2)}) collective-permute-start(bf16[256,2048]{1,0:T(8,128)(2,1)} %collective-permute-done.21.refs_8_.refs_16_), channel_id=1, source_target_pairs={{0,4},{4,0},{8,12},{12,8},{16,20},{20,16},{24,28},{28,24},{1,5},{5... | collective-permute-start | bytes 3145736 | tf_op jit(solution)/shard_map/ppermute | solution.py:895
  219.2 58.4 %collective-permute-start.27 = (bf16[256,2048]{1,0:T(8,128)(2,1)}, bf16[256,2048]{1,0:T(8,128)(2,1)}, u32[]{:S(2)}, u32[]{:S(2)}) collective-permute-start(bf16[256,2048]{1,0:T(8,128)(2,1)} %collective-permute-done.22.refs_9_.refs_17_), channel_id=1, source_target_pairs={{0,4},{4,0},{8,12},{12,8},{16,20},{20,16},{24,28},{28,24},{1,5},{5... | collective-permute-start | bytes 3145736 | tf_op jit(solution)/shard_map/ppermute | solution.py:895
  219.7 55.5 %collective-permute-start.28 = (bf16[128,2048]{1,0:T(8,128)(2,1)}, bf16[128,2048]{1,0:T(8,128)(2,1)}, u32[]{:S(2)}, u32[]{:S(2)}) collective-permute-start(bf16[128,2048]{1,0:T(8,128)(2,1)} %collective-permute-done.23.refs_10_.refs_18_), channel_id=1, source_target_pairs={{0,4},{4,0},{8,12},{12,8},{16,20},{20,16},{24,28},{28,24},{1,5},{5... | collective-permute-start | bytes 1572872 | tf_op jit(solution)/shard_map/ppermute | solution.py:895
  219.8 55.7 %collective-permute-start.29 = (bf16[128,2048]{1,0:T(8,128)(2,1)}, bf16[128,2048]{1,0:T(8,128)(2,1)}, u32[]{:S(2)}, u32[]{:S(2)}) collective-permute-start(bf16[128,2048]{1,0:T(8,128)(2,1)} %collective-permute-done.24.refs_11_.refs_19_), channel_id=1, source_target_pairs={{0,4},{4,0},{8,12},{12,8},{16,20},{20,16},{24,28},{28,24},{1,5},{5... | collective-permute-start | bytes 1572872 | tf_op jit(solution)/shard_map/ppermute | solution.py:895
  275.4 27.1 %collective-permute-start.39 = (bf16[352,2048]{1,0:T(8,128)(2,1)}, bf16[352,2048]{1,0:T(8,128)(2,1)}, u32[]{:S(2)}, u32[]{:S(2)}) collective-permute-start(bf16[352,2048]{1,0:T(8,128)(2,1)} %collective-permute-done.38.refs_13_), channel_id=1, source_target_pairs={{1,2},{2,3},{5,6},{6,7},{9,10},{10,11},{13,14},{14,15},{17,18},{18... | collective-permute-start | bytes 4325384 | tf_op jit(solution)/shard_map/ppermute | solution.py:941
  277.2 23.9 %collective-permute-start.57 = (bf16[256,2048]{1,0:T(8,128)(2,1)}, bf16[256,2048]{1,0:T(8,128)(2,1)}, u32[]{:S(2)}, u32[]{:S(2)}) collective-permute-start(bf16[256,2048]{1,0:T(8,128)(2,1)} %collective-permute-done.35.refs_9_), channel_id=1, source_target_pairs={{0,4},{4,0},{8,12},{12,8},{16,20},{20,16},{24,28},{28,24},{1,5},{5... | collective-permute-start | bytes 3145736 | tf_op jit(solution)/shard_map/ppermute | solution.py:895
  277.5 24.9 %collective-permute-start.58 = (bf16[128,2048]{1,0:T(8,128)(2,1)}, bf16[128,2048]{1,0:T(8,128)(2,1)}, u32[]{:S(2)}, u32[]{:S(2)}) collective-permute-start(bf16[128,2048]{1,0:T(8,128)(2,1)} %collective-permute-done.36.refs_10_), channel_id=1, source_target_pairs={{0,4},{4,0},{8,12},{12,8},{16,20},{20,16},{24,28},{28,24},{1,5},{5... | collective-permute-start | bytes 1572872 | tf_op jit(solution)/shard_map/ppermute | solution.py:895
  299.7 37.2 %collective-permute-start.42 = (bf16[352,2048]{1,0:T(8,128)(2,1)}, bf16[352,2048]{1,0:T(8,128)(2,1)S(1)}, u32[]{:S(2)}, u32[]{:S(2)}) collective-permute-start(bf16[352,2048]{1,0:T(8,128)(2,1)} %collective-permute-done.41.refs_16_), channel_id=1, source_target_pairs={{1,0},{2,1},{5,4},{6,5},{9,8},{10,9},{13,12},{14,13},{17,16},{18,1... | collective-permute-start | bytes 4325384 | tf_op jit(solution)/shard_map/ppermute | solution.py:944
  301.0 24.6 %collective-permute-start.31 = (bf16[256,2048]{1,0:T(8,128)(2,1)S(1)}, bf16[256,2048]{1,0:T(8,128)(2,1)S(1)}, u32[]{:S(2)}, u32[]{:S(2)}) collective-permute-start(bf16[256,2048]{1,0:T(8,128)(2,1)S(1)} %get-tuple-element.57.refs_2_), channel_id=1, source_target_pairs={{0,16},{4,20},{8,24},{12,28},{16,0},{20,4},{24,8},{28,12},{1,17},{... | collective-permute-start | bytes 3145736 | tf_op jit(solution)/shard_map/ppermute | solution.py:895
  302.5 35.8 %collective-permute-start.50 = (bf16[256,2048]{1,0:T(8,128)(2,1)S(1)}, bf16[256,2048]{1,0:T(8,128)(2,1)S(1)}, u32[]{:S(2)}, u32[]{:S(2)}) collective-permute-start(bf16[256,2048]{1,0:T(8,128)(2,1)S(1)} %get-tuple-element.57.refs_2_), channel_id=1, source_target_pairs={{0,4},{4,0},{8,12},{12,8},{16,20},{20,16},{24,28},{28,24},{1,5},{5... | collective-permute-start | bytes 3145736 | tf_op jit(solution)/shard_map/ppermute | solution.py:895
  304.4 35.5 %collective-permute-start.44 = (bf16[704,512]{1,0:T(8,128)(2,1)S(1)}, bf16[704,512]{1,0:T(8,128)(2,1)S(1)}, u32[]{:S(2)}, u32[]{:S(2)}) collective-permute-start(bf16[704,512]{1,0:T(8,128)(2,1)S(1)} %bitcast.186), channel_id=1, source_target_pairs={{0,1},{1,2},{2,3},{4,5},{5,6},{6,7},{8,9},{9,10},{10,11},{12,13},{... | collective-permute-start | bytes 2162696 | tf_op jit(solution)/shard_map/ppermute | solution.py:941
  322.8 31.6 %collective-permute-start.40 = (bf16[352,2048]{1,0:T(8,128)(2,1)}, bf16[352,2048]{1,0:T(8,128)(2,1)S(1)}, u32[]{:S(2)}, u32[]{:S(2)}) collective-permute-start(bf16[352,2048]{1,0:T(8,128)(2,1)} %collective-permute-done.39.refs_14_), channel_id=1, source_target_pairs={{2,3},{6,7},{10,11},{14,15},{18,19},{22,23},{26,27},{30,31}} | collective-permute-start | bytes 4325384 | tf_op jit(solution)/shard_map/ppermute | solution.py:941
  325.6 26.8 %collective-permute-start.47 = (bf16[704,512]{1,0:T(8,128)(2,1)S(1)}, bf16[704,512]{1,0:T(8,128)(2,1)S(1)}, u32[]{:S(2)}, u32[]{:S(2)}) collective-permute-start(bf16[704,512]{1,0:T(8,128)(2,1)S(1)} %bitcast.187), channel_id=1, source_target_pairs={{1,0},{2,1},{3,2},{5,4},{6,5},{7,6},{9,8},{10,9},{11,10},{13,12},{... | collective-permute-start | bytes 2162696 | tf_op jit(solution)/shard_map/ppermute | solution.py:944
  339.9 62.3 %collective-permute-start.43 = (bf16[352,2048]{1,0:T(8,128)(2,1)S(1)}, bf16[352,2048]{1,0:T(8,128)(2,1)S(1)}, u32[]{:S(2)}, u32[]{:S(2)}) collective-permute-start(bf16[352,2048]{1,0:T(8,128)(2,1)S(1)} %collective-permute-done.42.refs_17_), channel_id=1, source_target_pairs={{1,0},{5,4},{9,8},{13,12},{17,16},{21,20},{25,24},{29,28}} | collective-permute-start | bytes 4325384 | tf_op jit(solution)/shard_map/ppermute | solution.py:944
  352.4 49.9 %collective-permute-start.51 = (bf16[256,2048]{1,0:T(8,128)(2,1)S(1)}, bf16[256,2048]{1,0:T(8,128)(2,1)S(1)}, u32[]{:S(2)}, u32[]{:S(2)}) collective-permute-start(bf16[256,2048]{1,0:T(8,128)(2,1)S(1)} %collective-permute-done.30.refs_3_), channel_id=1, source_target_pairs={{0,4},{4,0},{8,12},{12,8},{16,20},{20,16},{24,28},{28,24},{1,5},{5... | collective-permute-start | bytes 3145736 | tf_op jit(solution)/shard_map/ppermute | solution.py:895
  353.2 44.3 %collective-permute-start.48 = (bf16[704,512]{1,0:T(8,128)(2,1)S(1)}, bf16[704,512]{1,0:T(8,128)(2,1)S(1)}, u32[]{:S(2)}, u32[]{:S(2)}) collective-permute-start(bf16[704,512]{1,0:T(8,128)(2,1)S(1)} %collective-permute-done.47.refs_23_), channel_id=1, source_target_pairs={{1,0},{2,1},{5,4},{6,5},{9,8},{10,9},{13,12},{14,13},{17,16},{18,1... | collective-permute-start | bytes 2162696 | tf_op jit(solution)/shard_map/ppermute | solution.py:944
  354.5 50.0 %collective-permute-start.52 = (bf16[256,2048]{1,0:T(8,128)(2,1)S(1)}, bf16[256,2048]{1,0:T(8,128)(2,1)S(1)}, u32[]{:S(2)}, u32[]{:S(2)}) collective-permute-start(bf16[256,2048]{1,0:T(8,128)(2,1)S(1)} %collective-permute-done.31.refs_4_), channel_id=1, source_target_pairs={{0,4},{4,0},{8,12},{12,8},{16,20},{20,16},{24,28},{28,24},{1,5},{5... | collective-permute-start | bytes 3145736 | tf_op jit(solution)/shard_map/ppermute | solution.py:895
  355.0 49.9 %collective-permute-start.46 = (bf16[704,512]{1,0:T(8,128)(2,1)S(1)}, bf16[704,512]{1,0:T(8,128)(2,1)S(1)}, u32[]{:S(2)}, u32[]{:S(2)}) collective-permute-start(bf16[704,512]{1,0:T(8,128)(2,1)S(1)} %collective-permute-done.45.refs_21_), channel_id=1, source_target_pairs={{2,3},{6,7},{10,11},{14,15},{18,19},{22,23},{26,27},{30,31}} | collective-permute-start | bytes 2162696 | tf_op jit(solution)/shard_map/ppermute | solution.py:941
  460.3 78.8 %collective-permute-start.60 = (bf16[1024,2048]{1,0:T(8,128)(2,1)}, bf16[1024,2048]{1,0:T(8,128)(2,1)}, u32[]{:S(2)}, u32[]{:S(2)}) collective-permute-start(bf16[1024,2048]{1,0:T(8,128)(2,1)} %get-tuple-element.63), channel_id=1, source_target_pairs={{0,4},{4,0},{8,12},{12,8},{16,20},{20,16},{24,28},{28,24},{1,5},{5... | collective-permute-start | bytes 12582920 | tf_op jit(solution)/shard_map/ppermute | solution.py:895
  460.4 80.7 %collective-permute-start.67 = (bf16[1024,2048]{1,0:T(8,128)(2,1)}, bf16[1024,2048]{1,0:T(8,128)(2,1)}, u32[]{:S(2)}, u32[]{:S(2)}) collective-permute-start(bf16[1024,2048]{1,0:T(8,128)(2,1)} %get-tuple-element.66), channel_id=1, source_target_pairs={{0,4},{4,0},{8,12},{12,8},{16,20},{20,16},{24,28},{28,24},{1,5},{5... | collective-permute-start | bytes 12582920 | tf_op jit(solution)/shard_map/ppermute | solution.py:895
  544.3 41.9 %collective-permute-start.68 = (bf16[128,2048]{1,0:T(8,128)(2,1)S(1)}, bf16[128,2048]{1,0:T(8,128)(2,1)S(1)}, u32[]{:S(2)}, u32[]{:S(2)}) collective-permute-start(bf16[128,2048]{1,0:T(8,128)(2,1)S(1)} %get-tuple-element.105), channel_id=1, source_target_pairs={{0,8},{4,12},{8,0},{12,4},{16,24},{20,28},{24,16},{28,20},{1,9},{5... | collective-permute-start | bytes 1572872 | tf_op jit(solution)/shard_map/ppermute | solution.py:895
  545.9 31.3 %collective-permute-start.71 = (bf16[128,2048]{1,0:T(8,128)(2,1)S(1)}, bf16[128,2048]{1,0:T(8,128)(2,1)S(1)}, u32[]{:S(2)}, u32[]{:S(2)}) collective-permute-start(bf16[128,2048]{1,0:T(8,128)(2,1)S(1)} %get-tuple-element.103), channel_id=1, source_target_pairs={{0,8},{4,12},{8,0},{12,4},{16,24},{20,28},{24,16},{28,20},{1,9},{5... | collective-permute-start | bytes 1572872 | tf_op jit(solution)/shard_map/ppermute | solution.py:895
  546.4 30.8 %collective-permute-start.69 = (bf16[128,2048]{1,0:T(8,128)(2,1)S(1)}, bf16[128,2048]{1,0:T(8,128)(2,1)S(1)}, u32[]{:S(2)}, u32[]{:S(2)}) collective-permute-start(bf16[128,2048]{1,0:T(8,128)(2,1)S(1)} %get-tuple-element.104), channel_id=1, source_target_pairs={{0,16},{4,20},{8,24},{12,28},{16,0},{20,4},{24,8},{28,12},{1,17},{... | collective-permute-start | bytes 1572872 | tf_op jit(solution)/shard_map/ppermute | solution.py:895
  547.9 38.9 %collective-permute-start.73 = (bf16[128,2048]{1,0:T(8,128)(2,1)S(1)}, bf16[128,2048]{1,0:T(8,128)(2,1)S(1)}, u32[]{:S(2)}, u32[]{:S(2)}) collective-permute-start(bf16[128,2048]{1,0:T(8,128)(2,1)S(1)} %get-tuple-element.102), channel_id=1, source_target_pairs={{0,16},{4,20},{8,24},{12,28},{16,0},{20,4},{24,8},{28,12},{1,17},{... | collective-permute-start | bytes 1572872 | tf_op jit(solution)/shard_map/ppermute | solution.py:895
  558.6 24.0 %collective-permute-start.62 = (bf16[128,2048]{1,0:T(8,128)(2,1)S(1)}, bf16[128,2048]{1,0:T(8,128)(2,1)S(1)}, u32[]{:S(2)}, u32[]{:S(2)}) collective-permute-start(bf16[128,2048]{1,0:T(8,128)(2,1)S(1)} %get-tuple-element.110), channel_id=1, source_target_pairs={{0,16},{4,20},{8,24},{12,28},{16,0},{20,4},{24,8},{28,12},{1,17},{... | collective-permute-start | bytes 1572872 | tf_op jit(solution)/shard_map/ppermute | solution.py:895
  582.6 163.3 %collective-permute-start.61 = (bf16[128,2048]{1,0:T(8,128)(2,1)}, bf16[128,2048]{1,0:T(8,128)(2,1)}, u32[]{:S(2)}, u32[]{:S(2)}) collective-permute-start(bf16[128,2048]{1,0:T(8,128)(2,1)} %get-tuple-element.111), channel_id=1, source_target_pairs={{0,8},{4,12},{8,0},{12,4},{16,24},{20,28},{24,16},{28,20},{1,9},{5... | collective-permute-start | bytes 1572872 | tf_op jit(solution)/shard_map/ppermute | solution.py:895
  586.2 160.3 %collective-permute-start.66 = (bf16[128,2048]{1,0:T(8,128)(2,1)}, bf16[128,2048]{1,0:T(8,128)(2,1)}, u32[]{:S(2)}, u32[]{:S(2)}) collective-permute-start(bf16[128,2048]{1,0:T(8,128)(2,1)} %get-tuple-element.109), channel_id=1, source_target_pairs={{0,16},{4,20},{8,24},{12,28},{16,0},{20,4},{24,8},{28,12},{1,17},{... | collective-permute-start | bytes 1572872 | tf_op jit(solution)/shard_map/ppermute | solution.py:895
  586.7 159.7 %collective-permute-start.65 = (bf16[128,2048]{1,0:T(8,128)(2,1)}, bf16[128,2048]{1,0:T(8,128)(2,1)}, u32[]{:S(2)}, u32[]{:S(2)}) collective-permute-start(bf16[128,2048]{1,0:T(8,128)(2,1)} %get-tuple-element.108), channel_id=1, source_target_pairs={{0,16},{4,20},{8,24},{12,28},{16,0},{20,4},{24,8},{28,12},{1,17},{... | collective-permute-start | bytes 1572872 | tf_op jit(solution)/shard_map/ppermute | solution.py:895
  594.2 152.3 %collective-permute-start.63 = (bf16[128,2048]{1,0:T(8,128)(2,1)}, bf16[128,2048]{1,0:T(8,128)(2,1)}, u32[]{:S(2)}, u32[]{:S(2)}) collective-permute-start(bf16[128,2048]{1,0:T(8,128)(2,1)} %add_convert_fusion.16), channel_id=1, source_target_pairs={{0,8},{4,12},{8,0},{12,4},{16,24},{20,28},{24,16},{28,20},{1,9},{5... | collective-permute-start | bytes 1572872 | tf_op jit(solution)/shard_map/ppermute | solution.py:895
  606.7 35.6 %all-to-all-start.1 = ((bf16[8,272,256]{2,1,0:T(8,128)(2,1)}), bf16[8,272,256]{2,1,0:T(8,128)(2,1)}, u32[]{:S(2)}, u32[]{:S(2)}) async-start(bf16[8,272,256]{2,1,0:T(8,128)(2,1)} %get-tuple-element.68), calls=%async_computation.1 | async-start | bytes 2228224 | tf_op jit(solution)/shard_map/all_to_all | solution.py:933
  612.4 113.7 %reduce-scatter.3.cloned.1.call-start = ((), (), s32[]{:S(2)}) async-start(), calls=%async_computation.8 | async-start | bytes 1179648 | tf_op jit(solution)/shard_map/reduce_scatter | solution.py:1118
  696.5 54.1 %reduce-scatter.5.cloned.1.call-start = ((), (), s32[]{:S(2)}) async-start(), calls=%async_computation.9 | async-start | bytes 1843200 | tf_op jit(solution)/shard_map/reduce_scatter | solution.py:1146
  706.2 34.1 %collective-permute-start.74 = (bf16[1024,2048]{1,0:T(8,128)(2,1)}, bf16[1024,2048]{1,0:T(8,128)(2,1)}, u32[]{:S(2)}, u32[]{:S(2)}) collective-permute-start(bf16[1024,2048]{1,0:T(8,128)(2,1)} %convolution_convert_fusion), channel_id=1, source_target_pairs={{0,4},{4,0},{8,12},{12,8},{16,20},{20,16},{24,28},{28,24},{1,5},{5... | collective-permute-start | bytes 12582920 | tf_op jit(solution)/shard_map/ppermute | solution.py:895
  735.9 48.4 %all-to-all-start.4 = ((f32[4,640,128]{2,1,0:T(8,128)}), f32[4,640,128]{2,1,0:T(8,128)}, u32[]{:S(2)}, u32[]{:S(2)}) async-start(f32[4,640,128]{2,1,0:T(8,128)} %constant_dynamic-update-slice_fusion), calls=%async_computation.5 | async-start | bytes 2621440 | tf_op jit(solution)/shard_map/all_to_all | solution.py:933
  751.5 32.9 %collective-permute-start.82 = (f32[352,128]{1,0:T(8,128)S(1)}, f32[352,128]{1,0:T(8,128)}, u32[]{:S(2)}, u32[]{:S(2)}) collective-permute-start(f32[352,128]{1,0:T(8,128)S(1)} %slice_bitcast_fusion.6), channel_id=1, source_target_pairs={{0,0},{1,8},{2,16},{3,24},{4,1},{5,9},{6,17},{7,25},{8,2},{9,10},{... | collective-permute-start | bytes 540680 | tf_op jit(solution)/shard_map/ppermute | solution.py:961
  755.0 26.6 %collective-permute-start.83 = (f32[176,128]{1,0:T(8,128)S(1)}, f32[176,128]{1,0:T(8,128)S(1)}, u32[]{:S(2)}, u32[]{:S(2)}) collective-permute-start(f32[176,128]{1,0:T(8,128)S(1)} %slice_bitcast_fusion.7), channel_id=1, source_target_pairs={{0,0},{1,1},{2,16},{3,17},{4,2},{5,3},{6,18},{7,19},{8,4},{9,5},{1... | collective-permute-start | bytes 270344 | tf_op jit(solution)/shard_map/ppermute | solution.py:961
  761.8 32.8 %collective-permute-start.75 = (bf16[128,2048]{1,0:T(8,128)(2,1)}, bf16[128,2048]{1,0:T(8,128)(2,1)S(1)}, u32[]{:S(2)}, u32[]{:S(2)}) collective-permute-start(bf16[128,2048]{1,0:T(8,128)(2,1)} %get-tuple-element.99), channel_id=1, source_target_pairs={{0,8},{4,12},{8,0},{12,4},{16,24},{20,28},{24,16},{28,20},{1,9},{5... | collective-permute-start | bytes 1572872 | tf_op jit(solution)/shard_map/ppermute | solution.py:895
  763.0 32.3 %collective-permute-start.80 = (bf16[128,2048]{1,0:T(8,128)(2,1)}, bf16[128,2048]{1,0:T(8,128)(2,1)S(1)}, u32[]{:S(2)}, u32[]{:S(2)}) collective-permute-start(bf16[128,2048]{1,0:T(8,128)(2,1)} %get-tuple-element.96), channel_id=1, source_target_pairs={{0,16},{4,20},{8,24},{12,28},{16,0},{20,4},{24,8},{28,12},{1,17},{... | collective-permute-start | bytes 1572872 | tf_op jit(solution)/shard_map/ppermute | solution.py:895
  766.4 29.7 %collective-permute-start.77 = (bf16[128,2048]{1,0:T(8,128)(2,1)}, bf16[128,2048]{1,0:T(8,128)(2,1)S(1)}, u32[]{:S(2)}, u32[]{:S(2)}) collective-permute-start(bf16[128,2048]{1,0:T(8,128)(2,1)} %get-tuple-element.101), channel_id=1, source_target_pairs={{0,8},{4,12},{8,0},{12,4},{16,24},{20,28},{24,16},{28,20},{1,9},{5... | collective-permute-start | bytes 1572872 | tf_op jit(solution)/shard_map/ppermute | solution.py:895
  (127 other events, 2593.5 us)
Sparse Core Ops, SparseCore 0:
  634.2 33.2 reduce-scatter.2
  707.1 31.9 reduce-scatter.4

commit v3 on v2

--- a/solution.py
+++ b/solution.py
@@ -109,8 +109,8 @@
     return pltpu.CompilerParams(vmem_limit_bytes=mebibytes * 2**20)
 
 
-def cost(flops, read):
-    return pl.CostEstimate(flops=int(flops), bytes_accessed=int(read), transcendentals=0)
+def cost(tera_ops):
+    return pl.CostEstimate(flops=int(tera_ops * 1e9), bytes_accessed=0, transcendentals=0)
 
 
 def block_order(count):
@@ -154,21 +154,28 @@
     ]
 
 
+def window(ref, start, size):
+    return ref.at[pl.ds(start, size)]
+
+
+def windows(pieces, refs):
+    return [window(ref, start, size) for ref, (_, start, size) in zip(refs, pieces)]
+
+
+def arrays_of(pieces):
+    return [array for array, _, _ in pieces]
+
+
 def line_copies(refs, place, target, sem):
     if len(refs) == 1:
         return [(None, pltpu.make_async_copy(refs[0], target(None), sem))]
-    count = (len(refs) + 1) // 2
-    rising, falling = refs[1:count], refs[count:]
-    copies = []
-    for step in range(count):
-        where = lax.rem(place + step, count)
-        if step == 0:
-            copies.append((None, pltpu.make_async_copy(refs[0], target(where), sem)))
-        else:
-            up = place + step < count
-            copies.append((up, pltpu.make_async_copy(falling[step - 1], target(where), sem)))
-            copies.append((jnp.logical_not(up), pltpu.make_async_copy(rising[count - step - 1], target(where), sem)))
-    return copies
+    own, up, down, a, b, c = refs
+    held = ((own, down, b, c), (up, own, down, a), (a, up, own, down), (c, b, up, own))
+    return [
+        (place == p, pltpu.make_async_copy(ref, target(w), sem))
+        for p, entries in enumerate(held)
+        for w, ref in enumerate(entries)
+    ]
 
 
 def go(copies, what):
@@ -182,15 +189,18 @@
 class Stream:
     def __init__(self, blocks):
         self.pieces = [piece for block in blocks for piece in block]
-        self.shapes = [[piece.shape[0] for piece in block] for block in blocks]
+        self.arrays = arrays_of(self.pieces)
+        self.blocks = [len(block) for block in blocks]
+        self.rows = sum(size for _, _, size in blocks[0])
 
     def bind(self, refs, slots, sems):
-        self.refs, self.slots, self.sems = refs, slots, sems
+        self.refs, self.slots, self.sems = windows(self.pieces, refs), slots, sems
 
     def copies(self, block, slot):
-        first = sum(len(shape) for shape in self.shapes[:block])
+        first = sum(self.blocks[:block])
         result, start = [], 0
-        for i, size in enumerate(self.shapes[block]):
+        for i in range(self.blocks[block]):
+            size = self.pieces[first + i][2]
             result.append(
                 pltpu.make_async_copy(
                     self.refs[first + i], self.slots.at[slot, pl.ds(start, size)], self.sems.at[slot, i]
@@ -200,7 +210,7 @@
         return result
 
     def fetch(self, step):
-        count = len(self.shapes)
+        count = len(self.blocks)
 
         @pl.when(step == 0)
         def _():
@@ -224,72 +234,46 @@
     return [pltpu.VMEM((2, rows, columns), jnp.bfloat16), pltpu.SemaphoreType.DMA((2, 2))]
 
 
-def lower_kernel(stream, wide, *refs):
-    mine_ref, refs = refs[0], refs[1:]
-    pieces, refs = refs[: len(stream.pieces)], refs[len(stream.pieces) :]
-    a_ref, mask_ref, hid_ref, mine_out_ref, slots, sems = refs
-    stream.bind(pieces, slots, sems)
-    step = pl.program_id(0)
-    block = stream.fetch(step)
-    lowered = mm(block, a_ref[...])
-    mask = mask_ref[...].astype(jnp.float32)
-    ranks = mask.shape[1]
-    for j in range(lowered.shape[1] // ranks):
-        lanes = slice(j * ranks, (j + 1) * ranks)
-        hid_ref[:, lanes] = (lowered[:, lanes] * mask).astype(jnp.bfloat16)
-    columns = pl.ds(pl.multiple_of(mine_ref[0] * wide, 128), wide)
-    mine_out_ref[...] = slots[lax.rem(step, 2), :, columns]
-
-
-def lower(mine, blocks, a_mat, mask, wide):
-    stream = Stream(blocks)
-    rows, columns = blocks[0][0].shape
-    total = rows * len(blocks)
-    ranks = a_mat.shape[1]
-    return pl.pallas_call(
-        lambda *refs: lower_kernel(stream, wide, *refs),
-        grid=(len(blocks),),
-        out_shape=(
-            jax.ShapeDtypeStruct((total, ranks), jnp.bfloat16),
-            jax.ShapeDtypeStruct((total, wide), jnp.bfloat16),
-        ),
-        in_specs=[SMEM] + [ANY] * len(stream.pieces)
-        + [pl.BlockSpec(a_mat.shape, lambda i: (0, 0)), tile_spec(rows, mask.shape[1])],
-        out_specs=(tile_spec(rows, ranks), tile_spec(rows, wide)),
-        scratch_shapes=stream_scratch(rows, columns),
-        compiler_params=params(32),
-        cost_estimate=cost(2 * total * columns * ranks, 2 * total * columns),
-    )(mine, *stream.pieces, a_mat, mask)
-
-
-def forward_kernel(stream, win_count, *refs):
+def projection_copies(refs, place, target, sem):
+    def at(w):
+        rows = refs[0].shape[0] if w is None else refs[0].shape[0] * w
+        return target.at[pl.ds(0, rows)] if w is None else target.at[pl.ds(rows, refs[0].shape[0])]
+
+    return line_copies(refs, place, at, sem)
+
+
+def forward_kernel(stream, win_pieces, *refs):
     ends_ref, mine_ref, place_ref, refs = refs[0], refs[1], refs[2], refs[3:]
     pieces, refs = refs[: len(stream.pieces)], refs[len(stream.pieces) :]
-    win_pieces, refs = refs[:win_count], refs[win_count:]
+    win_refs, refs = refs[: len(win_pieces)], refs[len(win_pieces) :]
     (
-        order_row_ref, order_column_ref, hid_ref, b_ref, gap_ref, gain_ref,
-        sent_ref, win_ref, zq_ref, zg_ref, mixed_ref, query_nat, forget_nat, value_nat, states_ref,
-        query_ref, forget_ref, value_ref, out_nat, state_now, slots, sems, win_sem,
+        order_row_ref, order_column_ref, a_ref, b_ref, mask_ref, gap_ref, gain_ref,
+        sent_ref, hid_ref, normed_mine_ref, zq_ref, zg_ref, mixed_ref, query_nat, forget_nat, value_nat, states_ref,
+        query_ref, forget_ref, value_ref, out_nat, state_now, win_ref, slots, sems, win_sem,
     ) = refs
     total, width = mixed_ref.shape
     heads = width // HEAD
     devices = sent_ref.shape[0]
     rows_each = total // devices
     stream.bind(pieces, slots, sems)
-    win_copies = line_copies(
-        win_pieces,
-        place_ref[0],
-        lambda w: win_ref if w is None else win_ref.at[pl.ds(pl.multiple_of(w * width, 128), width)],
-        win_sem,
-    )
+    win_copies = projection_copies(windows(win_pieces, win_refs), place_ref[0], win_ref, win_sem)
     go(win_copies, "start")
+    win_ref[4 * width :, :] = a_ref[...]
+    columns = pl.ds(pl.multiple_of(mine_ref[0] * width, 128), width)
+    ranks = mask_ref.shape[1]
     go(win_copies, "wait")
 
     @pl.loop(0, devices)
     def _(step):
         block = stream.fetch(step)
         rows = pl.ds(pl.multiple_of(step * rows_each, rows_each), rows_each)
-        main = mm(block, win_ref[...], NT) + mm(hid_ref[rows, :], b_ref[...], NT)
+        normed_mine_ref[rows, :] = slots[lax.rem(step, 2), :, columns]
+        main = mm(block, win_ref[...], NT)
+        mask = mask_ref[rows, :].astype(jnp.float32)
+        for j in range(4):
+            lowered = main[:, 4 * width + j * ranks : 4 * width + (j + 1) * ranks] * mask
+            hid_ref[rows, j * ranks : (j + 1) * ranks] = lowered.astype(jnp.bfloat16)
+        main = main[:, : 4 * width] + mm(hid_ref[rows, :], b_ref[...], NT)
         zq = main[:, 0:width]
         zq_ref[rows, :] = zq
         query_ref[rows, :] = (zq * jax.nn.sigmoid(zq)).astype(jnp.bfloat16)
@@ -304,7 +288,7 @@
     state_now[...] = jnp.zeros_like(state_now)
     lower = lower_ones()
 
-    @pl.loop(0, total // CHUNK)
+    @pl.loop(0, total // CHUNK, unroll=2)
     def _(chunk):
         start = pl.multiple_of(chunk * CHUNK, CHUNK)
         rows = pl.ds(start, CHUNK)
@@ -343,31 +327,32 @@
         sent_ref[target, rows_each : rows_each + 16, :] = packed_lines([squares], width)
 
 
-def mixer_forward(ends, mine, place, order, blocks, win_pieces, hid_in, in_b_wide, gap, gain):
+def mixer_forward(ends, mine, place, order, blocks, win_pieces, in_a_t, in_b_wide, mask, gap, gain):
     stream = Stream(blocks)
     devices = len(blocks)
-    rows_each, model = blocks[0][0].shape
-    total, width = rows_each * devices, gap.shape[0]
+    model = in_a_t.shape[1]
+    total, width = stream.rows * devices, gap.shape[0]
     heads = width // HEAD
+    ranks = mask.shape[1]
     rows = jax.ShapeDtypeStruct((total, width), jnp.bfloat16)
     wide_rows = jax.ShapeDtypeStruct((total, width), jnp.float32)
     states = jax.ShapeDtypeStruct((total // CHUNK + 1, heads, HEAD, HEAD), jnp.float32)
-    sent = jax.ShapeDtypeStruct((devices, rows_each + 16, width), jnp.bfloat16)
-    win = jax.ShapeDtypeStruct((4 * width, model), jnp.bfloat16)
+    sent = jax.ShapeDtypeStruct((devices, stream.rows + 16, width), jnp.bfloat16)
+    hid = jax.ShapeDtypeStruct((total, 4 * ranks), jnp.bfloat16)
     return pl.pallas_call(
-        lambda *refs: forward_kernel(stream, len(win_pieces), *refs),
-        out_shape=(sent, win, wide_rows, wide_rows, rows, rows, rows, rows, states),
-        in_specs=[SMEM] * 3 + [ANY] * (len(stream.pieces) + len(win_pieces)) + [VMEM] * 6,
-        out_specs=(VMEM,) * 9,
+        lambda *refs: forward_kernel(stream, win_pieces, *refs),
+        out_shape=(sent, hid, rows, wide_rows, wide_rows, rows, rows, rows, rows, states),
+        in_specs=[SMEM] * 3 + [ANY] * (len(stream.pieces) + len(win_pieces)) + [VMEM] * 7,
+        out_specs=(VMEM,) * 10,
         scratch_shapes=[pltpu.VMEM((total, width), jnp.bfloat16)] * 4
-        + [pltpu.VMEM((heads, HEAD, HEAD), jnp.float32)]
-        + stream_scratch(rows_each, model)
+        + [pltpu.VMEM((heads, HEAD, HEAD), jnp.float32), pltpu.VMEM((4 * (width + ranks), model), jnp.bfloat16)]
+        + stream_scratch(stream.rows, model)
         + [pltpu.SemaphoreType.DMA(())],
-        compiler_params=params(56),
-        cost_estimate=cost(2 * total * width * (4 * model + CHUNK * 12 + total * 4), 24 * total * width),
+        compiler_params=params(62),
+        cost_estimate=cost(57),
     )(
-        ends, mine, place, *stream.pieces, *win_pieces, order.reshape(1, total), order.reshape(total, 1),
-        hid_in, in_b_wide, gap.reshape(1, width), gain.reshape(1, width),
+        ends, mine, place, *stream.arrays, *arrays_of(win_pieces), *order,
+        in_a_t, in_b_wide, mask, gap.reshape(1, width), gain.reshape(1, width),
     )
 
 
@@ -407,7 +392,7 @@
     slope_now[...] = jnp.zeros_like(slope_now)
     lower = lower_ones()
 
-    @pl.loop(0, total // CHUNK)
+    @pl.loop(0, total // CHUNK, unroll=2)
     def _(step):
         chunk = total // CHUNK - 1 - step
         start = pl.multiple_of(chunk * CHUNK, CHUNK)
@@ -487,10 +472,10 @@
         out_specs=(VMEM,) * 4,
         scratch_shapes=[pltpu.VMEM((total, width), jnp.bfloat16)] * 5
         + [pltpu.VMEM((heads, HEAD, HEAD), jnp.float32)],
-        compiler_params=params(56),
-        cost_estimate=cost(2 * total * width * (CHUNK * 60 + total * 4), 30 * total * width),
+        compiler_params=params(62),
+        cost_estimate=cost(51),
     )(
-        ends, mine, order.reshape(1, total), order.reshape(total, 1), came, *kept,
+        ends, mine, *order, came, *kept,
         gap.reshape(1, width), gain.reshape(1, width), hid_in, in_b_wide, mask, fold,
     )
 
@@ -562,8 +547,8 @@
             pltpu.VMEM((model, ranks), jnp.bfloat16),
             pltpu.SemaphoreType.DMA((len(pieces),)),
         ],
-        compiler_params=params(40),
-        cost_estimate=cost(2 * rows * model * model, 2 * model * model),
+        compiler_params=params(62),
+        cost_estimate=cost(8),
     )(mine, came, x, out_a, out_b, mask_own, gain.reshape(1, model), *pieces)
 
 
@@ -659,8 +644,8 @@
             pltpu.VMEM((model, model), jnp.bfloat16),
             pltpu.SemaphoreType.DMA((len(pieces),)),
         ],
-        compiler_params=params(56),
-        cost_estimate=cost(2 * rows * model * model, 2 * model * model),
+        compiler_params=params(62),
+        cost_estimate=cost(12),
     )(mine, *fixed, own, other, *from_x, *from_y, *pieces)
 
 
@@ -688,144 +673,347 @@
         in_specs=[whole(x), whole(d_resid), first_block(rows, d_hid.shape[1]), whole(in_a), first_block(1, model)]
         + [first_block(rows, model)] * 2 + [whole(piece) for piece in from_x + from_y],
         out_specs=first_block(rows, model),
-        compiler_params=params(40),
-        cost_estimate=cost(2 * rows * model * in_a.shape[1], 16 * rows * model),
+        compiler_params=params(62),
+        cost_estimate=cost(4),
     )(x, d_resid, d_hid, in_a, gain.reshape(1, model), own, other, *from_x, *from_y)
 
 
-def ffn_kernel(streams, counts, wt, *refs):
+def both_copies(refs, place, target, padded, sem):
+    if len(refs) == 2:
+        size = refs[0].shape[0]
+        return [(None, pltpu.make_async_copy(refs[i], window(target, i * padded, size), sem)) for i in range(2)]
+    groups = [refs[i : i + 6] for i in range(0, len(refs), 6)]
+    units = sum(group[0].shape[0] for group in groups)
+    copies, first = [], 0
+    for group in groups:
+        size = group[0].shape[0]
+
+        def at(w, first=first, size=size):
+            return window(target, w // 2 * padded + w % 2 * units + first, size)
+
+        copies += line_copies(group, place, at, sem)
+        first += size
+    return copies
+
+
+def hidden_of(refs):
+    if len(refs) == 2:
+        return refs[0].shape[0]
+    return 2 * sum(refs[i].shape[0] for i in range(0, len(refs), 6))
+
+
+def load_both(refs, place, w_all, ffn_a_ref, padded, sem):
+    copies = both_copies(refs, place, w_all, padded, sem)
+    go(copies, "start")
+    hidden_units = hidden_of(refs)
+    if padded > hidden_units:
+        blank = jnp.zeros((padded - hidden_units, w_all.shape[1]), jnp.bfloat16)
+        w_all[hidden_units:padded, :] = blank
+        w_all[padded + hidden_units : 2 * padded, :] = blank
+    w_all[2 * padded :, :] = ffn_a_ref[...]
+    return copies
+
+
+def ffn_up_kernel(stream, ffn_pieces, *refs):
     mine_ref, place_ref, refs = refs[0], refs[1], refs[2:]
-    normed_pieces, refs = refs[: len(streams[0].pieces)], refs[len(streams[0].pieces) :]
-    cot_pieces, refs = refs[: len(streams[1].pieces)], refs[len(streams[1].pieces) :]
-    ffn_pieces, refs = refs[: counts[0]], refs[counts[0] :]
-    down_pieces, refs = refs[: counts[1]], refs[counts[1] :]
+    pieces, refs = refs[: len(stream.pieces)], refs[len(stream.pieces) :]
+    weights, refs = windows(ffn_pieces, refs), refs[len(ffn_pieces) :]
+    mask_ref, ffn_a_ref, both_b_ref, both_ref, hid_ref, mine_out_ref, w_all, slots, sems, ffn_sem = refs
+    step = pl.program_id(0)
+    stream.bind(pieces, slots, sems)
+    padded = both_b_ref.shape[0] // 2
+    wide = mine_out_ref.shape[1]
+
+    @pl.when(step == 0)
+    def _():
+        go(load_both(weights, place_ref[0], w_all, ffn_a_ref, padded, ffn_sem), "wait")
+
+    normed = stream.fetch(step)
+    columns = pl.ds(pl.multiple_of(mine_ref[0] * wide, 128), wide)
+    mine_out_ref[...] = slots[lax.rem(step, 2), :, columns]
+    mask = mask_ref[...].astype(jnp.float32)
+    main = mm(normed, w_all[...], NT)
+    hid = (main[:, 2 * padded :] * jnp.concatenate([mask, mask], axis=1)).astype(jnp.bfloat16)
+    hid_ref[...] = hid
+    both_ref[...] = main[:, : 2 * padded] + mm(hid, both_b_ref[...], NT)
+
+
+def ffn_up(mine, place, normed, weights, mask, ffn_a_t, both_b, wide):
+    stream = Stream(normed)
+    rows, model = stream.rows, ffn_a_t.shape[1]
+    total = rows * len(normed)
+    ranks = mask.shape[1]
+    padded = both_b.shape[0] // 2
+    return pl.pallas_call(
+        lambda *refs: ffn_up_kernel(stream, weights, *refs),
+        grid=(len(normed),),
+        out_shape=(
+            jax.ShapeDtypeStruct((total, 2 * padded), jnp.float32),
+            jax.ShapeDtypeStruct((total, 2 * ranks), jnp.bfloat16),
+            jax.ShapeDtypeStruct((total, wide), jnp.bfloat16),
+        ),
+        in_specs=[SMEM] * 2
+        + [ANY] * (len(stream.pieces) + len(weights))
+        + [tile_spec(rows, ranks), whole(ffn_a_t), whole(both_b)],
+        out_specs=(tile_spec(rows, 2 * padded), tile_spec(rows, 2 * ranks), tile_spec(rows, wide)),
+        scratch_shapes=[pltpu.VMEM((2 * padded + 2 * ranks, model), jnp.bfloat16)]
+        + stream_scratch(rows, model)
+        + [pltpu.SemaphoreType.DMA(())],
+        compiler_params=params(62),
+        cost_estimate=cost(28),
+    )(mine, place, *stream.arrays, *arrays_of(weights), mask, ffn_a_t, both_b)
+
+
+def ffn_back_kernel(stream, ffn_pieces, down_pieces, *refs):
+    mine_ref, place_ref, refs = refs[0], refs[1], refs[2:]
+    pieces, refs = refs[: len(stream.pieces)], refs[len(stream.pieces) :]
+    weights, refs = windows(ffn_pieces, refs), refs[len(ffn_pieces) :]
+    downs, refs = windows(down_pieces, refs), refs[len(down_pieces) :]
     (
-        mask_ref, ffn_a_ref, b_gate_ref, b_up_ref, down_a_ref, down_b_ref, fold_ref,
-        back_ref, down_ref, small_ref, normed_mine_ref, cot_mine_ref, down_a_rows, gate_rows, up_rows,
-        w_both, w_down, normed_slots, normed_sems, cot_slots, cot_sems, ffn_sem, down_sem,
+        both_ref, hid_ref, mask_ref, ffn_a_ref, both_b_ref, down_a_ref, down_b_ref, fold_ref,
+        back_ref, down_ref, small_ref, cot_mine_ref, down_rows, both_rows,
+        w_all, w_down, left_both, left_down, slots, sems, ffn_sem, down_sem,
     ) = refs
     step = pl.program_id(0)
-    streams[0].bind(normed_pieces, normed_slots, normed_sems)
-    streams[1].bind(cot_pieces, cot_slots, cot_sems)
-    hidden_units, model = w_down.shape
-    wide = normed_mine_ref.shape[1]
-    ranks = mask_ref.shape[1]
-    each, narrow = 2 * hidden_units // wt, model // wt
+    stream.bind(pieces, slots, sems)
+    padded = down_a_ref.shape[0]
+    model = w_down.shape[1]
+    wide = cot_mine_ref.shape[1]
 
     @pl.when(step == 0)
     def _():
-        ffn = line_copies(
-            ffn_pieces,
-            place_ref[0],
-            lambda w: w_both if w is None else w_both.at[pl.ds(pl.multiple_of(w * each, 16), each)],
-            ffn_sem,
-        )
-        down = line_copies(
-            down_pieces,
-            place_ref[0],
-            lambda w: w_down if w is None else w_down.at[:, pl.ds(pl.multiple_of(w * narrow, 128), narrow)],
-            down_sem,
-        )
-        go(ffn, "start")
+        hidden_units = hidden_of(weights)
+        if len(downs) == 1:
+            down = line_copies(downs, place_ref[0], lambda w: window(w_down, 0, hidden_units), down_sem)
+        else:
+            strip = downs[0].shape[0]
+            narrow = model * strip // hidden_units
+            down = []
+            for part in range(hidden_units // strip):
+                down += line_copies(
+                    [ref.at[:, pl.ds(part * narrow, narrow)] for ref in downs],
+                    place_ref[0],
+                    lambda w, part=part: w_down.at[pl.ds(part * strip, strip), pl.ds(w * narrow, narrow)],
+                    down_sem,
+                )
         go(down, "start")
-        go(ffn, "wait")
+        if padded > hidden_units:
+            w_down[hidden_units:padded, :] = jnp.zeros((padded - hidden_units, model), jnp.bfloat16)
+        w_down[padded:, :] = down_b_ref[...]
+        both = load_both(weights, place_ref[0], w_all, ffn_a_ref, padded, ffn_sem)
         go(down, "wait")
-        down_a_rows[...] = jnp.zeros_like(down_a_rows)
-        gate_rows[...] = jnp.zeros_like(gate_rows)
-        up_rows[...] = jnp.zeros_like(up_rows)
-
-    normed = streams[0].fetch(step)
-    cot = streams[1].fetch(step)
-    slot = lax.rem(step, 2)
+        go(both, "wait")
+        down_rows[...] = jnp.zeros_like(down_rows)
+        both_rows[...] = jnp.zeros_like(both_rows)
+
+    cot = stream.fetch(step)
     columns = pl.ds(pl.multiple_of(mine_ref[0] * wide, 128), wide)
-    normed_mine_ref[...] = normed_slots[slot, :, columns]
-    cot_mine_ref[...] = cot_slots[slot, :, columns]
+    cot_mine_ref[...] = slots[lax.rem(step, 2), :, columns]
     mask = mask_ref[...].astype(jnp.float32)
-    lowered = mm(normed, ffn_a_ref[...])
-    hid_gate = (lowered[:, :ranks] * mask).astype(jnp.bfloat16)
-    hid_up = (lowered[:, ranks:] * mask).astype(jnp.bfloat16)
-    gate = mm(normed, w_both[0:hidden_units, :], NT) + mm(hid_gate, b_gate_ref[...], NT)
-    upper = mm(normed, w_both[hidden_units:, :], NT) + mm(hid_up, b_up_ref[...], NT)
+    hid = hid_ref[...]
+    main = mm(cot, w_down[...], NT)
+    d_hid = (main[:, padded:] * mask).astype(jnp.bfloat16)
+    d_hidden = main[:, :padded] + mm(d_hid, down_a_ref[...], NT)
+    gate, upper = both_ref[:, :padded], both_ref[:, padded:]
     sigma = jax.nn.sigmoid(gate)
     silu = gate * sigma
-    hidden = (silu * upper).astype(jnp.bfloat16)
-    d_hid = (mm(cot, down_b_ref[...]) * mask).astype(jnp.bfloat16)
-    d_hidden = mm(cot, w_down[...], NT) + mm(d_hid, down_a_ref[...], NT)
-    d_gate = (d_hidden * upper * (sigma * (1.0 + gate * (1.0 - sigma)))).astype(jnp.bfloat16)
-    d_upper = (d_hidden * silu).astype(jnp.bfloat16)
-    through_gate = (mm(d_gate, b_gate_ref[...]) * mask).astype(jnp.bfloat16)
-    through_up = (mm(d_upper, b_up_ref[...]) * mask).astype(jnp.bfloat16)
-    through = jnp.concatenate([through_gate, through_up], axis=1)
-    back = mm(d_gate, w_both[0:hidden_units, :]) + mm(d_upper, w_both[hidden_units:, :])
-    back_ref[...] = (back + mm(through, ffn_a_ref[...], NT)).astype(jnp.bfloat16)
-    low = (mm(hidden, down_a_ref[...]) * mask).astype(jnp.bfloat16)
-    down_ref[...] = (mm(hidden, w_down[...]) + mm(low, down_b_ref[...], NT)).astype(jnp.bfloat16)
+    left_down[:, :padded] = (silu * upper).astype(jnp.bfloat16)
+    left_both[:, :padded] = (d_hidden * upper * (sigma * (1.0 + gate * (1.0 - sigma)))).astype(jnp.bfloat16)
+    left_both[:, padded : 2 * padded] = (d_hidden * silu).astype(jnp.bfloat16)
+    mask_two = jnp.concatenate([mask, mask], axis=1)
+    through = (mm(left_both[:, : 2 * padded], both_b_ref[...]) * mask_two).astype(jnp.bfloat16)
+    left_both[:, 2 * padded :] = through
+    back_ref[...] = mm(left_both[...], w_all[...]).astype(jnp.bfloat16)
+    low = (mm(left_down[:, :padded], down_a_ref[...]) * mask).astype(jnp.bfloat16)
+    left_down[:, padded:] = low
+    down_ref[...] = mm(left_down[...], w_down[...]).astype(jnp.bfloat16)
     small_ref[...] = mm(jnp.concatenate([low, through], axis=1), fold_ref[...]).astype(jnp.bfloat16)
-    down_a_rows[...] += mm(hidden, d_hid, TN)
-    gate_rows[...] += mm(d_gate, hid_gate, TN)
-    up_rows[...] += mm(d_upper, hid_up, TN)
-
-
-def feed_forward(mine, place, normed, cot, ffn_pieces, down_pieces, mask, ffn_a, b_gate, b_up, down_a, down_b, fold, wide, wt):
-    streams = [Stream(normed), Stream(cot)]
-    rows, model = normed[0][0].shape
-    blocks = len(normed)
+    down_rows[...] += mm(d_hid, left_down[:, :padded], TN)
+    both_rows[...] += mm(hid, left_both[:, : 2 * padded], TN)
+
+
+def ffn_back(mine, place, cot, weights, downs, both, hid, mask, first, ffn_a_t, both_b, down_a, down_b_t, fold, wide):
+    stream = Stream(cot)
+    rows, model = stream.rows, ffn_a_t.shape[1]
+    blocks = len(cot)
     total = rows * blocks
-    hidden_units, ranks = down_a.shape
-    fixed = [ffn_a, b_gate, b_up, down_a, down_b, fold]
+    padded, ranks = down_a.shape
+    fixed = [ffn_a_t, both_b, down_a, down_b_t, fold]
     grown = jax.ShapeDtypeStruct((total, model), jnp.bfloat16)
-    mine_columns = jax.ShapeDtypeStruct((total, wide), jnp.bfloat16)
-    term = jax.ShapeDtypeStruct((hidden_units, ranks), jnp.float32)
+
+    def from_first(columns):
+        return pl.BlockSpec((rows, columns), lambda i: (i + first, 0))
+
     return pl.pallas_call(
-        lambda *refs: ffn_kernel(streams, (len(ffn_pieces), len(down_pieces)), wt, *refs),
+        lambda *refs: ffn_back_kernel(stream, weights, downs, *refs),
         grid=(blocks,),
         out_shape=(
-            grown, grown, jax.ShapeDtypeStruct((total, ranks), jnp.bfloat16), mine_columns, mine_columns,
-            term, term, term,
+            grown, grown, jax.ShapeDtypeStruct((total, ranks), jnp.bfloat16),
+            jax.ShapeDtypeStruct((total, wide), jnp.bfloat16),
+            jax.ShapeDtypeStruct((ranks, padded), jnp.float32),
+            jax.ShapeDtypeStruct((2 * ranks, 2 * padded), jnp.float32),
         ),
         in_specs=[SMEM] * 2
-        + [ANY] * (len(streams[0].pieces) + len(streams[1].pieces) + len(ffn_pieces) + len(down_pieces))
-        + [tile_spec(rows, ranks)]
+        + [ANY] * (len(stream.pieces) + len(weights) + len(downs))
+        + [from_first(2 * padded), from_first(2 * ranks), from_first(ranks)]
         + [whole(array) for array in fixed],
         out_specs=(
-            tile_spec(rows, model), tile_spec(rows, model), tile_spec(rows, ranks),
-            tile_spec(rows, wide), tile_spec(rows, wide),
-        ) + (first_block(hidden_units, ranks),) * 3,
+            tile_spec(rows, model), tile_spec(rows, model), tile_spec(rows, ranks), tile_spec(rows, wide),
+            first_block(ranks, padded), first_block(2 * ranks, 2 * padded),
+        ),
         scratch_shapes=[
-            pltpu.VMEM((2 * hidden_units, model), jnp.bfloat16),
-            pltpu.VMEM((hidden_units, model), jnp.bfloat16),
+            pltpu.VMEM((2 * padded + 2 * ranks, model), jnp.bfloat16),
+            pltpu.VMEM((padded + ranks, model), jnp.bfloat16),
+            pltpu.VMEM((rows, 2 * padded + 2 * ranks), jnp.bfloat16),
+            pltpu.VMEM((rows, padded + ranks), jnp.bfloat16),
         ]
-        + stream_scratch(rows, model) * 2
+        + stream_scratch(rows, model)
         + [pltpu.SemaphoreType.DMA(()), pltpu.SemaphoreType.DMA(())],
-        compiler_params=params(58),
-        cost_estimate=cost(14 * total * model * hidden_units, 6 * hidden_units * model + 8 * total * model),
-    )(
-        mine, place, *streams[0].pieces, *streams[1].pieces, *ffn_pieces, *down_pieces, mask, *fixed,
-    )
-
-
-def assemble_kernel(count, *refs):
-    place_ref, pieces, out, sem = refs[0], refs[1 : 1 + count], refs[1 + count], refs[2 + count]
-    width = pieces[0].shape[1]
-    copies = line_copies(
-        pieces,
-        place_ref[0],
-        lambda w: out if w is None else out.at[:, pl.ds(pl.multiple_of(w * width, 128), width)],
-        sem,
-    )
+        compiler_params=params(62),
+        cost_estimate=cost(33),
+    )(mine, place, *stream.arrays, *arrays_of(weights), *arrays_of(downs), both, hid, mask, *fixed)
+
+
+def spread_kernel(win_pieces, *refs):
+    place_ref, refs = refs[0], refs[1:]
+    pieces, refs = windows(win_pieces, refs), refs[len(win_pieces) :]
+    x_ref, out_ref, win_ref, sem = refs
+    copies = projection_copies(pieces, place_ref[0], win_ref, sem)
+
+    @pl.when(pl.program_id(0) == 0)
+    def _():
+        go(copies, "start")
+        go(copies, "wait")
+
+    out_ref[...] = mm(x_ref[...], win_ref[...]).astype(jnp.bfloat16)
+
+
+def spread(place, values, win_pieces, first, blocks, rows):
+    inner = values.shape[1]
+    model = win_pieces[0][0].shape[1]
+    return pl.pallas_call(
+        lambda *refs: spread_kernel(win_pieces, *refs),
+        grid=(blocks,),
+        out_shape=jax.ShapeDtypeStruct((rows * blocks, model), jnp.bfloat16),
+        in_specs=[SMEM] + [ANY] * len(win_pieces) + [pl.BlockSpec((rows, inner), lambda i: (i + first, 0))],
+        out_specs=tile_spec(rows, model),
+        scratch_shapes=[pltpu.VMEM((inner, model), jnp.bfloat16), pltpu.SemaphoreType.DMA(())],
+        compiler_params=params(62),
+        cost_estimate=cost(8),
+    )(place, *arrays_of(win_pieces), values)
+
+
+def pack_in_kernel(mine_ref, win_ref, wout_ref, out_ref, window, sems):
+    wide, model = window.shape[1], window.shape[0]
+    narrow = wout_ref.shape[1]
+    strips = model // narrow
+    strip = wide // strips
+    start = pl.multiple_of(mine_ref[0] * wide, 128)
+    copies = [pltpu.make_async_copy(win_ref.at[:, pl.ds(start, wide)], window, sems.at[0])]
+    for part in range(strips):
+        copies.append(
+            pltpu.make_async_copy(
+                wout_ref.at[pl.ds(pl.multiple_of(start + part * strip, 16), strip)],
+                out_ref.at[pl.ds(wide, strip), pl.ds(part * narrow, narrow)],
+                sems.at[1 + part],
+            )
+        )
+    for copy in copies:
+        copy.start()
+    eye = lax.broadcasted_iota(jnp.int32, (wide, wide), 0) == lax.broadcasted_iota(jnp.int32, (wide, wide), 1)
+    eye = jnp.where(eye, 1.0, 0.0).astype(jnp.bfloat16)
+    for copy in copies:
+        copy.wait()
+    out_ref[0:wide, :] = mm(eye, window[...], NT).astype(jnp.bfloat16)
+
+
+def pack_in(mine, w_in, w_out, wide):
+    model, narrow = w_in.shape[0], w_out.shape[1]
+    strips = model // narrow
+    return pl.pallas_call(
+        pack_in_kernel,
+        out_shape=jax.ShapeDtypeStruct((wide + wide // strips, model), jnp.bfloat16),
+        in_specs=[SMEM, ANY, ANY],
+        out_specs=VMEM,
+        scratch_shapes=[pltpu.VMEM((model, wide), jnp.bfloat16), pltpu.SemaphoreType.DMA((1 + strips,))],
+        compiler_params=params(62),
+        cost_estimate=cost(3),
+    )(mine, w_in, w_out)
+
+
+def pack_ffn_kernel(units, mine_ref, wffn_ref, wdown_ref, out_ref, held, sems):
+    model, columns = wffn_ref.shape
+    span = held.shape[1]
+    narrow = wdown_ref.shape[1]
+    parts = model // narrow
+    shards = wdown_ref.shape[0] // (units * 8)
+    strip = units * shards // parts
+    wanted = mine_ref[0] * units
+    start = jnp.minimum(wanted // 128 * 128, columns - span)
+    copies = [pltpu.make_async_copy(wffn_ref.at[:, pl.ds(pl.multiple_of(start, 128), span)], held, sems.at[0])]
+    for part in range(parts):
+        shard, inside = part * strip // units, part * strip % units
+        source = shard * units * 8 + wanted + inside
+        copies.append(
+            pltpu.make_async_copy(
+                wdown_ref.at[pl.ds(pl.multiple_of(source, 16), strip)],
+                out_ref.at[pl.ds(units, strip), pl.ds(part * narrow, narrow)],
+                sems.at[1 + part],
+            )
+        )
+    for copy in copies:
+        copy.start()
+    rows = lax.broadcasted_iota(jnp.int32, (units, span), 0) + (wanted - start)
+    chosen = jnp.where(rows == lax.broadcasted_iota(jnp.int32, (units, span), 1), 1.0, 0.0).astype(jnp.bfloat16)
+    for copy in copies:
+        copy.wait()
+    out_ref[0:units, :] = mm(chosen, held[...], NT).astype(jnp.bfloat16)
+
+
+def pack_ffn(mine, w_ffn, w_down, units):
+    model, columns = w_ffn.shape
+    span = min(columns, (units + 127) // 128 * 128 + 128)
+    parts = model // w_down.shape[1]
+    return pl.pallas_call(
+        lambda *refs: pack_ffn_kernel(units, *refs),
+        out_shape=jax.ShapeDtypeStruct((units + 2 * units // parts, model), jnp.bfloat16),
+        in_specs=[SMEM, ANY, ANY],
+        out_specs=VMEM,
+        scratch_shapes=[pltpu.VMEM((model, span), jnp.bfloat16), pltpu.SemaphoreType.DMA((1 + parts,))],
+        compiler_params=params(62),
+        cost_estimate=cost(3),
+    )(mine, w_ffn, w_down)
+
+
+def unpack_out_kernel(pieces, *refs):
+    place_ref, out, sem = refs[0], refs[-2], refs[-1]
+    refs = windows(pieces, refs[1:-2])
+    strip = refs[0].shape[0]
+    strips = out.shape[0] // strip
+    narrow = out.shape[1] // strips
+    copies = []
+    for part in range(strips):
+        copies += line_copies(
+            [ref.at[:, pl.ds(part * narrow, narrow)] for ref in refs],
+            place_ref[0],
+            lambda w, part=part: out.at[pl.ds(part * strip, strip), pl.ds(w * narrow, narrow)],
+            sem,
+        )
     go(copies, "start")
     go(copies, "wait")
 
 
-def assemble(place, pieces, rows, columns):
+def unpack_out(place, pieces, wide):
+    model = pieces[0][0].shape[1]
     return pl.pallas_call(
-        lambda *refs: assemble_kernel(len(pieces), *refs),
-        out_shape=jax.ShapeDtypeStruct((rows, columns), pieces[0].dtype),
+        lambda *refs: unpack_out_kernel(pieces, *refs),
+        out_shape=jax.ShapeDtypeStruct((wide, model), pieces[0][0].dtype),
         in_specs=[SMEM] + [ANY] * len(pieces),
         out_specs=VMEM,
         scratch_shapes=[pltpu.SemaphoreType.DMA(())],
-        cost_estimate=cost(0, 4 * rows * columns),
-    )(place, *pieces)
+        compiler_params=params(62),
+        cost_estimate=cost(2),
+    )(place, *arrays_of(pieces))
 
 
 ADAPTERS = 8
@@ -849,9 +1037,9 @@
     )
 
 
-def adapter_mask(adapter):
-    columns = jnp.arange(RANKS, dtype=jnp.int32) // RANK
-    return (columns[None, :] == adapter[:, None]).astype(f32)
+def adapter_mask(adapter, count=1):
+    columns = jnp.arange(count * RANKS, dtype=jnp.int32) % RANKS // RANK
+    return (columns[None, :] == adapter[:, None]).astype(bf16)
 
 
 def norm_factor(values):
@@ -895,12 +1083,16 @@
     return lax.ppermute(values, axis, [(i, i ^ bits) for i in range(size)])
 
 
-def gather_near(block):
+def first_near(block):
     size = lax.axis_size("seq")
-    if size != 8:
-        return [[block]] + [[across(block, k)] for k in range(2, size, 2)]
+    return [across(block, k) for k in ((2, 4) if size == 8 else range(2, size, 2))]
+
+
+def more_near(block, first):
+    if len(first) != 2:
+        return [[block]] + [[other] for other in first]
+    by_x, by_y = first
     half = block.shape[0] // 2
-    by_x, by_y = across(block, 2), across(block, 4)
     return [[block], [by_x], [by_y], [across(by_x[:half], 4), across(by_y[half:], 2)]]
 
 
@@ -908,42 +1100,74 @@
     return [[across(piece, 1) for piece in block] for block in blocks]
 
 
-def scatter_near(near, other):
+def with_rows(blocks):
+    return [[(piece, 0, piece.shape[0]) for piece in block] for block in blocks]
+
+
+def two_blocks(blocks):
+    upper, lower = [], []
+    for block in blocks:
+        if len(block) == 1:
+            half = block[0].shape[0] // 2
+            upper.append([(block[0], 0, half)])
+            lower.append([(block[0], half, half)])
+        else:
+            upper.append([(block[0], 0, block[0].shape[0])])
+            lower.append([(block[1], 0, block[1].shape[0])])
+    return upper, lower
+
+
+def scatter_parts(near, other):
     size = lax.axis_size("seq")
     rows = near.shape[0] // (size // 2)
+    half = rows // 2
 
     def part(block, start, stop):
         at = slice(block * rows + start, block * rows + stop)
         return near[at].astype(f32) + other[at].astype(f32)
 
     if size != 8:
-        rest = sum([across(part(i, 0, rows).astype(bf16), 2 * i).astype(f32) for i in range(1, size // 2)])
-        return near, other, [rest.astype(bf16)], []
-    half = rows // 2
-    far_x, far_y = [part(3, i * half, (i + 1) * half).astype(bf16) for i in range(2)]
-    far_x, far_y = across(far_x, 2), across(far_y, 4)
-    by_x, by_y = part(1, 0, half).astype(bf16), part(2, half, rows).astype(bf16)
-    by_x, by_y = across(by_x, 2), across(by_y, 4)
-    by_x_more = across((part(1, half, rows) + far_y.astype(f32)).astype(bf16), 2)
-    by_y_more = across((part(2, 0, half) + far_x.astype(f32)).astype(bf16), 4)
-    return near, other, [by_x, by_x_more], [by_y_more, by_y]
+        return [part(i, 0, rows).astype(bf16) for i in range(1, size // 2)], []
+    sent = [part(3, 0, half), part(3, half, rows), part(1, 0, half), part(2, half, rows)]
+    return [piece.astype(bf16) for piece in sent], [part(1, half, rows), part(2, 0, half)]
+
+
+def scatter_first(sent):
+    bits = (2, 4, 2, 4) if lax.axis_size("seq") == 8 else [2 * i + 2 for i in range(len(sent))]
+    return [across(piece, bit) for piece, bit in zip(sent, bits)]
+
+
+def scatter_second(came, rest):
+    if not rest:
+        total = sum(piece.astype(f32) for piece in came).astype(bf16)
+        return [total], []
+    far_x, far_y, by_x, by_y = came
+    by_x_more = across((rest[0] + far_y.astype(f32)).astype(bf16), 2)
+    by_y_more = across((rest[1] + far_x.astype(f32)).astype(bf16), 4)
+    return [by_x, by_x_more], [by_y_more, by_y]
 
 
 def swap(values, axis="seq"):
     return lax.all_to_all(values, axis, split_axis=0, concat_axis=0, tiled=False)
 
 
-def line_pieces(block):
-    count = lax.axis_size("wt")
-    rising, falling = [block], [block]
-    for step in range(1, count):
-        rising.append(
-            lax.ppermute(rising[-1], "wt", [(i, i + 1) for i in range(step - 1, count - 1)])
-        )
-        falling.append(
-            lax.ppermute(falling[-1], "wt", [(i, i - 1) for i in range(1, count - step + 1)])
-        )
-    return [block] + rising[1:] + falling[1:]
+def along(values, pairs):
+    return lax.ppermute(values, "wt", pairs)
+
+
+def first_pieces(block):
+    return along(block, [(0, 1), (1, 2), (2, 3)]), along(block, [(1, 0), (2, 1), (3, 2)])
+
+
+def more_pieces(first, start, size):
+    place = lax.axis_index("wt")
+    up, down = [piece[start : start + size] for piece in first]
+    inner, outer = jnp.where(place == 1, up, down), jnp.where(place == 2, up, down)
+    return [along(inner, [(1, 2), (2, 1)]), along(outer, [(2, 3), (1, 0)]), along(inner, [(1, 3), (2, 0)])]
+
+
+def line_rows(block, first, more, start, size, more_start=0):
+    return [(piece, start, size) for piece in (block,) + tuple(first)] + [(piece, more_start, size) for piece in more]
 
 
 def after(values, *others):
@@ -961,10 +1185,10 @@
     return lax.ppermute(piece, ("seq", "wt"), moves)
 
 
-def fold_columns(count):
+def fold_columns(count, first):
     source = jnp.arange(count * RANKS)
     target = jnp.arange(RANKS)
-    wanted = (source // RANKS) * RANK + source % RANK
+    wanted = (first + source // RANKS) * RANK + source % RANK
     return (wanted[:, None] == target[None, :]).astype(bf16)
 
 
@@ -1000,9 +1224,10 @@
     rows, model = x_rows.shape
     total = n * rows
     wide = model // n
-    half = total // 2
     units = w_ffn.shape[1] // n
     hidden_units = wt // 2 * units
+    padded = (hidden_units + 127) // 128 * 128
+    blocks = n // 2
     on_line = wt == PROJECTIONS and n == 8
 
     def my_columns(values, extent, axis):
@@ -1011,17 +1236,34 @@
     def my_piece(values, axis):
         return lax.dynamic_index_in_dim(values, mine, axis, False)
 
+    def pad_rows(values):
+        return jnp.pad(values, ((0, padded - hidden_units), (0, 0)))
+
     if on_line:
-        win_pieces = line_pieces(my_columns(w_in, wide, 1).T)
-        w_out = after(w_out, win_pieces[2])
+        win_mine = pack_in(mine_ref, w_in, w_out, wide)
+        win_first = lax.optimization_barrier(first_pieces(win_mine))
+        win_more = more_pieces(win_first, 0, win_mine.shape[0])
+        ffn_mine = pack_ffn(mine_ref, w_ffn, w_down, units)
     else:
         spread_in = lax.all_gather(w_in, "wt", axis=1, tiled=True)
         spread_in = my_piece(spread_in.reshape(model, PROJECTIONS, n, wide), 2)
         win_pieces = [jnp.transpose(spread_in, (1, 2, 0)).reshape(PROJECTIONS * wide, model)]
-
+        win_pieces = [(win_pieces[0], 0, PROJECTIONS * wide)]
+        wout_mine = lax.all_gather(my_columns(w_out, wide, 0), "wt", axis=1, tiled=True)
+        down_mine = my_piece(w_down.reshape(wt // 2, n, units, -1), 1).reshape(hidden_units, -1)
+        down_pieces = [(lax.all_gather(down_mine, "wt", axis=1, tiled=True), 0, hidden_units)]
+        spread_ffn = lax.all_gather(my_columns(w_ffn, units, 1).T, "wt", axis=0)
+        spread_ffn = [spread_ffn[: wt // 2].reshape(-1, model), spread_ffn[wt // 2 :].reshape(-1, model)]
+        ffn_pieces = [(piece, 0, hidden_units) for piece in spread_ffn]
+
+    inputs = x_rows.astype(f32)
+    normed = (inputs * norm_factor(inputs) * gain_mix).astype(bf16)
+    pair = jnp.concatenate([normed, cot_rows])
+    pair_first = first_near(pair)
     order_mine = to_order(order[0].reshape(n, rows), mine).reshape(total)
     ends = jnp.cumsum(lengths[0])
-    mask = adapter_mask(adapter_of(sequence_of(order_mine, lengths[0]), adapter_ids[0])).astype(bf16)
+    adapter = adapter_of(sequence_of(order_mine, lengths[0]), adapter_ids[0])
+    mask = adapter_mask(adapter)
     mask_own = mask[:rows]
     gap_mine = my_columns(forget_gap, wide, 0)
     gain_mine = my_columns(gain_gate, wide, 0)
@@ -1029,130 +1271,164 @@
     in_b_wide = jnp.concatenate(
         [jnp.pad(in_b_mine[j], ((0, 0), (j * RANKS, (PROJECTIONS - 1 - j) * RANKS))) for j in range(PROJECTIONS)]
     )
-    fold_in, fold_ffn = fold_columns(PROJECTIONS), fold_columns(3)
-
-    inputs = x_rows.astype(f32)
-    normed = (inputs * norm_factor(inputs) * gain_mix).astype(bf16)
-    normed_near = gather_near(normed)
-    normed_blocks = normed_near + other_core(normed_near)
-    hid_in, normed_mine = lower(mine_ref, normed_blocks, in_a, mask, wide)
-
-    cot_near = gather_near(after(cot_rows, normed_near[1][0]))
-    cot_other = other_core(cot_near)
-
-    sent, win, *kept = mixer_forward(
-        ends, mine_ref, place_ref, order_mine, normed_blocks, win_pieces, hid_in, in_b_wide, gap_mine, gain_mine
+    fold_in, fold_ffn, fold_out = fold_columns(PROJECTIONS, 0), fold_columns(3, PROJECTIONS), fold_columns(1, PROJECTIONS + 3)
+    ffn_b_mine = my_piece(ffn_b.reshape(wt, n, units, RANKS), 1)
+    b_gate = pad_rows(ffn_b_mine[: wt // 2].reshape(-1, RANKS))
+    b_up = pad_rows(ffn_b_mine[wt // 2 :].reshape(-1, RANKS))
+    both_b = jnp.concatenate([jnp.pad(b_gate, ((0, 0), (0, RANKS))), jnp.pad(b_up, ((0, 0), (RANKS, 0)))])
+    down_a_mine = pad_rows(my_piece(down_a.reshape(wt // 2, n, units, RANKS), 1).reshape(-1, RANKS))
+    ready = lax.optimization_barrier(
+        (
+            pair_first, (order_mine.reshape(1, total), order_mine.reshape(total, 1)), mask, gap_mine, gain_mine,
+            in_b_wide, both_b, down_a_mine, down_b.T, ffn_a.T, in_a.T,
+        )
     )
+    pair_first, order_both, mask, gap_mine, gain_mine, in_b_wide, both_b, down_a_mine, down_b_t, ffn_a_t, in_a_t = ready
+    pair_near = more_near(pair, pair_first)
+    pair_other = other_core(pair_near)
+    normed_near, cot_near = two_blocks(pair_near)
+    normed_other, cot_other = two_blocks(pair_other)
 
     if on_line:
-        wout_pieces = line_pieces(my_columns(w_out, wide, 0))
-        w_ffn, w_down = after((w_ffn, w_down), wout_pieces[2])
-        ffn_pieces = line_pieces(my_columns(w_ffn, units, 1).T)
-        w_down = after(w_down, ffn_pieces[2])
-        down_pieces = my_piece(w_down.reshape(wt // 2, n, units, -1), 1).reshape(hidden_units, -1)
-        down_pieces = line_pieces(down_pieces)
+        win_more, ffn_mine = lax.optimization_barrier((win_more, ffn_mine))
+        win_pieces = line_rows(win_mine, win_first, win_more, 0, wide)
+        wout_mine = line_rows(win_mine, win_first, win_more, wide, win_mine.shape[0] - wide, wide)
+        wout_mine = unpack_out(place_ref, wout_mine, wide)
+    sent, hid_in, normed_mine, *kept = mixer_forward(
+        ends, mine_ref, place_ref, order_both, normed_near + normed_other, win_pieces,
+        after(in_a_t, wout_mine), in_b_wide, mask, gap_mine, gain_mine,
+    )
+    wout_first = [across(wout_mine, k) for k in range(2, n, 2)]
+    if on_line:
+        sent, wout_first, ffn_first = lax.optimization_barrier((sent, wout_first, first_pieces(ffn_mine)))
+        early = units // 48 * 16
+        early_more = more_pieces(ffn_first, 0, early)
+        strip = ffn_mine.shape[0] - units
     else:
-        wout_pieces = [lax.all_gather(my_columns(w_out, wide, 0), "wt", axis=1, tiled=True)]
-        ffn_pieces = [lax.all_gather(my_columns(w_ffn, units, 1).T, "wt", axis=0, tiled=True)]
-        down_pieces = my_piece(w_down.reshape(wt // 2, n, units, -1), 1).reshape(hidden_units, -1)
-        down_pieces = [lax.all_gather(down_pieces, "wt", axis=1, tiled=True)]
-    wout_near = gather_near(assemble(place_ref, wout_pieces, wide, model))
+        sent, wout_first = lax.optimization_barrier((sent, wout_first))
+    wout_near = [[wout_mine]] + [[block] for block in wout_first]
     wout_blocks = wout_near + other_core(wout_near)
-    ffn_b_mine = my_piece(ffn_b.reshape(wt, n, units, RANKS), 1)
-    b_gate = ffn_b_mine[: wt // 2].reshape(-1, RANKS)
-    b_up = ffn_b_mine[wt // 2 :].reshape(-1, RANKS)
-    down_a_mine = my_piece(down_a.reshape(wt // 2, n, units, RANKS), 1).reshape(-1, RANKS)
 
     came = swap(sent)
     resid, normed2, hid_out = token_forward(
         mine_ref, came, x_rows, out_a, out_b, mask_own, gain_ffn, wout_blocks
     )
 
-    normed2_near = gather_near(normed2)
-    ffn_args = (ffn_pieces, down_pieces)
-    ffn_rest = (ffn_a, b_gate, b_up, down_a_mine, down_b, fold_ffn, wide, wt)
+    if on_line:
+        normed2, early_more = lax.optimization_barrier((normed2, early_more))
+        late_more = more_pieces(after(ffn_first, *early_more), early, units - early)
+        ffn_pieces = line_rows(ffn_mine, ffn_first, early_more, 0, early)
+        ffn_pieces += line_rows(ffn_mine, ffn_first, late_more, early, units - early)
+        down_more = more_pieces(after(ffn_first, *late_more), units, strip)
+
+    normed2_near = more_near(normed2, first_near(normed2))
+    both, hid_ffn, normed2_mine = ffn_up(
+        mine_ref, place_ref, with_rows(normed2_near + other_core(normed2_near)), ffn_pieces, mask, ffn_a_t, both_b, wide
+    )
+    if on_line:
+        both, down_more = lax.optimization_barrier((both, down_more))
+        down_pieces = line_rows(ffn_mine, ffn_first, down_more, units, strip)
     sides = []
-    for blocks, cots, masks in (
-        (other_core(normed2_near), cot_other, mask[half:]),
-        (normed2_near, cot_near, mask[:half]),
-    ):
-        sides.append(feed_forward(mine_ref, place_ref, blocks, cots, *ffn_args, masks, *ffn_rest))
+    for cots, first in ((cot_other, blocks), (cot_near, 0)):
+        sides.append(
+            ffn_back(
+                mine_ref, place_ref, cots, ffn_pieces, down_pieces, both, hid_ffn, mask, first,
+                ffn_a_t, both_b, down_a_mine, down_b_t, fold_ffn, wide,
+            )
+        )
     back_far, down_far, small_far, *rest_far = sides[0]
     back, down, small, *rest = sides[1]
-    parts = scatter_near(back, across(back_far, 1))
+    back_far, down_far = across(back_far, 1), across(down_far, 1)
+    back, down, back_far, down_far = lax.optimization_barrier((back, down, back_far, down_far))
+    back_parts, back_rest = scatter_parts(back, back_far)
+    from_x, from_y = scatter_second(scatter_first(back_parts), back_rest)
     d_sent, d_resid, d_hid_out, out_b_part = token_backward(
-        mine_ref, came, cot_rows, resid, out_a, out_b, mask_own, gain_ffn, hid_out, parts, wout_blocks
+        mine_ref, came, cot_rows, resid, out_a, out_b, mask_own, gain_ffn, hid_out,
+        (back, back_far, from_x, from_y), wout_blocks,
     )
-
-    g_proj, gated_heads, small_in, in_b_rows = mixer_backward(
-        ends, mine_ref, order_mine, swap(d_sent), kept, gap_mine, gain_mine, hid_in, in_b_wide, mask, fold_in
-    )
-    back_in_far = across(mm(g_proj[half:], win).astype(bf16), 1)
-    back_in = mm(g_proj[:half], win).astype(bf16)
-    parts_in = scatter_near(back_in, back_in_far)
-    small_in = jnp.sum(swap(from_order(small_in.reshape(n, rows, RANKS), mine)).astype(f32), axis=0).astype(bf16)
-    small_in = swap(jnp.broadcast_to(small_in, (n, rows, RANKS)))
-    small_in = to_order(small_in, mine).reshape(total, RANKS)
-    d_hid_in = (mm(small_in, fold_in, NT) * jnp.tile(mask, (1, PROJECTIONS))).astype(bf16)
-    tokens_grad = token_end(x_rows, d_resid, d_hid_in, in_a, gain_mix, parts_in)
-
-    near, other, from_x, from_y = scatter_near(down, across(down_far, 1))
-    block_out = resid + near[:rows].astype(f32) + other[:rows].astype(f32)
-    for pieces in (from_x, from_y):
-        if pieces:
-            block_out = block_out + jnp.concatenate(pieces).astype(f32)
-    block_out = block_out.astype(bf16)
-
-    small_ffn = jnp.concatenate([small, small_far]).reshape(n, rows, RANKS)
-    small_ffn = jnp.sum(swap(from_order(small_ffn, mine)).astype(f32), axis=0).astype(bf16)
-    small_ffn = to_order(lax.all_gather(small_ffn, "seq", axis=0), mine).reshape(total, RANKS)
-    spread = (mm(small_ffn, fold_ffn, NT) * jnp.tile(mask, (1, 3))).astype(bf16)
-    hid_down, d_hid_ffn = spread[:, :RANKS], spread[:, RANKS:]
-    normed2_mine, cot_mine = [jnp.concatenate([rest[i], rest_far[i]]) for i in range(2)]
-    down_a_rows, gate_rows, up_rows = [rest[i] + rest_far[i] for i in range(2, 5)]
-    down_b_rows = mm(cot_mine, hid_down, TN)
-    ffn_a_rows = mm(normed2_mine, d_hid_ffn, TN)
-    ffn_b_rows = jnp.concatenate([gate_rows, up_rows])
-    d_hid_out_all = to_order(lax.all_gather(d_hid_out, "seq", axis=0), mine).reshape(total, RANKS)
-    out_a_rows = mm(gated_heads, d_hid_out_all, TN)
-    out_b_rows = lax.psum_scatter(out_b_part, "seq", scatter_dimension=0, tiled=True)
-    in_a_rows = mm(normed_mine, d_hid_in, TN)
-
-    def reduced(arrays, how):
-        packed = [
-            jnp.concatenate(
-                [
-                    array[:, c * RANKS : (c + 1) * RANKS].reshape(wt, -1, RANKS)
-                    for c in range(array.shape[1] // RANKS)
-                ],
-                axis=1,
-            )
-            for array in arrays
-        ]
-        summed = how(jnp.concatenate(packed, axis=1))
+    cot_mine = jnp.concatenate([rest[0], rest_far[0]])
+    down_rows, both_rows = [rest[i] + rest_far[i] for i in (1, 2)]
+    down_a_rows = down_rows[:, :hidden_units].T
+    ffn_b_rows = jnp.concatenate(
+        [both_rows[:RANKS, :hidden_units], both_rows[RANKS:, padded : padded + hidden_units]], axis=1
+    ).T
+
+    def packed_rows(arrays):
+        return jnp.concatenate(
+            [
+                array[:, c * RANKS : (c + 1) * RANKS].reshape(wt, -1, RANKS)
+                for array in arrays
+                for c in range(array.shape[1] // RANKS)
+            ],
+            axis=1,
+        )
+
+    def unpacked_rows(summed, arrays):
         results, start = [], 0
         for array in arrays:
             height = array.shape[0] // wt
-            count = array.shape[1] // RANKS
-            results.append(
-                jnp.concatenate(
-                    [summed[start + c * height : start + (c + 1) * height] for c in range(count)], axis=1
-                )
-            )
-            start += count * height
+            parts = []
+            for _ in range(array.shape[1] // RANKS):
+                parts.append(summed[start : start + height])
+                start += height
+            results.append(jnp.concatenate(parts, axis=1))
         return results
 
-    def by_offload(values):
-        return lax.psum_scatter(values, "wt", scatter_dimension=0, tiled=False)
-
-    def by_swap(values):
-        return jnp.sum(swap(values, "wt"), axis=0)
-
-    ffn_b_grad, down_a_grad, down_b_grad, ffn_a_grad = reduced(
-        [ffn_b_rows, down_a_rows, down_b_rows, ffn_a_rows], by_offload
+    early = [ffn_b_rows, down_a_rows]
+    early_sum = lax.psum_scatter(packed_rows(early), "wt", scatter_dimension=0, tiled=False)
+
+    out_parts = [
+        (down[i * rows : (i + 1) * rows].astype(f32) + down_far[i * rows : (i + 1) * rows].astype(f32)).astype(bf16)
+        for i in range(1, blocks)
+    ]
+    out_came = [across(part, 2 * i + 2) for i, part in enumerate(after(out_parts, d_sent))]
+    d_came = swap(d_sent)
+    g_proj, gated_heads, small_in, in_b_rows = mixer_backward(
+        ends, mine_ref, order_both, d_came, kept, gap_mine, gain_mine, hid_in, in_b_wide, mask, fold_in
     )
-    out_a_grad, out_b_grad, in_a_grad, in_b_grad = reduced(
-        [out_a_rows, out_b_rows, in_a_rows, in_b_rows], by_swap
+    g_proj, small_in, out_came, early_sum = lax.optimization_barrier((g_proj, small_in, out_came, early_sum))
+    ffn_b_grad, down_a_grad = unpacked_rows(early_sum, early)
+
+    small = (small_in + jnp.concatenate([small, small_far])).reshape(n, rows, RANKS)
+    small = jnp.concatenate([from_order(small, mine), out_b_part.astype(bf16).reshape(n, rows, -1)], axis=2)
+    small, g_proj = lax.optimization_barrier((small, g_proj))
+    small = swap(small)
+    back_in_far = across(spread(place_ref, g_proj, win_pieces, blocks, blocks, rows), 1)
+    back_in = spread(place_ref, g_proj, win_pieces, 0, blocks, rows)
+    in_parts, in_rest = scatter_parts(back_in, back_in_far)
+    in_came = scatter_first(in_parts)
+    small = jnp.sum(after(small, *in_parts, *in_rest).astype(f32), axis=0)
+    out_b_rows = small[:, RANKS:].reshape(wide, RANKS)
+    small = small[:, :RANKS].astype(bf16)
+    d_hid_in_own = (mm(small, fold_in, NT) * adapter_mask(adapter[:rows], PROJECTIONS)).astype(bf16)
+    small = small + mm(d_hid_out, fold_out).astype(bf16)
+    small = swap(jnp.broadcast_to(small, (n,) + small.shape))
+    block_out = resid + down[:rows].astype(f32) + down_far[:rows].astype(f32)
+    block_out = (block_out + sum(piece.astype(f32) for piece in out_came)).astype(bf16)
+    in_came, block_out = lax.optimization_barrier((in_came, block_out))
+    if in_rest:
+        in_rest = [in_rest[0] + in_came[1].astype(f32), in_rest[1] + in_came[0].astype(f32)]
+        in_rest = [part.astype(bf16) for part in in_rest]
+        small, in_rest = lax.optimization_barrier((small, in_rest))
+        from_x, from_y = [in_came[2], across(in_rest[0], 2)], [across(in_rest[1], 4), in_came[3]]
+    else:
+        from_x, from_y = scatter_second(in_came, in_rest)
+    small = to_order(small, mine).reshape(total, RANKS)
+    d_hid_in = (mm(small, fold_in, NT) * adapter_mask(adapter, PROJECTIONS)).astype(bf16)
+
+    wide_ffn = (mm(small, fold_ffn, NT) * adapter_mask(adapter, 3)).astype(bf16)
+    late = [
+        mm(cot_mine, wide_ffn[:, :RANKS], TN),
+        mm(normed2_mine, wide_ffn[:, RANKS:], TN),
+        mm(gated_heads, (mm(small, fold_out, NT) * mask).astype(bf16), TN),
+        out_b_rows,
+        mm(normed_mine, d_hid_in, TN),
+        in_b_rows,
+    ]
+    late_sum = jnp.sum(swap(packed_rows(late).astype(bf16), "wt").astype(f32), axis=0)
+    down_b_grad, ffn_a_grad, out_a_grad, out_b_grad, in_a_grad, in_b_grad = unpacked_rows(late_sum, late)
+    tokens_grad = token_end(
+        x_rows, d_resid, d_hid_in_own, in_a, gain_mix, (back_in, back_in_far, from_x, from_y)
     )
     return (
         block_out[None],

time: 838 us -> 647 us (0.77)
  local copies, waits for them, and re-layouts: 103 us -> 33 us
  waiting for transfers between devices: 265 us -> 209 us
  starting transfers between devices: 123 us -> 88.6 us
  blocking collectives: 30.7 us -> 0 us
  Pallas kernels: 216 us -> 240 us
  matrix products: 24 us -> 6.6 us
    ppermute x24 -> x16, waiting for transfers between devices: 155 us -> 66.6 us  [along(): return lax.ppermute(values, 'wt', pairs)]
    ppermute x57 -> x43, waiting for transfers between devices: 75.1 us -> 107 us  [across(): return lax.ppermute(values, axis, [(i, i ^ bits) for i in range(size)])]
    all_gather x2 -> x0, blocking collectives: 30.7 us -> none  [the longest x1 20.7 us: local(): lax.all_gather(d_hid_out, 'seq', axis=0)]
    unnamed x217 -> x122, local copies, waits for them, and re-layouts: 48.8 us -> 18.2 us
    pallas_call x5 -> x9, Pallas kernels: 146 us -> 167 us  [the longest x2 60.3 us: ffn_back(): pl.pallas_call(lambda *refs: ffn_back_kernel(stream, weights, downs, *ref...]
    ppermute x24 -> x16, starting transfers between devices: 43.6 us -> 25.3 us  [along(): return lax.ppermute(values, 'wt', pairs)]
    dot_general x8 -> x7, matrix products: 24 us -> 6.6 us  [mm(): lax.dot_general(left, right, dims, preferred_element_type=jnp.float32)]
    optimization_barrier x1, local copies, waits for them, and re-layouts: 15.1 us -> 1.35 us  [local(): lax.optimization_barrier((pair_first, (order_mine.reshape(1, total), orde...]
  transfers between devices with their start and end apart: 92 -> 68, of which waited for: 26 -> 27; matrix products, arithmetic and copies ran while one was open for 16% -> 9% of each run, Pallas kernels for 21% -> 29%
where the time goes in v3:
time: 647 us; the launch traced here: 638 us
  Pallas kernels  240 us (37%)
  waiting for transfers between devices  209 us (32%)
  starting transfers between devices  88.6 us (14%)
  other arithmetic  45 us (7%)
  local copies, waits for them, and re-layouts  33 us (5%)
  between operations  15.8 us (2%)
  matrix products  6.6 us (1%)
    ppermute x43, waiting for transfers between devices, across(): return lax.ppermute(values, axis, [(i, i ^ bits) for i in range(size)])  107 us
    ppermute x16, waiting for transfers between devices, along(): return lax.ppermute(values, 'wt', pairs)  66.6 us
    pallas_call x2, Pallas kernels, ffn_back(): pl.pallas_call(lambda *refs: ffn_back_kernel(stream, weights, downs, *ref...  60.3 us
    pallas_call x1, Pallas kernels, mixer_forward(): pl.pallas_call(lambda *refs: forward_kernel(stream, win_pieces, *refs), o...  52 us
    pallas_call x1, Pallas kernels, mixer_backward(): pl.pallas_call(backward_kernel, out_shape=(jax.ShapeDtypeStruct((total, 4...  46.5 us
    ppermute x43, starting transfers between devices, across(): return lax.ppermute(values, axis, [(i, i ^ bits) for i in range(size)])  28.5 us
    pallas_call x1, Pallas kernels, ffn_up(): pl.pallas_call(lambda *refs: ffn_up_kernel(stream, weights, *refs), grid=...  26 us
    ppermute x16, starting transfers between devices, along(): return lax.ppermute(values, 'wt', pairs)  25.3 us
  transfers between devices with their start and end apart: 68, of which 27 were waited for; matrix products, arithmetic and copies ran while one was open for 9% of the time, Pallas kernels for 29%

profile of v3, /device:TPU:4, one launch (start us, length us, event | category | flops | bytes accessed | tf_op | source)
XLA Modules:
  0.0 637.7 jit_solution(12034434676747715514)
XLA Ops:
  7.2 2.9 shard_map.276.refs_1_.refs_11_
  10.2 4.7 collective-permute-start
  16.8 1.6 pad_maximum_fusion.refs_3_.refs_2_
  22.1 2.0 constant_dynamic-slice_fusion
  26.8 2.1 copy.54
  30.3 2.5 copy.56
  33.6 8.5 %collective-permute-done.refs_2_.refs_12_ = bf16[320,2048]{1,0:T(8,128)(2,1)} collective-permute-done((bf16[320,2048]{1,0:T(8,128)(2,1)}, bf16[320,2048]{1,0:T(8,128)(2,1)}, u32[]{:S(2)}, u32[]{:S(2)}) %collective-permute-start) | collective-permute-done | bytes 1310752 | tf_op jit(solution)/shard_map/ppermute | solution.py:1155
  42.1 5.2 collective-permute-done.1.refs_3_.refs_13_
  47.3 3.0 broadcast_select_fusion
  56.6 9.3 %collective-permute-done.5.refs_4_.refs_3_ = bf16[512,2048]{1,0:T(8,128)(2,1)} collective-permute-done((bf16[512,2048]{1,0:T(8,128)(2,1)}, bf16[512,2048]{1,0:T(8,128)(2,1)}, u32[]{:S(2)}, u32[]{:S(2)}) %collective-permute-start.5) | collective-permute-done | bytes 2097184 | tf_op jit(solution)/shard_map/ppermute | solution.py:1083
  69.5 15.6 %collective-permute-done.3.refs_5_.refs_15_ = bf16[320,2048]{1,0:T(8,128)(2,1)} collective-permute-done((bf16[320,2048]{1,0:T(8,128)(2,1)S(1)}, bf16[320,2048]{1,0:T(8,128)(2,1)}, u32[]{:S(2)}, u32[]{:S(2)}) %collective-permute-start.3) | collective-permute-done | bytes 1310752 | tf_op jit(solution)/shard_map/ppermute | solution.py:1155
  86.4 7.9 %collective-permute-done.7.refs_6_ = bf16[256,2048]{1,0:T(8,128)(2,1)} collective-permute-done((bf16[256,2048]{1,0:T(8,128)(2,1)S(1)}, bf16[256,2048]{1,0:T(8,128)(2,1)}, u32[]{:S(2)}, u32[]{:S(2)}) %collective-permute-start.7) | collective-permute-done | bytes 1048608 | tf_op jit(solution)/shard_map/ppermute | solution.py:1083
  94.2 4.1 shard_map.277.refs_12_.refs_18_.refs_6_
  99.7 16.8 %collective-permute-done.4.refs_6_.refs_16_ = bf16[320,2048]{1,0:T(8,128)(2,1)} collective-permute-done((bf16[320,2048]{1,0:T(8,128)(2,1)}, bf16[320,2048]{1,0:T(8,128)(2,1)}, u32[]{:S(2)}, u32[]{:S(2)}) %collective-permute-start.4) | collective-permute-done | bytes 1310752 | tf_op jit(solution)/shard_map/ppermute | solution.py:1155
  116.6 2.2 shard_map.278.refs_7_.refs_15_
  118.8 1.5 collective-permute-start.12
  122.4 2.6 collective-permute-start.15
  126.5 52.0 %shard_map.279 = (bf16[8,272,256]{2,1,0:T(8,128)(2,1)}, bf16[2048,512]{1,0:T(8,128)(2,1)}, bf16[2048,256]{1,0:T(8,128)(2,1)}, f32[2048,256]{1,0:T(8,128)}, f32[2...) custom-call(s32[4]{0:T(128)} %bitcast.162, ...), custom_call_target="tpu_custom_call" | custom-call | flops 57000001536 | tf_op jit(solution)/shard_map/pallas_call | solution.py:342
  179.7 4.2 all-to-all-start
  185.4 2.0 broadcast_select_fusion.6
  191.5 7.1 %all-to-all-done.refs_1_ = bf16[8,272,256]{2,1,0:T(8,128)(2,1)S(1)} async-done(((bf16[8,272,256]{2,1,0:T(8,128)(2,1)}), bf16[8,272,256]{2,1,0:T(8,128)(2,1)S(1)}, u32[]{:S(2)}, u32[]{:S(2)}) %all-to-all-start) | async-done | bytes 1114144 | tf_op jit(solution)/shard_map/all_to_all | solution.py:1151
  199.6 9.7 %shard_map.280 = (f32[256,2048]{1,0:T(8,128)}, bf16[256,2048]{1,0:T(8,128)(2,1)}, bf16[256,128]{1,0:T(8,128)(2,1)}) custom-call(s32[1]{0:T(128)} %bitcast.1.mine_ref.refs_0_.refs_1_, bf16[8,272,256]{2,1,0:T(8,128)(2,1)} %copy-done.7, bf16[256,2048]{1,0:T(8,128)(2,1)} %bitcast.101, bf16[2048,128]{1,0:T(8,128)(2,1)} %refs_4_.3, bf16[2048,128]{1,0:T(8,128)(2,1)} %refs_5_.1, ...), custom_call_target="tpu_custom_call" | custom-call | flops 8000000000 | tf_op jit(solution)/shard_map/pallas_call | solution.py:535
  209.3 9.4 %collective-permute-done.23.refs_16_.refs_10_ = bf16[112,2048]{1,0:T(8,128)(2,1)} collective-permute-done((bf16[112,2048]{1,0:T(8,128)(2,1)}, bf16[112,2048]{1,0:T(8,128)(2,1)}, u32[]{:S(2)}, u32[]{:S(2)}) %collective-permute-start.23) | collective-permute-done | bytes 458784 | tf_op jit(solution)/shard_map/ppermute | solution.py:1155
  222.4 1.6 broadcast_select_fusion.2
  226.1 18.9 %collective-permute-done.28.refs_3_ = bf16[256,2048]{1,0:T(8,128)(2,1)S(1)} collective-permute-done((bf16[256,2048]{1,0:T(8,128)(2,1)}, bf16[256,2048]{1,0:T(8,128)(2,1)S(1)}, u32[]{:S(2)}, u32[]{:S(2)}) %collective-permute-start.28) | collective-permute-done | bytes 1048608 | tf_op jit(solution)/shard_map/ppermute | solution.py:1083
  246.8 19.1 %collective-permute-done.21.refs_5_ = bf16[256,2048]{1,0:T(8,128)(2,1)} collective-permute-done((bf16[256,2048]{1,0:T(8,128)(2,1)S(1)}, bf16[256,2048]{1,0:T(8,128)(2,1)}, u32[]{:S(2)}, u32[]{:S(2)}) %collective-permute-start.21) | collective-permute-done | bytes 1048608 | tf_op jit(solution)/shard_map/ppermute | solution.py:1083
  267.3 3.1 collective-permute-done.26.refs_22_.refs_16_
  271.0 7.1 %collective-permute-done.31.refs_6_ = bf16[128,2048]{1,0:T(8,128)(2,1)S(1)} collective-permute-done((bf16[128,2048]{1,0:T(8,128)(2,1)S(1)}, bf16[128,2048]{1,0:T(8,128)(2,1)S(1)}, u32[]{:S(2)}, u32[]{:S(2)}) %collective-permute-start.31) | collective-permute-done | bytes 524320 | tf_op jit(solution)/shard_map/ppermute | solution.py:1083
  280.9 1.6 collective-permute-start.37
  283.8 1.7 collective-permute-start.38
  285.6 26.0 %shard_map.281 = (f32[2048,1536]{1,0:T(8,128)}, bf16[2048,256]{1,0:T(8,128)(2,1)}, bf16[2048,256]{1,0:T(8,128)(2,1)}) custom-call(s32[1]{0:T(128)} %bitcast.1.mine_ref.refs_0_.refs_1_, s32[1]{0:T(128)} %bitcast.refs_0_.refs_2_.refs_1_, bf16[256,2048]{1,0:T(8,128)(2,1)} %get-tuple-element.139.refs_2_, bf16[256,2048]{1,0:T(8,128)(2,1)} %copy-done.23, ...), custom_call_target="tpu_custom_call" | custom-call | flops 28000000000 | tf_op jit(solution)/shard_map/pallas_call | solution.py:747
  311.6 7.9 %collective-permute-done.38.refs_22_ = bf16[176,2048]{1,0:T(8,128)(2,1)} collective-permute-done((bf16[176,2048]{1,0:T(8,128)(2,1)S(1)}, bf16[176,2048]{1,0:T(8,128)(2,1)}, u32[]{:S(2)}, u32[]{:S(2)}) %collective-permute-start.38) | collective-permute-done | bytes 720928 | tf_op jit(solution)/shard_map/ppermute | solution.py:1155
  319.4 30.2 %shard_map.283 = (bf16[1024,2048]{1,0:T(8,128)(2,1)}, bf16[1024,2048]{1,0:T(8,128)(2,1)}, bf16[1024,128]{1,0:T(8,128)(2,1)}, bf16[1024,256]{1,0:T(8,128)(2,1)}, f32[128,768]{1,0:T(8,128)}, /*index=5*/f32[256,1536]{1,0:T(8,128)}) custom-call(s32[1]{0:T(128)} %bitcast.1.mine_ref.refs_0_.refs_1_, s32[1]{0:T(128)} %bitcast.refs_0_.refs_2_.refs_1_, ...), custom_call_target="tpu_custom_call" | custom-call | flops 32999999488 | tf_op jit(solution)/shard_map/pallas_call | solution.py:847
  350.2 30.1 %shard_map.282 = (bf16[1024,2048]{1,0:T(8,128)(2,1)}, bf16[1024,2048]{1,0:T(8,128)(2,1)}, bf16[1024,128]{1,0:T(8,128)(2,1)}, bf16[1024,256]{1,0:T(8,128)(2,1)}, f32[128,768]{1,0:T(8,128)}, /*index=5*/f32[256,1536]{1,0:T(8,128)}) custom-call(s32[1]{0:T(128)} %bitcast.1.mine_ref.refs_0_.refs_1_, s32[1]{0:T(128)} %bitcast.refs_0_.refs_2_.refs_1_, ...), custom_call_target="tpu_custom_call" | custom-call | flops 32999999488 | tf_op jit(solution)/shard_map/pallas_call | solution.py:847
  380.4 2.9 add_convert_fusion.10
  383.3 1.5 collective-permute-start.46
  387.4 10.7 %collective-permute-done.46 = bf16[128,2048]{1,0:T(8,128)(2,1)S(1)} collective-permute-done((bf16[128,2048]{1,0:T(8,128)(2,1)S(1)}, bf16[128,2048]{1,0:T(8,128)(2,1)S(1)}, u32[]{:S(2)}, u32[]{:S(2)}) %collective-permute-start.46) | collective-permute-done | bytes 524320 | tf_op jit(solution)/shard_map/ppermute | solution.py:1083
  399.7 2.0 add_convert_fusion.11
  404.6 4.8 collective-permute-done.43.refs_11_
  410.9 8.9 %collective-permute-done.45.refs_12_ = bf16[128,2048]{1,0:T(8,128)(2,1)S(1)} collective-permute-done((bf16[128,2048]{1,0:T(8,128)(2,1)S(1)}, bf16[128,2048]{1,0:T(8,128)(2,1)S(1)}, u32[]{:S(2)}, u32[]{:S(2)}) %collective-permute-start.45) | collective-permute-done | bytes 524320 | tf_op jit(solution)/shard_map/ppermute | solution.py:1083
  421.8 10.9 %shard_map.284 = (bf16[8,272,256]{2,1,0:T(8,128)(2,1)}, f32[256,2048]{1,0:T(8,128)}, bf16[256,128]{1,0:T(8,128)(2,1)}, f32[2048,128]{1,0:T(8,128)}) custom-call(s32[1]{0:T(128)} %bitcast.1.mine_ref.refs_0_.refs_1_, bf16[8,272,256]{2,1,0:T(8,128)(2,1)} %copy-done.7, bf16[256,2048]{1,0:T(8,128)(2,1)} %bitcast.121, f32[256,2048]{1,0:T(8,128)} %get-tuple-element.129.refs_3_, ...), custom_call_target="tpu_custom_call" | custom-call | flops 12000000000 | tf_op jit(solution)/shard_map/pallas_call | solution.py:626
  432.7 5.1 all-to-all-start.1
  439.6 5.8 add_convert_fusion.1
  445.5 1.5 collective-permute-start.49
  449.1 4.0 all-to-all-done.1.came_ref
  453.1 46.5 %shard_map.285 = (bf16[2048,1024]{1,0:T(8,128)(2,1)}, bf16[2048,256]{1,0:T(8,128)(2,1)}, bf16[2048,128]{1,0:T(8,128)(2,1)}, f32[1024,128]{1,0:T(8,128)}) custom-call(s32[4]{0:T(128)} %bitcast.163, s32[1]{0:T(128)} %bitcast.1.mine_ref.refs_0_.refs_1_, s32[1,2048]{1,0:T(1,128)} %bitcast.148, s32[2048,1]{1,0:T(8,128)} %copy.58.refs_18_.order_column_ref, ...), custom_call_target="tpu_custom_call" | custom-call | flops 51000000512 | tf_op jit(solution)/shard_map/pallas_call | solution.py:463
  502.5 9.5 %shard_map.287 = bf16[1024,2048]{1,0:T(8,128)(2,1)} custom-call(s32[1]{0:T(128)} %bitcast.refs_0_.refs_2_.refs_1_, bf16[320,2048]{1,0:T(8,128)(2,1)} %shard_map.276.refs_1_.refs_11_, bf16[320,2048]{1,0:T(8,128)(2,1)} %collective-permute-done.refs_2_.refs_12_, bf16[320,2048]{1,0:T(8,128)(2,1)} %collective-permute-done.1.refs_3_.refs_13_, ...), custom_call_target="tpu_custom_call" | custom-call | flops 8000000000 | tf_op jit(solution)/shard_map/pallas_call | solution.py:894
  512.2 5.0 all-to-all-start.2
  517.2 9.5 %shard_map.286.refs_5_ = bf16[1024,2048]{1,0:T(8,128)(2,1)} custom-call(s32[1]{0:T(128)} %bitcast.refs_0_.refs_2_.refs_1_, bf16[320,2048]{1,0:T(8,128)(2,1)} %shard_map.276.refs_1_.refs_11_, bf16[320,2048]{1,0:T(8,128)(2,1)} %collective-permute-done.refs_2_.refs_12_, bf16[320,2048]{1,0:T(8,128)(2,1)} %collective-permute-done.1.refs_3_.refs_13_, ...), custom_call_target="tpu_custom_call" | custom-call | flops 8000000000 | tf_op jit(solution)/shard_map/pallas_call | solution.py:894
  526.7 4.1 add_convert_fusion.6
  533.0 1.9 collective-permute-start.56
  534.9 4.6 add_convert_fusion
  540.8 4.5 all-to-all-start.3
  547.4 9.7 %collective-permute-done.55.refs_7_ = bf16[128,2048]{1,0:T(8,128)(2,1)} collective-permute-done((bf16[128,2048]{1,0:T(8,128)(2,1)S(1)}, bf16[128,2048]{1,0:T(8,128)(2,1)}, u32[]{:S(2)}, u32[]{:S(2)}) %collective-permute-start.55) | collective-permute-done | bytes 524320 | tf_op jit(solution)/shard_map/ppermute | solution.py:1083
  557.2 3.0 collective-permute-done.56.refs_10_
  560.2 3.2 add_convert_fusion.4
  567.7 2.6 fusion.13
  576.3 4.4 all-to-all-start.4
  581.9 1.9 collective-permute-start.60
  583.8 7.7 %collective-permute-start.61 = (f32[176,128]{1,0:T(8,128)S(1)}, f32[176,128]{1,0:T(8,128)S(1)}, u32[]{:S(2)}, u32[]{:S(2)}) collective-permute-start(f32[176,128]{1,0:T(8,128)S(1)} %slice.343), channel_id=1, source_target_pairs={{0,0},{1,1},{2,16},{3,17},{4,2},{5,3},{6,18},{7,19},{8,4},{9,5},{1... | collective-permute-start | bytes 270344 | tf_op jit(solution)/shard_map/ppermute | solution.py:1185
  591.6 18.5 %collective-permute-done.61 = f32[176,128]{1,0:T(8,128)S(1)} collective-permute-done((f32[176,128]{1,0:T(8,128)S(1)}, f32[176,128]{1,0:T(8,128)S(1)}, u32[]{:S(2)}, u32[]{:S(2)}) %collective-permute-start.61) | collective-permute-done | bytes 90144 | tf_op jit(solution)/shard_map/ppermute | solution.py:1185
  612.7 6.3 shard_map.288
  619.8 1.9 collective-permute-start.59
  623.1 5.4 collective-permute-done.59
  (304 shorter events, 89.0 us)
Async XLA Ops:
  10.2 32.0 %collective-permute-start = (bf16[320,2048]{1,0:T(8,128)(2,1)}, bf16[320,2048]{1,0:T(8,128)(2,1)}, u32[]{:S(2)}, u32[]{:S(2)}) collective-permute-start(bf16[320,2048]{1,0:T(8,128)(2,1)} %shard_map.276.refs_1_.refs_11_), channel_id=1, source_target_pairs={{0,1},{1,2},{2,3},{4,5},{5,6},{6,7},{8,9},{9,10},{10,11},{12,13},{... | collective-permute-start | bytes 3932168 | tf_op jit(solution)/shard_map/ppermute | solution.py:1155
  14.9 32.4 %collective-permute-start.1 = (bf16[320,2048]{1,0:T(8,128)(2,1)}, bf16[320,2048]{1,0:T(8,128)(2,1)}, u32[]{:S(2)}, u32[]{:S(2)}) collective-permute-start(bf16[320,2048]{1,0:T(8,128)(2,1)} %shard_map.276.refs_1_.refs_11_), channel_id=1, source_target_pairs={{1,0},{2,1},{3,2},{5,4},{6,5},{7,6},{9,8},{10,9},{11,10},{13,12},{... | collective-permute-start | bytes 3932168 | tf_op jit(solution)/shard_map/ppermute | solution.py:1155
  18.5 47.4 %collective-permute-start.5 = (bf16[512,2048]{1,0:T(8,128)(2,1)}, bf16[512,2048]{1,0:T(8,128)(2,1)}, u32[]{:S(2)}, u32[]{:S(2)}) collective-permute-start(bf16[512,2048]{1,0:T(8,128)(2,1)} %pad_maximum_fusion.refs_3_.refs_2_), channel_id=1, source_target_pairs={{0,8},{4,12},{8,0},{12,4},{16,24},{20,28},{24,16},{28,20},{1,9},{5... | collective-permute-start | bytes 6291464 | tf_op jit(solution)/shard_map/ppermute | solution.py:1083
  20.0 47.1 %collective-permute-start.6 = (bf16[512,2048]{1,0:T(8,128)(2,1)}, bf16[512,2048]{1,0:T(8,128)(2,1)}, u32[]{:S(2)}, u32[]{:S(2)}) collective-permute-start(bf16[512,2048]{1,0:T(8,128)(2,1)} %pad_maximum_fusion.refs_3_.refs_2_), channel_id=1, source_target_pairs={{0,16},{4,20},{8,24},{12,28},{16,0},{20,4},{24,8},{28,12},{1,17},{... | collective-permute-start | bytes 6291464 | tf_op jit(solution)/shard_map/ppermute | solution.py:1083
  20.5 99.9 %collective-permute-start.8 = (bf16[512,2048]{1,0:T(8,128)(2,1)}, bf16[512,2048]{1,0:T(8,128)(2,1)}, u32[]{:S(2)}, u32[]{:S(2)}) collective-permute-start(bf16[512,2048]{1,0:T(8,128)(2,1)} %pad_maximum_fusion.refs_3_.refs_2_), channel_id=1, source_target_pairs={{0,4},{4,0},{8,12},{12,8},{16,20},{20,16},{24,28},{28,24},{1,5},{5... | collective-permute-start | bytes 6291464 | tf_op jit(solution)/shard_map/ppermute | solution.py:1083
  50.3 18.7 %collective-permute-start.2 = (bf16[320,2048]{1,0:T(8,128)(2,1)}, bf16[320,2048]{1,0:T(8,128)(2,1)S(1)}, u32[]{:S(2)}, u32[]{:S(2)}) collective-permute-start(bf16[320,2048]{1,0:T(8,128)(2,1)} %get-tuple-element.230), channel_id=1, source_target_pairs={{1,2},{2,1},{5,6},{6,5},{9,10},{10,9},{13,14},{14,13},{17,18},{18,... | collective-permute-start | bytes 3932168 | tf_op jit(solution)/shard_map/ppermute | solution.py:1155
  53.2 31.9 %collective-permute-start.3 = (bf16[320,2048]{1,0:T(8,128)(2,1)S(1)}, bf16[320,2048]{1,0:T(8,128)(2,1)}, u32[]{:S(2)}, u32[]{:S(2)}) collective-permute-start(bf16[320,2048]{1,0:T(8,128)(2,1)S(1)} %get-tuple-element.229), channel_id=1, source_target_pairs={{2,3},{1,0},{6,7},{5,4},{10,11},{9,8},{14,15},{13,12},{18,19},{17,... | collective-permute-start | bytes 3932168 | tf_op jit(solution)/shard_map/ppermute | solution.py:1155
  68.4 52.5 %collective-permute-start.9 = (bf16[512,2048]{1,0:T(8,128)(2,1)}, bf16[512,2048]{1,0:T(8,128)(2,1)}, u32[]{:S(2)}, u32[]{:S(2)}) collective-permute-start(bf16[512,2048]{1,0:T(8,128)(2,1)} %collective-permute-done.5.refs_4_.refs_3_), channel_id=1, source_target_pairs={{0,4},{4,0},{8,12},{12,8},{16,20},{20,16},{24,28},{28,24},{1,5},{5... | collective-permute-start | bytes 6291464 | tf_op jit(solution)/shard_map/ppermute | solution.py:1083
  68.5 53.9 %collective-permute-start.10 = (bf16[512,2048]{1,0:T(8,128)(2,1)}, bf16[512,2048]{1,0:T(8,128)(2,1)}, u32[]{:S(2)}, u32[]{:S(2)}) collective-permute-start(bf16[512,2048]{1,0:T(8,128)(2,1)} %collective-permute-done.6.refs_5_.refs_4_), channel_id=1, source_target_pairs={{0,4},{4,0},{8,12},{12,8},{16,20},{20,16},{24,28},{28,24},{1,5},{5... | collective-permute-start | bytes 6291464 | tf_op jit(solution)/shard_map/ppermute | solution.py:1083
  69.0 25.2 %collective-permute-start.7 = (bf16[256,2048]{1,0:T(8,128)(2,1)S(1)}, bf16[256,2048]{1,0:T(8,128)(2,1)}, u32[]{:S(2)}, u32[]{:S(2)}) collective-permute-start(bf16[256,2048]{1,0:T(8,128)(2,1)S(1)} %slice.272), channel_id=1, source_target_pairs={{0,16},{4,20},{8,24},{12,28},{16,0},{20,4},{24,8},{28,12},{1,17},{... | collective-permute-start | bytes 3145736 | tf_op jit(solution)/shard_map/ppermute | solution.py:1083
  85.1 31.5 %collective-permute-start.4 = (bf16[320,2048]{1,0:T(8,128)(2,1)}, bf16[320,2048]{1,0:T(8,128)(2,1)}, u32[]{:S(2)}, u32[]{:S(2)}) collective-permute-start(bf16[320,2048]{1,0:T(8,128)(2,1)} %get-tuple-element.230), channel_id=1, source_target_pairs={{1,3},{2,0},{5,7},{6,4},{9,11},{10,8},{13,15},{14,12},{17,19},{18,... | collective-permute-start | bytes 3932168 | tf_op jit(solution)/shard_map/ppermute | solution.py:1155
  94.2 30.8 %collective-permute-start.11 = (bf16[256,2048]{1,0:T(8,128)(2,1)}, bf16[256,2048]{1,0:T(8,128)(2,1)}, u32[]{:S(2)}, u32[]{:S(2)}) collective-permute-start(bf16[256,2048]{1,0:T(8,128)(2,1)} %collective-permute-done.7.refs_6_), channel_id=1, source_target_pairs={{0,4},{4,0},{8,12},{12,8},{16,20},{20,16},{24,28},{28,24},{1,5},{5... | collective-permute-start | bytes 3145736 | tf_op jit(solution)/shard_map/ppermute | solution.py:1083
  118.8 59.7 %collective-permute-start.12 = (bf16[256,2048]{1,0:T(8,128)(2,1)}, bf16[256,2048]{1,0:T(8,128)(2,1)}, u32[]{:S(2)}, u32[]{:S(2)}) collective-permute-start(bf16[256,2048]{1,0:T(8,128)(2,1)} %shard_map.278.refs_7_.refs_15_), channel_id=1, source_target_pairs={{0,8},{4,12},{8,0},{12,4},{16,24},{20,28},{24,16},{28,20},{1,9},{5... | collective-permute-start | bytes 3145736 | tf_op jit(solution)/shard_map/ppermute | solution.py:1083
  120.4 58.3 %collective-permute-start.13 = (bf16[256,2048]{1,0:T(8,128)(2,1)}, bf16[256,2048]{1,0:T(8,128)(2,1)}, u32[]{:S(2)}, u32[]{:S(2)}) collective-permute-start(bf16[256,2048]{1,0:T(8,128)(2,1)} %shard_map.278.refs_7_.refs_15_), channel_id=1, source_target_pairs={{0,16},{4,20},{8,24},{12,28},{16,0},{20,4},{24,8},{28,12},{1,17},{... | collective-permute-start | bytes 3145736 | tf_op jit(solution)/shard_map/ppermute | solution.py:1083
  120.9 57.8 %collective-permute-start.14 = (bf16[256,2048]{1,0:T(8,128)(2,1)}, bf16[256,2048]{1,0:T(8,128)(2,1)}, u32[]{:S(2)}, u32[]{:S(2)}) collective-permute-start(bf16[256,2048]{1,0:T(8,128)(2,1)} %shard_map.278.refs_7_.refs_15_), channel_id=1, source_target_pairs={{0,24},{4,28},{8,16},{12,20},{16,8},{20,12},{24,0},{28,4},{1,25},{... | collective-permute-start | bytes 3145736 | tf_op jit(solution)/shard_map/ppermute | solution.py:1083
  122.4 56.3 %collective-permute-start.15 = (bf16[528,2048]{1,0:T(8,128)(2,1)}, bf16[528,2048]{1,0:T(8,128)(2,1)}, u32[]{:S(2)}, u32[]{:S(2)}) collective-permute-start(bf16[528,2048]{1,0:T(8,128)(2,1)} %shard_map.277.refs_12_.refs_18_.refs_6_), channel_id=1, source_target_pairs={{0,1},{1,2},{2,3},{4,5},{5,6},{6,7},{8,9},{9,10},{10,11},{12,13},{... | collective-permute-start | bytes 6488072 | tf_op jit(solution)/shard_map/ppermute | solution.py:1155
  125.0 53.7 %collective-permute-start.16 = (bf16[528,2048]{1,0:T(8,128)(2,1)}, bf16[528,2048]{1,0:T(8,128)(2,1)}, u32[]{:S(2)}, u32[]{:S(2)}) collective-permute-start(bf16[528,2048]{1,0:T(8,128)(2,1)} %shard_map.277.refs_12_.refs_18_.refs_6_), channel_id=1, source_target_pairs={{1,0},{2,1},{3,2},{5,4},{6,5},{7,6},{9,8},{10,9},{11,10},{13,12},{... | collective-permute-start | bytes 6488072 | tf_op jit(solution)/shard_map/ppermute | solution.py:1155
  178.7 11.5 %collective-permute-start.18 = (bf16[256,2048]{1,0:T(8,128)(2,1)}, bf16[256,2048]{1,0:T(8,128)(2,1)}, u32[]{:S(2)}, u32[]{:S(2)}) collective-permute-start(bf16[256,2048]{1,0:T(8,128)(2,1)} %collective-permute-done.12.refs_8_.refs_16_), channel_id=1, source_target_pairs={{0,4},{4,0},{8,12},{12,8},{16,20},{20,16},{24,28},{28,24},{1,5},{5... | collective-permute-start | bytes 3145736 | tf_op jit(solution)/shard_map/ppermute | solution.py:1083
  179.2 19.4 %collective-permute-start.19 = (bf16[256,2048]{1,0:T(8,128)(2,1)}, bf16[256,2048]{1,0:T(8,128)(2,1)}, u32[]{:S(2)}, u32[]{:S(2)}) collective-permute-start(bf16[256,2048]{1,0:T(8,128)(2,1)} %collective-permute-done.13.refs_9_.refs_17_), channel_id=1, source_target_pairs={{0,4},{4,0},{8,12},{12,8},{16,20},{20,16},{24,28},{28,24},{1,5},{5... | collective-permute-start | bytes 3145736 | tf_op jit(solution)/shard_map/ppermute | solution.py:1083
  179.3 19.3 %collective-permute-start.20 = (bf16[256,2048]{1,0:T(8,128)(2,1)}, bf16[256,2048]{1,0:T(8,128)(2,1)}, u32[]{:S(2)}, u32[]{:S(2)}) collective-permute-start(bf16[256,2048]{1,0:T(8,128)(2,1)} %collective-permute-done.14.refs_10_.refs_18_), channel_id=1, source_target_pairs={{0,4},{4,0},{8,12},{12,8},{16,20},{20,16},{24,28},{28,24},{1,5},{5... | collective-permute-start | bytes 3145736 | tf_op jit(solution)/shard_map/ppermute | solution.py:1083
  179.7 18.9 %all-to-all-start = ((bf16[8,272,256]{2,1,0:T(8,128)(2,1)}), bf16[8,272,256]{2,1,0:T(8,128)(2,1)S(1)}, u32[]{:S(2)}, u32[]{:S(2)}) async-start(bf16[8,272,256]{2,1,0:T(8,128)(2,1)} %get-tuple-element.125), calls=%async_computation | async-start | bytes 2228224 | tf_op jit(solution)/shard_map/all_to_all | solution.py:1151
  187.4 21.9 %collective-permute-start.22 = (bf16[112,2048]{1,0:T(8,128)(2,1)S(1)}, bf16[112,2048]{1,0:T(8,128)(2,1)}, u32[]{:S(2)}, u32[]{:S(2)}) collective-permute-start(bf16[112,2048]{1,0:T(8,128)(2,1)S(1)} %get-tuple-element.226), channel_id=1, source_target_pairs={{1,2},{2,1},{5,6},{6,5},{9,10},{10,9},{13,14},{14,13},{17,18},{18,... | collective-permute-start | bytes 1376264 | tf_op jit(solution)/shard_map/ppermute | solution.py:1155
  188.9 29.8 %collective-permute-start.24 = (bf16[112,2048]{1,0:T(8,128)(2,1)S(1)}, bf16[112,2048]{1,0:T(8,128)(2,1)}, u32[]{:S(2)}, u32[]{:S(2)}) collective-permute-start(bf16[112,2048]{1,0:T(8,128)(2,1)S(1)} %get-tuple-element.226), channel_id=1, source_target_pairs={{1,3},{2,0},{5,7},{6,4},{9,11},{10,8},{13,15},{14,12},{17,19},{18,... | collective-permute-start | bytes 1376264 | tf_op jit(solution)/shard_map/ppermute | solution.py:1155
  190.2 28.5 %collective-permute-start.23 = (bf16[112,2048]{1,0:T(8,128)(2,1)}, bf16[112,2048]{1,0:T(8,128)(2,1)}, u32[]{:S(2)}, u32[]{:S(2)}) collective-permute-start(bf16[112,2048]{1,0:T(8,128)(2,1)} %get-tuple-element.225), channel_id=1, source_target_pairs={{2,3},{1,0},{6,7},{5,4},{10,11},{9,8},{14,15},{13,12},{18,19},{17,... | collective-permute-start | bytes 1376264 | tf_op jit(solution)/shard_map/ppermute | solution.py:1155
  218.7 26.3 %collective-permute-start.28 = (bf16[256,2048]{1,0:T(8,128)(2,1)}, bf16[256,2048]{1,0:T(8,128)(2,1)S(1)}, u32[]{:S(2)}, u32[]{:S(2)}) collective-permute-start(bf16[256,2048]{1,0:T(8,128)(2,1)} %get-tuple-element.139.refs_2_), channel_id=1, source_target_pairs={{0,8},{4,12},{8,0},{12,4},{16,24},{20,28},{24,16},{28,20},{1,9},{5... | collective-permute-start | bytes 3145736 | tf_op jit(solution)/shard_map/ppermute | solution.py:1083
  221.5 44.4 %collective-permute-start.21 = (bf16[256,2048]{1,0:T(8,128)(2,1)S(1)}, bf16[256,2048]{1,0:T(8,128)(2,1)}, u32[]{:S(2)}, u32[]{:S(2)}) collective-permute-start(bf16[256,2048]{1,0:T(8,128)(2,1)S(1)} %slice.274), channel_id=1, source_target_pairs={{0,8},{4,12},{8,0},{12,4},{16,24},{20,28},{24,16},{28,20},{1,9},{5... | collective-permute-start | bytes 3145736 | tf_op jit(solution)/shard_map/ppermute | solution.py:1083
  222.1 24.3 %collective-permute-start.29 = (bf16[256,2048]{1,0:T(8,128)(2,1)S(1)}, bf16[256,2048]{1,0:T(8,128)(2,1)S(1)}, u32[]{:S(2)}, u32[]{:S(2)}) collective-permute-start(bf16[256,2048]{1,0:T(8,128)(2,1)S(1)} %copy-done.36), channel_id=1, source_target_pairs={{0,16},{4,20},{8,24},{12,28},{16,0},{20,4},{24,8},{28,12},{1,17},{... | collective-permute-start | bytes 3145736 | tf_op jit(solution)/shard_map/ppermute | solution.py:1083
  224.1 43.3 %collective-permute-start.25 = (bf16[240,2048]{1,0:T(8,128)(2,1)S(1)}, bf16[240,2048]{1,0:T(8,128)(2,1)S(1)}, u32[]{:S(2)}, u32[]{:S(2)}) collective-permute-start(bf16[240,2048]{1,0:T(8,128)(2,1)S(1)} %get-tuple-element.224), channel_id=1, source_target_pairs={{1,2},{2,1},{5,6},{6,5},{9,10},{10,9},{13,14},{14,13},{17,18},{18,... | collective-permute-start | bytes 2949128 | tf_op jit(solution)/shard_map/ppermute | solution.py:1155
  224.8 45.6 %collective-permute-start.26 = (bf16[240,2048]{1,0:T(8,128)(2,1)S(1)}, bf16[240,2048]{1,0:T(8,128)(2,1)}, u32[]{:S(2)}, u32[]{:S(2)}) collective-permute-start(bf16[240,2048]{1,0:T(8,128)(2,1)S(1)} %get-tuple-element.223), channel_id=1, source_target_pairs={{2,3},{1,0},{6,7},{5,4},{10,11},{9,8},{14,15},{13,12},{18,19},{17,... | collective-permute-start | bytes 2949128 | tf_op jit(solution)/shard_map/ppermute | solution.py:1155
  245.0 25.4 %collective-permute-start.27 = (bf16[240,2048]{1,0:T(8,128)(2,1)S(1)}, bf16[240,2048]{1,0:T(8,128)(2,1)}, u32[]{:S(2)}, u32[]{:S(2)}) collective-permute-start(bf16[240,2048]{1,0:T(8,128)(2,1)S(1)} %get-tuple-element.224), channel_id=1, source_target_pairs={{1,3},{2,0},{5,7},{6,4},{9,11},{10,8},{13,15},{14,12},{17,19},{18,... | collective-permute-start | bytes 2949128 | tf_op jit(solution)/shard_map/ppermute | solution.py:1155
  246.4 24.6 %collective-permute-start.30 = (bf16[128,2048]{1,0:T(8,128)(2,1)S(1)}, bf16[128,2048]{1,0:T(8,128)(2,1)S(1)}, u32[]{:S(2)}, u32[]{:S(2)}) collective-permute-start(bf16[128,2048]{1,0:T(8,128)(2,1)S(1)} %slice.348), channel_id=1, source_target_pairs={{0,16},{4,20},{8,24},{12,28},{16,0},{20,4},{24,8},{28,12},{1,17},{... | collective-permute-start | bytes 1572872 | tf_op jit(solution)/shard_map/ppermute | solution.py:1083
  265.9 12.2 %collective-permute-start.31 = (bf16[128,2048]{1,0:T(8,128)(2,1)S(1)}, bf16[128,2048]{1,0:T(8,128)(2,1)S(1)}, u32[]{:S(2)}, u32[]{:S(2)}) collective-permute-start(bf16[128,2048]{1,0:T(8,128)(2,1)S(1)} %slice.349), channel_id=1, source_target_pairs={{0,8},{4,12},{8,0},{12,4},{16,24},{20,28},{24,16},{28,20},{1,9},{5... | collective-permute-start | bytes 1572872 | tf_op jit(solution)/shard_map/ppermute | solution.py:1083
  267.3 13.0 %collective-permute-start.32 = (bf16[256,2048]{1,0:T(8,128)(2,1)S(1)}, bf16[256,2048]{1,0:T(8,128)(2,1)S(1)}, u32[]{:S(2)}, u32[]{:S(2)}) collective-permute-start(bf16[256,2048]{1,0:T(8,128)(2,1)S(1)} %copy-done.36), channel_id=1, source_target_pairs={{0,4},{4,0},{8,12},{12,8},{16,20},{20,16},{24,28},{28,24},{1,5},{5... | collective-permute-start | bytes 3145736 | tf_op jit(solution)/shard_map/ppermute | solution.py:1083
  270.4 12.1 %collective-permute-start.34 = (bf16[256,2048]{1,0:T(8,128)(2,1)S(1)}, bf16[256,2048]{1,0:T(8,128)(2,1)S(1)}, u32[]{:S(2)}, u32[]{:S(2)}) collective-permute-start(bf16[256,2048]{1,0:T(8,128)(2,1)S(1)} %collective-permute-done.29.refs_4_), channel_id=1, source_target_pairs={{0,4},{4,0},{8,12},{12,8},{16,20},{20,16},{24,28},{28,24},{1,5},{5... | collective-permute-start | bytes 3145736 | tf_op jit(solution)/shard_map/ppermute | solution.py:1083
  271.0 12.8 %collective-permute-start.35 = (bf16[128,2048]{1,0:T(8,128)(2,1)S(1)}, bf16[128,2048]{1,0:T(8,128)(2,1)S(1)}, u32[]{:S(2)}, u32[]{:S(2)}) collective-permute-start(bf16[128,2048]{1,0:T(8,128)(2,1)S(1)} %collective-permute-done.30.refs_5_), channel_id=1, source_target_pairs={{0,4},{4,0},{8,12},{12,8},{16,20},{20,16},{24,28},{28,24},{1,5},{5... | collective-permute-start | bytes 1572872 | tf_op jit(solution)/shard_map/ppermute | solution.py:1083
  280.4 39.1 %collective-permute-start.40 = (bf16[256,2048]{1,0:T(8,128)(2,1)}, bf16[256,2048]{1,0:T(8,128)(2,1)}, u32[]{:S(2)}, u32[]{:S(2)}) collective-permute-start(bf16[256,2048]{1,0:T(8,128)(2,1)} %collective-permute-done.21.refs_5_), channel_id=1, source_target_pairs={{0,4},{4,0},{8,12},{12,8},{16,20},{20,16},{24,28},{28,24},{1,5},{5... | collective-permute-start | bytes 3145736 | tf_op jit(solution)/shard_map/ppermute | solution.py:1083
  280.9 30.7 %collective-permute-start.37 = (bf16[176,2048]{1,0:T(8,128)(2,1)S(1)}, bf16[176,2048]{1,0:T(8,128)(2,1)}, u32[]{:S(2)}, u32[]{:S(2)}) collective-permute-start(bf16[176,2048]{1,0:T(8,128)(2,1)S(1)} %get-tuple-element.222), channel_id=1, source_target_pairs={{1,2},{2,1},{5,6},{6,5},{9,10},{10,9},{13,14},{14,13},{17,18},{18,... | collective-permute-start | bytes 2162696 | tf_op jit(solution)/shard_map/ppermute | solution.py:1155
  282.5 36.9 %collective-permute-start.39 = (bf16[176,2048]{1,0:T(8,128)(2,1)S(1)}, bf16[176,2048]{1,0:T(8,128)(2,1)}, u32[]{:S(2)}, u32[]{:S(2)}) collective-permute-start(bf16[176,2048]{1,0:T(8,128)(2,1)S(1)} %get-tuple-element.222), channel_id=1, source_target_pairs={{1,3},{2,0},{5,7},{6,4},{9,11},{10,8},{13,15},{14,12},{17,19},{18,... | collective-permute-start | bytes 2162696 | tf_op jit(solution)/shard_map/ppermute | solution.py:1155
  283.8 35.6 %collective-permute-start.38 = (bf16[176,2048]{1,0:T(8,128)(2,1)S(1)}, bf16[176,2048]{1,0:T(8,128)(2,1)}, u32[]{:S(2)}, u32[]{:S(2)}) collective-permute-start(bf16[176,2048]{1,0:T(8,128)(2,1)S(1)} %get-tuple-element.221), channel_id=1, source_target_pairs={{2,3},{1,0},{6,7},{5,4},{10,11},{9,8},{14,15},{13,12},{18,19},{17,... | collective-permute-start | bytes 2162696 | tf_op jit(solution)/shard_map/ppermute | solution.py:1155
  349.7 30.7 %collective-permute-start.41 = (bf16[1024,2048]{1,0:T(8,128)(2,1)}, bf16[1024,2048]{1,0:T(8,128)(2,1)}, u32[]{:S(2)}, u32[]{:S(2)}) collective-permute-start(bf16[1024,2048]{1,0:T(8,128)(2,1)} %get-tuple-element.154), channel_id=1, source_target_pairs={{0,4},{4,0},{8,12},{12,8},{16,20},{20,16},{24,28},{28,24},{1,5},{5... | collective-permute-start | bytes 12582920 | tf_op jit(solution)/shard_map/ppermute | solution.py:1083
  349.7 30.6 %collective-permute-start.42 = (bf16[1024,2048]{1,0:T(8,128)(2,1)}, bf16[1024,2048]{1,0:T(8,128)(2,1)}, u32[]{:S(2)}, u32[]{:S(2)}) collective-permute-start(bf16[1024,2048]{1,0:T(8,128)(2,1)} %get-tuple-element.155), channel_id=1, source_target_pairs={{0,4},{4,0},{8,12},{12,8},{16,20},{20,16},{24,28},{28,24},{1,5},{5... | collective-permute-start | bytes 12582920 | tf_op jit(solution)/shard_map/ppermute | solution.py:1083
  383.3 14.8 %collective-permute-start.46 = (bf16[128,2048]{1,0:T(8,128)(2,1)S(1)}, bf16[128,2048]{1,0:T(8,128)(2,1)S(1)}, u32[]{:S(2)}, u32[]{:S(2)}) collective-permute-start(bf16[128,2048]{1,0:T(8,128)(2,1)S(1)} %get-tuple-element.216), channel_id=1, source_target_pairs={{0,8},{4,12},{8,0},{12,4},{16,24},{20,28},{24,16},{28,20},{1,9},{5... | collective-permute-start | bytes 1572872 | tf_op jit(solution)/shard_map/ppermute | solution.py:1083
  384.9 14.8 %collective-permute-start.44 = (bf16[128,2048]{1,0:T(8,128)(2,1)S(1)}, bf16[128,2048]{1,0:T(8,128)(2,1)S(1)}, u32[]{:S(2)}, u32[]{:S(2)}) collective-permute-start(bf16[128,2048]{1,0:T(8,128)(2,1)S(1)} %get-tuple-element.217), channel_id=1, source_target_pairs={{0,16},{4,20},{8,24},{12,28},{16,0},{20,4},{24,8},{28,12},{1,17},{... | collective-permute-start | bytes 1572872 | tf_op jit(solution)/shard_map/ppermute | solution.py:1083
  385.4 24.0 %collective-permute-start.43 = (bf16[128,2048]{1,0:T(8,128)(2,1)S(1)}, bf16[128,2048]{1,0:T(8,128)(2,1)S(1)}, u32[]{:S(2)}, u32[]{:S(2)}) collective-permute-start(bf16[128,2048]{1,0:T(8,128)(2,1)S(1)} %get-tuple-element.218), channel_id=1, source_target_pairs={{0,8},{4,12},{8,0},{12,4},{16,24},{20,28},{24,16},{28,20},{1,9},{5... | collective-permute-start | bytes 1572872 | tf_op jit(solution)/shard_map/ppermute | solution.py:1083
  386.6 24.3 %collective-permute-start.48 = (bf16[128,2048]{1,0:T(8,128)(2,1)S(1)}, bf16[128,2048]{1,0:T(8,128)(2,1)S(1)}, u32[]{:S(2)}, u32[]{:S(2)}) collective-permute-start(bf16[128,2048]{1,0:T(8,128)(2,1)S(1)} %get-tuple-element.215), channel_id=1, source_target_pairs={{0,16},{4,20},{8,24},{12,28},{16,0},{20,4},{24,8},{28,12},{1,17},{... | collective-permute-start | bytes 1572872 | tf_op jit(solution)/shard_map/ppermute | solution.py:1083
  401.7 18.1 %collective-permute-start.45 = (bf16[128,2048]{1,0:T(8,128)(2,1)S(1)}, bf16[128,2048]{1,0:T(8,128)(2,1)S(1)}, u32[]{:S(2)}, u32[]{:S(2)}) collective-permute-start(bf16[128,2048]{1,0:T(8,128)(2,1)S(1)} %get-tuple-element.220), channel_id=1, source_target_pairs={{0,8},{4,12},{8,0},{12,4},{16,24},{20,28},{24,16},{28,20},{1,9},{5... | collective-permute-start | bytes 1572872 | tf_op jit(solution)/shard_map/ppermute | solution.py:1083
  402.3 18.6 %collective-permute-start.47 = (bf16[128,2048]{1,0:T(8,128)(2,1)S(1)}, bf16[128,2048]{1,0:T(8,128)(2,1)S(1)}, u32[]{:S(2)}, u32[]{:S(2)}) collective-permute-start(bf16[128,2048]{1,0:T(8,128)(2,1)S(1)} %get-tuple-element.219), channel_id=1, source_target_pairs={{0,16},{4,20},{8,24},{12,28},{16,0},{20,4},{24,8},{28,12},{1,17},{... | collective-permute-start | bytes 1572872 | tf_op jit(solution)/shard_map/ppermute | solution.py:1083
  432.7 20.4 %all-to-all-start.1 = ((bf16[8,272,256]{2,1,0:T(8,128)(2,1)}), bf16[8,272,256]{2,1,0:T(8,128)(2,1)}, u32[]{:S(2)}, u32[]{:S(2)}) async-start(bf16[8,272,256]{2,1,0:T(8,128)(2,1)} %get-tuple-element.158), calls=%async_computation.1 | async-start | bytes 2228224 | tf_op jit(solution)/shard_map/all_to_all | solution.py:1151
  437.8 61.8 %reduce-scatter.2.cloned.1.call-start = ((), (), s32[]{:S(2)}) async-start(), calls=%async_computation.6 | async-start | bytes 1351680 | tf_op jit(solution)/shard_map/reduce_scatter | solution.py:1378
  445.5 54.1 %collective-permute-start.49 = (bf16[256,2048]{1,0:T(8,128)(2,1)}, bf16[256,2048]{1,0:T(8,128)(2,1)}, u32[]{:S(2)}, u32[]{:S(2)}) collective-permute-start(bf16[256,2048]{1,0:T(8,128)(2,1)} %get-tuple-element.171), channel_id=1, source_target_pairs={{0,8},{4,12},{8,0},{12,4},{16,24},{20,28},{24,16},{28,20},{1,9},{5... | collective-permute-start | bytes 3145736 | tf_op jit(solution)/shard_map/ppermute | solution.py:1083
  447.1 52.6 %collective-permute-start.50 = (bf16[256,2048]{1,0:T(8,128)(2,1)}, bf16[256,2048]{1,0:T(8,128)(2,1)}, u32[]{:S(2)}, u32[]{:S(2)}) collective-permute-start(bf16[256,2048]{1,0:T(8,128)(2,1)} %get-tuple-element.172), channel_id=1, source_target_pairs={{0,16},{4,20},{8,24},{12,28},{16,0},{20,4},{24,8},{28,12},{1,17},{... | collective-permute-start | bytes 3145736 | tf_op jit(solution)/shard_map/ppermute | solution.py:1083
  447.6 52.0 %collective-permute-start.51 = (bf16[256,2048]{1,0:T(8,128)(2,1)S(1)}, bf16[256,2048]{1,0:T(8,128)(2,1)}, u32[]{:S(2)}, u32[]{:S(2)}) collective-permute-start(bf16[256,2048]{1,0:T(8,128)(2,1)S(1)} %get-tuple-element.173), channel_id=1, source_target_pairs={{0,24},{4,28},{8,16},{12,20},{16,8},{20,12},{24,0},{28,4},{1,25},{... | collective-permute-start | bytes 3145736 | tf_op jit(solution)/shard_map/ppermute | solution.py:1083
  512.1 14.6 %collective-permute-start.52 = (bf16[1024,2048]{1,0:T(8,128)(2,1)}, bf16[1024,2048]{1,0:T(8,128)(2,1)}, u32[]{:S(2)}, u32[]{:S(2)}) collective-permute-start(bf16[1024,2048]{1,0:T(8,128)(2,1)} %shard_map.287), channel_id=1, source_target_pairs={{0,4},{4,0},{8,12},{12,8},{16,20},{20,16},{24,28},{28,24},{1,5},{5... | collective-permute-start | bytes 12582920 | tf_op jit(solution)/shard_map/ppermute | solution.py:1083
  512.2 27.2 %all-to-all-start.2 = ((bf16[8,256,256]{2,1,0:T(8,128)(2,1)}), bf16[8,256,256]{2,1,0:T(8,128)(2,1)S(1)}, u32[]{:S(2)}, u32[]{:S(2)}) async-start(bf16[8,256,256]{2,1,0:T(8,128)(2,1)} %pad_maximum_fusion.2), calls=%async_computation.3 | async-start | bytes 2097152 | tf_op jit(solution)/shard_map/all_to_all | solution.py:1151
  530.8 15.1 %collective-permute-start.53 = (bf16[128,2048]{1,0:T(8,128)(2,1)}, bf16[128,2048]{1,0:T(8,128)(2,1)}, u32[]{:S(2)}, u32[]{:S(2)}) collective-permute-start(bf16[128,2048]{1,0:T(8,128)(2,1)} %get-tuple-element.211), channel_id=1, source_target_pairs={{0,8},{4,12},{8,0},{12,4},{16,24},{20,28},{24,16},{28,20},{1,9},{5... | collective-permute-start | bytes 1572872 | tf_op jit(solution)/shard_map/ppermute | solution.py:1083
  532.3 15.1 %collective-permute-start.54 = (bf16[128,2048]{1,0:T(8,128)(2,1)}, bf16[128,2048]{1,0:T(8,128)(2,1)}, u32[]{:S(2)}, u32[]{:S(2)}) collective-permute-start(bf16[128,2048]{1,0:T(8,128)(2,1)} %get-tuple-element.210), channel_id=1, source_target_pairs={{0,16},{4,20},{8,24},{12,28},{16,0},{20,4},{24,8},{28,12},{1,17},{... | collective-permute-start | bytes 1572872 | tf_op jit(solution)/shard_map/ppermute | solution.py:1083
  532.9 24.3 %collective-permute-start.55 = (bf16[128,2048]{1,0:T(8,128)(2,1)S(1)}, bf16[128,2048]{1,0:T(8,128)(2,1)}, u32[]{:S(2)}, u32[]{:S(2)}) collective-permute-start(bf16[128,2048]{1,0:T(8,128)(2,1)S(1)} %get-tuple-element.209), channel_id=1, source_target_pairs={{0,8},{4,12},{8,0},{12,4},{16,24},{20,28},{24,16},{28,20},{1,9},{5... | collective-permute-start | bytes 1572872 | tf_op jit(solution)/shard_map/ppermute | solution.py:1083
  533.0 27.2 %collective-permute-start.56 = (bf16[128,2048]{1,0:T(8,128)(2,1)S(1)}, bf16[128,2048]{1,0:T(8,128)(2,1)}, u32[]{:S(2)}, u32[]{:S(2)}) collective-permute-start(bf16[128,2048]{1,0:T(8,128)(2,1)S(1)} %get-tuple-element.208), channel_id=1, source_target_pairs={{0,16},{4,20},{8,24},{12,28},{16,0},{20,4},{24,8},{28,12},{1,17},{... | collective-permute-start | bytes 1572872 | tf_op jit(solution)/shard_map/ppermute | solution.py:1083
  540.8 22.6 %all-to-all-start.3 = ((bf16[8,256,128]{2,1,0:T(8,128)(2,1)}), bf16[8,256,128]{2,1,0:T(8,128)(2,1)S(1)}, u32[]{:S(2)}, u32[]{:S(2)}) async-start(bf16[8,256,128]{2,1,0:T(8,128)(2,1)} %broadcast_in_dim.10), calls=%async_computation.4 | async-start | bytes 1048576 | tf_op jit(solution)/shard_map/all_to_all | solution.py:1151
  576.3 42.8 %all-to-all-start.4 = ((bf16[4,832,128]{2,1,0:T(8,128)(2,1)}), bf16[4,832,128]{2,1,0:T(8,128)(2,1)S(1)}, u32[]{:S(2)}, u32[]{:S(2)}) async-start(bf16[4,832,128]{2,1,0:T(8,128)(2,1)} %constant_dynamic-update-slice_fusion), calls=%async_computation.5 | async-start | bytes 1703936 | tf_op jit(solution)/shard_map/all_to_all | solution.py:1151
  580.7 30.4 %collective-permute-start.57 = (bf16[128,2048]{1,0:T(8,128)(2,1)S(1)}, bf16[128,2048]{1,0:T(8,128)(2,1)S(1)}, u32[]{:S(2)}, u32[]{:S(2)}) collective-permute-start(bf16[128,2048]{1,0:T(8,128)(2,1)S(1)} %copy-done.17), channel_id=1, source_target_pairs={{0,8},{4,12},{8,0},{12,4},{16,24},{20,28},{24,16},{28,20},{1,9},{5... | collective-permute-start | bytes 1572872 | tf_op jit(solution)/shard_map/ppermute | solution.py:1083
  581.8 29.3 %collective-permute-start.58 = (bf16[128,2048]{1,0:T(8,128)(2,1)S(1)}, bf16[128,2048]{1,0:T(8,128)(2,1)S(1)}, u32[]{:S(2)}, u32[]{:S(2)}) collective-permute-start(bf16[128,2048]{1,0:T(8,128)(2,1)S(1)} %get-tuple-element.196), channel_id=1, source_target_pairs={{0,16},{4,20},{8,24},{12,28},{16,0},{20,4},{24,8},{28,12},{1,17},{... | collective-permute-start | bytes 1572872 | tf_op jit(solution)/shard_map/ppermute | solution.py:1083
  581.9 28.2 %collective-permute-start.60 = (f32[352,128]{1,0:T(8,128)S(1)}, f32[352,128]{1,0:T(8,128)S(1)}, u32[]{:S(2)}, u32[]{:S(2)}) collective-permute-start(f32[352,128]{1,0:T(8,128)S(1)} %slice.342), channel_id=1, source_target_pairs={{0,0},{1,8},{2,16},{3,24},{4,1},{5,9},{6,17},{7,25},{8,2},{9,10},{... | collective-permute-start | bytes 540680 | tf_op jit(solution)/shard_map/ppermute | solution.py:1185
  583.8 26.2 %collective-permute-start.61 = (f32[176,128]{1,0:T(8,128)S(1)}, f32[176,128]{1,0:T(8,128)S(1)}, u32[]{:S(2)}, u32[]{:S(2)}) collective-permute-start(f32[176,128]{1,0:T(8,128)S(1)} %slice.343), channel_id=1, source_target_pairs={{0,0},{1,1},{2,16},{3,17},{4,2},{5,3},{6,18},{7,19},{8,4},{9,5},{1... | collective-permute-start | bytes 270344 | tf_op jit(solution)/shard_map/ppermute | solution.py:1185
  (58 other events, 680.3 us)
Sparse Core Ops, SparseCore 0:
  441.0 28.3 reduce-scatter.1

commit v4 on v3

--- a/solution.py
+++ b/solution.py
@@ -248,9 +248,13 @@
     win_refs, refs = refs[: len(win_pieces)], refs[len(win_pieces) :]
     (
         order_row_ref, order_column_ref, a_ref, b_ref, mask_ref, gap_ref, gain_ref,
-        sent_ref, hid_ref, normed_mine_ref, zq_ref, zg_ref, mixed_ref, query_nat, forget_nat, value_nat, states_ref,
+        sent_ref, hid_out, normed_mine_out, zq_out, zg_out, mixed_ref, query_out, forget_out, value_out, states_ref,
         query_ref, forget_ref, value_ref, out_nat, state_now, win_ref, slots, sems, win_sem,
+        hid_ref, normed_mine_ref, zq_ref, zg_ref, query_nat, forget_nat, value_nat, out_sems,
     ) = refs
+    early = [(hid_ref, hid_out), (normed_mine_ref, normed_mine_out), (zq_ref, zq_out), (zg_ref, zg_out)]
+    early += [(query_nat, query_out), (forget_nat, forget_out), (value_nat, value_out)]
+    early = [pltpu.make_async_copy(here, there, out_sems.at[i]) for i, (here, there) in enumerate(early)]
     total, width = mixed_ref.shape
     heads = width // HEAD
     devices = sent_ref.shape[0]
@@ -281,10 +285,14 @@
         value_ref[rows, :] = main[:, 2 * width : 3 * width].astype(jnp.bfloat16)
         zg_ref[rows, :] = main[:, 3 * width : 4 * width]
 
+    for copy in early[:4]:
+        copy.start()
     move_rows(
         picks_natural(order_row_ref),
         ((query_ref, query_nat), (forget_ref, forget_nat), (value_ref, value_nat)),
     )
+    for copy in early[4:]:
+        copy.start()
     state_now[...] = jnp.zeros_like(state_now)
     lower = lower_ones()
 
@@ -325,6 +333,8 @@
         ones = jnp.ones((8, width), jnp.bfloat16)
         squares = (mm(ones, squares[0], NT) + mm(ones, squares[1], NT))[0:1]
         sent_ref[target, rows_each : rows_each + 16, :] = packed_lines([squares], width)
+    for copy in early:
+        copy.wait()
 
 
 def mixer_forward(ends, mine, place, order, blocks, win_pieces, in_a_t, in_b_wide, mask, gap, gain):
@@ -343,11 +353,13 @@
         lambda *refs: forward_kernel(stream, win_pieces, *refs),
         out_shape=(sent, hid, rows, wide_rows, wide_rows, rows, rows, rows, rows, states),
         in_specs=[SMEM] * 3 + [ANY] * (len(stream.pieces) + len(win_pieces)) + [VMEM] * 7,
-        out_specs=(VMEM,) * 10,
+        out_specs=(VMEM, ANY, ANY, ANY, ANY, VMEM, ANY, ANY, ANY, VMEM),
         scratch_shapes=[pltpu.VMEM((total, width), jnp.bfloat16)] * 4
         + [pltpu.VMEM((heads, HEAD, HEAD), jnp.float32), pltpu.VMEM((4 * (width + ranks), model), jnp.bfloat16)]
         + stream_scratch(stream.rows, model)
-        + [pltpu.SemaphoreType.DMA(())],
+        + [pltpu.SemaphoreType.DMA(())]
+        + [pltpu.VMEM(array.shape, array.dtype) for array in (hid, rows, wide_rows, wide_rows, rows, rows, rows)]
+        + [pltpu.SemaphoreType.DMA((7,))],
         compiler_params=params(62),
         cost_estimate=cost(57),
     )(
@@ -356,12 +368,27 @@
     )
 
 
-def backward_kernel(
-    ends_ref, mine_ref, order_row_ref, order_column_ref, came_ref, zq_ref, zg_ref, mixed_ref,
-    query_nat, forget_nat, value_nat, states_ref, gap_ref, gain_ref, hid_ref, b_ref, mask_ref, fold_ref,
-    g_proj_ref, gated_ref, small_ref, b_rows_ref,
-    grad_ref, grad_nat, d_query_nat, d_forget_nat, d_value_nat, slope_now,
-):
+def backward_kernel(win_pieces, *refs):
+    ends_ref, mine_ref, place_ref, refs = refs[0], refs[1], refs[2], refs[3:]
+    win_refs, refs = windows(win_pieces, refs), refs[len(win_pieces) :]
+    late, refs = refs[:7], refs[7:]
+    (
+        order_row_ref, order_column_ref, came_ref, zg_ref, mixed_ref, gap_ref, gain_ref, mask_ref, fold_ref,
+        g_proj_ref, gated_ref, small_ref, b_rows_ref, spread_out,
+        grad_ref, grad_nat, d_query_nat, d_forget_nat, d_value_nat, slope_now,
+        query_nat, forget_nat, value_nat, states_ref, zq_ref, hid_ref, b_ref, late_sems,
+        win_ref, win_sem, spread_ref, spread_sems,
+    ) = refs
+    late = [
+        pltpu.make_async_copy(there, here, late_sems.at[i])
+        for i, (there, here) in enumerate(
+            zip(late, (query_nat, forget_nat, value_nat, states_ref, zq_ref, hid_ref, b_ref))
+        )
+    ]
+    for copy in late:
+        copy.start()
+    win_copies = projection_copies(win_refs, place_ref[0], win_ref, win_sem)
+    go(win_copies, "start")
     total, width = mixed_ref.shape
     heads = width // HEAD
     devices = came_ref.shape[0]
@@ -389,6 +416,8 @@
         grad_ref[rows, :] = (factor * scaled - mixed * (cube * mean)).astype(jnp.bfloat16)
 
     move_rows(picks_natural(order_row_ref), ((grad_ref, grad_nat),))
+    for copy in late[:4]:
+        copy.wait()
     slope_now[...] = jnp.zeros_like(slope_now)
     lower = lower_ones()
 
@@ -430,6 +459,8 @@
             d_value_nat[rows, lanes] = d_value.astype(jnp.bfloat16)
 
     picks = picks_packed(order_column_ref)
+    for copy in late[4:]:
+        copy.wait()
 
     @pl.loop(0, total // TILE)
     def _(tile):
@@ -448,35 +479,66 @@
         parts = [(through[:, j * ranks : (j + 1) * ranks] * mask).astype(jnp.bfloat16) for j in range(4)]
         small_ref[rows, :] = mm(jnp.concatenate(parts, axis=1), fold_ref[...]).astype(jnp.bfloat16)
 
+    go(win_copies, "wait")
+    half = devices // 2
+
+    def spread_copy(block, slot):
+        rows = pl.ds(pl.multiple_of(block * rows_each, rows_each), rows_each)
+        return pltpu.make_async_copy(spread_ref.at[slot], spread_out.at[rows], spread_sems.at[slot])
+
+    @pl.loop(0, half)
+    def _(block):
+        slot = lax.rem(block, 2)
+
+        @pl.when(block >= 2)
+        def _():
+            spread_copy(block - 2, slot).wait()
+
+        rows = pl.ds(pl.multiple_of((block + half) * rows_each, rows_each), rows_each)
+        spread_ref[slot] = mm(g_proj_ref[rows, :], win_ref[...]).astype(jnp.bfloat16)
+        spread_copy(block, slot).start()
+
     ranks = mask_ref.shape[1]
     for j in range(4):
-        b_rows_ref[j * width : (j + 1) * width, :] = mm(
-            g_proj_ref[:, j * width : (j + 1) * width], hid_ref[:, j * ranks : (j + 1) * ranks], TN
+        b_rows_ref[:, j * width : (j + 1) * width] = mm(
+            hid_ref[:, j * ranks : (j + 1) * ranks], g_proj_ref[:, j * width : (j + 1) * width], TN
         )
-
-
-def mixer_backward(ends, mine, order, came, kept, gap, gain, hid_in, in_b_wide, mask, fold):
-    total, width = kept[0].shape
+    for block in range(half - 2, half):
+        spread_copy(block, block % 2).wait()
+
+
+def mixer_backward(ends, mine, place, order, came, kept, win_pieces, gap, gain, hid_in, in_b_wide, mask, fold):
+    zq, zg, mixed, query, forget, value, states = kept
+    total, width = zq.shape
     ranks = mask.shape[1]
     heads = width // HEAD
+    devices = came.shape[0]
+    rows_each = total // devices
+    model = win_pieces[0][0].shape[1]
     rows = jax.ShapeDtypeStruct((total, width), jnp.bfloat16)
+    late = (query, forget, value, states, zq, hid_in, in_b_wide)
     return pl.pallas_call(
-        backward_kernel,
+        lambda *refs: backward_kernel(win_pieces, *refs),
         out_shape=(
             jax.ShapeDtypeStruct((total, 4 * width), jnp.bfloat16),
             rows,
             jax.ShapeDtypeStruct((total, ranks), jnp.bfloat16),
-            jax.ShapeDtypeStruct((4 * width, ranks), jnp.float32),
+            jax.ShapeDtypeStruct((ranks, 4 * width), jnp.float32),
+            jax.ShapeDtypeStruct((total // 2, model), jnp.bfloat16),
         ),
-        in_specs=[SMEM] * 2 + [VMEM] * 16,
-        out_specs=(VMEM,) * 4,
+        in_specs=[SMEM] * 3 + [ANY] * (len(win_pieces) + len(late)) + [VMEM] * 9,
+        out_specs=(VMEM,) * 4 + (ANY,),
         scratch_shapes=[pltpu.VMEM((total, width), jnp.bfloat16)] * 5
-        + [pltpu.VMEM((heads, HEAD, HEAD), jnp.float32)],
+        + [pltpu.VMEM((heads, HEAD, HEAD), jnp.float32)]
+        + [pltpu.VMEM(array.shape, array.dtype) for array in late]
+        + [pltpu.SemaphoreType.DMA((len(late),))]
+        + [pltpu.VMEM((4 * width, model), jnp.bfloat16), pltpu.SemaphoreType.DMA(())]
+        + [pltpu.VMEM((2, rows_each, model), jnp.bfloat16), pltpu.SemaphoreType.DMA((2,))],
         compiler_params=params(62),
         cost_estimate=cost(51),
     )(
-        ends, mine, *order, came, *kept,
-        gap.reshape(1, width), gain.reshape(1, width), hid_in, in_b_wide, mask, fold,
+        ends, mine, place, *arrays_of(win_pieces), *late, *order, came, zg, mixed,
+        gap.reshape(1, width), gain.reshape(1, width), mask, fold,
     )
 
 
@@ -800,9 +862,8 @@
         if padded > hidden_units:
             w_down[hidden_units:padded, :] = jnp.zeros((padded - hidden_units, model), jnp.bfloat16)
         w_down[padded:, :] = down_b_ref[...]
-        both = load_both(weights, place_ref[0], w_all, ffn_a_ref, padded, ffn_sem)
+        load_both(weights, place_ref[0], w_all, ffn_a_ref, padded, ffn_sem)
         go(down, "wait")
-        go(both, "wait")
         down_rows[...] = jnp.zeros_like(down_rows)
         both_rows[...] = jnp.zeros_like(both_rows)
 
@@ -821,6 +882,11 @@
     left_both[:, :padded] = (d_hidden * upper * (sigma * (1.0 + gate * (1.0 - sigma)))).astype(jnp.bfloat16)
     left_both[:, padded : 2 * padded] = (d_hidden * silu).astype(jnp.bfloat16)
     mask_two = jnp.concatenate([mask, mask], axis=1)
+
+    @pl.when(step == 0)
+    def _():
+        go(both_copies(weights, place_ref[0], w_all, padded, ffn_sem), "wait")
+
     through = (mm(left_both[:, : 2 * padded], both_b_ref[...]) * mask_two).astype(jnp.bfloat16)
     left_both[:, 2 * padded :] = through
     back_ref[...] = mm(left_both[...], w_all[...]).astype(jnp.bfloat16)
@@ -1105,16 +1171,9 @@
 
 
 def two_blocks(blocks):
-    upper, lower = [], []
-    for block in blocks:
-        if len(block) == 1:
-            half = block[0].shape[0] // 2
-            upper.append([(block[0], 0, half)])
-            lower.append([(block[0], half, half)])
-        else:
-            upper.append([(block[0], 0, block[0].shape[0])])
-            lower.append([(block[1], 0, block[1].shape[0])])
-    return upper, lower
+    half = blocks[0][0].shape[0] // 2
+    upper = [[(block[0], 0, half)] for block in blocks]
+    return upper, [[(block[0], half, half)] for block in blocks if block[0].shape[0] == 2 * half]
 
 
 def scatter_parts(near, other):
@@ -1256,10 +1315,9 @@
         spread_ffn = [spread_ffn[: wt // 2].reshape(-1, model), spread_ffn[wt // 2 :].reshape(-1, model)]
         ffn_pieces = [(piece, 0, hidden_units) for piece in spread_ffn]
 
-    inputs = x_rows.astype(f32)
+    inputs = (after(x_rows, win_mine) if on_line else x_rows).astype(f32)
     normed = (inputs * norm_factor(inputs) * gain_mix).astype(bf16)
     pair = jnp.concatenate([normed, cot_rows])
-    pair_first = first_near(pair)
     order_mine = to_order(order[0].reshape(n, rows), mine).reshape(total)
     ends = jnp.cumsum(lengths[0])
     adapter = adapter_of(sequence_of(order_mine, lengths[0]), adapter_ids[0])
@@ -1277,6 +1335,7 @@
     b_up = pad_rows(ffn_b_mine[wt // 2 :].reshape(-1, RANKS))
     both_b = jnp.concatenate([jnp.pad(b_gate, ((0, 0), (0, RANKS))), jnp.pad(b_up, ((0, 0), (RANKS, 0)))])
     down_a_mine = pad_rows(my_piece(down_a.reshape(wt // 2, n, units, RANKS), 1).reshape(-1, RANKS))
+    pair_first = first_near(after(pair, in_b_wide, both_b))
     ready = lax.optimization_barrier(
         (
             pair_first, (order_mine.reshape(1, total), order_mine.reshape(total, 1)), mask, gap_mine, gain_mine,
@@ -1284,8 +1343,10 @@
         )
     )
     pair_first, order_both, mask, gap_mine, gain_mine, in_b_wide, both_b, down_a_mine, down_b_t, ffn_a_t, in_a_t = ready
-    pair_near = more_near(pair, pair_first)
-    pair_other = other_core(pair_near)
+    pair_near = [[pair]] + [[block] for block in pair_first]
+    if n == 8:
+        pair_near.append([across(pair_first[1][:rows], 2)])
+    pair_other = [[across(after(pair, *pair_first), 1)]] + other_core(pair_near[1:])
     normed_near, cot_near = two_blocks(pair_near)
     normed_other, cot_other = two_blocks(pair_other)
 
@@ -1301,7 +1362,7 @@
     wout_first = [across(wout_mine, k) for k in range(2, n, 2)]
     if on_line:
         sent, wout_first, ffn_first = lax.optimization_barrier((sent, wout_first, first_pieces(ffn_mine)))
-        early = units // 48 * 16
+        early = units // 64 * 16
         early_more = more_pieces(ffn_first, 0, early)
         strip = ffn_mine.shape[0] - units
     else:
@@ -1317,16 +1378,21 @@
     if on_line:
         normed2, early_more = lax.optimization_barrier((normed2, early_more))
         late_more = more_pieces(after(ffn_first, *early_more), early, units - early)
+
+    normed2_near = more_near(normed2, first_near(normed2))
+    if on_line:
+        normed2_near, late_more = lax.optimization_barrier((normed2_near, late_more))
         ffn_pieces = line_rows(ffn_mine, ffn_first, early_more, 0, early)
         ffn_pieces += line_rows(ffn_mine, ffn_first, late_more, early, units - early)
         down_more = more_pieces(after(ffn_first, *late_more), units, strip)
-
-    normed2_near = more_near(normed2, first_near(normed2))
     both, hid_ffn, normed2_mine = ffn_up(
         mine_ref, place_ref, with_rows(normed2_near + other_core(normed2_near)), ffn_pieces, mask, ffn_a_t, both_b, wide
     )
     if on_line:
-        both, down_more = lax.optimization_barrier((both, down_more))
+        cot_far = across(after(cot_rows, normed2), 6)
+        both, down_more, cot_far = lax.optimization_barrier((both, down_more, cot_far))
+        cot_near.append([(cot_far, 0, rows)])
+        cot_other.append([(across(cot_far, 1), 0, rows)])
         down_pieces = line_rows(ffn_mine, ffn_first, down_more, units, strip)
     sides = []
     for cots, first in ((cot_other, blocks), (cot_near, 0)):
@@ -1381,39 +1447,44 @@
         (down[i * rows : (i + 1) * rows].astype(f32) + down_far[i * rows : (i + 1) * rows].astype(f32)).astype(bf16)
         for i in range(1, blocks)
     ]
-    out_came = [across(part, 2 * i + 2) for i, part in enumerate(after(out_parts, d_sent))]
-    d_came = swap(d_sent)
-    g_proj, gated_heads, small_in, in_b_rows = mixer_backward(
-        ends, mine_ref, order_both, d_came, kept, gap_mine, gain_mine, hid_in, in_b_wide, mask, fold_in
+    out_parts = after(out_parts, d_sent)
+    d_came = after(swap(d_sent), *out_parts)
+    out_came = [across(part, 2 * i + 2) for i, part in enumerate(out_parts)]
+    g_proj, gated_heads, small_in, in_b_rows, back_in_far = mixer_backward(
+        ends, mine_ref, place_ref, order_both, d_came, kept, win_pieces, gap_mine, gain_mine, hid_in, in_b_wide,
+        mask, fold_in,
     )
-    g_proj, small_in, out_came, early_sum = lax.optimization_barrier((g_proj, small_in, out_came, early_sum))
+    g_proj, gated_heads, small_in, in_b_rows, back_in_far, out_came, early_sum = lax.optimization_barrier(
+        (g_proj, gated_heads, small_in, in_b_rows, back_in_far, out_came, early_sum)
+    )
+    in_b_early = [in_b_rows.T]
+    in_b_sum = lax.psum_scatter(packed_rows(in_b_early), "wt", scatter_dimension=0, tiled=False)
     ffn_b_grad, down_a_grad = unpacked_rows(early_sum, early)
 
     small = (small_in + jnp.concatenate([small, small_far])).reshape(n, rows, RANKS)
-    small = jnp.concatenate([from_order(small, mine), out_b_part.astype(bf16).reshape(n, rows, -1)], axis=2)
-    small, g_proj = lax.optimization_barrier((small, g_proj))
+    small, g_proj = lax.optimization_barrier((from_order(small, mine), g_proj))
     small = swap(small)
-    back_in_far = across(spread(place_ref, g_proj, win_pieces, blocks, blocks, rows), 1)
+    back_in_far = across(back_in_far, 1)
     back_in = spread(place_ref, g_proj, win_pieces, 0, blocks, rows)
     in_parts, in_rest = scatter_parts(back_in, back_in_far)
     in_came = scatter_first(in_parts)
     small = jnp.sum(after(small, *in_parts, *in_rest).astype(f32), axis=0)
-    out_b_rows = small[:, RANKS:].reshape(wide, RANKS)
-    small = small[:, :RANKS].astype(bf16)
+    small = small.astype(bf16)
     d_hid_in_own = (mm(small, fold_in, NT) * adapter_mask(adapter[:rows], PROJECTIONS)).astype(bf16)
     small = small + mm(d_hid_out, fold_out).astype(bf16)
-    small = swap(jnp.broadcast_to(small, (n,) + small.shape))
+    small = jnp.broadcast_to(small, (n,) + small.shape)
+    small = swap(jnp.concatenate([small, out_b_part.astype(bf16).reshape(n, rows, -1)], axis=2))
     block_out = resid + down[:rows].astype(f32) + down_far[:rows].astype(f32)
     block_out = (block_out + sum(piece.astype(f32) for piece in out_came)).astype(bf16)
-    in_came, block_out = lax.optimization_barrier((in_came, block_out))
     if in_rest:
+        in_came[0], in_came[1], small = lax.optimization_barrier((in_came[0], in_came[1], small))
         in_rest = [in_rest[0] + in_came[1].astype(f32), in_rest[1] + in_came[0].astype(f32)]
         in_rest = [part.astype(bf16) for part in in_rest]
-        small, in_rest = lax.optimization_barrier((small, in_rest))
         from_x, from_y = [in_came[2], across(in_rest[0], 2)], [across(in_rest[1], 4), in_came[3]]
     else:
         from_x, from_y = scatter_second(in_came, in_rest)
-    small = to_order(small, mine).reshape(total, RANKS)
+    out_b_rows = jnp.sum(small[:, :, RANKS:].astype(f32), axis=0).reshape(wide, RANKS)
+    small = to_order(small[:, :, :RANKS], mine).reshape(total, RANKS)
     d_hid_in = (mm(small, fold_in, NT) * adapter_mask(adapter, PROJECTIONS)).astype(bf16)
 
     wide_ffn = (mm(small, fold_ffn, NT) * adapter_mask(adapter, 3)).astype(bf16)
@@ -1423,10 +1494,12 @@
         mm(gated_heads, (mm(small, fold_out, NT) * mask).astype(bf16), TN),
         out_b_rows,
         mm(normed_mine, d_hid_in, TN),
-        in_b_rows,
     ]
-    late_sum = jnp.sum(swap(packed_rows(late).astype(bf16), "wt").astype(f32), axis=0)
-    down_b_grad, ffn_a_grad, out_a_grad, out_b_grad, in_a_grad, in_b_grad = unpacked_rows(late_sum, late)
+    in_b_sum, small = lax.optimization_barrier((in_b_sum, small))
+    (in_b_grad,) = unpacked_rows(in_b_sum, in_b_early)
+    packed, from_x, from_y = lax.optimization_barrier((packed_rows(late).astype(bf16), from_x, from_y))
+    late_sum = jnp.sum(swap(packed, "wt").astype(f32), axis=0)
+    down_b_grad, ffn_a_grad, out_a_grad, out_b_grad, in_a_grad = unpacked_rows(late_sum, late)
     tokens_grad = token_end(
         x_rows, d_resid, d_hid_in_own, in_a, gain_mix, (back_in, back_in_far, from_x, from_y)
     )

time: 647 us -> 630 us (0.974)
  waiting for transfers between devices: 209 us -> 198 us
  Pallas kernels: 240 us -> 233 us
    ppermute x3, waiting for transfers between devices: 23.9 us -> 10.5 us  [to_owner(): return lax.ppermute(piece, ('seq', 'wt'), moves)]
    ppermute x16, waiting for transfers between devices: 66.6 us -> 79.7 us  [along(): return lax.ppermute(values, 'wt', pairs)]
    ppermute x43, waiting for transfers between devices: 107 us -> 95.9 us  [across(): return lax.ppermute(values, axis, [(i, i ^ bits) for i in range(size)])]
    pallas_call x2 -> x1, Pallas kernels: 19 us -> 9.5 us  [spread(): pl.pallas_call(lambda *refs: spread_kernel(win_pieces, *refs), grid=(bloc...]
    unnamed x122 -> x119, local copies, waits for them, and re-layouts: 18.2 us -> 21.4 us
  transfers between devices with their start and end apart: 68 -> 69, of which waited for: 27 -> 26; matrix products, arithmetic and copies ran while one was open for 9% -> 12% of each run, Pallas kernels for 29% -> 30%
where the time goes in v4:
time: 630 us; the launch traced here: 624 us
  Pallas kernels  233 us (37%)
  waiting for transfers between devices  198 us (31%)
  starting transfers between devices  86.6 us (14%)
  other arithmetic  46.5 us (7%)
  local copies, waits for them, and re-layouts  37.5 us (6%)
  between operations  15.8 us (3%)
  matrix products  6.57 us (1%)
    ppermute x43, waiting for transfers between devices, across(): return lax.ppermute(values, axis, [(i, i ^ bits) for i in range(size)])  95.9 us
    ppermute x16, waiting for transfers between devices, along(): return lax.ppermute(values, 'wt', pairs)  79.7 us
    pallas_call x2, Pallas kernels, ffn_back(): pl.pallas_call(lambda *refs: ffn_back_kernel(stream, weights, downs, *ref...  61 us
    pallas_call x1, Pallas kernels, mixer_forward(): pl.pallas_call(lambda *refs: forward_kernel(stream, win_pieces, *refs), o...  50.1 us
    pallas_call x1, Pallas kernels, mixer_backward(): pl.pallas_call(lambda *refs: backward_kernel(win_pieces, *refs), out_shap...  49.9 us
    ppermute x43, starting transfers between devices, across(): return lax.ppermute(values, axis, [(i, i ^ bits) for i in range(size)])  31.3 us
    pallas_call x1, Pallas kernels, ffn_up(): pl.pallas_call(lambda *refs: ffn_up_kernel(stream, weights, *refs), grid=...  26 us
    ppermute x16, starting transfers between devices, along(): return lax.ppermute(values, 'wt', pairs)  24.3 us
  transfers between devices with their start and end apart: 69, of which 26 were waited for; matrix products, arithmetic and copies ran while one was open for 12% of the time, Pallas kernels for 30%

profile of v4, /device:TPU:4, one launch (start us, length us, event | category | flops | bytes accessed | tf_op | source)
XLA Modules:
  0.0 623.9 jit_solution(10459189548883005508)
XLA Ops:
  7.2 2.9 shard_map.276.refs_1_.refs_11_.refs_3_
  10.1 3.6 collective-permute-start.7
  16.5 1.6 pad_maximum_fusion.refs_3_.refs_2_
  18.2 1.8 constant_dynamic-slice_fusion
  26.6 15.4 %collective-permute-done.7.refs_2_.refs_12_.refs_4_ = bf16[320,2048]{1,0:T(8,128)(2,1)S(1)} collective-permute-done((bf16[320,2048]{1,0:T(8,128)(2,1)}, bf16[320,2048]{1,0:T(8,128)(2,1)S(1)}, u32[]{:S(2)}, u32[]{:S(2)}) %collective-permute-start.7) | collective-permute-done | bytes 1310752 | tf_op jit(solution)/shard_map/ppermute | solution.py:1214
  42.0 4.2 collective-permute-done.8.refs_3_.refs_13_.refs_5_
  46.2 3.0 broadcast_select_fusion
  54.0 2.0 copy.57
  56.1 2.3 copy.58
  58.4 2.5 copy.59
  60.9 1.6 pad.42.refs_29_
  63.9 6.5 %collective-permute-done.refs_4_.refs_3_ = bf16[512,2048]{1,0:T(8,128)(2,1)} collective-permute-done((bf16[512,2048]{1,0:T(8,128)(2,1)}, bf16[512,2048]{1,0:T(8,128)(2,1)}, u32[]{:S(2)}, u32[]{:S(2)}) %collective-permute-start) | collective-permute-done | bytes 2097184 | tf_op jit(solution)/shard_map/ppermute | solution.py:1149
  74.1 9.1 %collective-permute-done.10.refs_5_.refs_15_.refs_7_ = bf16[320,2048]{1,0:T(8,128)(2,1)} collective-permute-done((bf16[320,2048]{1,0:T(8,128)(2,1)}, bf16[320,2048]{1,0:T(8,128)(2,1)}, u32[]{:S(2)}, u32[]{:S(2)}) %collective-permute-start.10) | collective-permute-done | bytes 1310752 | tf_op jit(solution)/shard_map/ppermute | solution.py:1214
  84.5 14.7 %collective-permute-done.2.refs_6_ = bf16[256,2048]{1,0:T(8,128)(2,1)} collective-permute-done((bf16[256,2048]{1,0:T(8,128)(2,1)S(1)}, bf16[256,2048]{1,0:T(8,128)(2,1)}, u32[]{:S(2)}, u32[]{:S(2)}) %collective-permute-start.2) | collective-permute-done | bytes 1048608 | tf_op jit(solution)/shard_map/ppermute | solution.py:1149
  99.2 4.1 shard_map.277.refs_12_.refs_18_.refs_6_
  104.7 10.0 %collective-permute-done.11.refs_6_.refs_16_.refs_8_ = bf16[320,2048]{1,0:T(8,128)(2,1)} collective-permute-done((bf16[320,2048]{1,0:T(8,128)(2,1)}, bf16[320,2048]{1,0:T(8,128)(2,1)}, u32[]{:S(2)}, u32[]{:S(2)}) %collective-permute-start.11) | collective-permute-done | bytes 1310752 | tf_op jit(solution)/shard_map/ppermute | solution.py:1214
  114.7 2.2 shard_map.278.refs_7_.refs_15_
  117.0 1.6 collective-permute-start.12
  120.5 2.6 collective-permute-start.15
  124.7 50.1 %shard_map.279 = (bf16[8,272,256]{2,1,0:T(8,128)(2,1)}, bf16[2048,512]{1,0:T(8,128)(2,1)}, bf16[2048,256]{1,0:T(8,128)(2,1)}, f32[2048,256]{1,0:T(8,128)}, f32[2...) custom-call(s32[4]{0:T(128)} %bitcast.167, ...), custom_call_target="tpu_custom_call" | custom-call | flops 57000001536 | tf_op jit(solution)/shard_map/pallas_call | solution.py:352
  175.9 4.2 all-to-all-start
  186.8 8.1 %all-to-all-done.refs_1_ = bf16[8,272,256]{2,1,0:T(8,128)(2,1)S(1)} async-done(((bf16[8,272,256]{2,1,0:T(8,128)(2,1)}), bf16[8,272,256]{2,1,0:T(8,128)(2,1)S(1)}, u32[]{:S(2)}, u32[]{:S(2)}) %all-to-all-start) | async-done | bytes 1114144 | tf_op jit(solution)/shard_map/all_to_all | solution.py:1210
  195.8 9.7 %shard_map.280 = (f32[256,2048]{1,0:T(8,128)}, bf16[256,2048]{1,0:T(8,128)(2,1)}, bf16[256,128]{1,0:T(8,128)(2,1)}) custom-call(s32[1]{0:T(128)} %bitcast.mine_ref.refs_0_.refs_1_, bf16[8,272,256]{2,1,0:T(8,128)(2,1)} %copy-done.7, bf16[256,2048]{1,0:T(8,128)(2,1)} %bitcast.103, bf16[2048,128]{1,0:T(8,128)(2,1)} %refs_4_.3, bf16[2048,128]{1,0:T(8,128)(2,1)} %refs_5_.1, ...), custom_call_target="tpu_custom_call" | custom-call | flops 8000000000 | tf_op jit(solution)/shard_map/pallas_call | solution.py:597
  205.5 2.6 collective-permute-done.22.refs_16_.refs_10_
  210.2 1.7 broadcast_select_fusion.2
  215.4 17.4 %collective-permute-done.24.refs_3_ = bf16[256,2048]{1,0:T(8,128)(2,1)S(1)} collective-permute-done((bf16[256,2048]{1,0:T(8,128)(2,1)}, bf16[256,2048]{1,0:T(8,128)(2,1)S(1)}, u32[]{:S(2)}, u32[]{:S(2)}) %collective-permute-start.24) | collective-permute-done | bytes 1048608 | tf_op jit(solution)/shard_map/ppermute | solution.py:1149
  235.0 28.8 %collective-permute-done.29.refs_22_.refs_16_ = bf16[272,2048]{1,0:T(8,128)(2,1)S(1)} collective-permute-done((bf16[272,2048]{1,0:T(8,128)(2,1)S(1)}, bf16[272,2048]{1,0:T(8,128)(2,1)S(1)}, u32[]{:S(2)}, u32[]{:S(2)}) %collective-permute-start.29) | collective-permute-done | bytes 1114144 | tf_op jit(solution)/shard_map/ppermute | solution.py:1214
  265.1 2.3 broadcast_select_fusion.4
  267.4 2.9 collective-permute-done.34.refs_10_
  274.7 1.7 collective-permute-start.37
  276.4 26.0 %shard_map.281 = (f32[2048,1536]{1,0:T(8,128)}, bf16[2048,256]{1,0:T(8,128)(2,1)}, bf16[2048,256]{1,0:T(8,128)(2,1)}) custom-call(s32[1]{0:T(128)} %bitcast.mine_ref.refs_0_.refs_1_, s32[1]{0:T(128)} %bitcast.3.refs_0_.refs_2_.refs_1_, bf16[256,2048]{1,0:T(8,128)(2,1)} %get-tuple-element.161.refs_2_, bf16[256,2048]{1,0:T(8,128)(2,1)} %copy-done.18, ...), custom_call_target="tpu_custom_call" | custom-call | flops 28000000000 | tf_op jit(solution)/shard_map/pallas_call | solution.py:809
  302.4 9.6 %collective-permute-done.37.refs_22_ = bf16[176,2048]{1,0:T(8,128)(2,1)} collective-permute-done((bf16[176,2048]{1,0:T(8,128)(2,1)}, bf16[176,2048]{1,0:T(8,128)(2,1)}, u32[]{:S(2)}, u32[]{:S(2)}) %collective-permute-start.37) | collective-permute-done | bytes 720928 | tf_op jit(solution)/shard_map/ppermute | solution.py:1214
  315.9 30.4 %shard_map.283 = (bf16[1024,2048]{1,0:T(8,128)(2,1)}, bf16[1024,2048]{1,0:T(8,128)(2,1)}, bf16[1024,128]{1,0:T(8,128)(2,1)}, bf16[1024,256]{1,0:T(8,128)(2,1)}, f32[128,768]{1,0:T(8,128)}, /*index=5*/f32[256,1536]{1,0:T(8,128)}) custom-call(s32[1]{0:T(128)} %bitcast.mine_ref.refs_0_.refs_1_, s32[1]{0:T(128)} %bitcast.3.refs_0_.refs_2_.refs_1_, ...), custom_call_target="tpu_custom_call" | custom-call | flops 32999999488 | tf_op jit(solution)/shard_map/pallas_call | solution.py:913
  346.9 30.6 %shard_map.282 = (bf16[1024,2048]{1,0:T(8,128)(2,1)}, bf16[1024,2048]{1,0:T(8,128)(2,1)}, bf16[1024,128]{1,0:T(8,128)(2,1)}, bf16[1024,256]{1,0:T(8,128)(2,1)}, f32[128,768]{1,0:T(8,128)}, /*index=5*/f32[256,1536]{1,0:T(8,128)}) custom-call(s32[1]{0:T(128)} %bitcast.mine_ref.refs_0_.refs_1_, s32[1]{0:T(128)} %bitcast.3.refs_0_.refs_2_.refs_1_, ...), custom_call_target="tpu_custom_call" | custom-call | flops 32999999488 | tf_op jit(solution)/shard_map/pallas_call | solution.py:913
  377.5 2.9 add_convert_fusion.10
  381.3 1.7 collective-permute-start.44
  384.6 10.7 %collective-permute-done.46 = bf16[128,2048]{1,0:T(8,128)(2,1)S(1)} collective-permute-done((bf16[128,2048]{1,0:T(8,128)(2,1)S(1)}, bf16[128,2048]{1,0:T(8,128)(2,1)S(1)}, u32[]{:S(2)}, u32[]{:S(2)}) %collective-permute-start.46) | collective-permute-done | bytes 524320 | tf_op jit(solution)/shard_map/ppermute | solution.py:1149
  396.1 2.0 add_convert_fusion.11
  401.3 5.2 collective-permute-done.43.refs_11_
  407.3 9.6 %collective-permute-done.45.refs_12_ = bf16[128,2048]{1,0:T(8,128)(2,1)S(1)} collective-permute-done((bf16[128,2048]{1,0:T(8,128)(2,1)S(1)}, bf16[128,2048]{1,0:T(8,128)(2,1)S(1)}, u32[]{:S(2)}, u32[]{:S(2)}) %collective-permute-start.45) | collective-permute-done | bytes 524320 | tf_op jit(solution)/shard_map/ppermute | solution.py:1149
  418.5 10.9 %shard_map.284 = (bf16[8,272,256]{2,1,0:T(8,128)(2,1)}, f32[256,2048]{1,0:T(8,128)}, bf16[256,128]{1,0:T(8,128)(2,1)}, f32[2048,128]{1,0:T(8,128)}) custom-call(s32[1]{0:T(128)} %bitcast.mine_ref.refs_0_.refs_1_, bf16[8,272,256]{2,1,0:T(8,128)(2,1)} %copy-done.7, bf16[256,2048]{1,0:T(8,128)(2,1)} %bitcast.124, f32[256,2048]{1,0:T(8,128)} %get-tuple-element.151.refs_3_, ...), custom_call_target="tpu_custom_call" | custom-call | flops 12000000000 | tf_op jit(solution)/shard_map/pallas_call | solution.py:688
  429.5 5.7 all-to-all-start.1
  437.1 5.7 add_convert_fusion.1
  446.3 4.1 all-to-all-done.1.refs_18_
  450.4 49.9 %shard_map.285 = (bf16[2048,1024]{1,0:T(8,128)(2,1)}, bf16[2048,256]{1,0:T(8,128)(2,1)}, bf16[2048,128]{1,0:T(8,128)(2,1)}, f32[128,1024]{1,0:T(8,128)}, bf16[1024,2048]{1,0:T(8,128)(2,1)}) custom-call(s32[4]{0:T(128)} %bitcast.168, s32[1]{0:T(128)} %bitcast.mine_ref.refs_0_.refs_1_, s32[1]{0:T(128)} %bitcast.3.refs_0_.refs_2_.refs_1_, ...), custom_call_target="tpu_custom_call" | custom-call | flops 51000000512 | tf_op jit(solution)/shard_map/pallas_call | solution.py:520
  504.2 5.2 all-to-all-start.2
  509.4 9.5 %shard_map.286.refs_5_ = bf16[1024,2048]{1,0:T(8,128)(2,1)} custom-call(s32[1]{0:T(128)} %bitcast.3.refs_0_.refs_2_.refs_1_, bf16[320,2048]{1,0:T(8,128)(2,1)} %shard_map.276.refs_1_.refs_11_.refs_3_, bf16[320,2048]{1,0:T(8,128)(2,1)} %copy-done.2, bf16[320,2048]{1,0:T(8,128)(2,1)} %collective-permute-done.8.refs_3_.refs_13_.refs_5_, ...), custom_call_target="tpu_custom_call" | custom-call | flops 8000000000 | tf_op jit(solution)/shard_map/pallas_call | solution.py:960
  518.9 3.9 add_convert_fusion.6
  524.4 4.3 all-to-all-start.3
  531.5 2.0 copy.67
  533.6 2.6 collective-permute-start.60
  538.0 18.3 %collective-permute-done.53 = bf16[128,2048]{1,0:T(8,128)(2,1)} collective-permute-done((bf16[128,2048]{1,0:T(8,128)(2,1)S(1)}, bf16[128,2048]{1,0:T(8,128)(2,1)}, u32[]{:S(2)}, u32[]{:S(2)}) %collective-permute-start.53) | collective-permute-done | bytes 524320 | tf_op jit(solution)/shard_map/ppermute | solution.py:1149
  560.7 2.6 fusion.13
  563.4 2.4 add_convert_fusion.4
  565.8 2.6 collective-permute-start.56
  573.6 3.4 collective-permute-start.61
  577.0 2.9 collective-permute-done.56.refs_8_
  580.7 2.4 collective-permute-done.57.refs_9_
  583.2 3.5 all-to-all-start.4
  586.7 5.2 fusion.18
  591.9 1.9 collective-permute-start.59
  594.9 10.5 %collective-permute-done.59 = f32[256,128]{1,0:T(8,128)S(1)} collective-permute-done((f32[256,128]{1,0:T(8,128)}, f32[256,128]{1,0:T(8,128)S(1)}, u32[]{:S(2)}, u32[]{:S(2)}) %collective-permute-start.59) | collective-permute-done | bytes 131104 | tf_op jit(solution)/shard_map/ppermute | solution.py:1244
  605.3 6.3 %shard_map.287 = bf16[256,2048]{1,0:T(8,128)(2,1)} custom-call(bf16[256,2048]{1,0:T(8,128)(2,1)} %bitcast.104, f32[256,2048]{1,0:T(8,128)} %get-tuple-element.217.refs_1_, bf16[256,512]{1,0:T(8,128)(2,1)} %fusion.12.refs_2_, bf16[2048,512]{1,0:T(8,128)(2,1)} %refs_3_.3, f32[1,2048]{1,0:T(1,128)} %bitcast.149, bf16[1024,2048]{1,0:T(8,128)(2,1)} %shard_map.286.refs_5_, ...), custom_call_target="tpu_custom_call" | custom-call | flops 4000000000 | tf_op jit(solution)/shard_map/pallas_call | solution.py:731
  614.3 1.6 copy.92
  (300 shorter events, 90.7 us)
Async XLA Ops:
  10.1 31.8 %collective-permute-start.7 = (bf16[320,2048]{1,0:T(8,128)(2,1)}, bf16[320,2048]{1,0:T(8,128)(2,1)S(1)}, u32[]{:S(2)}, u32[]{:S(2)}) collective-permute-start(bf16[320,2048]{1,0:T(8,128)(2,1)} %shard_map.276.refs_1_.refs_11_.refs_3_), channel_id=1, source_target_pairs={{0,1},{1,2},{2,3},{4,5},{5,6},{6,7},{8,9},{9,10},{10,11},{12,13},{... | collective-permute-start | bytes 3932168 | tf_op jit(solution)/shard_map/ppermute | solution.py:1214
  13.7 32.5 %collective-permute-start.8 = (bf16[320,2048]{1,0:T(8,128)(2,1)}, bf16[320,2048]{1,0:T(8,128)(2,1)}, u32[]{:S(2)}, u32[]{:S(2)}) collective-permute-start(bf16[320,2048]{1,0:T(8,128)(2,1)} %shard_map.276.refs_1_.refs_11_.refs_3_), channel_id=1, source_target_pairs={{1,0},{2,1},{3,2},{5,4},{6,5},{7,6},{9,8},{10,9},{11,10},{13,12},{... | collective-permute-start | bytes 3932168 | tf_op jit(solution)/shard_map/ppermute | solution.py:1214
  23.0 47.4 %collective-permute-start = (bf16[512,2048]{1,0:T(8,128)(2,1)}, bf16[512,2048]{1,0:T(8,128)(2,1)}, u32[]{:S(2)}, u32[]{:S(2)}) collective-permute-start(bf16[512,2048]{1,0:T(8,128)(2,1)} %pad_maximum_fusion.refs_3_.refs_2_), channel_id=1, source_target_pairs={{0,8},{4,12},{8,0},{12,4},{16,24},{20,28},{24,16},{28,20},{1,9},{5... | collective-permute-start | bytes 6291464 | tf_op jit(solution)/shard_map/ppermute | solution.py:1149
  24.5 47.1 %collective-permute-start.1 = (bf16[512,2048]{1,0:T(8,128)(2,1)}, bf16[512,2048]{1,0:T(8,128)(2,1)}, u32[]{:S(2)}, u32[]{:S(2)}) collective-permute-start(bf16[512,2048]{1,0:T(8,128)(2,1)} %pad_maximum_fusion.refs_3_.refs_2_), channel_id=1, source_target_pairs={{0,16},{4,20},{8,24},{12,28},{16,0},{20,4},{24,8},{28,12},{1,17},{... | collective-permute-start | bytes 6291464 | tf_op jit(solution)/shard_map/ppermute | solution.py:1149
  49.2 24.3 %collective-permute-start.9 = (bf16[320,2048]{1,0:T(8,128)(2,1)}, bf16[320,2048]{1,0:T(8,128)(2,1)S(1)}, u32[]{:S(2)}, u32[]{:S(2)}) collective-permute-start(bf16[320,2048]{1,0:T(8,128)(2,1)} %get-tuple-element.268), channel_id=1, source_target_pairs={{1,2},{2,1},{5,6},{6,5},{9,10},{10,9},{13,14},{14,13},{17,18},{18,... | collective-permute-start | bytes 3932168 | tf_op jit(solution)/shard_map/ppermute | solution.py:1214
  50.1 33.1 %collective-permute-start.10 = (bf16[320,2048]{1,0:T(8,128)(2,1)}, bf16[320,2048]{1,0:T(8,128)(2,1)}, u32[]{:S(2)}, u32[]{:S(2)}) collective-permute-start(bf16[320,2048]{1,0:T(8,128)(2,1)} %get-tuple-element.267), channel_id=1, source_target_pairs={{2,3},{1,0},{6,7},{5,4},{10,11},{9,8},{14,15},{13,12},{18,19},{17,... | collective-permute-start | bytes 3932168 | tf_op jit(solution)/shard_map/ppermute | solution.py:1214
  71.6 46.9 %collective-permute-start.3 = (bf16[512,2048]{1,0:T(8,128)(2,1)}, bf16[512,2048]{1,0:T(8,128)(2,1)}, u32[]{:S(2)}, u32[]{:S(2)}) collective-permute-start(bf16[512,2048]{1,0:T(8,128)(2,1)} %pad_maximum_fusion.refs_3_.refs_2_), channel_id=1, source_target_pairs={{0,4},{4,0},{8,12},{12,8},{16,20},{20,16},{24,28},{28,24},{1,5},{5... | collective-permute-start | bytes 6291464 | tf_op jit(solution)/shard_map/ppermute | solution.py:1149
  71.6 47.4 %collective-permute-start.4 = (bf16[512,2048]{1,0:T(8,128)(2,1)}, bf16[512,2048]{1,0:T(8,128)(2,1)}, u32[]{:S(2)}, u32[]{:S(2)}) collective-permute-start(bf16[512,2048]{1,0:T(8,128)(2,1)} %collective-permute-done.refs_4_.refs_3_), channel_id=1, source_target_pairs={{0,4},{4,0},{8,12},{12,8},{16,20},{20,16},{24,28},{28,24},{1,5},{5... | collective-permute-start | bytes 6291464 | tf_op jit(solution)/shard_map/ppermute | solution.py:1149
  73.4 47.1 %collective-permute-start.5 = (bf16[512,2048]{1,0:T(8,128)(2,1)}, bf16[512,2048]{1,0:T(8,128)(2,1)}, u32[]{:S(2)}, u32[]{:S(2)}) collective-permute-start(bf16[512,2048]{1,0:T(8,128)(2,1)} %collective-permute-done.1.refs_5_.refs_4_), channel_id=1, source_target_pairs={{0,4},{4,0},{8,12},{12,8},{16,20},{20,16},{24,28},{28,24},{1,5},{5... | collective-permute-start | bytes 6291464 | tf_op jit(solution)/shard_map/ppermute | solution.py:1149
  73.5 25.7 %collective-permute-start.2 = (bf16[256,2048]{1,0:T(8,128)(2,1)S(1)}, bf16[256,2048]{1,0:T(8,128)(2,1)}, u32[]{:S(2)}, u32[]{:S(2)}) collective-permute-start(bf16[256,2048]{1,0:T(8,128)(2,1)S(1)} %slice.264), channel_id=1, source_target_pairs={{0,8},{4,12},{8,0},{12,4},{16,24},{20,28},{24,16},{28,20},{1,9},{5... | collective-permute-start | bytes 3145736 | tf_op jit(solution)/shard_map/ppermute | solution.py:1149
  83.2 31.5 %collective-permute-start.11 = (bf16[320,2048]{1,0:T(8,128)(2,1)}, bf16[320,2048]{1,0:T(8,128)(2,1)}, u32[]{:S(2)}, u32[]{:S(2)}) collective-permute-start(bf16[320,2048]{1,0:T(8,128)(2,1)} %get-tuple-element.268), channel_id=1, source_target_pairs={{1,3},{2,0},{5,7},{6,4},{9,11},{10,8},{13,15},{14,12},{17,19},{18,... | collective-permute-start | bytes 3932168 | tf_op jit(solution)/shard_map/ppermute | solution.py:1214
  99.2 24.0 %collective-permute-start.6 = (bf16[256,2048]{1,0:T(8,128)(2,1)}, bf16[256,2048]{1,0:T(8,128)(2,1)}, u32[]{:S(2)}, u32[]{:S(2)}) collective-permute-start(bf16[256,2048]{1,0:T(8,128)(2,1)} %collective-permute-done.2.refs_6_), channel_id=1, source_target_pairs={{0,4},{4,0},{8,12},{12,8},{16,20},{20,16},{24,28},{28,24},{1,5},{5... | collective-permute-start | bytes 3145736 | tf_op jit(solution)/shard_map/ppermute | solution.py:1149
  117.0 57.8 %collective-permute-start.12 = (bf16[256,2048]{1,0:T(8,128)(2,1)}, bf16[256,2048]{1,0:T(8,128)(2,1)}, u32[]{:S(2)}, u32[]{:S(2)}) collective-permute-start(bf16[256,2048]{1,0:T(8,128)(2,1)} %shard_map.278.refs_7_.refs_15_), channel_id=1, source_target_pairs={{0,8},{4,12},{8,0},{12,4},{16,24},{20,28},{24,16},{28,20},{1,9},{5... | collective-permute-start | bytes 3145736 | tf_op jit(solution)/shard_map/ppermute | solution.py:1149
  118.5 56.3 %collective-permute-start.13 = (bf16[256,2048]{1,0:T(8,128)(2,1)}, bf16[256,2048]{1,0:T(8,128)(2,1)}, u32[]{:S(2)}, u32[]{:S(2)}) collective-permute-start(bf16[256,2048]{1,0:T(8,128)(2,1)} %shard_map.278.refs_7_.refs_15_), channel_id=1, source_target_pairs={{0,16},{4,20},{8,24},{12,28},{16,0},{20,4},{24,8},{28,12},{1,17},{... | collective-permute-start | bytes 3145736 | tf_op jit(solution)/shard_map/ppermute | solution.py:1149
  119.0 55.8 %collective-permute-start.14 = (bf16[256,2048]{1,0:T(8,128)(2,1)}, bf16[256,2048]{1,0:T(8,128)(2,1)}, u32[]{:S(2)}, u32[]{:S(2)}) collective-permute-start(bf16[256,2048]{1,0:T(8,128)(2,1)} %shard_map.278.refs_7_.refs_15_), channel_id=1, source_target_pairs={{0,24},{4,28},{8,16},{12,20},{16,8},{20,12},{24,0},{28,4},{1,25},{... | collective-permute-start | bytes 3145736 | tf_op jit(solution)/shard_map/ppermute | solution.py:1149
  120.5 54.3 %collective-permute-start.15 = (bf16[528,2048]{1,0:T(8,128)(2,1)}, bf16[528,2048]{1,0:T(8,128)(2,1)}, u32[]{:S(2)}, u32[]{:S(2)}) collective-permute-start(bf16[528,2048]{1,0:T(8,128)(2,1)} %shard_map.277.refs_12_.refs_18_.refs_6_), channel_id=1, source_target_pairs={{0,1},{1,2},{2,3},{4,5},{5,6},{6,7},{8,9},{9,10},{10,11},{12,13},{... | collective-permute-start | bytes 6488072 | tf_op jit(solution)/shard_map/ppermute | solution.py:1214
  123.2 51.7 %collective-permute-start.16 = (bf16[528,2048]{1,0:T(8,128)(2,1)}, bf16[528,2048]{1,0:T(8,128)(2,1)}, u32[]{:S(2)}, u32[]{:S(2)}) collective-permute-start(bf16[528,2048]{1,0:T(8,128)(2,1)} %shard_map.277.refs_12_.refs_18_.refs_6_), channel_id=1, source_target_pairs={{1,0},{2,1},{3,2},{5,4},{6,5},{7,6},{9,8},{10,9},{11,10},{13,12},{... | collective-permute-start | bytes 6488072 | tf_op jit(solution)/shard_map/ppermute | solution.py:1214
  174.9 10.6 %collective-permute-start.18 = (bf16[256,2048]{1,0:T(8,128)(2,1)}, bf16[256,2048]{1,0:T(8,128)(2,1)}, u32[]{:S(2)}, u32[]{:S(2)}) collective-permute-start(bf16[256,2048]{1,0:T(8,128)(2,1)} %collective-permute-done.12.refs_8_.refs_16_), channel_id=1, source_target_pairs={{0,4},{4,0},{8,12},{12,8},{16,20},{20,16},{24,28},{28,24},{1,5},{5... | collective-permute-start | bytes 3145736 | tf_op jit(solution)/shard_map/ppermute | solution.py:1149
  175.4 19.4 %collective-permute-start.19 = (bf16[256,2048]{1,0:T(8,128)(2,1)}, bf16[256,2048]{1,0:T(8,128)(2,1)}, u32[]{:S(2)}, u32[]{:S(2)}) collective-permute-start(bf16[256,2048]{1,0:T(8,128)(2,1)} %collective-permute-done.13.refs_9_.refs_17_), channel_id=1, source_target_pairs={{0,4},{4,0},{8,12},{12,8},{16,20},{20,16},{24,28},{28,24},{1,5},{5... | collective-permute-start | bytes 3145736 | tf_op jit(solution)/shard_map/ppermute | solution.py:1149
  175.5 19.3 %collective-permute-start.20 = (bf16[256,2048]{1,0:T(8,128)(2,1)}, bf16[256,2048]{1,0:T(8,128)(2,1)}, u32[]{:S(2)}, u32[]{:S(2)}) collective-permute-start(bf16[256,2048]{1,0:T(8,128)(2,1)} %collective-permute-done.14.refs_10_.refs_18_), channel_id=1, source_target_pairs={{0,4},{4,0},{8,12},{12,8},{16,20},{20,16},{24,28},{28,24},{1,5},{5... | collective-permute-start | bytes 3145736 | tf_op jit(solution)/shard_map/ppermute | solution.py:1149
  175.9 18.9 %all-to-all-start = ((bf16[8,272,256]{2,1,0:T(8,128)(2,1)}), bf16[8,272,256]{2,1,0:T(8,128)(2,1)S(1)}, u32[]{:S(2)}, u32[]{:S(2)}) async-start(bf16[8,272,256]{2,1,0:T(8,128)(2,1)} %get-tuple-element.147), calls=%async_computation | async-start | bytes 2228224 | tf_op jit(solution)/shard_map/all_to_all | solution.py:1210
  182.8 22.7 %collective-permute-start.21 = (bf16[80,2048]{1,0:T(8,128)(2,1)S(1)}, bf16[80,2048]{1,0:T(8,128)(2,1)}, u32[]{:S(2)}, u32[]{:S(2)}) collective-permute-start(bf16[80,2048]{1,0:T(8,128)(2,1)S(1)} %get-tuple-element.264), channel_id=1, source_target_pairs={{1,2},{2,1},{5,6},{6,5},{9,10},{10,9},{13,14},{14,13},{17,18},{18,... | collective-permute-start | bytes 983048 | tf_op jit(solution)/shard_map/ppermute | solution.py:1214
  184.2 24.0 %collective-permute-start.23 = (bf16[80,2048]{1,0:T(8,128)(2,1)S(1)}, bf16[80,2048]{1,0:T(8,128)(2,1)}, u32[]{:S(2)}, u32[]{:S(2)}) collective-permute-start(bf16[80,2048]{1,0:T(8,128)(2,1)S(1)} %get-tuple-element.264), channel_id=1, source_target_pairs={{1,3},{2,0},{5,7},{6,4},{9,11},{10,8},{13,15},{14,12},{17,19},{18,... | collective-permute-start | bytes 983048 | tf_op jit(solution)/shard_map/ppermute | solution.py:1214
  185.5 22.7 %collective-permute-start.22 = (bf16[80,2048]{1,0:T(8,128)(2,1)S(1)}, bf16[80,2048]{1,0:T(8,128)(2,1)}, u32[]{:S(2)}, u32[]{:S(2)}) collective-permute-start(bf16[80,2048]{1,0:T(8,128)(2,1)S(1)} %get-tuple-element.263), channel_id=1, source_target_pairs={{2,3},{1,0},{6,7},{5,4},{10,11},{9,8},{14,15},{13,12},{18,19},{17,... | collective-permute-start | bytes 983048 | tf_op jit(solution)/shard_map/ppermute | solution.py:1214
  208.1 24.6 %collective-permute-start.24 = (bf16[256,2048]{1,0:T(8,128)(2,1)}, bf16[256,2048]{1,0:T(8,128)(2,1)S(1)}, u32[]{:S(2)}, u32[]{:S(2)}) collective-permute-start(bf16[256,2048]{1,0:T(8,128)(2,1)} %get-tuple-element.161.refs_2_), channel_id=1, source_target_pairs={{0,8},{4,12},{8,0},{12,4},{16,24},{20,28},{24,16},{28,20},{1,9},{5... | collective-permute-start | bytes 3145736 | tf_op jit(solution)/shard_map/ppermute | solution.py:1149
  209.6 24.3 %collective-permute-start.25 = (bf16[256,2048]{1,0:T(8,128)(2,1)}, bf16[256,2048]{1,0:T(8,128)(2,1)S(1)}, u32[]{:S(2)}, u32[]{:S(2)}) collective-permute-start(bf16[256,2048]{1,0:T(8,128)(2,1)} %get-tuple-element.161.refs_2_), channel_id=1, source_target_pairs={{0,16},{4,20},{8,24},{12,28},{16,0},{20,4},{24,8},{28,12},{1,17},{... | collective-permute-start | bytes 3145736 | tf_op jit(solution)/shard_map/ppermute | solution.py:1149
  211.9 23.1 %collective-permute-start.28 = (bf16[272,2048]{1,0:T(8,128)(2,1)S(1)}, bf16[272,2048]{1,0:T(8,128)(2,1)S(1)}, u32[]{:S(2)}, u32[]{:S(2)}) collective-permute-start(bf16[272,2048]{1,0:T(8,128)(2,1)S(1)} %get-tuple-element.262), channel_id=1, source_target_pairs={{1,2},{2,1},{5,6},{6,5},{9,10},{10,9},{13,14},{14,13},{17,18},{18,... | collective-permute-start | bytes 3342344 | tf_op jit(solution)/shard_map/ppermute | solution.py:1214
  212.8 51.0 %collective-permute-start.29 = (bf16[272,2048]{1,0:T(8,128)(2,1)S(1)}, bf16[272,2048]{1,0:T(8,128)(2,1)S(1)}, u32[]{:S(2)}, u32[]{:S(2)}) collective-permute-start(bf16[272,2048]{1,0:T(8,128)(2,1)S(1)} %get-tuple-element.261), channel_id=1, source_target_pairs={{2,3},{1,0},{6,7},{5,4},{10,11},{9,8},{14,15},{13,12},{18,19},{17,... | collective-permute-start | bytes 3342344 | tf_op jit(solution)/shard_map/ppermute | solution.py:1214
  214.1 49.7 %collective-permute-start.30 = (bf16[272,2048]{1,0:T(8,128)(2,1)S(1)}, bf16[272,2048]{1,0:T(8,128)(2,1)S(1)}, u32[]{:S(2)}, u32[]{:S(2)}) collective-permute-start(bf16[272,2048]{1,0:T(8,128)(2,1)S(1)} %get-tuple-element.262), channel_id=1, source_target_pairs={{1,3},{2,0},{5,7},{6,4},{9,11},{10,8},{13,15},{14,12},{17,19},{18,... | collective-permute-start | bytes 3342344 | tf_op jit(solution)/shard_map/ppermute | solution.py:1214
  232.8 31.0 %collective-permute-start.26 = (bf16[128,2048]{1,0:T(8,128)(2,1)S(1)}, bf16[128,2048]{1,0:T(8,128)(2,1)S(1)}, u32[]{:S(2)}, u32[]{:S(2)}) collective-permute-start(bf16[128,2048]{1,0:T(8,128)(2,1)S(1)} %slice.338), channel_id=1, source_target_pairs={{0,16},{4,20},{8,24},{12,28},{16,0},{20,4},{24,8},{28,12},{1,17},{... | collective-permute-start | bytes 1572872 | tf_op jit(solution)/shard_map/ppermute | solution.py:1149
  234.0 29.8 %collective-permute-start.27 = (bf16[128,2048]{1,0:T(8,128)(2,1)S(1)}, bf16[128,2048]{1,0:T(8,128)(2,1)S(1)}, u32[]{:S(2)}, u32[]{:S(2)}) collective-permute-start(bf16[128,2048]{1,0:T(8,128)(2,1)S(1)} %slice.339), channel_id=1, source_target_pairs={{0,8},{4,12},{8,0},{12,4},{16,24},{20,28},{24,16},{28,20},{1,9},{5... | collective-permute-start | bytes 1572872 | tf_op jit(solution)/shard_map/ppermute | solution.py:1149
  263.9 10.7 %collective-permute-start.32 = (bf16[256,2048]{1,0:T(8,128)(2,1)S(1)}, bf16[256,2048]{1,0:T(8,128)(2,1)S(1)}, u32[]{:S(2)}, u32[]{:S(2)}) collective-permute-start(bf16[256,2048]{1,0:T(8,128)(2,1)S(1)} %collective-permute-done.24.refs_3_), channel_id=1, source_target_pairs={{0,4},{4,0},{8,12},{12,8},{16,20},{20,16},{24,28},{28,24},{1,5},{5... | collective-permute-start | bytes 3145736 | tf_op jit(solution)/shard_map/ppermute | solution.py:1149
  264.4 12.0 %collective-permute-start.33 = (bf16[256,2048]{1,0:T(8,128)(2,1)S(1)}, bf16[256,2048]{1,0:T(8,128)(2,1)}, u32[]{:S(2)}, u32[]{:S(2)}) collective-permute-start(bf16[256,2048]{1,0:T(8,128)(2,1)S(1)} %collective-permute-done.25.refs_4_), channel_id=1, source_target_pairs={{0,4},{4,0},{8,12},{12,8},{16,20},{20,16},{24,28},{28,24},{1,5},{5... | collective-permute-start | bytes 3145736 | tf_op jit(solution)/shard_map/ppermute | solution.py:1149
  270.3 32.1 %collective-permute-start.39 = (bf16[256,2048]{1,0:T(8,128)(2,1)S(1)}, bf16[256,2048]{1,0:T(8,128)(2,1)}, u32[]{:S(2)}, u32[]{:S(2)}) collective-permute-start(bf16[256,2048]{1,0:T(8,128)(2,1)S(1)} %bitcast.126), channel_id=1, source_target_pairs={{0,24},{4,28},{8,16},{12,20},{16,8},{20,12},{24,0},{28,4},{1,25},{... | collective-permute-start | bytes 3145736 | tf_op jit(solution)/shard_map/ppermute | solution.py:1149
  271.8 30.6 %collective-permute-start.36 = (bf16[176,2048]{1,0:T(8,128)(2,1)S(1)}, bf16[176,2048]{1,0:T(8,128)(2,1)}, u32[]{:S(2)}, u32[]{:S(2)}) collective-permute-start(bf16[176,2048]{1,0:T(8,128)(2,1)S(1)} %get-tuple-element.260), channel_id=1, source_target_pairs={{1,2},{2,1},{5,6},{6,5},{9,10},{10,9},{13,14},{14,13},{17,18},{18,... | collective-permute-start | bytes 2162696 | tf_op jit(solution)/shard_map/ppermute | solution.py:1214
  273.3 38.7 %collective-permute-start.38 = (bf16[176,2048]{1,0:T(8,128)(2,1)S(1)}, bf16[176,2048]{1,0:T(8,128)(2,1)}, u32[]{:S(2)}, u32[]{:S(2)}) collective-permute-start(bf16[176,2048]{1,0:T(8,128)(2,1)S(1)} %get-tuple-element.260), channel_id=1, source_target_pairs={{1,3},{2,0},{5,7},{6,4},{9,11},{10,8},{13,15},{14,12},{17,19},{18,... | collective-permute-start | bytes 2162696 | tf_op jit(solution)/shard_map/ppermute | solution.py:1214
  274.7 37.4 %collective-permute-start.37 = (bf16[176,2048]{1,0:T(8,128)(2,1)}, bf16[176,2048]{1,0:T(8,128)(2,1)}, u32[]{:S(2)}, u32[]{:S(2)}) collective-permute-start(bf16[176,2048]{1,0:T(8,128)(2,1)} %get-tuple-element.259), channel_id=1, source_target_pairs={{2,3},{1,0},{6,7},{5,4},{10,11},{9,8},{14,15},{13,12},{18,19},{17,... | collective-permute-start | bytes 2162696 | tf_op jit(solution)/shard_map/ppermute | solution.py:1214
  346.3 31.2 %collective-permute-start.41 = (bf16[1024,2048]{1,0:T(8,128)(2,1)}, bf16[1024,2048]{1,0:T(8,128)(2,1)}, u32[]{:S(2)}, u32[]{:S(2)}) collective-permute-start(bf16[1024,2048]{1,0:T(8,128)(2,1)} %get-tuple-element.185), channel_id=1, source_target_pairs={{0,4},{4,0},{8,12},{12,8},{16,20},{20,16},{24,28},{28,24},{1,5},{5... | collective-permute-start | bytes 12582920 | tf_op jit(solution)/shard_map/ppermute | solution.py:1149
  346.5 31.0 %collective-permute-start.42 = (bf16[1024,2048]{1,0:T(8,128)(2,1)}, bf16[1024,2048]{1,0:T(8,128)(2,1)}, u32[]{:S(2)}, u32[]{:S(2)}) collective-permute-start(bf16[1024,2048]{1,0:T(8,128)(2,1)} %get-tuple-element.186), channel_id=1, source_target_pairs={{0,4},{4,0},{8,12},{12,8},{16,20},{20,16},{24,28},{28,24},{1,5},{5... | collective-permute-start | bytes 12582920 | tf_op jit(solution)/shard_map/ppermute | solution.py:1149
  380.4 14.8 %collective-permute-start.46 = (bf16[128,2048]{1,0:T(8,128)(2,1)S(1)}, bf16[128,2048]{1,0:T(8,128)(2,1)S(1)}, u32[]{:S(2)}, u32[]{:S(2)}) collective-permute-start(bf16[128,2048]{1,0:T(8,128)(2,1)S(1)} %get-tuple-element.254), channel_id=1, source_target_pairs={{0,8},{4,12},{8,0},{12,4},{16,24},{20,28},{24,16},{28,20},{1,9},{5... | collective-permute-start | bytes 1572872 | tf_op jit(solution)/shard_map/ppermute | solution.py:1149
  381.3 14.8 %collective-permute-start.44 = (bf16[128,2048]{1,0:T(8,128)(2,1)S(1)}, bf16[128,2048]{1,0:T(8,128)(2,1)S(1)}, u32[]{:S(2)}, u32[]{:S(2)}) collective-permute-start(bf16[128,2048]{1,0:T(8,128)(2,1)S(1)} %get-tuple-element.255), channel_id=1, source_target_pairs={{0,16},{4,20},{8,24},{12,28},{16,0},{20,4},{24,8},{28,12},{1,17},{... | collective-permute-start | bytes 1572872 | tf_op jit(solution)/shard_map/ppermute | solution.py:1149
  383.0 23.6 %collective-permute-start.43 = (bf16[128,2048]{1,0:T(8,128)(2,1)S(1)}, bf16[128,2048]{1,0:T(8,128)(2,1)S(1)}, u32[]{:S(2)}, u32[]{:S(2)}) collective-permute-start(bf16[128,2048]{1,0:T(8,128)(2,1)S(1)} %get-tuple-element.256), channel_id=1, source_target_pairs={{0,8},{4,12},{8,0},{12,4},{16,24},{20,28},{24,16},{28,20},{1,9},{5... | collective-permute-start | bytes 1572872 | tf_op jit(solution)/shard_map/ppermute | solution.py:1149
  383.3 24.0 %collective-permute-start.48 = (bf16[128,2048]{1,0:T(8,128)(2,1)S(1)}, bf16[128,2048]{1,0:T(8,128)(2,1)S(1)}, u32[]{:S(2)}, u32[]{:S(2)}) collective-permute-start(bf16[128,2048]{1,0:T(8,128)(2,1)S(1)} %get-tuple-element.253), channel_id=1, source_target_pairs={{0,16},{4,20},{8,24},{12,28},{16,0},{20,4},{24,8},{28,12},{1,17},{... | collective-permute-start | bytes 1572872 | tf_op jit(solution)/shard_map/ppermute | solution.py:1149
  398.1 18.8 %collective-permute-start.45 = (bf16[128,2048]{1,0:T(8,128)(2,1)S(1)}, bf16[128,2048]{1,0:T(8,128)(2,1)S(1)}, u32[]{:S(2)}, u32[]{:S(2)}) collective-permute-start(bf16[128,2048]{1,0:T(8,128)(2,1)S(1)} %get-tuple-element.258), channel_id=1, source_target_pairs={{0,8},{4,12},{8,0},{12,4},{16,24},{20,28},{24,16},{28,20},{1,9},{5... | collective-permute-start | bytes 1572872 | tf_op jit(solution)/shard_map/ppermute | solution.py:1149
  399.4 18.0 %collective-permute-start.47 = (bf16[128,2048]{1,0:T(8,128)(2,1)S(1)}, bf16[128,2048]{1,0:T(8,128)(2,1)S(1)}, u32[]{:S(2)}, u32[]{:S(2)}) collective-permute-start(bf16[128,2048]{1,0:T(8,128)(2,1)S(1)} %get-tuple-element.257), channel_id=1, source_target_pairs={{0,16},{4,20},{8,24},{12,28},{16,0},{20,4},{24,8},{28,12},{1,17},{... | collective-permute-start | bytes 1572872 | tf_op jit(solution)/shard_map/ppermute | solution.py:1149
  429.5 20.9 %all-to-all-start.1 = ((bf16[8,272,256]{2,1,0:T(8,128)(2,1)}), bf16[8,272,256]{2,1,0:T(8,128)(2,1)}, u32[]{:S(2)}, u32[]{:S(2)}) async-start(bf16[8,272,256]{2,1,0:T(8,128)(2,1)} %get-tuple-element.198), calls=%async_computation.1 | async-start | bytes 2228224 | tf_op jit(solution)/shard_map/all_to_all | solution.py:1210
  435.1 65.2 %reduce-scatter.3.cloned.1.call-start = ((), (), s32[]{:S(2)}) async-start(), calls=%async_computation.7 | async-start | bytes 1351680 | tf_op jit(solution)/shard_map/reduce_scatter | solution.py:1444
  442.9 57.5 %collective-permute-start.49 = (bf16[256,2048]{1,0:T(8,128)(2,1)}, bf16[256,2048]{1,0:T(8,128)(2,1)}, u32[]{:S(2)}, u32[]{:S(2)}) collective-permute-start(bf16[256,2048]{1,0:T(8,128)(2,1)} %get-tuple-element.199), channel_id=1, source_target_pairs={{0,8},{4,12},{8,0},{12,4},{16,24},{20,28},{24,16},{28,20},{1,9},{5... | collective-permute-start | bytes 3145736 | tf_op jit(solution)/shard_map/ppermute | solution.py:1149
  444.3 56.0 %collective-permute-start.50 = (bf16[256,2048]{1,0:T(8,128)(2,1)}, bf16[256,2048]{1,0:T(8,128)(2,1)}, u32[]{:S(2)}, u32[]{:S(2)}) collective-permute-start(bf16[256,2048]{1,0:T(8,128)(2,1)} %get-tuple-element.200), channel_id=1, source_target_pairs={{0,16},{4,20},{8,24},{12,28},{16,0},{20,4},{24,8},{28,12},{1,17},{... | collective-permute-start | bytes 3145736 | tf_op jit(solution)/shard_map/ppermute | solution.py:1149
  444.9 55.5 %collective-permute-start.51 = (bf16[256,2048]{1,0:T(8,128)(2,1)S(1)}, bf16[256,2048]{1,0:T(8,128)(2,1)}, u32[]{:S(2)}, u32[]{:S(2)}) collective-permute-start(bf16[256,2048]{1,0:T(8,128)(2,1)S(1)} %get-tuple-element.201), channel_id=1, source_target_pairs={{0,24},{4,28},{8,16},{12,20},{16,8},{20,12},{24,0},{28,4},{1,25},{... | collective-permute-start | bytes 3145736 | tf_op jit(solution)/shard_map/ppermute | solution.py:1149
  500.3 18.6 %collective-permute-start.52 = (bf16[1024,2048]{1,0:T(8,128)(2,1)}, bf16[1024,2048]{1,0:T(8,128)(2,1)}, u32[]{:S(2)}, u32[]{:S(2)}) collective-permute-start(bf16[1024,2048]{1,0:T(8,128)(2,1)} %get-tuple-element.224), channel_id=1, source_target_pairs={{0,4},{4,0},{8,12},{12,8},{16,20},{20,16},{24,28},{28,24},{1,5},{5... | collective-permute-start | bytes 12582920 | tf_op jit(solution)/shard_map/ppermute | solution.py:1149
  504.2 18.7 %all-to-all-start.2 = ((bf16[8,256,128]{2,1,0:T(8,128)(2,1)}), bf16[8,256,128]{2,1,0:T(8,128)(2,1)S(1)}, u32[]{:S(2)}, u32[]{:S(2)}) async-start(bf16[8,256,128]{2,1,0:T(8,128)(2,1)} %bitcast.36), calls=%async_computation.3 | async-start | bytes 1048576 | tf_op jit(solution)/shard_map/all_to_all | solution.py:1210
  524.4 32.0 %all-to-all-start.3 = ((bf16[8,256,256]{2,1,0:T(8,128)(2,1)}), bf16[8,256,256]{2,1,0:T(8,128)(2,1)S(1)}, u32[]{:S(2)}, u32[]{:S(2)}) async-start(bf16[8,256,256]{2,1,0:T(8,128)(2,1)} %pad_maximum_fusion.2), calls=%async_computation.4 | async-start | bytes 2097152 | tf_op jit(solution)/shard_map/all_to_all | solution.py:1210
  528.7 63.2 %reduce-scatter.5.cloned.1.call-start = ((), (), s32[]{:S(2)}) async-start(), calls=%async_computation.8 | async-start | bytes 655360 | tf_op jit(solution)/shard_map/reduce_scatter | solution.py:1461
  528.7 27.6 %collective-permute-start.53 = (bf16[128,2048]{1,0:T(8,128)(2,1)S(1)}, bf16[128,2048]{1,0:T(8,128)(2,1)}, u32[]{:S(2)}, u32[]{:S(2)}) collective-permute-start(bf16[128,2048]{1,0:T(8,128)(2,1)S(1)} %copy-done.13), channel_id=1, source_target_pairs={{0,8},{4,12},{8,0},{12,4},{16,24},{20,28},{24,16},{28,20},{1,9},{5... | collective-permute-start | bytes 1572872 | tf_op jit(solution)/shard_map/ppermute | solution.py:1149
  530.2 26.1 %collective-permute-start.54 = (bf16[128,2048]{1,0:T(8,128)(2,1)S(1)}, bf16[128,2048]{1,0:T(8,128)(2,1)}, u32[]{:S(2)}, u32[]{:S(2)}) collective-permute-start(bf16[128,2048]{1,0:T(8,128)(2,1)S(1)} %copy-done.12), channel_id=1, source_target_pairs={{0,16},{4,20},{8,24},{12,28},{16,0},{20,4},{24,8},{28,12},{1,17},{... | collective-permute-start | bytes 1572872 | tf_op jit(solution)/shard_map/ppermute | solution.py:1149
  533.6 58.3 %collective-permute-start.60 = (f32[352,128]{1,0:T(8,128)}, f32[352,128]{1,0:T(8,128)}, u32[]{:S(2)}, u32[]{:S(2)}) collective-permute-start(f32[352,128]{1,0:T(8,128)} %slice.332), channel_id=1, source_target_pairs={{0,0},{1,8},{2,16},{3,24},{4,1},{5,9},{6,17},{7,25},{8,2},{9,10},{... | collective-permute-start | bytes 540680 | tf_op jit(solution)/shard_map/ppermute | solution.py:1244
  536.2 37.5 %collective-permute-start.55 = (bf16[128,2048]{1,0:T(8,128)(2,1)}, bf16[128,2048]{1,0:T(8,128)(2,1)}, u32[]{:S(2)}, u32[]{:S(2)}) collective-permute-start(bf16[128,2048]{1,0:T(8,128)(2,1)} %get-tuple-element.247), channel_id=1, source_target_pairs={{0,8},{4,12},{8,0},{12,4},{16,24},{20,28},{24,16},{28,20},{1,9},{5... | collective-permute-start | bytes 1572872 | tf_op jit(solution)/shard_map/ppermute | solution.py:1149
  536.5 40.5 %collective-permute-start.58 = (bf16[128,2048]{1,0:T(8,128)(2,1)S(1)}, bf16[128,2048]{1,0:T(8,128)(2,1)}, u32[]{:S(2)}, u32[]{:S(2)}) collective-permute-start(bf16[128,2048]{1,0:T(8,128)(2,1)S(1)} %get-tuple-element.246), channel_id=1, source_target_pairs={{0,16},{4,20},{8,24},{12,28},{16,0},{20,4},{24,8},{28,12},{1,17},{... | collective-permute-start | bytes 1572872 | tf_op jit(solution)/shard_map/ppermute | solution.py:1149
  565.8 14.2 %collective-permute-start.56 = (bf16[128,2048]{1,0:T(8,128)(2,1)S(1)}, bf16[128,2048]{1,0:T(8,128)(2,1)S(1)}, u32[]{:S(2)}, u32[]{:S(2)}) collective-permute-start(bf16[128,2048]{1,0:T(8,128)(2,1)S(1)} %get-tuple-element.245), channel_id=1, source_target_pairs={{0,8},{4,12},{8,0},{12,4},{16,24},{20,28},{24,16},{28,20},{1,9},{5... | collective-permute-start | bytes 1572872 | tf_op jit(solution)/shard_map/ppermute | solution.py:1149
  568.4 14.7 %collective-permute-start.57 = (bf16[128,2048]{1,0:T(8,128)(2,1)S(1)}, bf16[128,2048]{1,0:T(8,128)(2,1)}, u32[]{:S(2)}, u32[]{:S(2)}) collective-permute-start(bf16[128,2048]{1,0:T(8,128)(2,1)S(1)} %get-tuple-element.244), channel_id=1, source_target_pairs={{0,16},{4,20},{8,24},{12,28},{16,0},{20,4},{24,8},{28,12},{1,17},{... | collective-permute-start | bytes 1572872 | tf_op jit(solution)/shard_map/ppermute | solution.py:1149
  573.6 18.2 %collective-permute-start.61 = (f32[176,128]{1,0:T(8,128)S(1)}, f32[176,128]{1,0:T(8,128)S(1)}, u32[]{:S(2)}, u32[]{:S(2)}) collective-permute-start(f32[176,128]{1,0:T(8,128)S(1)} %slice.333), channel_id=1, source_target_pairs={{0,0},{1,1},{2,16},{3,17},{4,2},{5,3},{6,18},{7,19},{8,4},{9,5},{1... | collective-permute-start | bytes 270344 | tf_op jit(solution)/shard_map/ppermute | solution.py:1244
  583.2 28.5 %all-to-all-start.4 = ((bf16[4,576,128]{2,1,0:T(8,128)(2,1)}), bf16[4,576,128]{2,1,0:T(8,128)(2,1)S(1)}, u32[]{:S(2)}, u32[]{:S(2)}) async-start(bf16[4,576,128]{2,1,0:T(8,128)(2,1)} %constant_dynamic-update-slice_fusion), calls=%async_computation.5 | async-start | bytes 1179648 | tf_op jit(solution)/shard_map/all_to_all | solution.py:1210
  591.9 13.4 %collective-permute-start.59 = (f32[256,128]{1,0:T(8,128)}, f32[256,128]{1,0:T(8,128)S(1)}, u32[]{:S(2)}, u32[]{:S(2)}) collective-permute-start(f32[256,128]{1,0:T(8,128)} %bitcast.163), channel_id=1, source_target_pairs={{0,0},{1,8},{2,16},{3,24},{4,1},{5,9},{6,17},{7,25},{8,2},{9,10},{... | collective-permute-start | bytes 393224 | tf_op jit(solution)/shard_map/ppermute | solution.py:1244
  (57 other events, 663.6 us)
Sparse Core Ops, SparseCore 0:
  438.3 26.2 reduce-scatter.2
  533.7 22.1 reduce-scatter.4

commit v5 on v4

--- a/solution.py
+++ b/solution.py
@@ -374,7 +374,7 @@
     late, refs = refs[:7], refs[7:]
     (
         order_row_ref, order_column_ref, came_ref, zg_ref, mixed_ref, gap_ref, gain_ref, mask_ref, fold_ref,
-        g_proj_ref, gated_ref, small_ref, b_rows_ref, spread_out,
+        gated_ref, small_ref, b_rows_ref, spread_far, spread_near, g_proj_ref,
         grad_ref, grad_nat, d_query_nat, d_forget_nat, d_value_nat, slope_now,
         query_nat, forget_nat, value_nat, states_ref, zq_ref, hid_ref, b_ref, late_sems,
         win_ref, win_sem, spread_ref, spread_sems,
@@ -482,21 +482,23 @@
     go(win_copies, "wait")
     half = devices // 2
 
-    def spread_copy(block, slot):
+    def spread_copy(out, block, slot):
         rows = pl.ds(pl.multiple_of(block * rows_each, rows_each), rows_each)
-        return pltpu.make_async_copy(spread_ref.at[slot], spread_out.at[rows], spread_sems.at[slot])
-
-    @pl.loop(0, half)
-    def _(block):
-        slot = lax.rem(block, 2)
-
-        @pl.when(block >= 2)
-        def _():
-            spread_copy(block - 2, slot).wait()
-
-        rows = pl.ds(pl.multiple_of((block + half) * rows_each, rows_each), rows_each)
-        spread_ref[slot] = mm(g_proj_ref[rows, :], win_ref[...]).astype(jnp.bfloat16)
-        spread_copy(block, slot).start()
+        return pltpu.make_async_copy(spread_ref.at[slot], out.at[rows], spread_sems.at[slot])
+
+    for out, first in ((spread_far, half), (spread_near, 0)):
+
+        @pl.loop(0, half)
+        def _(block, out=out, first=first):
+            slot = lax.rem(block, 2)
+
+            @pl.when((block >= 2) | (first == 0))
+            def _():
+                spread_copy(out, 0, slot).wait()
+
+            rows = pl.ds(pl.multiple_of((block + first) * rows_each, rows_each), rows_each)
+            spread_ref[slot] = mm(g_proj_ref[rows, :], win_ref[...]).astype(jnp.bfloat16)
+            spread_copy(out, block, slot).start()
 
     ranks = mask_ref.shape[1]
     for j in range(4):
@@ -504,7 +506,7 @@
             hid_ref[:, j * ranks : (j + 1) * ranks], g_proj_ref[:, j * width : (j + 1) * width], TN
         )
     for block in range(half - 2, half):
-        spread_copy(block, block % 2).wait()
+        spread_copy(spread_near, block, block % 2).wait()
 
 
 def mixer_backward(ends, mine, place, order, came, kept, win_pieces, gap, gain, hid_in, in_b_wide, mask, fold):
@@ -520,15 +522,16 @@
     return pl.pallas_call(
         lambda *refs: backward_kernel(win_pieces, *refs),
         out_shape=(
-            jax.ShapeDtypeStruct((total, 4 * width), jnp.bfloat16),
             rows,
             jax.ShapeDtypeStruct((total, ranks), jnp.bfloat16),
             jax.ShapeDtypeStruct((ranks, 4 * width), jnp.float32),
             jax.ShapeDtypeStruct((total // 2, model), jnp.bfloat16),
+            jax.ShapeDtypeStruct((total // 2, model), jnp.bfloat16),
         ),
         in_specs=[SMEM] * 3 + [ANY] * (len(win_pieces) + len(late)) + [VMEM] * 9,
-        out_specs=(VMEM,) * 4 + (ANY,),
-        scratch_shapes=[pltpu.VMEM((total, width), jnp.bfloat16)] * 5
+        out_specs=(VMEM,) * 3 + (ANY,) * 2,
+        scratch_shapes=[pltpu.VMEM((total, 4 * width), jnp.bfloat16)]
+        + [pltpu.VMEM((total, width), jnp.bfloat16)] * 5
         + [pltpu.VMEM((heads, HEAD, HEAD), jnp.float32)]
         + [pltpu.VMEM(array.shape, array.dtype) for array in late]
         + [pltpu.SemaphoreType.DMA((len(late),))]
@@ -938,35 +941,6 @@
         compiler_params=params(62),
         cost_estimate=cost(33),
     )(mine, place, *stream.arrays, *arrays_of(weights), *arrays_of(downs), both, hid, mask, *fixed)
-
-
-def spread_kernel(win_pieces, *refs):
-    place_ref, refs = refs[0], refs[1:]
-    pieces, refs = windows(win_pieces, refs), refs[len(win_pieces) :]
-    x_ref, out_ref, win_ref, sem = refs
-    copies = projection_copies(pieces, place_ref[0], win_ref, sem)
-
-    @pl.when(pl.program_id(0) == 0)
-    def _():
-        go(copies, "start")
-        go(copies, "wait")
-
-    out_ref[...] = mm(x_ref[...], win_ref[...]).astype(jnp.bfloat16)
-
-
-def spread(place, values, win_pieces, first, blocks, rows):
-    inner = values.shape[1]
-    model = win_pieces[0][0].shape[1]
-    return pl.pallas_call(
-        lambda *refs: spread_kernel(win_pieces, *refs),
-        grid=(blocks,),
-        out_shape=jax.ShapeDtypeStruct((rows * blocks, model), jnp.bfloat16),
-        in_specs=[SMEM] + [ANY] * len(win_pieces) + [pl.BlockSpec((rows, inner), lambda i: (i + first, 0))],
-        out_specs=tile_spec(rows, model),
-        scratch_shapes=[pltpu.VMEM((inner, model), jnp.bfloat16), pltpu.SemaphoreType.DMA(())],
-        compiler_params=params(62),
-        cost_estimate=cost(8),
-    )(place, *arrays_of(win_pieces), values)
 
 
 def pack_in_kernel(mine_ref, win_ref, wout_ref, out_ref, window, sems):
@@ -1450,39 +1424,39 @@
     out_parts = after(out_parts, d_sent)
     d_came = after(swap(d_sent), *out_parts)
     out_came = [across(part, 2 * i + 2) for i, part in enumerate(out_parts)]
-    g_proj, gated_heads, small_in, in_b_rows, back_in_far = mixer_backward(
+    gated_heads, small_in, in_b_rows, back_in_far, back_in = mixer_backward(
         ends, mine_ref, place_ref, order_both, d_came, kept, win_pieces, gap_mine, gain_mine, hid_in, in_b_wide,
         mask, fold_in,
     )
-    g_proj, gated_heads, small_in, in_b_rows, back_in_far, out_came, early_sum = lax.optimization_barrier(
-        (g_proj, gated_heads, small_in, in_b_rows, back_in_far, out_came, early_sum)
+    gated_heads, small_in, in_b_rows, back_in_far, back_in, out_came, early_sum = lax.optimization_barrier(
+        (gated_heads, small_in, in_b_rows, back_in_far, back_in, out_came, early_sum)
     )
     in_b_early = [in_b_rows.T]
     in_b_sum = lax.psum_scatter(packed_rows(in_b_early), "wt", scatter_dimension=0, tiled=False)
     ffn_b_grad, down_a_grad = unpacked_rows(early_sum, early)
 
     small = (small_in + jnp.concatenate([small, small_far])).reshape(n, rows, RANKS)
-    small, g_proj = lax.optimization_barrier((from_order(small, mine), g_proj))
-    small = swap(small)
     back_in_far = across(back_in_far, 1)
-    back_in = spread(place_ref, g_proj, win_pieces, 0, blocks, rows)
+    small = swap(from_order(small, mine))
     in_parts, in_rest = scatter_parts(back_in, back_in_far)
     in_came = scatter_first(in_parts)
+    block_out = resid + down[:rows].astype(f32) + down_far[:rows].astype(f32)
+    block_out = (block_out + sum(piece.astype(f32) for piece in out_came)).astype(bf16)
+    if in_rest:
+        in_came[0], in_came[1], block_out = lax.optimization_barrier((in_came[0], in_came[1], block_out))
+        in_rest = [in_rest[0] + in_came[1].astype(f32), in_rest[1] + in_came[0].astype(f32)]
+        in_rest = [part.astype(bf16) for part in in_rest]
+        from_x, from_y = [in_came[2], across(in_rest[0], 2)], [across(in_rest[1], 4), in_came[3]]
+    else:
+        from_x, from_y = scatter_second(in_came, in_rest)
     small = jnp.sum(after(small, *in_parts, *in_rest).astype(f32), axis=0)
     small = small.astype(bf16)
     d_hid_in_own = (mm(small, fold_in, NT) * adapter_mask(adapter[:rows], PROJECTIONS)).astype(bf16)
     small = small + mm(d_hid_out, fold_out).astype(bf16)
     small = jnp.broadcast_to(small, (n,) + small.shape)
     small = swap(jnp.concatenate([small, out_b_part.astype(bf16).reshape(n, rows, -1)], axis=2))
-    block_out = resid + down[:rows].astype(f32) + down_far[:rows].astype(f32)
-    block_out = (block_out + sum(piece.astype(f32) for piece in out_came)).astype(bf16)
     if in_rest:
-        in_came[0], in_came[1], small = lax.optimization_barrier((in_came[0], in_came[1], small))
-        in_rest = [in_rest[0] + in_came[1].astype(f32), in_rest[1] + in_came[0].astype(f32)]
-        in_rest = [part.astype(bf16) for part in in_rest]
-        from_x, from_y = [in_came[2], across(in_rest[0], 2)], [across(in_rest[1], 4), in_came[3]]
-    else:
-        from_x, from_y = scatter_second(in_came, in_rest)
+        small, from_x[0], from_y[1] = lax.optimization_barrier((small, from_x[0], from_y[1]))
     out_b_rows = jnp.sum(small[:, :, RANKS:].astype(f32), axis=0).reshape(wide, RANKS)
     small = to_order(small[:, :, :RANKS], mine).reshape(total, RANKS)
     d_hid_in = (mm(small, fold_in, NT) * adapter_mask(adapter, PROJECTIONS)).astype(bf16)

time: 630 us -> 638 us (1.013)
  waiting for transfers between devices: 198 us -> 214 us
    pallas_call x1 -> x0, Pallas kernels: 9.5 us -> none  [spread(): pl.pallas_call(lambda *refs: spread_kernel(win_pieces, *refs), grid=(bloc...]
    ppermute x3, waiting for transfers between devices: 10.5 us -> 19.8 us  [to_owner(): return lax.ppermute(piece, ('seq', 'wt'), moves)]
    ppermute x43, waiting for transfers between devices: 95.9 us -> 102 us  [across(): return lax.ppermute(values, axis, [(i, i ^ bits) for i in range(size)])]
    unnamed x119 -> x117, local copies, waits for them, and re-layouts: 21.4 us -> 19.7 us
  transfers between devices with their start and end apart: 69 -> 69, of which waited for: 26 -> 26; matrix products, arithmetic and copies ran while one was open for 12% -> 11% of each run, Pallas kernels for 30% -> 29%
where the time goes in v5:
time: 638 us; the launch traced here: 631 us
  Pallas kernels  227 us (36%)
  waiting for transfers between devices  214 us (34%)
  starting transfers between devices  88.2 us (14%)
  other arithmetic  44.4 us (7%)
  local copies, waits for them, and re-layouts  35.1 us (6%)
  between operations  15.8 us (2%)
  matrix products  6.59 us (1%)
    ppermute x43, waiting for transfers between devices, across(): return lax.ppermute(values, axis, [(i, i ^ bits) for i in range(size)])  102 us
    ppermute x16, waiting for transfers between devices, along(): return lax.ppermute(values, 'wt', pairs)  79.8 us
    pallas_call x2, Pallas kernels, ffn_back(): pl.pallas_call(lambda *refs: ffn_back_kernel(stream, weights, downs, *ref...  61 us
    pallas_call x1, Pallas kernels, mixer_backward(): pl.pallas_call(lambda *refs: backward_kernel(win_pieces, *refs), out_shap...  53.5 us
    pallas_call x1, Pallas kernels, mixer_forward(): pl.pallas_call(lambda *refs: forward_kernel(stream, win_pieces, *refs), o...  50.1 us
    ppermute x43, starting transfers between devices, across(): return lax.ppermute(values, axis, [(i, i ^ bits) for i in range(size)])  30.9 us
    pallas_call x1, Pallas kernels, ffn_up(): pl.pallas_call(lambda *refs: ffn_up_kernel(stream, weights, *refs), grid=...  26 us
    ppermute x16, starting transfers between devices, along(): return lax.ppermute(values, 'wt', pairs)  24.4 us
  transfers between devices with their start and end apart: 69, of which 26 were waited for; matrix products, arithmetic and copies ran while one was open for 11% of the time, Pallas kernels for 29%

profile of v5, /device:TPU:4, one launch (start us, length us, event | category | flops | bytes accessed | tf_op | source)
XLA Modules:
  0.0 630.8 jit_solution(5819765719360185572)
XLA Ops:
  7.2 2.9 shard_map.276.refs_1_.refs_11_.refs_3_
  10.1 3.6 collective-permute-start
  16.5 1.6 pad_maximum_fusion.refs_3_.refs_2_
  18.1 1.8 constant_dynamic-slice_fusion
  26.6 15.4 %collective-permute-done.refs_2_.refs_12_.refs_4_ = bf16[320,2048]{1,0:T(8,128)(2,1)S(1)} collective-permute-done((bf16[320,2048]{1,0:T(8,128)(2,1)}, bf16[320,2048]{1,0:T(8,128)(2,1)S(1)}, u32[]{:S(2)}, u32[]{:S(2)}) %collective-permute-start) | collective-permute-done | bytes 1310752 | tf_op jit(solution)/shard_map/ppermute | solution.py:1188
  41.9 4.2 collective-permute-done.1.refs_3_.refs_13_.refs_5_
  46.1 3.0 broadcast_select_fusion
  54.0 2.0 copy.57
  56.1 2.3 copy.58
  58.4 2.4 copy.59
  60.8 1.6 pad.42.refs_29_
  63.8 6.6 %collective-permute-done.5.refs_4_.refs_3_ = bf16[512,2048]{1,0:T(8,128)(2,1)} collective-permute-done((bf16[512,2048]{1,0:T(8,128)(2,1)}, bf16[512,2048]{1,0:T(8,128)(2,1)}, u32[]{:S(2)}, u32[]{:S(2)}) %collective-permute-start.5) | collective-permute-done | bytes 2097184 | tf_op jit(solution)/shard_map/ppermute | solution.py:1123
  74.1 9.1 %collective-permute-done.3.refs_5_.refs_15_.refs_7_ = bf16[320,2048]{1,0:T(8,128)(2,1)} collective-permute-done((bf16[320,2048]{1,0:T(8,128)(2,1)}, bf16[320,2048]{1,0:T(8,128)(2,1)}, u32[]{:S(2)}, u32[]{:S(2)}) %collective-permute-start.3) | collective-permute-done | bytes 1310752 | tf_op jit(solution)/shard_map/ppermute | solution.py:1188
  84.5 14.7 %collective-permute-done.7.refs_6_ = bf16[256,2048]{1,0:T(8,128)(2,1)} collective-permute-done((bf16[256,2048]{1,0:T(8,128)(2,1)S(1)}, bf16[256,2048]{1,0:T(8,128)(2,1)}, u32[]{:S(2)}, u32[]{:S(2)}) %collective-permute-start.7) | collective-permute-done | bytes 1048608 | tf_op jit(solution)/shard_map/ppermute | solution.py:1123
  99.2 4.1 shard_map.277.refs_12_.refs_18_.refs_6_
  104.7 10.0 %collective-permute-done.4.refs_6_.refs_16_.refs_8_ = bf16[320,2048]{1,0:T(8,128)(2,1)} collective-permute-done((bf16[320,2048]{1,0:T(8,128)(2,1)}, bf16[320,2048]{1,0:T(8,128)(2,1)}, u32[]{:S(2)}, u32[]{:S(2)}) %collective-permute-start.4) | collective-permute-done | bytes 1310752 | tf_op jit(solution)/shard_map/ppermute | solution.py:1188
  114.7 2.2 shard_map.278.refs_7_.refs_15_
  117.0 1.6 collective-permute-start.12
  120.5 2.6 collective-permute-start.15
  124.7 50.1 %shard_map.279 = (bf16[8,272,256]{2,1,0:T(8,128)(2,1)}, bf16[2048,512]{1,0:T(8,128)(2,1)}, bf16[2048,256]{1,0:T(8,128)(2,1)}, f32[2048,256]{1,0:T(8,128)}, f32[2...) custom-call(s32[4]{0:T(128)} %bitcast.167, ...), custom_call_target="tpu_custom_call" | custom-call | flops 57000001536 | tf_op jit(solution)/shard_map/pallas_call | solution.py:352
  175.9 4.2 all-to-all-start
  186.8 8.0 %all-to-all-done.refs_1_ = bf16[8,272,256]{2,1,0:T(8,128)(2,1)S(1)} async-done(((bf16[8,272,256]{2,1,0:T(8,128)(2,1)}), bf16[8,272,256]{2,1,0:T(8,128)(2,1)S(1)}, u32[]{:S(2)}, u32[]{:S(2)}) %all-to-all-start) | async-done | bytes 1114144 | tf_op jit(solution)/shard_map/all_to_all | solution.py:1184
  195.8 9.7 %shard_map.280 = (f32[256,2048]{1,0:T(8,128)}, bf16[256,2048]{1,0:T(8,128)(2,1)}, bf16[256,128]{1,0:T(8,128)(2,1)}) custom-call(s32[1]{0:T(128)} %bitcast.2.mine_ref.refs_0_.refs_1_, bf16[8,272,256]{2,1,0:T(8,128)(2,1)} %copy-done.9, bf16[256,2048]{1,0:T(8,128)(2,1)} %bitcast.102, bf16[2048,128]{1,0:T(8,128)(2,1)} %refs_4_.3, bf16[2048,128]{1,0:T(8,128)(2,1)} %refs_5_.1, ...), custom_call_target="tpu_custom_call" | custom-call | flops 8000000000 | tf_op jit(solution)/shard_map/pallas_call | solution.py:600
  205.5 2.6 collective-permute-done.22.refs_16_.refs_10_
  210.2 1.7 broadcast_select_fusion.2
  215.4 17.4 %collective-permute-done.24.refs_3_ = bf16[256,2048]{1,0:T(8,128)(2,1)S(1)} collective-permute-done((bf16[256,2048]{1,0:T(8,128)(2,1)}, bf16[256,2048]{1,0:T(8,128)(2,1)S(1)}, u32[]{:S(2)}, u32[]{:S(2)}) %collective-permute-start.24) | collective-permute-done | bytes 1048608 | tf_op jit(solution)/shard_map/ppermute | solution.py:1123
  235.0 28.8 %collective-permute-done.29.refs_22_.refs_16_ = bf16[272,2048]{1,0:T(8,128)(2,1)S(1)} collective-permute-done((bf16[272,2048]{1,0:T(8,128)(2,1)S(1)}, bf16[272,2048]{1,0:T(8,128)(2,1)S(1)}, u32[]{:S(2)}, u32[]{:S(2)}) %collective-permute-start.29) | collective-permute-done | bytes 1114144 | tf_op jit(solution)/shard_map/ppermute | solution.py:1188
  265.1 2.3 broadcast_select_fusion.4
  267.4 2.9 collective-permute-done.34.refs_10_
  271.8 1.6 collective-permute-start.36
  274.7 1.7 collective-permute-start.37
  276.4 26.0 %shard_map.281 = (f32[2048,1536]{1,0:T(8,128)}, bf16[2048,256]{1,0:T(8,128)(2,1)}, bf16[2048,256]{1,0:T(8,128)(2,1)}) custom-call(s32[1]{0:T(128)} %bitcast.2.mine_ref.refs_0_.refs_1_, s32[1]{0:T(128)} %bitcast.3.refs_0_.refs_2_.refs_1_, bf16[256,2048]{1,0:T(8,128)(2,1)} %get-tuple-element.169.refs_2_, bf16[256,2048]{1,0:T(8,128)(2,1)} %copy-done.17, ...), custom_call_target="tpu_custom_call" | custom-call | flops 28000000000 | tf_op jit(solution)/shard_map/pallas_call | solution.py:812
  302.4 9.6 %collective-permute-done.37.refs_22_ = bf16[176,2048]{1,0:T(8,128)(2,1)} collective-permute-done((bf16[176,2048]{1,0:T(8,128)(2,1)}, bf16[176,2048]{1,0:T(8,128)(2,1)}, u32[]{:S(2)}, u32[]{:S(2)}) %collective-permute-start.37) | collective-permute-done | bytes 720928 | tf_op jit(solution)/shard_map/ppermute | solution.py:1188
  315.9 30.4 %shard_map.283 = (bf16[1024,2048]{1,0:T(8,128)(2,1)}, bf16[1024,2048]{1,0:T(8,128)(2,1)}, bf16[1024,128]{1,0:T(8,128)(2,1)}, bf16[1024,256]{1,0:T(8,128)(2,1)}, f32[128,768]{1,0:T(8,128)}, /*index=5*/f32[256,1536]{1,0:T(8,128)}) custom-call(s32[1]{0:T(128)} %bitcast.2.mine_ref.refs_0_.refs_1_, s32[1]{0:T(128)} %bitcast.3.refs_0_.refs_2_.refs_1_, ...), custom_call_target="tpu_custom_call" | custom-call | flops 32999999488 | tf_op jit(solution)/shard_map/pallas_call | solution.py:916
  346.9 30.6 %shard_map.282 = (bf16[1024,2048]{1,0:T(8,128)(2,1)}, bf16[1024,2048]{1,0:T(8,128)(2,1)}, bf16[1024,128]{1,0:T(8,128)(2,1)}, bf16[1024,256]{1,0:T(8,128)(2,1)}, f32[128,768]{1,0:T(8,128)}, /*index=5*/f32[256,1536]{1,0:T(8,128)}) custom-call(s32[1]{0:T(128)} %bitcast.2.mine_ref.refs_0_.refs_1_, s32[1]{0:T(128)} %bitcast.3.refs_0_.refs_2_.refs_1_, ...), custom_call_target="tpu_custom_call" | custom-call | flops 32999999488 | tf_op jit(solution)/shard_map/pallas_call | solution.py:916
  377.6 2.9 add_convert_fusion.10
  381.4 1.7 collective-permute-start.44
  384.6 10.7 %collective-permute-done.46 = bf16[128,2048]{1,0:T(8,128)(2,1)S(1)} collective-permute-done((bf16[128,2048]{1,0:T(8,128)(2,1)S(1)}, bf16[128,2048]{1,0:T(8,128)(2,1)S(1)}, u32[]{:S(2)}, u32[]{:S(2)}) %collective-permute-start.46) | collective-permute-done | bytes 524320 | tf_op jit(solution)/shard_map/ppermute | solution.py:1123
  396.2 2.0 add_convert_fusion.11
  401.4 5.2 collective-permute-done.43.refs_11_
  407.4 9.6 %collective-permute-done.45.refs_12_ = bf16[128,2048]{1,0:T(8,128)(2,1)S(1)} collective-permute-done((bf16[128,2048]{1,0:T(8,128)(2,1)S(1)}, bf16[128,2048]{1,0:T(8,128)(2,1)S(1)}, u32[]{:S(2)}, u32[]{:S(2)}) %collective-permute-start.45) | collective-permute-done | bytes 524320 | tf_op jit(solution)/shard_map/ppermute | solution.py:1123
  418.7 11.0 %shard_map.284 = (bf16[8,272,256]{2,1,0:T(8,128)(2,1)}, f32[256,2048]{1,0:T(8,128)}, bf16[256,128]{1,0:T(8,128)(2,1)}, f32[2048,128]{1,0:T(8,128)}) custom-call(s32[1]{0:T(128)} %bitcast.2.mine_ref.refs_0_.refs_1_, bf16[8,272,256]{2,1,0:T(8,128)(2,1)} %copy-done.9, bf16[256,2048]{1,0:T(8,128)(2,1)} %bitcast.123, f32[256,2048]{1,0:T(8,128)} %get-tuple-element.158.refs_3_, ...), custom_call_target="tpu_custom_call" | custom-call | flops 12000000000 | tf_op jit(solution)/shard_map/pallas_call | solution.py:691
  429.7 5.6 all-to-all-start.1
  437.4 5.8 add_convert_fusion.1
  446.7 4.0 all-to-all-done.1.refs_18_
  450.7 53.5 %shard_map.285 = (bf16[2048,256]{1,0:T(8,128)(2,1)}, bf16[2048,128]{1,0:T(8,128)(2,1)}, f32[128,1024]{1,0:T(8,128)}, bf16[1024,2048]{1,0:T(8,128)(2,1)}, bf16[1024,2048]{1,0:T(8,128)(2,1)}) custom-call(s32[4]{0:T(128)} %bitcast.168, s32[1]{0:T(128)} %bitcast.2.mine_ref.refs_0_.refs_1_, s32[1]{0:T(128)} %bitcast.3.refs_0_.refs_2_.refs_1_, ...), custom_call_target="tpu_custom_call" | custom-call | flops 51000000512 | tf_op jit(solution)/shard_map/pallas_call | solution.py:522
  508.1 5.0 all-to-all-start.2
  513.1 1.9 add_convert_fusion.8
  515.0 1.5 collective-permute-start.53
  517.1 4.8 add_convert_fusion
  522.0 10.7 %collective-permute-done.53 = bf16[128,2048]{1,0:T(8,128)(2,1)S(1)} collective-permute-done((bf16[128,2048]{1,0:T(8,128)(2,1)S(1)}, bf16[128,2048]{1,0:T(8,128)(2,1)S(1)}, u32[]{:S(2)}, u32[]{:S(2)}) %collective-permute-start.53) | collective-permute-done | bytes 524320 | tf_op jit(solution)/shard_map/ppermute | solution.py:1123
  532.7 2.5 add_convert_fusion.4
  536.7 4.0 all-to-all-start.3
  543.1 2.0 copy.67
  545.4 1.9 collective-permute-start.58
  547.2 19.3 %collective-permute-done.55.refs_7_ = bf16[128,2048]{1,0:T(8,128)(2,1)} collective-permute-done((bf16[128,2048]{1,0:T(8,128)(2,1)S(1)}, bf16[128,2048]{1,0:T(8,128)(2,1)}, u32[]{:S(2)}, u32[]{:S(2)}) %collective-permute-start.55) | collective-permute-done | bytes 524320 | tf_op jit(solution)/shard_map/ppermute | solution.py:1123
  570.9 2.6 fusion.13
  578.8 3.5 all-to-all-start.4
  582.3 1.9 collective-permute-start.60
  584.2 6.2 collective-permute-start.61
  590.5 17.0 %collective-permute-done.61 = f32[176,128]{1,0:T(8,128)S(1)} collective-permute-done((f32[176,128]{1,0:T(8,128)S(1)}, f32[176,128]{1,0:T(8,128)S(1)}, u32[]{:S(2)}, u32[]{:S(2)}) %collective-permute-start.61) | collective-permute-done | bytes 90144 | tf_op jit(solution)/shard_map/ppermute | solution.py:1218
  608.5 1.9 collective-permute-start.59
  610.5 6.3 %shard_map.286 = bf16[256,2048]{1,0:T(8,128)(2,1)} custom-call(bf16[256,2048]{1,0:T(8,128)(2,1)} %bitcast.103, f32[256,2048]{1,0:T(8,128)} %get-tuple-element.221.refs_1_, bf16[256,512]{1,0:T(8,128)(2,1)} %fusion.12.refs_2_, bf16[2048,512]{1,0:T(8,128)(2,1)} %refs_3_.3, f32[1,2048]{1,0:T(1,128)} %bitcast.149, bf16[1024,2048]{1,0:T(8,128)(2,1)} %get-tuple-element.215.refs_5_, ...), custom_call_target="tpu_custom_call" | custom-call | flops 4000000000 | tf_op jit(solution)/shard_map/pallas_call | solution.py:734
  616.8 2.8 collective-permute-done.59
  (297 shorter events, 87.6 us)
Async XLA Ops:
  10.1 31.8 %collective-permute-start = (bf16[320,2048]{1,0:T(8,128)(2,1)}, bf16[320,2048]{1,0:T(8,128)(2,1)S(1)}, u32[]{:S(2)}, u32[]{:S(2)}) collective-permute-start(bf16[320,2048]{1,0:T(8,128)(2,1)} %shard_map.276.refs_1_.refs_11_.refs_3_), channel_id=1, source_target_pairs={{0,1},{1,2},{2,3},{4,5},{5,6},{6,7},{8,9},{9,10},{10,11},{12,13},{... | collective-permute-start | bytes 3932168 | tf_op jit(solution)/shard_map/ppermute | solution.py:1188
  13.7 32.5 %collective-permute-start.1 = (bf16[320,2048]{1,0:T(8,128)(2,1)}, bf16[320,2048]{1,0:T(8,128)(2,1)}, u32[]{:S(2)}, u32[]{:S(2)}) collective-permute-start(bf16[320,2048]{1,0:T(8,128)(2,1)} %shard_map.276.refs_1_.refs_11_.refs_3_), channel_id=1, source_target_pairs={{1,0},{2,1},{3,2},{5,4},{6,5},{7,6},{9,8},{10,9},{11,10},{13,12},{... | collective-permute-start | bytes 3932168 | tf_op jit(solution)/shard_map/ppermute | solution.py:1188
  23.0 47.4 %collective-permute-start.5 = (bf16[512,2048]{1,0:T(8,128)(2,1)}, bf16[512,2048]{1,0:T(8,128)(2,1)}, u32[]{:S(2)}, u32[]{:S(2)}) collective-permute-start(bf16[512,2048]{1,0:T(8,128)(2,1)} %pad_maximum_fusion.refs_3_.refs_2_), channel_id=1, source_target_pairs={{0,8},{4,12},{8,0},{12,4},{16,24},{20,28},{24,16},{28,20},{1,9},{5... | collective-permute-start | bytes 6291464 | tf_op jit(solution)/shard_map/ppermute | solution.py:1123
  24.5 47.1 %collective-permute-start.6 = (bf16[512,2048]{1,0:T(8,128)(2,1)}, bf16[512,2048]{1,0:T(8,128)(2,1)}, u32[]{:S(2)}, u32[]{:S(2)}) collective-permute-start(bf16[512,2048]{1,0:T(8,128)(2,1)} %pad_maximum_fusion.refs_3_.refs_2_), channel_id=1, source_target_pairs={{0,16},{4,20},{8,24},{12,28},{16,0},{20,4},{24,8},{28,12},{1,17},{... | collective-permute-start | bytes 6291464 | tf_op jit(solution)/shard_map/ppermute | solution.py:1123
  49.2 24.3 %collective-permute-start.2 = (bf16[320,2048]{1,0:T(8,128)(2,1)}, bf16[320,2048]{1,0:T(8,128)(2,1)S(1)}, u32[]{:S(2)}, u32[]{:S(2)}) collective-permute-start(bf16[320,2048]{1,0:T(8,128)(2,1)} %get-tuple-element.270), channel_id=1, source_target_pairs={{1,2},{2,1},{5,6},{6,5},{9,10},{10,9},{13,14},{14,13},{17,18},{18,... | collective-permute-start | bytes 3932168 | tf_op jit(solution)/shard_map/ppermute | solution.py:1188
  50.1 33.1 %collective-permute-start.3 = (bf16[320,2048]{1,0:T(8,128)(2,1)}, bf16[320,2048]{1,0:T(8,128)(2,1)}, u32[]{:S(2)}, u32[]{:S(2)}) collective-permute-start(bf16[320,2048]{1,0:T(8,128)(2,1)} %get-tuple-element.269), channel_id=1, source_target_pairs={{2,3},{1,0},{6,7},{5,4},{10,11},{9,8},{14,15},{13,12},{18,19},{17,... | collective-permute-start | bytes 3932168 | tf_op jit(solution)/shard_map/ppermute | solution.py:1188
  71.6 46.9 %collective-permute-start.8 = (bf16[512,2048]{1,0:T(8,128)(2,1)}, bf16[512,2048]{1,0:T(8,128)(2,1)}, u32[]{:S(2)}, u32[]{:S(2)}) collective-permute-start(bf16[512,2048]{1,0:T(8,128)(2,1)} %pad_maximum_fusion.refs_3_.refs_2_), channel_id=1, source_target_pairs={{0,4},{4,0},{8,12},{12,8},{16,20},{20,16},{24,28},{28,24},{1,5},{5... | collective-permute-start | bytes 6291464 | tf_op jit(solution)/shard_map/ppermute | solution.py:1123
  71.6 47.4 %collective-permute-start.9 = (bf16[512,2048]{1,0:T(8,128)(2,1)}, bf16[512,2048]{1,0:T(8,128)(2,1)}, u32[]{:S(2)}, u32[]{:S(2)}) collective-permute-start(bf16[512,2048]{1,0:T(8,128)(2,1)} %collective-permute-done.5.refs_4_.refs_3_), channel_id=1, source_target_pairs={{0,4},{4,0},{8,12},{12,8},{16,20},{20,16},{24,28},{28,24},{1,5},{5... | collective-permute-start | bytes 6291464 | tf_op jit(solution)/shard_map/ppermute | solution.py:1123
  73.4 47.1 %collective-permute-start.10 = (bf16[512,2048]{1,0:T(8,128)(2,1)}, bf16[512,2048]{1,0:T(8,128)(2,1)}, u32[]{:S(2)}, u32[]{:S(2)}) collective-permute-start(bf16[512,2048]{1,0:T(8,128)(2,1)} %collective-permute-done.6.refs_5_.refs_4_), channel_id=1, source_target_pairs={{0,4},{4,0},{8,12},{12,8},{16,20},{20,16},{24,28},{28,24},{1,5},{5... | collective-permute-start | bytes 6291464 | tf_op jit(solution)/shard_map/ppermute | solution.py:1123
  73.5 25.7 %collective-permute-start.7 = (bf16[256,2048]{1,0:T(8,128)(2,1)S(1)}, bf16[256,2048]{1,0:T(8,128)(2,1)}, u32[]{:S(2)}, u32[]{:S(2)}) collective-permute-start(bf16[256,2048]{1,0:T(8,128)(2,1)S(1)} %slice.264), channel_id=1, source_target_pairs={{0,8},{4,12},{8,0},{12,4},{16,24},{20,28},{24,16},{28,20},{1,9},{5... | collective-permute-start | bytes 3145736 | tf_op jit(solution)/shard_map/ppermute | solution.py:1123
  83.2 31.5 %collective-permute-start.4 = (bf16[320,2048]{1,0:T(8,128)(2,1)}, bf16[320,2048]{1,0:T(8,128)(2,1)}, u32[]{:S(2)}, u32[]{:S(2)}) collective-permute-start(bf16[320,2048]{1,0:T(8,128)(2,1)} %get-tuple-element.270), channel_id=1, source_target_pairs={{1,3},{2,0},{5,7},{6,4},{9,11},{10,8},{13,15},{14,12},{17,19},{18,... | collective-permute-start | bytes 3932168 | tf_op jit(solution)/shard_map/ppermute | solution.py:1188
  99.2 24.0 %collective-permute-start.11 = (bf16[256,2048]{1,0:T(8,128)(2,1)}, bf16[256,2048]{1,0:T(8,128)(2,1)}, u32[]{:S(2)}, u32[]{:S(2)}) collective-permute-start(bf16[256,2048]{1,0:T(8,128)(2,1)} %collective-permute-done.7.refs_6_), channel_id=1, source_target_pairs={{0,4},{4,0},{8,12},{12,8},{16,20},{20,16},{24,28},{28,24},{1,5},{5... | collective-permute-start | bytes 3145736 | tf_op jit(solution)/shard_map/ppermute | solution.py:1123
  117.0 57.8 %collective-permute-start.12 = (bf16[256,2048]{1,0:T(8,128)(2,1)}, bf16[256,2048]{1,0:T(8,128)(2,1)}, u32[]{:S(2)}, u32[]{:S(2)}) collective-permute-start(bf16[256,2048]{1,0:T(8,128)(2,1)} %shard_map.278.refs_7_.refs_15_), channel_id=1, source_target_pairs={{0,8},{4,12},{8,0},{12,4},{16,24},{20,28},{24,16},{28,20},{1,9},{5... | collective-permute-start | bytes 3145736 | tf_op jit(solution)/shard_map/ppermute | solution.py:1123
  118.5 56.3 %collective-permute-start.13 = (bf16[256,2048]{1,0:T(8,128)(2,1)}, bf16[256,2048]{1,0:T(8,128)(2,1)}, u32[]{:S(2)}, u32[]{:S(2)}) collective-permute-start(bf16[256,2048]{1,0:T(8,128)(2,1)} %shard_map.278.refs_7_.refs_15_), channel_id=1, source_target_pairs={{0,16},{4,20},{8,24},{12,28},{16,0},{20,4},{24,8},{28,12},{1,17},{... | collective-permute-start | bytes 3145736 | tf_op jit(solution)/shard_map/ppermute | solution.py:1123
  119.0 55.8 %collective-permute-start.14 = (bf16[256,2048]{1,0:T(8,128)(2,1)}, bf16[256,2048]{1,0:T(8,128)(2,1)}, u32[]{:S(2)}, u32[]{:S(2)}) collective-permute-start(bf16[256,2048]{1,0:T(8,128)(2,1)} %shard_map.278.refs_7_.refs_15_), channel_id=1, source_target_pairs={{0,24},{4,28},{8,16},{12,20},{16,8},{20,12},{24,0},{28,4},{1,25},{... | collective-permute-start | bytes 3145736 | tf_op jit(solution)/shard_map/ppermute | solution.py:1123
  120.5 54.3 %collective-permute-start.15 = (bf16[528,2048]{1,0:T(8,128)(2,1)}, bf16[528,2048]{1,0:T(8,128)(2,1)}, u32[]{:S(2)}, u32[]{:S(2)}) collective-permute-start(bf16[528,2048]{1,0:T(8,128)(2,1)} %shard_map.277.refs_12_.refs_18_.refs_6_), channel_id=1, source_target_pairs={{0,1},{1,2},{2,3},{4,5},{5,6},{6,7},{8,9},{9,10},{10,11},{12,13},{... | collective-permute-start | bytes 6488072 | tf_op jit(solution)/shard_map/ppermute | solution.py:1188
  123.2 51.7 %collective-permute-start.16 = (bf16[528,2048]{1,0:T(8,128)(2,1)}, bf16[528,2048]{1,0:T(8,128)(2,1)}, u32[]{:S(2)}, u32[]{:S(2)}) collective-permute-start(bf16[528,2048]{1,0:T(8,128)(2,1)} %shard_map.277.refs_12_.refs_18_.refs_6_), channel_id=1, source_target_pairs={{1,0},{2,1},{3,2},{5,4},{6,5},{7,6},{9,8},{10,9},{11,10},{13,12},{... | collective-permute-start | bytes 6488072 | tf_op jit(solution)/shard_map/ppermute | solution.py:1188
  174.9 10.6 %collective-permute-start.18 = (bf16[256,2048]{1,0:T(8,128)(2,1)}, bf16[256,2048]{1,0:T(8,128)(2,1)}, u32[]{:S(2)}, u32[]{:S(2)}) collective-permute-start(bf16[256,2048]{1,0:T(8,128)(2,1)} %collective-permute-done.12.refs_8_.refs_16_), channel_id=1, source_target_pairs={{0,4},{4,0},{8,12},{12,8},{16,20},{20,16},{24,28},{28,24},{1,5},{5... | collective-permute-start | bytes 3145736 | tf_op jit(solution)/shard_map/ppermute | solution.py:1123
  175.4 19.4 %collective-permute-start.19 = (bf16[256,2048]{1,0:T(8,128)(2,1)}, bf16[256,2048]{1,0:T(8,128)(2,1)}, u32[]{:S(2)}, u32[]{:S(2)}) collective-permute-start(bf16[256,2048]{1,0:T(8,128)(2,1)} %collective-permute-done.13.refs_9_.refs_17_), channel_id=1, source_target_pairs={{0,4},{4,0},{8,12},{12,8},{16,20},{20,16},{24,28},{28,24},{1,5},{5... | collective-permute-start | bytes 3145736 | tf_op jit(solution)/shard_map/ppermute | solution.py:1123
  175.5 19.3 %collective-permute-start.20 = (bf16[256,2048]{1,0:T(8,128)(2,1)}, bf16[256,2048]{1,0:T(8,128)(2,1)}, u32[]{:S(2)}, u32[]{:S(2)}) collective-permute-start(bf16[256,2048]{1,0:T(8,128)(2,1)} %collective-permute-done.14.refs_10_.refs_18_), channel_id=1, source_target_pairs={{0,4},{4,0},{8,12},{12,8},{16,20},{20,16},{24,28},{28,24},{1,5},{5... | collective-permute-start | bytes 3145736 | tf_op jit(solution)/shard_map/ppermute | solution.py:1123
  175.9 18.9 %all-to-all-start = ((bf16[8,272,256]{2,1,0:T(8,128)(2,1)}), bf16[8,272,256]{2,1,0:T(8,128)(2,1)S(1)}, u32[]{:S(2)}, u32[]{:S(2)}) async-start(bf16[8,272,256]{2,1,0:T(8,128)(2,1)} %get-tuple-element.154), calls=%async_computation | async-start | bytes 2228224 | tf_op jit(solution)/shard_map/all_to_all | solution.py:1184
  182.8 22.8 %collective-permute-start.21 = (bf16[80,2048]{1,0:T(8,128)(2,1)S(1)}, bf16[80,2048]{1,0:T(8,128)(2,1)}, u32[]{:S(2)}, u32[]{:S(2)}) collective-permute-start(bf16[80,2048]{1,0:T(8,128)(2,1)S(1)} %get-tuple-element.266), channel_id=1, source_target_pairs={{1,2},{2,1},{5,6},{6,5},{9,10},{10,9},{13,14},{14,13},{17,18},{18,... | collective-permute-start | bytes 983048 | tf_op jit(solution)/shard_map/ppermute | solution.py:1188
  184.2 24.0 %collective-permute-start.23 = (bf16[80,2048]{1,0:T(8,128)(2,1)S(1)}, bf16[80,2048]{1,0:T(8,128)(2,1)}, u32[]{:S(2)}, u32[]{:S(2)}) collective-permute-start(bf16[80,2048]{1,0:T(8,128)(2,1)S(1)} %get-tuple-element.266), channel_id=1, source_target_pairs={{1,3},{2,0},{5,7},{6,4},{9,11},{10,8},{13,15},{14,12},{17,19},{18,... | collective-permute-start | bytes 983048 | tf_op jit(solution)/shard_map/ppermute | solution.py:1188
  185.5 22.7 %collective-permute-start.22 = (bf16[80,2048]{1,0:T(8,128)(2,1)S(1)}, bf16[80,2048]{1,0:T(8,128)(2,1)}, u32[]{:S(2)}, u32[]{:S(2)}) collective-permute-start(bf16[80,2048]{1,0:T(8,128)(2,1)S(1)} %get-tuple-element.265), channel_id=1, source_target_pairs={{2,3},{1,0},{6,7},{5,4},{10,11},{9,8},{14,15},{13,12},{18,19},{17,... | collective-permute-start | bytes 983048 | tf_op jit(solution)/shard_map/ppermute | solution.py:1188
  208.1 24.6 %collective-permute-start.24 = (bf16[256,2048]{1,0:T(8,128)(2,1)}, bf16[256,2048]{1,0:T(8,128)(2,1)S(1)}, u32[]{:S(2)}, u32[]{:S(2)}) collective-permute-start(bf16[256,2048]{1,0:T(8,128)(2,1)} %get-tuple-element.169.refs_2_), channel_id=1, source_target_pairs={{0,8},{4,12},{8,0},{12,4},{16,24},{20,28},{24,16},{28,20},{1,9},{5... | collective-permute-start | bytes 3145736 | tf_op jit(solution)/shard_map/ppermute | solution.py:1123
  209.6 24.3 %collective-permute-start.25 = (bf16[256,2048]{1,0:T(8,128)(2,1)}, bf16[256,2048]{1,0:T(8,128)(2,1)S(1)}, u32[]{:S(2)}, u32[]{:S(2)}) collective-permute-start(bf16[256,2048]{1,0:T(8,128)(2,1)} %get-tuple-element.169.refs_2_), channel_id=1, source_target_pairs={{0,16},{4,20},{8,24},{12,28},{16,0},{20,4},{24,8},{28,12},{1,17},{... | collective-permute-start | bytes 3145736 | tf_op jit(solution)/shard_map/ppermute | solution.py:1123
  211.9 23.1 %collective-permute-start.28 = (bf16[272,2048]{1,0:T(8,128)(2,1)S(1)}, bf16[272,2048]{1,0:T(8,128)(2,1)S(1)}, u32[]{:S(2)}, u32[]{:S(2)}) collective-permute-start(bf16[272,2048]{1,0:T(8,128)(2,1)S(1)} %get-tuple-element.264), channel_id=1, source_target_pairs={{1,2},{2,1},{5,6},{6,5},{9,10},{10,9},{13,14},{14,13},{17,18},{18,... | collective-permute-start | bytes 3342344 | tf_op jit(solution)/shard_map/ppermute | solution.py:1188
  212.8 51.0 %collective-permute-start.29 = (bf16[272,2048]{1,0:T(8,128)(2,1)S(1)}, bf16[272,2048]{1,0:T(8,128)(2,1)S(1)}, u32[]{:S(2)}, u32[]{:S(2)}) collective-permute-start(bf16[272,2048]{1,0:T(8,128)(2,1)S(1)} %get-tuple-element.263), channel_id=1, source_target_pairs={{2,3},{1,0},{6,7},{5,4},{10,11},{9,8},{14,15},{13,12},{18,19},{17,... | collective-permute-start | bytes 3342344 | tf_op jit(solution)/shard_map/ppermute | solution.py:1188
  214.1 49.7 %collective-permute-start.30 = (bf16[272,2048]{1,0:T(8,128)(2,1)S(1)}, bf16[272,2048]{1,0:T(8,128)(2,1)S(1)}, u32[]{:S(2)}, u32[]{:S(2)}) collective-permute-start(bf16[272,2048]{1,0:T(8,128)(2,1)S(1)} %get-tuple-element.264), channel_id=1, source_target_pairs={{1,3},{2,0},{5,7},{6,4},{9,11},{10,8},{13,15},{14,12},{17,19},{18,... | collective-permute-start | bytes 3342344 | tf_op jit(solution)/shard_map/ppermute | solution.py:1188
  232.8 31.0 %collective-permute-start.26 = (bf16[128,2048]{1,0:T(8,128)(2,1)S(1)}, bf16[128,2048]{1,0:T(8,128)(2,1)S(1)}, u32[]{:S(2)}, u32[]{:S(2)}) collective-permute-start(bf16[128,2048]{1,0:T(8,128)(2,1)S(1)} %slice.338), channel_id=1, source_target_pairs={{0,16},{4,20},{8,24},{12,28},{16,0},{20,4},{24,8},{28,12},{1,17},{... | collective-permute-start | bytes 1572872 | tf_op jit(solution)/shard_map/ppermute | solution.py:1123
  234.0 29.8 %collective-permute-start.27 = (bf16[128,2048]{1,0:T(8,128)(2,1)S(1)}, bf16[128,2048]{1,0:T(8,128)(2,1)S(1)}, u32[]{:S(2)}, u32[]{:S(2)}) collective-permute-start(bf16[128,2048]{1,0:T(8,128)(2,1)S(1)} %slice.339), channel_id=1, source_target_pairs={{0,8},{4,12},{8,0},{12,4},{16,24},{20,28},{24,16},{28,20},{1,9},{5... | collective-permute-start | bytes 1572872 | tf_op jit(solution)/shard_map/ppermute | solution.py:1123
  263.8 9.5 %collective-permute-start.31 = (bf16[256,2048]{1,0:T(8,128)(2,1)S(1)}, bf16[256,2048]{1,0:T(8,128)(2,1)S(1)}, u32[]{:S(2)}, u32[]{:S(2)}) collective-permute-start(bf16[256,2048]{1,0:T(8,128)(2,1)S(1)} %copy-done.34), channel_id=1, source_target_pairs={{0,4},{4,0},{8,12},{12,8},{16,20},{20,16},{24,28},{28,24},{1,5},{5... | collective-permute-start | bytes 3145736 | tf_op jit(solution)/shard_map/ppermute | solution.py:1123
  263.9 10.7 %collective-permute-start.32 = (bf16[256,2048]{1,0:T(8,128)(2,1)S(1)}, bf16[256,2048]{1,0:T(8,128)(2,1)S(1)}, u32[]{:S(2)}, u32[]{:S(2)}) collective-permute-start(bf16[256,2048]{1,0:T(8,128)(2,1)S(1)} %collective-permute-done.24.refs_3_), channel_id=1, source_target_pairs={{0,4},{4,0},{8,12},{12,8},{16,20},{20,16},{24,28},{28,24},{1,5},{5... | collective-permute-start | bytes 3145736 | tf_op jit(solution)/shard_map/ppermute | solution.py:1123
  264.4 12.0 %collective-permute-start.33 = (bf16[256,2048]{1,0:T(8,128)(2,1)S(1)}, bf16[256,2048]{1,0:T(8,128)(2,1)}, u32[]{:S(2)}, u32[]{:S(2)}) collective-permute-start(bf16[256,2048]{1,0:T(8,128)(2,1)S(1)} %collective-permute-done.25.refs_4_), channel_id=1, source_target_pairs={{0,4},{4,0},{8,12},{12,8},{16,20},{20,16},{24,28},{28,24},{1,5},{5... | collective-permute-start | bytes 3145736 | tf_op jit(solution)/shard_map/ppermute | solution.py:1123
  270.3 32.1 %collective-permute-start.39 = (bf16[256,2048]{1,0:T(8,128)(2,1)S(1)}, bf16[256,2048]{1,0:T(8,128)(2,1)}, u32[]{:S(2)}, u32[]{:S(2)}) collective-permute-start(bf16[256,2048]{1,0:T(8,128)(2,1)S(1)} %bitcast.125), channel_id=1, source_target_pairs={{0,24},{4,28},{8,16},{12,20},{16,8},{20,12},{24,0},{28,4},{1,25},{... | collective-permute-start | bytes 3145736 | tf_op jit(solution)/shard_map/ppermute | solution.py:1123
  271.8 30.7 %collective-permute-start.36 = (bf16[176,2048]{1,0:T(8,128)(2,1)S(1)}, bf16[176,2048]{1,0:T(8,128)(2,1)}, u32[]{:S(2)}, u32[]{:S(2)}) collective-permute-start(bf16[176,2048]{1,0:T(8,128)(2,1)S(1)} %get-tuple-element.262), channel_id=1, source_target_pairs={{1,2},{2,1},{5,6},{6,5},{9,10},{10,9},{13,14},{14,13},{17,18},{18,... | collective-permute-start | bytes 2162696 | tf_op jit(solution)/shard_map/ppermute | solution.py:1188
  273.3 38.7 %collective-permute-start.38 = (bf16[176,2048]{1,0:T(8,128)(2,1)S(1)}, bf16[176,2048]{1,0:T(8,128)(2,1)}, u32[]{:S(2)}, u32[]{:S(2)}) collective-permute-start(bf16[176,2048]{1,0:T(8,128)(2,1)S(1)} %get-tuple-element.262), channel_id=1, source_target_pairs={{1,3},{2,0},{5,7},{6,4},{9,11},{10,8},{13,15},{14,12},{17,19},{18,... | collective-permute-start | bytes 2162696 | tf_op jit(solution)/shard_map/ppermute | solution.py:1188
  274.7 37.4 %collective-permute-start.37 = (bf16[176,2048]{1,0:T(8,128)(2,1)}, bf16[176,2048]{1,0:T(8,128)(2,1)}, u32[]{:S(2)}, u32[]{:S(2)}) collective-permute-start(bf16[176,2048]{1,0:T(8,128)(2,1)} %get-tuple-element.261), channel_id=1, source_target_pairs={{2,3},{1,0},{6,7},{5,4},{10,11},{9,8},{14,15},{13,12},{18,19},{17,... | collective-permute-start | bytes 2162696 | tf_op jit(solution)/shard_map/ppermute | solution.py:1188
  346.4 31.2 %collective-permute-start.41 = (bf16[1024,2048]{1,0:T(8,128)(2,1)}, bf16[1024,2048]{1,0:T(8,128)(2,1)}, u32[]{:S(2)}, u32[]{:S(2)}) collective-permute-start(bf16[1024,2048]{1,0:T(8,128)(2,1)} %get-tuple-element.193), channel_id=1, source_target_pairs={{0,4},{4,0},{8,12},{12,8},{16,20},{20,16},{24,28},{28,24},{1,5},{5... | collective-permute-start | bytes 12582920 | tf_op jit(solution)/shard_map/ppermute | solution.py:1123
  346.5 31.0 %collective-permute-start.42 = (bf16[1024,2048]{1,0:T(8,128)(2,1)}, bf16[1024,2048]{1,0:T(8,128)(2,1)}, u32[]{:S(2)}, u32[]{:S(2)}) collective-permute-start(bf16[1024,2048]{1,0:T(8,128)(2,1)} %get-tuple-element.194), channel_id=1, source_target_pairs={{0,4},{4,0},{8,12},{12,8},{16,20},{20,16},{24,28},{28,24},{1,5},{5... | collective-permute-start | bytes 12582920 | tf_op jit(solution)/shard_map/ppermute | solution.py:1123
  380.5 14.8 %collective-permute-start.46 = (bf16[128,2048]{1,0:T(8,128)(2,1)S(1)}, bf16[128,2048]{1,0:T(8,128)(2,1)S(1)}, u32[]{:S(2)}, u32[]{:S(2)}) collective-permute-start(bf16[128,2048]{1,0:T(8,128)(2,1)S(1)} %get-tuple-element.256), channel_id=1, source_target_pairs={{0,8},{4,12},{8,0},{12,4},{16,24},{20,28},{24,16},{28,20},{1,9},{5... | collective-permute-start | bytes 1572872 | tf_op jit(solution)/shard_map/ppermute | solution.py:1123
  381.4 14.8 %collective-permute-start.44 = (bf16[128,2048]{1,0:T(8,128)(2,1)S(1)}, bf16[128,2048]{1,0:T(8,128)(2,1)S(1)}, u32[]{:S(2)}, u32[]{:S(2)}) collective-permute-start(bf16[128,2048]{1,0:T(8,128)(2,1)S(1)} %get-tuple-element.257), channel_id=1, source_target_pairs={{0,16},{4,20},{8,24},{12,28},{16,0},{20,4},{24,8},{28,12},{1,17},{... | collective-permute-start | bytes 1572872 | tf_op jit(solution)/shard_map/ppermute | solution.py:1123
  383.0 23.5 %collective-permute-start.43 = (bf16[128,2048]{1,0:T(8,128)(2,1)S(1)}, bf16[128,2048]{1,0:T(8,128)(2,1)S(1)}, u32[]{:S(2)}, u32[]{:S(2)}) collective-permute-start(bf16[128,2048]{1,0:T(8,128)(2,1)S(1)} %get-tuple-element.258), channel_id=1, source_target_pairs={{0,8},{4,12},{8,0},{12,4},{16,24},{20,28},{24,16},{28,20},{1,9},{5... | collective-permute-start | bytes 1572872 | tf_op jit(solution)/shard_map/ppermute | solution.py:1123
  383.4 24.0 %collective-permute-start.48 = (bf16[128,2048]{1,0:T(8,128)(2,1)S(1)}, bf16[128,2048]{1,0:T(8,128)(2,1)S(1)}, u32[]{:S(2)}, u32[]{:S(2)}) collective-permute-start(bf16[128,2048]{1,0:T(8,128)(2,1)S(1)} %get-tuple-element.255), channel_id=1, source_target_pairs={{0,16},{4,20},{8,24},{12,28},{16,0},{20,4},{24,8},{28,12},{1,17},{... | collective-permute-start | bytes 1572872 | tf_op jit(solution)/shard_map/ppermute | solution.py:1123
  398.2 18.8 %collective-permute-start.45 = (bf16[128,2048]{1,0:T(8,128)(2,1)S(1)}, bf16[128,2048]{1,0:T(8,128)(2,1)S(1)}, u32[]{:S(2)}, u32[]{:S(2)}) collective-permute-start(bf16[128,2048]{1,0:T(8,128)(2,1)S(1)} %get-tuple-element.260), channel_id=1, source_target_pairs={{0,8},{4,12},{8,0},{12,4},{16,24},{20,28},{24,16},{28,20},{1,9},{5... | collective-permute-start | bytes 1572872 | tf_op jit(solution)/shard_map/ppermute | solution.py:1123
  399.5 18.0 %collective-permute-start.47 = (bf16[128,2048]{1,0:T(8,128)(2,1)S(1)}, bf16[128,2048]{1,0:T(8,128)(2,1)S(1)}, u32[]{:S(2)}, u32[]{:S(2)}) collective-permute-start(bf16[128,2048]{1,0:T(8,128)(2,1)S(1)} %get-tuple-element.259), channel_id=1, source_target_pairs={{0,16},{4,20},{8,24},{12,28},{16,0},{20,4},{24,8},{28,12},{1,17},{... | collective-permute-start | bytes 1572872 | tf_op jit(solution)/shard_map/ppermute | solution.py:1123
  429.7 20.9 %all-to-all-start.1 = ((bf16[8,272,256]{2,1,0:T(8,128)(2,1)}), bf16[8,272,256]{2,1,0:T(8,128)(2,1)}, u32[]{:S(2)}, u32[]{:S(2)}) async-start(bf16[8,272,256]{2,1,0:T(8,128)(2,1)} %get-tuple-element.197), calls=%async_computation.1 | async-start | bytes 2228224 | tf_op jit(solution)/shard_map/all_to_all | solution.py:1184
  435.4 68.8 %reduce-scatter.3.cloned.1.call-start = ((), (), s32[]{:S(2)}) async-start(), calls=%async_computation.7 | async-start | bytes 1351680 | tf_op jit(solution)/shard_map/reduce_scatter | solution.py:1418
  443.2 61.0 %collective-permute-start.49 = (bf16[256,2048]{1,0:T(8,128)(2,1)}, bf16[256,2048]{1,0:T(8,128)(2,1)}, u32[]{:S(2)}, u32[]{:S(2)}) collective-permute-start(bf16[256,2048]{1,0:T(8,128)(2,1)} %get-tuple-element.200), channel_id=1, source_target_pairs={{0,8},{4,12},{8,0},{12,4},{16,24},{20,28},{24,16},{28,20},{1,9},{5... | collective-permute-start | bytes 3145736 | tf_op jit(solution)/shard_map/ppermute | solution.py:1123
  444.7 59.5 %collective-permute-start.50 = (bf16[256,2048]{1,0:T(8,128)(2,1)}, bf16[256,2048]{1,0:T(8,128)(2,1)}, u32[]{:S(2)}, u32[]{:S(2)}) collective-permute-start(bf16[256,2048]{1,0:T(8,128)(2,1)} %get-tuple-element.201), channel_id=1, source_target_pairs={{0,16},{4,20},{8,24},{12,28},{16,0},{20,4},{24,8},{28,12},{1,17},{... | collective-permute-start | bytes 3145736 | tf_op jit(solution)/shard_map/ppermute | solution.py:1123
  445.2 59.0 %collective-permute-start.51 = (bf16[256,2048]{1,0:T(8,128)(2,1)S(1)}, bf16[256,2048]{1,0:T(8,128)(2,1)}, u32[]{:S(2)}, u32[]{:S(2)}) collective-permute-start(bf16[256,2048]{1,0:T(8,128)(2,1)S(1)} %get-tuple-element.202), channel_id=1, source_target_pairs={{0,24},{4,28},{8,16},{12,20},{16,8},{20,12},{24,0},{28,4},{1,25},{... | collective-permute-start | bytes 3145736 | tf_op jit(solution)/shard_map/ppermute | solution.py:1123
  508.1 27.1 %all-to-all-start.2 = ((bf16[8,256,128]{2,1,0:T(8,128)(2,1)}), bf16[8,256,128]{2,1,0:T(8,128)(2,1)S(1)}, u32[]{:S(2)}, u32[]{:S(2)}) async-start(bf16[8,256,128]{2,1,0:T(8,128)(2,1)} %bitcast.36), calls=%async_computation.3 | async-start | bytes 1048576 | tf_op jit(solution)/shard_map/all_to_all | solution.py:1184
  515.0 17.6 %collective-permute-start.53 = (bf16[128,2048]{1,0:T(8,128)(2,1)S(1)}, bf16[128,2048]{1,0:T(8,128)(2,1)S(1)}, u32[]{:S(2)}, u32[]{:S(2)}) collective-permute-start(bf16[128,2048]{1,0:T(8,128)(2,1)S(1)} %get-tuple-element.251), channel_id=1, source_target_pairs={{0,8},{4,12},{8,0},{12,4},{16,24},{20,28},{24,16},{28,20},{1,9},{5... | collective-permute-start | bytes 1572872 | tf_op jit(solution)/shard_map/ppermute | solution.py:1123
  516.6 16.1 %collective-permute-start.54 = (bf16[128,2048]{1,0:T(8,128)(2,1)S(1)}, bf16[128,2048]{1,0:T(8,128)(2,1)S(1)}, u32[]{:S(2)}, u32[]{:S(2)}) collective-permute-start(bf16[128,2048]{1,0:T(8,128)(2,1)S(1)} %get-tuple-element.250), channel_id=1, source_target_pairs={{0,16},{4,20},{8,24},{12,28},{16,0},{20,4},{24,8},{28,12},{1,17},{... | collective-permute-start | bytes 1572872 | tf_op jit(solution)/shard_map/ppermute | solution.py:1123
  536.7 29.9 %all-to-all-start.3 = ((bf16[8,256,256]{2,1,0:T(8,128)(2,1)}), bf16[8,256,256]{2,1,0:T(8,128)(2,1)S(1)}, u32[]{:S(2)}, u32[]{:S(2)}) async-start(bf16[8,256,256]{2,1,0:T(8,128)(2,1)} %pad_maximum_fusion.2), calls=%async_computation.4 | async-start | bytes 2097152 | tf_op jit(solution)/shard_map/all_to_all | solution.py:1184
  540.7 67.8 %reduce-scatter.5.cloned.1.call-start = ((), (), s32[]{:S(2)}) async-start(), calls=%async_computation.8 | async-start | bytes 655360 | tf_op jit(solution)/shard_map/reduce_scatter | solution.py:1435
  541.0 25.6 %collective-permute-start.55 = (bf16[128,2048]{1,0:T(8,128)(2,1)S(1)}, bf16[128,2048]{1,0:T(8,128)(2,1)}, u32[]{:S(2)}, u32[]{:S(2)}) collective-permute-start(bf16[128,2048]{1,0:T(8,128)(2,1)S(1)} %get-tuple-element.249), channel_id=1, source_target_pairs={{0,8},{4,12},{8,0},{12,4},{16,24},{20,28},{24,16},{28,20},{1,9},{5... | collective-permute-start | bytes 1572872 | tf_op jit(solution)/shard_map/ppermute | solution.py:1123
  542.5 24.0 %collective-permute-start.56 = (bf16[128,2048]{1,0:T(8,128)(2,1)S(1)}, bf16[128,2048]{1,0:T(8,128)(2,1)}, u32[]{:S(2)}, u32[]{:S(2)}) collective-permute-start(bf16[128,2048]{1,0:T(8,128)(2,1)S(1)} %get-tuple-element.248), channel_id=1, source_target_pairs={{0,16},{4,20},{8,24},{12,28},{16,0},{20,4},{24,8},{28,12},{1,17},{... | collective-permute-start | bytes 1572872 | tf_op jit(solution)/shard_map/ppermute | solution.py:1123
  545.1 33.6 %collective-permute-start.57 = (bf16[128,2048]{1,0:T(8,128)(2,1)S(1)}, bf16[128,2048]{1,0:T(8,128)(2,1)}, u32[]{:S(2)}, u32[]{:S(2)}) collective-permute-start(bf16[128,2048]{1,0:T(8,128)(2,1)S(1)} %get-tuple-element.247), channel_id=1, source_target_pairs={{0,8},{4,12},{8,0},{12,4},{16,24},{20,28},{24,16},{28,20},{1,9},{5... | collective-permute-start | bytes 1572872 | tf_op jit(solution)/shard_map/ppermute | solution.py:1123
  545.4 33.4 %collective-permute-start.58 = (bf16[128,2048]{1,0:T(8,128)(2,1)S(1)}, bf16[128,2048]{1,0:T(8,128)(2,1)}, u32[]{:S(2)}, u32[]{:S(2)}) collective-permute-start(bf16[128,2048]{1,0:T(8,128)(2,1)S(1)} %get-tuple-element.246), channel_id=1, source_target_pairs={{0,16},{4,20},{8,24},{12,28},{16,0},{20,4},{24,8},{28,12},{1,17},{... | collective-permute-start | bytes 1572872 | tf_op jit(solution)/shard_map/ppermute | solution.py:1123
  578.8 40.8 %all-to-all-start.4 = ((bf16[4,576,128]{2,1,0:T(8,128)(2,1)}), bf16[4,576,128]{2,1,0:T(8,128)(2,1)S(1)}, u32[]{:S(2)}, u32[]{:S(2)}) async-start(bf16[4,576,128]{2,1,0:T(8,128)(2,1)} %constant_dynamic-update-slice_fusion), calls=%async_computation.5 | async-start | bytes 1179648 | tf_op jit(solution)/shard_map/all_to_all | solution.py:1184
  582.3 25.2 %collective-permute-start.60 = (f32[352,128]{1,0:T(8,128)S(1)}, f32[352,128]{1,0:T(8,128)S(1)}, u32[]{:S(2)}, u32[]{:S(2)}) collective-permute-start(f32[352,128]{1,0:T(8,128)S(1)} %slice.332), channel_id=1, source_target_pairs={{0,0},{1,8},{2,16},{3,24},{4,1},{5,9},{6,17},{7,25},{8,2},{9,10},{... | collective-permute-start | bytes 540680 | tf_op jit(solution)/shard_map/ppermute | solution.py:1218
  584.2 23.2 %collective-permute-start.61 = (f32[176,128]{1,0:T(8,128)S(1)}, f32[176,128]{1,0:T(8,128)S(1)}, u32[]{:S(2)}, u32[]{:S(2)}) collective-permute-start(f32[176,128]{1,0:T(8,128)S(1)} %slice.333), channel_id=1, source_target_pairs={{0,0},{1,1},{2,16},{3,17},{4,2},{5,3},{6,18},{7,19},{8,4},{9,5},{1... | collective-permute-start | bytes 270344 | tf_op jit(solution)/shard_map/ppermute | solution.py:1218
  608.5 11.0 %collective-permute-start.59 = (f32[256,128]{1,0:T(8,128)}, f32[256,128]{1,0:T(8,128)S(1)}, u32[]{:S(2)}, u32[]{:S(2)}) collective-permute-start(f32[256,128]{1,0:T(8,128)} %bitcast.163), channel_id=1, source_target_pairs={{0,0},{1,8},{2,16},{3,24},{4,1},{5,9},{6,17},{7,25},{8,2},{9,10},{... | collective-permute-start | bytes 393224 | tf_op jit(solution)/shard_map/ppermute | solution.py:1218
  (56 other events, 720.6 us)
Sparse Core Ops, SparseCore 0:
  438.5 26.2 reduce-scatter.2
  545.3 19.6 reduce-scatter.4

commit v6 on v4

--- a/solution.py
+++ b/solution.py
@@ -1477,9 +1477,10 @@
     block_out = resid + down[:rows].astype(f32) + down_far[:rows].astype(f32)
     block_out = (block_out + sum(piece.astype(f32) for piece in out_came)).astype(bf16)
     if in_rest:
-        in_came[0], in_came[1], small = lax.optimization_barrier((in_came[0], in_came[1], small))
+        in_came[0], in_came[1], small, block_out = lax.optimization_barrier((in_came[0], in_came[1], small, block_out))
         in_rest = [in_rest[0] + in_came[1].astype(f32), in_rest[1] + in_came[0].astype(f32)]
         in_rest = [part.astype(bf16) for part in in_rest]
+        small = after(small, *in_rest)
         from_x, from_y = [in_came[2], across(in_rest[0], 2)], [across(in_rest[1], 4), in_came[3]]
     else:
         from_x, from_y = scatter_second(in_came, in_rest)

time: 630 us -> 641 us (1.017)
  waiting for transfers between devices: 198 us -> 210 us
    ppermute x3, waiting for transfers between devices: 10.5 us -> 25.5 us  [to_owner(): return lax.ppermute(piece, ('seq', 'wt'), moves)]
    unnamed x119 -> x117, local copies, waits for them, and re-layouts: 21.4 us -> 20.5 us
where the time goes in v6:
time: 641 us; the launch traced here: 635 us
  Pallas kernels  233 us (36%)
  waiting for transfers between devices  210 us (33%)
  starting transfers between devices  87.2 us (14%)
  other arithmetic  46.1 us (7%)
  local copies, waits for them, and re-layouts  35.9 us (6%)
  between operations  15.8 us (2%)
  matrix products  6.57 us (1%)
    ppermute x43, waiting for transfers between devices, across(): return lax.ppermute(values, axis, [(i, i ^ bits) for i in range(size)])  93 us
    ppermute x16, waiting for transfers between devices, along(): return lax.ppermute(values, 'wt', pairs)  79.8 us
    pallas_call x2, Pallas kernels, ffn_back(): pl.pallas_call(lambda *refs: ffn_back_kernel(stream, weights, downs, *ref...  61 us
    pallas_call x1, Pallas kernels, mixer_forward(): pl.pallas_call(lambda *refs: forward_kernel(stream, win_pieces, *refs), o...  50.1 us
    pallas_call x1, Pallas kernels, mixer_backward(): pl.pallas_call(lambda *refs: backward_kernel(win_pieces, *refs), out_shap...  49.8 us
    ppermute x43, starting transfers between devices, across(): return lax.ppermute(values, axis, [(i, i ^ bits) for i in range(size)])  29.6 us
    pallas_call x1, Pallas kernels, ffn_up(): pl.pallas_call(lambda *refs: ffn_up_kernel(stream, weights, *refs), grid=...  26 us
    ppermute x3, waiting for transfers between devices, to_owner(): return lax.ppermute(piece, ('seq', 'wt'), moves)  25.5 us
  transfers between devices with their start and end apart: 69, of which 26 were waited for; matrix products, arithmetic and copies ran while one was open for 12% of the time, Pallas kernels for 30%

profile of v6, /device:TPU:4, one launch (start us, length us, event | category | flops | bytes accessed | tf_op | source)
XLA Modules:
  0.0 634.6 jit_solution(7676167226178618360)
XLA Ops:
  7.2 2.9 shard_map.276.refs_1_.refs_11_.refs_3_
  10.1 3.6 collective-permute-start
  16.5 1.6 pad_maximum_fusion.refs_3_.refs_2_
  18.1 1.8 constant_dynamic-slice_fusion
  26.6 15.4 %collective-permute-done.refs_2_.refs_12_.refs_4_ = bf16[320,2048]{1,0:T(8,128)(2,1)S(1)} collective-permute-done((bf16[320,2048]{1,0:T(8,128)(2,1)}, bf16[320,2048]{1,0:T(8,128)(2,1)S(1)}, u32[]{:S(2)}, u32[]{:S(2)}) %collective-permute-start) | collective-permute-done | bytes 1310752 | tf_op jit(solution)/shard_map/ppermute | solution.py:1214
  41.9 4.2 collective-permute-done.1.refs_3_.refs_13_.refs_5_
  46.1 3.0 broadcast_select_fusion
  54.0 2.0 copy.57
  56.1 2.3 copy.58
  58.4 2.5 copy.59
  60.8 1.6 pad.42.refs_29_
  63.8 6.6 %collective-permute-done.5.refs_4_.refs_3_ = bf16[512,2048]{1,0:T(8,128)(2,1)} collective-permute-done((bf16[512,2048]{1,0:T(8,128)(2,1)}, bf16[512,2048]{1,0:T(8,128)(2,1)}, u32[]{:S(2)}, u32[]{:S(2)}) %collective-permute-start.5) | collective-permute-done | bytes 2097184 | tf_op jit(solution)/shard_map/ppermute | solution.py:1149
  74.1 9.1 %collective-permute-done.3.refs_5_.refs_15_.refs_7_ = bf16[320,2048]{1,0:T(8,128)(2,1)} collective-permute-done((bf16[320,2048]{1,0:T(8,128)(2,1)}, bf16[320,2048]{1,0:T(8,128)(2,1)}, u32[]{:S(2)}, u32[]{:S(2)}) %collective-permute-start.3) | collective-permute-done | bytes 1310752 | tf_op jit(solution)/shard_map/ppermute | solution.py:1214
  84.5 14.7 %collective-permute-done.7.refs_6_ = bf16[256,2048]{1,0:T(8,128)(2,1)} collective-permute-done((bf16[256,2048]{1,0:T(8,128)(2,1)S(1)}, bf16[256,2048]{1,0:T(8,128)(2,1)}, u32[]{:S(2)}, u32[]{:S(2)}) %collective-permute-start.7) | collective-permute-done | bytes 1048608 | tf_op jit(solution)/shard_map/ppermute | solution.py:1149
  99.2 4.1 shard_map.277.refs_12_.refs_18_.refs_6_
  104.7 10.0 %collective-permute-done.4.refs_6_.refs_16_.refs_8_ = bf16[320,2048]{1,0:T(8,128)(2,1)} collective-permute-done((bf16[320,2048]{1,0:T(8,128)(2,1)}, bf16[320,2048]{1,0:T(8,128)(2,1)}, u32[]{:S(2)}, u32[]{:S(2)}) %collective-permute-start.4) | collective-permute-done | bytes 1310752 | tf_op jit(solution)/shard_map/ppermute | solution.py:1214
  114.7 2.2 shard_map.278.refs_7_.refs_15_
  117.0 1.6 collective-permute-start.12
  120.5 2.6 collective-permute-start.15
  124.7 50.1 %shard_map.279 = (bf16[8,272,256]{2,1,0:T(8,128)(2,1)}, bf16[2048,512]{1,0:T(8,128)(2,1)}, bf16[2048,256]{1,0:T(8,128)(2,1)}, f32[2048,256]{1,0:T(8,128)}, f32[2...) custom-call(s32[4]{0:T(128)} %bitcast.167, ...), custom_call_target="tpu_custom_call" | custom-call | flops 57000001536 | tf_op jit(solution)/shard_map/pallas_call | solution.py:352
  176.0 4.2 all-to-all-start
  186.8 8.0 %all-to-all-done.refs_1_ = bf16[8,272,256]{2,1,0:T(8,128)(2,1)S(1)} async-done(((bf16[8,272,256]{2,1,0:T(8,128)(2,1)}), bf16[8,272,256]{2,1,0:T(8,128)(2,1)S(1)}, u32[]{:S(2)}, u32[]{:S(2)}) %all-to-all-start) | async-done | bytes 1114144 | tf_op jit(solution)/shard_map/all_to_all | solution.py:1210
  195.8 9.7 %shard_map.280 = (f32[256,2048]{1,0:T(8,128)}, bf16[256,2048]{1,0:T(8,128)(2,1)}, bf16[256,128]{1,0:T(8,128)(2,1)}) custom-call(s32[1]{0:T(128)} %bitcast.1.mine_ref.refs_0_.refs_1_, bf16[8,272,256]{2,1,0:T(8,128)(2,1)} %copy-done.8, bf16[256,2048]{1,0:T(8,128)(2,1)} %bitcast.102, bf16[2048,128]{1,0:T(8,128)(2,1)} %refs_4_.3, bf16[2048,128]{1,0:T(8,128)(2,1)} %refs_5_.1, ...), custom_call_target="tpu_custom_call" | custom-call | flops 8000000000 | tf_op jit(solution)/shard_map/pallas_call | solution.py:597
  205.5 2.6 collective-permute-done.22.refs_16_.refs_10_
  210.2 1.7 broadcast_select_fusion.2
  215.4 17.4 %collective-permute-done.24.refs_3_ = bf16[256,2048]{1,0:T(8,128)(2,1)S(1)} collective-permute-done((bf16[256,2048]{1,0:T(8,128)(2,1)}, bf16[256,2048]{1,0:T(8,128)(2,1)S(1)}, u32[]{:S(2)}, u32[]{:S(2)}) %collective-permute-start.24) | collective-permute-done | bytes 1048608 | tf_op jit(solution)/shard_map/ppermute | solution.py:1149
  235.0 28.8 %collective-permute-done.29.refs_22_.refs_16_ = bf16[272,2048]{1,0:T(8,128)(2,1)S(1)} collective-permute-done((bf16[272,2048]{1,0:T(8,128)(2,1)S(1)}, bf16[272,2048]{1,0:T(8,128)(2,1)S(1)}, u32[]{:S(2)}, u32[]{:S(2)}) %collective-permute-start.29) | collective-permute-done | bytes 1114144 | tf_op jit(solution)/shard_map/ppermute | solution.py:1214
  265.1 2.3 broadcast_select_fusion.4
  267.4 2.9 collective-permute-done.34.refs_10_
  271.8 1.6 collective-permute-start.36
  274.7 1.7 collective-permute-start.37
  276.4 26.0 %shard_map.281 = (f32[2048,1536]{1,0:T(8,128)}, bf16[2048,256]{1,0:T(8,128)(2,1)}, bf16[2048,256]{1,0:T(8,128)(2,1)}) custom-call(s32[1]{0:T(128)} %bitcast.1.mine_ref.refs_0_.refs_1_, s32[1]{0:T(128)} %bitcast.refs_0_.refs_2_.refs_1_, bf16[256,2048]{1,0:T(8,128)(2,1)} %get-tuple-element.170.refs_2_, bf16[256,2048]{1,0:T(8,128)(2,1)} %copy-done.17, ...), custom_call_target="tpu_custom_call" | custom-call | flops 28000000000 | tf_op jit(solution)/shard_map/pallas_call | solution.py:809
  302.4 9.6 %collective-permute-done.37.refs_22_ = bf16[176,2048]{1,0:T(8,128)(2,1)} collective-permute-done((bf16[176,2048]{1,0:T(8,128)(2,1)}, bf16[176,2048]{1,0:T(8,128)(2,1)}, u32[]{:S(2)}, u32[]{:S(2)}) %collective-permute-start.37) | collective-permute-done | bytes 720928 | tf_op jit(solution)/shard_map/ppermute | solution.py:1214
  315.9 30.4 %shard_map.283 = (bf16[1024,2048]{1,0:T(8,128)(2,1)}, bf16[1024,2048]{1,0:T(8,128)(2,1)}, bf16[1024,128]{1,0:T(8,128)(2,1)}, bf16[1024,256]{1,0:T(8,128)(2,1)}, f32[128,768]{1,0:T(8,128)}, /*index=5*/f32[256,1536]{1,0:T(8,128)}) custom-call(s32[1]{0:T(128)} %bitcast.1.mine_ref.refs_0_.refs_1_, s32[1]{0:T(128)} %bitcast.refs_0_.refs_2_.refs_1_, ...), custom_call_target="tpu_custom_call" | custom-call | flops 32999999488 | tf_op jit(solution)/shard_map/pallas_call | solution.py:913
  346.9 30.6 %shard_map.282 = (bf16[1024,2048]{1,0:T(8,128)(2,1)}, bf16[1024,2048]{1,0:T(8,128)(2,1)}, bf16[1024,128]{1,0:T(8,128)(2,1)}, bf16[1024,256]{1,0:T(8,128)(2,1)}, f32[128,768]{1,0:T(8,128)}, /*index=5*/f32[256,1536]{1,0:T(8,128)}) custom-call(s32[1]{0:T(128)} %bitcast.1.mine_ref.refs_0_.refs_1_, s32[1]{0:T(128)} %bitcast.refs_0_.refs_2_.refs_1_, ...), custom_call_target="tpu_custom_call" | custom-call | flops 32999999488 | tf_op jit(solution)/shard_map/pallas_call | solution.py:913
  377.6 2.9 add_convert_fusion.10
  381.4 1.7 collective-permute-start.44
  384.6 10.7 %collective-permute-done.46 = bf16[128,2048]{1,0:T(8,128)(2,1)S(1)} collective-permute-done((bf16[128,2048]{1,0:T(8,128)(2,1)S(1)}, bf16[128,2048]{1,0:T(8,128)(2,1)S(1)}, u32[]{:S(2)}, u32[]{:S(2)}) %collective-permute-start.46) | collective-permute-done | bytes 524320 | tf_op jit(solution)/shard_map/ppermute | solution.py:1149
  396.2 2.0 add_convert_fusion.11
  401.4 5.2 collective-permute-done.43.refs_11_
  407.4 9.6 %collective-permute-done.45.refs_12_ = bf16[128,2048]{1,0:T(8,128)(2,1)S(1)} collective-permute-done((bf16[128,2048]{1,0:T(8,128)(2,1)S(1)}, bf16[128,2048]{1,0:T(8,128)(2,1)S(1)}, u32[]{:S(2)}, u32[]{:S(2)}) %collective-permute-start.45) | collective-permute-done | bytes 524320 | tf_op jit(solution)/shard_map/ppermute | solution.py:1149
  418.6 10.9 %shard_map.284 = (bf16[8,272,256]{2,1,0:T(8,128)(2,1)}, f32[256,2048]{1,0:T(8,128)}, bf16[256,128]{1,0:T(8,128)(2,1)}, f32[2048,128]{1,0:T(8,128)}) custom-call(s32[1]{0:T(128)} %bitcast.1.mine_ref.refs_0_.refs_1_, bf16[8,272,256]{2,1,0:T(8,128)(2,1)} %copy-done.8, bf16[256,2048]{1,0:T(8,128)(2,1)} %bitcast.123, f32[256,2048]{1,0:T(8,128)} %get-tuple-element.159.refs_3_, ...), custom_call_target="tpu_custom_call" | custom-call | flops 12000000000 | tf_op jit(solution)/shard_map/pallas_call | solution.py:688
  429.6 5.7 all-to-all-start.1
  437.3 5.7 add_convert_fusion.1
  446.5 4.0 all-to-all-done.1.refs_18_
  450.5 49.8 %shard_map.285 = (bf16[2048,1024]{1,0:T(8,128)(2,1)}, bf16[2048,256]{1,0:T(8,128)(2,1)}, bf16[2048,128]{1,0:T(8,128)(2,1)}, f32[128,1024]{1,0:T(8,128)}, bf16[1024,2048]{1,0:T(8,128)(2,1)}) custom-call(s32[4]{0:T(128)} %bitcast.168, s32[1]{0:T(128)} %bitcast.1.mine_ref.refs_0_.refs_1_, s32[1]{0:T(128)} %bitcast.refs_0_.refs_2_.refs_1_, ...), custom_call_target="tpu_custom_call" | custom-call | flops 51000000512 | tf_op jit(solution)/shard_map/pallas_call | solution.py:520
  504.3 5.2 all-to-all-start.2
  509.5 9.5 %shard_map.286.refs_5_ = bf16[1024,2048]{1,0:T(8,128)(2,1)} custom-call(s32[1]{0:T(128)} %bitcast.refs_0_.refs_2_.refs_1_, bf16[320,2048]{1,0:T(8,128)(2,1)} %shard_map.276.refs_1_.refs_11_.refs_3_, bf16[320,2048]{1,0:T(8,128)(2,1)} %copy-done.2, bf16[320,2048]{1,0:T(8,128)(2,1)} %collective-permute-done.1.refs_3_.refs_13_.refs_5_, ...), custom_call_target="tpu_custom_call" | custom-call | flops 8000000000 | tf_op jit(solution)/shard_map/pallas_call | solution.py:960
  519.0 4.2 add_convert_fusion.6
  524.6 4.3 all-to-all-start.3
  529.0 2.1 copy.67
  533.2 4.6 add_convert_fusion
  537.8 1.9 collective-permute-start.58
  539.8 14.9 %collective-permute-done.53 = bf16[128,2048]{1,0:T(8,128)(2,1)S(1)} collective-permute-done((bf16[128,2048]{1,0:T(8,128)(2,1)}, bf16[128,2048]{1,0:T(8,128)(2,1)S(1)}, u32[]{:S(2)}, u32[]{:S(2)}) %collective-permute-start.53) | collective-permute-done | bytes 524320 | tf_op jit(solution)/shard_map/ppermute | solution.py:1149
  555.5 2.4 add_convert_fusion.4
  565.0 2.6 fusion.13
  571.0 5.8 collective-permute-done.56.refs_8_
  576.8 3.5 all-to-all-start.4
  580.3 1.9 collective-permute-start.60
  582.3 6.2 collective-permute-start.61
  588.5 17.5 %collective-permute-done.61 = f32[176,128]{1,0:T(8,128)S(1)} collective-permute-done((f32[176,128]{1,0:T(8,128)S(1)}, f32[176,128]{1,0:T(8,128)S(1)}, u32[]{:S(2)}, u32[]{:S(2)}) %collective-permute-start.61) | collective-permute-done | bytes 90144 | tf_op jit(solution)/shard_map/ppermute | solution.py:1244
  606.0 1.9 collective-permute-start.59
  609.0 8.0 %collective-permute-done.59 = f32[256,128]{1,0:T(8,128)S(1)} collective-permute-done((f32[256,128]{1,0:T(8,128)}, f32[256,128]{1,0:T(8,128)S(1)}, u32[]{:S(2)}, u32[]{:S(2)}) %collective-permute-start.59) | collective-permute-done | bytes 131104 | tf_op jit(solution)/shard_map/ppermute | solution.py:1244
  617.0 6.3 shard_map.287
  (298 shorter events, 88.2 us)
Async XLA Ops:
  10.1 31.8 %collective-permute-start = (bf16[320,2048]{1,0:T(8,128)(2,1)}, bf16[320,2048]{1,0:T(8,128)(2,1)S(1)}, u32[]{:S(2)}, u32[]{:S(2)}) collective-permute-start(bf16[320,2048]{1,0:T(8,128)(2,1)} %shard_map.276.refs_1_.refs_11_.refs_3_), channel_id=1, source_target_pairs={{0,1},{1,2},{2,3},{4,5},{5,6},{6,7},{8,9},{9,10},{10,11},{12,13},{... | collective-permute-start | bytes 3932168 | tf_op jit(solution)/shard_map/ppermute | solution.py:1214
  13.7 32.5 %collective-permute-start.1 = (bf16[320,2048]{1,0:T(8,128)(2,1)}, bf16[320,2048]{1,0:T(8,128)(2,1)}, u32[]{:S(2)}, u32[]{:S(2)}) collective-permute-start(bf16[320,2048]{1,0:T(8,128)(2,1)} %shard_map.276.refs_1_.refs_11_.refs_3_), channel_id=1, source_target_pairs={{1,0},{2,1},{3,2},{5,4},{6,5},{7,6},{9,8},{10,9},{11,10},{13,12},{... | collective-permute-start | bytes 3932168 | tf_op jit(solution)/shard_map/ppermute | solution.py:1214
  23.0 47.4 %collective-permute-start.5 = (bf16[512,2048]{1,0:T(8,128)(2,1)}, bf16[512,2048]{1,0:T(8,128)(2,1)}, u32[]{:S(2)}, u32[]{:S(2)}) collective-permute-start(bf16[512,2048]{1,0:T(8,128)(2,1)} %pad_maximum_fusion.refs_3_.refs_2_), channel_id=1, source_target_pairs={{0,8},{4,12},{8,0},{12,4},{16,24},{20,28},{24,16},{28,20},{1,9},{5... | collective-permute-start | bytes 6291464 | tf_op jit(solution)/shard_map/ppermute | solution.py:1149
  24.5 47.1 %collective-permute-start.6 = (bf16[512,2048]{1,0:T(8,128)(2,1)}, bf16[512,2048]{1,0:T(8,128)(2,1)}, u32[]{:S(2)}, u32[]{:S(2)}) collective-permute-start(bf16[512,2048]{1,0:T(8,128)(2,1)} %pad_maximum_fusion.refs_3_.refs_2_), channel_id=1, source_target_pairs={{0,16},{4,20},{8,24},{12,28},{16,0},{20,4},{24,8},{28,12},{1,17},{... | collective-permute-start | bytes 6291464 | tf_op jit(solution)/shard_map/ppermute | solution.py:1149
  49.2 24.3 %collective-permute-start.2 = (bf16[320,2048]{1,0:T(8,128)(2,1)}, bf16[320,2048]{1,0:T(8,128)(2,1)S(1)}, u32[]{:S(2)}, u32[]{:S(2)}) collective-permute-start(bf16[320,2048]{1,0:T(8,128)(2,1)} %get-tuple-element.272), channel_id=1, source_target_pairs={{1,2},{2,1},{5,6},{6,5},{9,10},{10,9},{13,14},{14,13},{17,18},{18,... | collective-permute-start | bytes 3932168 | tf_op jit(solution)/shard_map/ppermute | solution.py:1214
  50.1 33.1 %collective-permute-start.3 = (bf16[320,2048]{1,0:T(8,128)(2,1)}, bf16[320,2048]{1,0:T(8,128)(2,1)}, u32[]{:S(2)}, u32[]{:S(2)}) collective-permute-start(bf16[320,2048]{1,0:T(8,128)(2,1)} %get-tuple-element.271), channel_id=1, source_target_pairs={{2,3},{1,0},{6,7},{5,4},{10,11},{9,8},{14,15},{13,12},{18,19},{17,... | collective-permute-start | bytes 3932168 | tf_op jit(solution)/shard_map/ppermute | solution.py:1214
  71.6 46.9 %collective-permute-start.8 = (bf16[512,2048]{1,0:T(8,128)(2,1)}, bf16[512,2048]{1,0:T(8,128)(2,1)}, u32[]{:S(2)}, u32[]{:S(2)}) collective-permute-start(bf16[512,2048]{1,0:T(8,128)(2,1)} %pad_maximum_fusion.refs_3_.refs_2_), channel_id=1, source_target_pairs={{0,4},{4,0},{8,12},{12,8},{16,20},{20,16},{24,28},{28,24},{1,5},{5... | collective-permute-start | bytes 6291464 | tf_op jit(solution)/shard_map/ppermute | solution.py:1149
  71.6 47.4 %collective-permute-start.9 = (bf16[512,2048]{1,0:T(8,128)(2,1)}, bf16[512,2048]{1,0:T(8,128)(2,1)}, u32[]{:S(2)}, u32[]{:S(2)}) collective-permute-start(bf16[512,2048]{1,0:T(8,128)(2,1)} %collective-permute-done.5.refs_4_.refs_3_), channel_id=1, source_target_pairs={{0,4},{4,0},{8,12},{12,8},{16,20},{20,16},{24,28},{28,24},{1,5},{5... | collective-permute-start | bytes 6291464 | tf_op jit(solution)/shard_map/ppermute | solution.py:1149
  73.4 47.1 %collective-permute-start.10 = (bf16[512,2048]{1,0:T(8,128)(2,1)}, bf16[512,2048]{1,0:T(8,128)(2,1)}, u32[]{:S(2)}, u32[]{:S(2)}) collective-permute-start(bf16[512,2048]{1,0:T(8,128)(2,1)} %collective-permute-done.6.refs_5_.refs_4_), channel_id=1, source_target_pairs={{0,4},{4,0},{8,12},{12,8},{16,20},{20,16},{24,28},{28,24},{1,5},{5... | collective-permute-start | bytes 6291464 | tf_op jit(solution)/shard_map/ppermute | solution.py:1149
  73.5 25.7 %collective-permute-start.7 = (bf16[256,2048]{1,0:T(8,128)(2,1)S(1)}, bf16[256,2048]{1,0:T(8,128)(2,1)}, u32[]{:S(2)}, u32[]{:S(2)}) collective-permute-start(bf16[256,2048]{1,0:T(8,128)(2,1)S(1)} %slice.264), channel_id=1, source_target_pairs={{0,8},{4,12},{8,0},{12,4},{16,24},{20,28},{24,16},{28,20},{1,9},{5... | collective-permute-start | bytes 3145736 | tf_op jit(solution)/shard_map/ppermute | solution.py:1149
  83.2 31.5 %collective-permute-start.4 = (bf16[320,2048]{1,0:T(8,128)(2,1)}, bf16[320,2048]{1,0:T(8,128)(2,1)}, u32[]{:S(2)}, u32[]{:S(2)}) collective-permute-start(bf16[320,2048]{1,0:T(8,128)(2,1)} %get-tuple-element.272), channel_id=1, source_target_pairs={{1,3},{2,0},{5,7},{6,4},{9,11},{10,8},{13,15},{14,12},{17,19},{18,... | collective-permute-start | bytes 3932168 | tf_op jit(solution)/shard_map/ppermute | solution.py:1214
  99.2 24.0 %collective-permute-start.11 = (bf16[256,2048]{1,0:T(8,128)(2,1)}, bf16[256,2048]{1,0:T(8,128)(2,1)}, u32[]{:S(2)}, u32[]{:S(2)}) collective-permute-start(bf16[256,2048]{1,0:T(8,128)(2,1)} %collective-permute-done.7.refs_6_), channel_id=1, source_target_pairs={{0,4},{4,0},{8,12},{12,8},{16,20},{20,16},{24,28},{28,24},{1,5},{5... | collective-permute-start | bytes 3145736 | tf_op jit(solution)/shard_map/ppermute | solution.py:1149
  117.0 57.8 %collective-permute-start.12 = (bf16[256,2048]{1,0:T(8,128)(2,1)}, bf16[256,2048]{1,0:T(8,128)(2,1)}, u32[]{:S(2)}, u32[]{:S(2)}) collective-permute-start(bf16[256,2048]{1,0:T(8,128)(2,1)} %shard_map.278.refs_7_.refs_15_), channel_id=1, source_target_pairs={{0,8},{4,12},{8,0},{12,4},{16,24},{20,28},{24,16},{28,20},{1,9},{5... | collective-permute-start | bytes 3145736 | tf_op jit(solution)/shard_map/ppermute | solution.py:1149
  118.5 56.3 %collective-permute-start.13 = (bf16[256,2048]{1,0:T(8,128)(2,1)}, bf16[256,2048]{1,0:T(8,128)(2,1)}, u32[]{:S(2)}, u32[]{:S(2)}) collective-permute-start(bf16[256,2048]{1,0:T(8,128)(2,1)} %shard_map.278.refs_7_.refs_15_), channel_id=1, source_target_pairs={{0,16},{4,20},{8,24},{12,28},{16,0},{20,4},{24,8},{28,12},{1,17},{... | collective-permute-start | bytes 3145736 | tf_op jit(solution)/shard_map/ppermute | solution.py:1149
  119.0 55.8 %collective-permute-start.14 = (bf16[256,2048]{1,0:T(8,128)(2,1)}, bf16[256,2048]{1,0:T(8,128)(2,1)}, u32[]{:S(2)}, u32[]{:S(2)}) collective-permute-start(bf16[256,2048]{1,0:T(8,128)(2,1)} %shard_map.278.refs_7_.refs_15_), channel_id=1, source_target_pairs={{0,24},{4,28},{8,16},{12,20},{16,8},{20,12},{24,0},{28,4},{1,25},{... | collective-permute-start | bytes 3145736 | tf_op jit(solution)/shard_map/ppermute | solution.py:1149
  120.5 54.3 %collective-permute-start.15 = (bf16[528,2048]{1,0:T(8,128)(2,1)}, bf16[528,2048]{1,0:T(8,128)(2,1)}, u32[]{:S(2)}, u32[]{:S(2)}) collective-permute-start(bf16[528,2048]{1,0:T(8,128)(2,1)} %shard_map.277.refs_12_.refs_18_.refs_6_), channel_id=1, source_target_pairs={{0,1},{1,2},{2,3},{4,5},{5,6},{6,7},{8,9},{9,10},{10,11},{12,13},{... | collective-permute-start | bytes 6488072 | tf_op jit(solution)/shard_map/ppermute | solution.py:1214
  123.2 51.7 %collective-permute-start.16 = (bf16[528,2048]{1,0:T(8,128)(2,1)}, bf16[528,2048]{1,0:T(8,128)(2,1)}, u32[]{:S(2)}, u32[]{:S(2)}) collective-permute-start(bf16[528,2048]{1,0:T(8,128)(2,1)} %shard_map.277.refs_12_.refs_18_.refs_6_), channel_id=1, source_target_pairs={{1,0},{2,1},{3,2},{5,4},{6,5},{7,6},{9,8},{10,9},{11,10},{13,12},{... | collective-permute-start | bytes 6488072 | tf_op jit(solution)/shard_map/ppermute | solution.py:1214
  174.9 10.6 %collective-permute-start.18 = (bf16[256,2048]{1,0:T(8,128)(2,1)}, bf16[256,2048]{1,0:T(8,128)(2,1)}, u32[]{:S(2)}, u32[]{:S(2)}) collective-permute-start(bf16[256,2048]{1,0:T(8,128)(2,1)} %collective-permute-done.12.refs_8_.refs_16_), channel_id=1, source_target_pairs={{0,4},{4,0},{8,12},{12,8},{16,20},{20,16},{24,28},{28,24},{1,5},{5... | collective-permute-start | bytes 3145736 | tf_op jit(solution)/shard_map/ppermute | solution.py:1149
  175.4 19.4 %collective-permute-start.19 = (bf16[256,2048]{1,0:T(8,128)(2,1)}, bf16[256,2048]{1,0:T(8,128)(2,1)}, u32[]{:S(2)}, u32[]{:S(2)}) collective-permute-start(bf16[256,2048]{1,0:T(8,128)(2,1)} %collective-permute-done.13.refs_9_.refs_17_), channel_id=1, source_target_pairs={{0,4},{4,0},{8,12},{12,8},{16,20},{20,16},{24,28},{28,24},{1,5},{5... | collective-permute-start | bytes 3145736 | tf_op jit(solution)/shard_map/ppermute | solution.py:1149
  175.5 19.3 %collective-permute-start.20 = (bf16[256,2048]{1,0:T(8,128)(2,1)}, bf16[256,2048]{1,0:T(8,128)(2,1)}, u32[]{:S(2)}, u32[]{:S(2)}) collective-permute-start(bf16[256,2048]{1,0:T(8,128)(2,1)} %collective-permute-done.14.refs_10_.refs_18_), channel_id=1, source_target_pairs={{0,4},{4,0},{8,12},{12,8},{16,20},{20,16},{24,28},{28,24},{1,5},{5... | collective-permute-start | bytes 3145736 | tf_op jit(solution)/shard_map/ppermute | solution.py:1149
  176.0 18.9 %all-to-all-start = ((bf16[8,272,256]{2,1,0:T(8,128)(2,1)}), bf16[8,272,256]{2,1,0:T(8,128)(2,1)S(1)}, u32[]{:S(2)}, u32[]{:S(2)}) async-start(bf16[8,272,256]{2,1,0:T(8,128)(2,1)} %get-tuple-element.155), calls=%async_computation | async-start | bytes 2228224 | tf_op jit(solution)/shard_map/all_to_all | solution.py:1210
  182.8 22.8 %collective-permute-start.21 = (bf16[80,2048]{1,0:T(8,128)(2,1)S(1)}, bf16[80,2048]{1,0:T(8,128)(2,1)}, u32[]{:S(2)}, u32[]{:S(2)}) collective-permute-start(bf16[80,2048]{1,0:T(8,128)(2,1)S(1)} %get-tuple-element.268), channel_id=1, source_target_pairs={{1,2},{2,1},{5,6},{6,5},{9,10},{10,9},{13,14},{14,13},{17,18},{18,... | collective-permute-start | bytes 983048 | tf_op jit(solution)/shard_map/ppermute | solution.py:1214
  184.2 24.0 %collective-permute-start.23 = (bf16[80,2048]{1,0:T(8,128)(2,1)S(1)}, bf16[80,2048]{1,0:T(8,128)(2,1)}, u32[]{:S(2)}, u32[]{:S(2)}) collective-permute-start(bf16[80,2048]{1,0:T(8,128)(2,1)S(1)} %get-tuple-element.268), channel_id=1, source_target_pairs={{1,3},{2,0},{5,7},{6,4},{9,11},{10,8},{13,15},{14,12},{17,19},{18,... | collective-permute-start | bytes 983048 | tf_op jit(solution)/shard_map/ppermute | solution.py:1214
  185.5 22.7 %collective-permute-start.22 = (bf16[80,2048]{1,0:T(8,128)(2,1)S(1)}, bf16[80,2048]{1,0:T(8,128)(2,1)}, u32[]{:S(2)}, u32[]{:S(2)}) collective-permute-start(bf16[80,2048]{1,0:T(8,128)(2,1)S(1)} %get-tuple-element.267), channel_id=1, source_target_pairs={{2,3},{1,0},{6,7},{5,4},{10,11},{9,8},{14,15},{13,12},{18,19},{17,... | collective-permute-start | bytes 983048 | tf_op jit(solution)/shard_map/ppermute | solution.py:1214
  208.1 24.6 %collective-permute-start.24 = (bf16[256,2048]{1,0:T(8,128)(2,1)}, bf16[256,2048]{1,0:T(8,128)(2,1)S(1)}, u32[]{:S(2)}, u32[]{:S(2)}) collective-permute-start(bf16[256,2048]{1,0:T(8,128)(2,1)} %get-tuple-element.170.refs_2_), channel_id=1, source_target_pairs={{0,8},{4,12},{8,0},{12,4},{16,24},{20,28},{24,16},{28,20},{1,9},{5... | collective-permute-start | bytes 3145736 | tf_op jit(solution)/shard_map/ppermute | solution.py:1149
  209.6 24.3 %collective-permute-start.25 = (bf16[256,2048]{1,0:T(8,128)(2,1)}, bf16[256,2048]{1,0:T(8,128)(2,1)S(1)}, u32[]{:S(2)}, u32[]{:S(2)}) collective-permute-start(bf16[256,2048]{1,0:T(8,128)(2,1)} %get-tuple-element.170.refs_2_), channel_id=1, source_target_pairs={{0,16},{4,20},{8,24},{12,28},{16,0},{20,4},{24,8},{28,12},{1,17},{... | collective-permute-start | bytes 3145736 | tf_op jit(solution)/shard_map/ppermute | solution.py:1149
  211.9 23.1 %collective-permute-start.28 = (bf16[272,2048]{1,0:T(8,128)(2,1)S(1)}, bf16[272,2048]{1,0:T(8,128)(2,1)S(1)}, u32[]{:S(2)}, u32[]{:S(2)}) collective-permute-start(bf16[272,2048]{1,0:T(8,128)(2,1)S(1)} %get-tuple-element.266), channel_id=1, source_target_pairs={{1,2},{2,1},{5,6},{6,5},{9,10},{10,9},{13,14},{14,13},{17,18},{18,... | collective-permute-start | bytes 3342344 | tf_op jit(solution)/shard_map/ppermute | solution.py:1214
  212.8 51.0 %collective-permute-start.29 = (bf16[272,2048]{1,0:T(8,128)(2,1)S(1)}, bf16[272,2048]{1,0:T(8,128)(2,1)S(1)}, u32[]{:S(2)}, u32[]{:S(2)}) collective-permute-start(bf16[272,2048]{1,0:T(8,128)(2,1)S(1)} %get-tuple-element.265), channel_id=1, source_target_pairs={{2,3},{1,0},{6,7},{5,4},{10,11},{9,8},{14,15},{13,12},{18,19},{17,... | collective-permute-start | bytes 3342344 | tf_op jit(solution)/shard_map/ppermute | solution.py:1214
  214.1 49.7 %collective-permute-start.30 = (bf16[272,2048]{1,0:T(8,128)(2,1)S(1)}, bf16[272,2048]{1,0:T(8,128)(2,1)S(1)}, u32[]{:S(2)}, u32[]{:S(2)}) collective-permute-start(bf16[272,2048]{1,0:T(8,128)(2,1)S(1)} %get-tuple-element.266), channel_id=1, source_target_pairs={{1,3},{2,0},{5,7},{6,4},{9,11},{10,8},{13,15},{14,12},{17,19},{18,... | collective-permute-start | bytes 3342344 | tf_op jit(solution)/shard_map/ppermute | solution.py:1214
  232.8 31.0 %collective-permute-start.26 = (bf16[128,2048]{1,0:T(8,128)(2,1)S(1)}, bf16[128,2048]{1,0:T(8,128)(2,1)S(1)}, u32[]{:S(2)}, u32[]{:S(2)}) collective-permute-start(bf16[128,2048]{1,0:T(8,128)(2,1)S(1)} %slice.338), channel_id=1, source_target_pairs={{0,16},{4,20},{8,24},{12,28},{16,0},{20,4},{24,8},{28,12},{1,17},{... | collective-permute-start | bytes 1572872 | tf_op jit(solution)/shard_map/ppermute | solution.py:1149
  234.0 29.8 %collective-permute-start.27 = (bf16[128,2048]{1,0:T(8,128)(2,1)S(1)}, bf16[128,2048]{1,0:T(8,128)(2,1)S(1)}, u32[]{:S(2)}, u32[]{:S(2)}) collective-permute-start(bf16[128,2048]{1,0:T(8,128)(2,1)S(1)} %slice.339), channel_id=1, source_target_pairs={{0,8},{4,12},{8,0},{12,4},{16,24},{20,28},{24,16},{28,20},{1,9},{5... | collective-permute-start | bytes 1572872 | tf_op jit(solution)/shard_map/ppermute | solution.py:1149
  263.9 10.7 %collective-permute-start.32 = (bf16[256,2048]{1,0:T(8,128)(2,1)S(1)}, bf16[256,2048]{1,0:T(8,128)(2,1)S(1)}, u32[]{:S(2)}, u32[]{:S(2)}) collective-permute-start(bf16[256,2048]{1,0:T(8,128)(2,1)S(1)} %collective-permute-done.24.refs_3_), channel_id=1, source_target_pairs={{0,4},{4,0},{8,12},{12,8},{16,20},{20,16},{24,28},{28,24},{1,5},{5... | collective-permute-start | bytes 3145736 | tf_op jit(solution)/shard_map/ppermute | solution.py:1149
  264.4 12.0 %collective-permute-start.33 = (bf16[256,2048]{1,0:T(8,128)(2,1)S(1)}, bf16[256,2048]{1,0:T(8,128)(2,1)}, u32[]{:S(2)}, u32[]{:S(2)}) collective-permute-start(bf16[256,2048]{1,0:T(8,128)(2,1)S(1)} %collective-permute-done.25.refs_4_), channel_id=1, source_target_pairs={{0,4},{4,0},{8,12},{12,8},{16,20},{20,16},{24,28},{28,24},{1,5},{5... | collective-permute-start | bytes 3145736 | tf_op jit(solution)/shard_map/ppermute | solution.py:1149
  270.3 32.1 %collective-permute-start.39 = (bf16[256,2048]{1,0:T(8,128)(2,1)S(1)}, bf16[256,2048]{1,0:T(8,128)(2,1)}, u32[]{:S(2)}, u32[]{:S(2)}) collective-permute-start(bf16[256,2048]{1,0:T(8,128)(2,1)S(1)} %bitcast.125), channel_id=1, source_target_pairs={{0,24},{4,28},{8,16},{12,20},{16,8},{20,12},{24,0},{28,4},{1,25},{... | collective-permute-start | bytes 3145736 | tf_op jit(solution)/shard_map/ppermute | solution.py:1149
  271.8 30.6 %collective-permute-start.36 = (bf16[176,2048]{1,0:T(8,128)(2,1)S(1)}, bf16[176,2048]{1,0:T(8,128)(2,1)}, u32[]{:S(2)}, u32[]{:S(2)}) collective-permute-start(bf16[176,2048]{1,0:T(8,128)(2,1)S(1)} %get-tuple-element.264), channel_id=1, source_target_pairs={{1,2},{2,1},{5,6},{6,5},{9,10},{10,9},{13,14},{14,13},{17,18},{18,... | collective-permute-start | bytes 2162696 | tf_op jit(solution)/shard_map/ppermute | solution.py:1214
  273.4 38.7 %collective-permute-start.38 = (bf16[176,2048]{1,0:T(8,128)(2,1)S(1)}, bf16[176,2048]{1,0:T(8,128)(2,1)}, u32[]{:S(2)}, u32[]{:S(2)}) collective-permute-start(bf16[176,2048]{1,0:T(8,128)(2,1)S(1)} %get-tuple-element.264), channel_id=1, source_target_pairs={{1,3},{2,0},{5,7},{6,4},{9,11},{10,8},{13,15},{14,12},{17,19},{18,... | collective-permute-start | bytes 2162696 | tf_op jit(solution)/shard_map/ppermute | solution.py:1214
  274.7 37.4 %collective-permute-start.37 = (bf16[176,2048]{1,0:T(8,128)(2,1)}, bf16[176,2048]{1,0:T(8,128)(2,1)}, u32[]{:S(2)}, u32[]{:S(2)}) collective-permute-start(bf16[176,2048]{1,0:T(8,128)(2,1)} %get-tuple-element.263), channel_id=1, source_target_pairs={{2,3},{1,0},{6,7},{5,4},{10,11},{9,8},{14,15},{13,12},{18,19},{17,... | collective-permute-start | bytes 2162696 | tf_op jit(solution)/shard_map/ppermute | solution.py:1214
  346.4 31.2 %collective-permute-start.41 = (bf16[1024,2048]{1,0:T(8,128)(2,1)}, bf16[1024,2048]{1,0:T(8,128)(2,1)}, u32[]{:S(2)}, u32[]{:S(2)}) collective-permute-start(bf16[1024,2048]{1,0:T(8,128)(2,1)} %get-tuple-element.194), channel_id=1, source_target_pairs={{0,4},{4,0},{8,12},{12,8},{16,20},{20,16},{24,28},{28,24},{1,5},{5... | collective-permute-start | bytes 12582920 | tf_op jit(solution)/shard_map/ppermute | solution.py:1149
  346.5 31.0 %collective-permute-start.42 = (bf16[1024,2048]{1,0:T(8,128)(2,1)}, bf16[1024,2048]{1,0:T(8,128)(2,1)}, u32[]{:S(2)}, u32[]{:S(2)}) collective-permute-start(bf16[1024,2048]{1,0:T(8,128)(2,1)} %get-tuple-element.195), channel_id=1, source_target_pairs={{0,4},{4,0},{8,12},{12,8},{16,20},{20,16},{24,28},{28,24},{1,5},{5... | collective-permute-start | bytes 12582920 | tf_op jit(solution)/shard_map/ppermute | solution.py:1149
  380.5 14.8 %collective-permute-start.46 = (bf16[128,2048]{1,0:T(8,128)(2,1)S(1)}, bf16[128,2048]{1,0:T(8,128)(2,1)S(1)}, u32[]{:S(2)}, u32[]{:S(2)}) collective-permute-start(bf16[128,2048]{1,0:T(8,128)(2,1)S(1)} %get-tuple-element.258), channel_id=1, source_target_pairs={{0,8},{4,12},{8,0},{12,4},{16,24},{20,28},{24,16},{28,20},{1,9},{5... | collective-permute-start | bytes 1572872 | tf_op jit(solution)/shard_map/ppermute | solution.py:1149
  381.4 14.8 %collective-permute-start.44 = (bf16[128,2048]{1,0:T(8,128)(2,1)S(1)}, bf16[128,2048]{1,0:T(8,128)(2,1)S(1)}, u32[]{:S(2)}, u32[]{:S(2)}) collective-permute-start(bf16[128,2048]{1,0:T(8,128)(2,1)S(1)} %get-tuple-element.259), channel_id=1, source_target_pairs={{0,16},{4,20},{8,24},{12,28},{16,0},{20,4},{24,8},{28,12},{1,17},{... | collective-permute-start | bytes 1572872 | tf_op jit(solution)/shard_map/ppermute | solution.py:1149
  383.0 23.6 %collective-permute-start.43 = (bf16[128,2048]{1,0:T(8,128)(2,1)S(1)}, bf16[128,2048]{1,0:T(8,128)(2,1)S(1)}, u32[]{:S(2)}, u32[]{:S(2)}) collective-permute-start(bf16[128,2048]{1,0:T(8,128)(2,1)S(1)} %get-tuple-element.260), channel_id=1, source_target_pairs={{0,8},{4,12},{8,0},{12,4},{16,24},{20,28},{24,16},{28,20},{1,9},{5... | collective-permute-start | bytes 1572872 | tf_op jit(solution)/shard_map/ppermute | solution.py:1149
  383.4 24.0 %collective-permute-start.48 = (bf16[128,2048]{1,0:T(8,128)(2,1)S(1)}, bf16[128,2048]{1,0:T(8,128)(2,1)S(1)}, u32[]{:S(2)}, u32[]{:S(2)}) collective-permute-start(bf16[128,2048]{1,0:T(8,128)(2,1)S(1)} %get-tuple-element.257), channel_id=1, source_target_pairs={{0,16},{4,20},{8,24},{12,28},{16,0},{20,4},{24,8},{28,12},{1,17},{... | collective-permute-start | bytes 1572872 | tf_op jit(solution)/shard_map/ppermute | solution.py:1149
  398.2 18.8 %collective-permute-start.45 = (bf16[128,2048]{1,0:T(8,128)(2,1)S(1)}, bf16[128,2048]{1,0:T(8,128)(2,1)S(1)}, u32[]{:S(2)}, u32[]{:S(2)}) collective-permute-start(bf16[128,2048]{1,0:T(8,128)(2,1)S(1)} %get-tuple-element.262), channel_id=1, source_target_pairs={{0,8},{4,12},{8,0},{12,4},{16,24},{20,28},{24,16},{28,20},{1,9},{5... | collective-permute-start | bytes 1572872 | tf_op jit(solution)/shard_map/ppermute | solution.py:1149
  399.5 18.0 %collective-permute-start.47 = (bf16[128,2048]{1,0:T(8,128)(2,1)S(1)}, bf16[128,2048]{1,0:T(8,128)(2,1)S(1)}, u32[]{:S(2)}, u32[]{:S(2)}) collective-permute-start(bf16[128,2048]{1,0:T(8,128)(2,1)S(1)} %get-tuple-element.261), channel_id=1, source_target_pairs={{0,16},{4,20},{8,24},{12,28},{16,0},{20,4},{24,8},{28,12},{1,17},{... | collective-permute-start | bytes 1572872 | tf_op jit(solution)/shard_map/ppermute | solution.py:1149
  429.6 20.9 %all-to-all-start.1 = ((bf16[8,272,256]{2,1,0:T(8,128)(2,1)}), bf16[8,272,256]{2,1,0:T(8,128)(2,1)}, u32[]{:S(2)}, u32[]{:S(2)}) async-start(bf16[8,272,256]{2,1,0:T(8,128)(2,1)} %get-tuple-element.198), calls=%async_computation.1 | async-start | bytes 2228224 | tf_op jit(solution)/shard_map/all_to_all | solution.py:1210
  435.3 65.1 %reduce-scatter.3.cloned.1.call-start = ((), (), s32[]{:S(2)}) async-start(), calls=%async_computation.7 | async-start | bytes 1351680 | tf_op jit(solution)/shard_map/reduce_scatter | solution.py:1444
  443.0 57.4 %collective-permute-start.49 = (bf16[256,2048]{1,0:T(8,128)(2,1)}, bf16[256,2048]{1,0:T(8,128)(2,1)}, u32[]{:S(2)}, u32[]{:S(2)}) collective-permute-start(bf16[256,2048]{1,0:T(8,128)(2,1)} %get-tuple-element.201), channel_id=1, source_target_pairs={{0,8},{4,12},{8,0},{12,4},{16,24},{20,28},{24,16},{28,20},{1,9},{5... | collective-permute-start | bytes 3145736 | tf_op jit(solution)/shard_map/ppermute | solution.py:1149
  444.5 55.9 %collective-permute-start.50 = (bf16[256,2048]{1,0:T(8,128)(2,1)}, bf16[256,2048]{1,0:T(8,128)(2,1)}, u32[]{:S(2)}, u32[]{:S(2)}) collective-permute-start(bf16[256,2048]{1,0:T(8,128)(2,1)} %get-tuple-element.202), channel_id=1, source_target_pairs={{0,16},{4,20},{8,24},{12,28},{16,0},{20,4},{24,8},{28,12},{1,17},{... | collective-permute-start | bytes 3145736 | tf_op jit(solution)/shard_map/ppermute | solution.py:1149
  445.0 55.4 %collective-permute-start.51 = (bf16[256,2048]{1,0:T(8,128)(2,1)S(1)}, bf16[256,2048]{1,0:T(8,128)(2,1)}, u32[]{:S(2)}, u32[]{:S(2)}) collective-permute-start(bf16[256,2048]{1,0:T(8,128)(2,1)S(1)} %get-tuple-element.203), channel_id=1, source_target_pairs={{0,24},{4,28},{8,16},{12,20},{16,8},{20,12},{24,0},{28,4},{1,25},{... | collective-permute-start | bytes 3145736 | tf_op jit(solution)/shard_map/ppermute | solution.py:1149
  500.4 18.6 %collective-permute-start.52 = (bf16[1024,2048]{1,0:T(8,128)(2,1)}, bf16[1024,2048]{1,0:T(8,128)(2,1)}, u32[]{:S(2)}, u32[]{:S(2)}) collective-permute-start(bf16[1024,2048]{1,0:T(8,128)(2,1)} %get-tuple-element.221), channel_id=1, source_target_pairs={{0,4},{4,0},{8,12},{12,8},{16,20},{20,16},{24,28},{28,24},{1,5},{5... | collective-permute-start | bytes 12582920 | tf_op jit(solution)/shard_map/ppermute | solution.py:1149
  504.3 18.9 %all-to-all-start.2 = ((bf16[8,256,128]{2,1,0:T(8,128)(2,1)}), bf16[8,256,128]{2,1,0:T(8,128)(2,1)S(1)}, u32[]{:S(2)}, u32[]{:S(2)}) async-start(bf16[8,256,128]{2,1,0:T(8,128)(2,1)} %bitcast.35), calls=%async_computation.3 | async-start | bytes 1048576 | tf_op jit(solution)/shard_map/all_to_all | solution.py:1210
  524.6 30.9 %all-to-all-start.3 = ((bf16[8,256,256]{2,1,0:T(8,128)(2,1)}), bf16[8,256,256]{2,1,0:T(8,128)(2,1)S(1)}, u32[]{:S(2)}, u32[]{:S(2)}) async-start(bf16[8,256,256]{2,1,0:T(8,128)(2,1)} %pad_maximum_fusion.2), calls=%async_computation.4 | async-start | bytes 2097152 | tf_op jit(solution)/shard_map/all_to_all | solution.py:1210
  529.0 77.0 %reduce-scatter.5.cloned.1.call-start = ((), (), s32[]{:S(2)}) async-start(), calls=%async_computation.8 | async-start | bytes 655360 | tf_op jit(solution)/shard_map/reduce_scatter | solution.py:1461
  531.1 23.6 %collective-permute-start.53 = (bf16[128,2048]{1,0:T(8,128)(2,1)}, bf16[128,2048]{1,0:T(8,128)(2,1)S(1)}, u32[]{:S(2)}, u32[]{:S(2)}) collective-permute-start(bf16[128,2048]{1,0:T(8,128)(2,1)} %get-tuple-element.253), channel_id=1, source_target_pairs={{0,8},{4,12},{8,0},{12,4},{16,24},{20,28},{24,16},{28,20},{1,9},{5... | collective-permute-start | bytes 1572872 | tf_op jit(solution)/shard_map/ppermute | solution.py:1149
  532.6 22.9 %collective-permute-start.54 = (bf16[128,2048]{1,0:T(8,128)(2,1)}, bf16[128,2048]{1,0:T(8,128)(2,1)}, u32[]{:S(2)}, u32[]{:S(2)}) collective-permute-start(bf16[128,2048]{1,0:T(8,128)(2,1)} %get-tuple-element.252), channel_id=1, source_target_pairs={{0,16},{4,20},{8,24},{12,28},{16,0},{20,4},{24,8},{28,12},{1,17},{... | collective-permute-start | bytes 1572872 | tf_op jit(solution)/shard_map/ppermute | solution.py:1149
  537.7 33.2 %collective-permute-start.55 = (bf16[128,2048]{1,0:T(8,128)(2,1)}, bf16[128,2048]{1,0:T(8,128)(2,1)}, u32[]{:S(2)}, u32[]{:S(2)}) collective-permute-start(bf16[128,2048]{1,0:T(8,128)(2,1)} %get-tuple-element.251), channel_id=1, source_target_pairs={{0,8},{4,12},{8,0},{12,4},{16,24},{20,28},{24,16},{28,20},{1,9},{5... | collective-permute-start | bytes 1572872 | tf_op jit(solution)/shard_map/ppermute | solution.py:1149
  537.8 33.1 %collective-permute-start.58 = (bf16[128,2048]{1,0:T(8,128)(2,1)}, bf16[128,2048]{1,0:T(8,128)(2,1)}, u32[]{:S(2)}, u32[]{:S(2)}) collective-permute-start(bf16[128,2048]{1,0:T(8,128)(2,1)} %get-tuple-element.250), channel_id=1, source_target_pairs={{0,16},{4,20},{8,24},{12,28},{16,0},{20,4},{24,8},{28,12},{1,17},{... | collective-permute-start | bytes 1572872 | tf_op jit(solution)/shard_map/ppermute | solution.py:1149
  557.9 18.9 %collective-permute-start.56 = (bf16[128,2048]{1,0:T(8,128)(2,1)S(1)}, bf16[128,2048]{1,0:T(8,128)(2,1)}, u32[]{:S(2)}, u32[]{:S(2)}) collective-permute-start(bf16[128,2048]{1,0:T(8,128)(2,1)S(1)} %get-tuple-element.249), channel_id=1, source_target_pairs={{0,8},{4,12},{8,0},{12,4},{16,24},{20,28},{24,16},{28,20},{1,9},{5... | collective-permute-start | bytes 1572872 | tf_op jit(solution)/shard_map/ppermute | solution.py:1149
  558.5 18.3 %collective-permute-start.57 = (bf16[128,2048]{1,0:T(8,128)(2,1)S(1)}, bf16[128,2048]{1,0:T(8,128)(2,1)}, u32[]{:S(2)}, u32[]{:S(2)}) collective-permute-start(bf16[128,2048]{1,0:T(8,128)(2,1)S(1)} %get-tuple-element.248), channel_id=1, source_target_pairs={{0,16},{4,20},{8,24},{12,28},{16,0},{20,4},{24,8},{28,12},{1,17},{... | collective-permute-start | bytes 1572872 | tf_op jit(solution)/shard_map/ppermute | solution.py:1149
  576.8 46.5 %all-to-all-start.4 = ((bf16[4,576,128]{2,1,0:T(8,128)(2,1)}), bf16[4,576,128]{2,1,0:T(8,128)(2,1)S(1)}, u32[]{:S(2)}, u32[]{:S(2)}) async-start(bf16[4,576,128]{2,1,0:T(8,128)(2,1)} %constant_dynamic-update-slice_fusion), calls=%async_computation.5 | async-start | bytes 1179648 | tf_op jit(solution)/shard_map/all_to_all | solution.py:1210
  580.3 25.7 %collective-permute-start.60 = (f32[352,128]{1,0:T(8,128)S(1)}, f32[352,128]{1,0:T(8,128)S(1)}, u32[]{:S(2)}, u32[]{:S(2)}) collective-permute-start(f32[352,128]{1,0:T(8,128)S(1)} %slice.332), channel_id=1, source_target_pairs={{0,0},{1,8},{2,16},{3,24},{4,1},{5,9},{6,17},{7,25},{8,2},{9,10},{... | collective-permute-start | bytes 540680 | tf_op jit(solution)/shard_map/ppermute | solution.py:1244
  582.3 23.7 %collective-permute-start.61 = (f32[176,128]{1,0:T(8,128)S(1)}, f32[176,128]{1,0:T(8,128)S(1)}, u32[]{:S(2)}, u32[]{:S(2)}) collective-permute-start(f32[176,128]{1,0:T(8,128)S(1)} %slice.333), channel_id=1, source_target_pairs={{0,0},{1,1},{2,16},{3,17},{4,2},{5,3},{6,18},{7,19},{8,4},{9,5},{1... | collective-permute-start | bytes 270344 | tf_op jit(solution)/shard_map/ppermute | solution.py:1244
  606.0 11.0 %collective-permute-start.59 = (f32[256,128]{1,0:T(8,128)}, f32[256,128]{1,0:T(8,128)S(1)}, u32[]{:S(2)}, u32[]{:S(2)}) collective-permute-start(f32[256,128]{1,0:T(8,128)} %bitcast.163), channel_id=1, source_target_pairs={{0,0},{1,8},{2,16},{3,24},{4,1},{5,9},{6,17},{7,25},{8,2},{9,10},{... | collective-permute-start | bytes 393224 | tf_op jit(solution)/shard_map/ppermute | solution.py:1244
  (56 other events, 699.1 us)
Sparse Core Ops, SparseCore 0:
  438.4 26.2 reduce-scatter.2
  532.1 20.4 reduce-scatter.4
